TPU v7x, 32 devices: a whole 2x2x4 slice. The times are simulated.
32 devices in a mesh: rcv: 2 (over x), shot: 16 (over z, y, core).
Axes of the slice: x: 2, y: 2, z: 4, core: 2. Of those that a mesh axis runs over, the one named last changes fastest.
Arguments:
- record_data: float32 [16, 16, 128, 256], P(None, 'shot', None, 'rcv'), may hold values from -20 to 20
- offsets: int32 [256], replicated, may hold values from 0 to 240, as said below
- thresholds: float32 [128], replicated, may hold values from 0.3 to 1.5
Outputs:
- model: bfloat16 [256, 4, 128, 256], P('shot', None, None, 'rcv')
- residual: float32 [16, 16, 128, 256], P(None, 'shot', None, 'rcv')
Inputs may be any that keep to these rules, and one draw needn't show every extreme that they name: offsets[s] + 3 < 256. Shot s belongs to shot group s // 16. Among the blocks of the 16 shots of one group, at most 6 land on record blocks of one owner (block g belongs to owner g % 16), and those cover at most 3 distinct record blocks; every group reaches both bounds at some owner.
All inputs are finite; a program needn't handle non-finite values.
Results may differ from a plain program's by a relative error of at most 0.0087.
Values may be sent and summed in bfloat16 or wider, within the bound.
No kernel may reach another device: no remote copies, remote signals or barrier semaphores. Data moves between devices by JAX's collectives and lax.ppermute only.
A program may use at most 64 MiB of HBM per device.

v0:
```python
import jax
import jax.numpy as jnp
from jax import lax
from jax.sharding import PartitionSpec as P

SHOT_BLK = 4


momentum = 0.5
epsilon = 1e-06


def cosine_table(length):
    rows = jnp.arange(length, dtype=jnp.float32)[:, None]
    cols = jnp.arange(length, dtype=jnp.float32)[None, :]
    table = jnp.cos(jnp.pi * (cols + 0.5) * rows / length) * jnp.sqrt(2.0 / length)
    return jnp.where(rows == 0, table * jnp.sqrt(0.5), table)


def analysis(table, values):
    return jnp.einsum("kn,sbnr->sbkr", table, values, precision=lax.Precision.HIGHEST)


def synthesis(table, coefficients):
    return jnp.einsum("kn,sbkr->sbnr", table, coefficients, precision=lax.Precision.HIGHEST)


def segment_targets(active_emitters, holding_processors, emitter_segment):
    segment_traversals = jnp.arange(emitter_segment, dtype=jnp.int32)
    assigned_segments = (active_emitters[:, None] + segment_traversals[None, :]).reshape(-1)
    owner_of = assigned_segments % holding_processors
    window_of = assigned_segments // holding_processors
    position = jnp.arange(assigned_segments.shape[0], dtype=jnp.int32)
    earlier = position[None, :] < position[:, None]
    same_owner = owner_of[:, None] == owner_of[None, :]
    slot_raw = jnp.sum(jnp.where(same_owner & earlier, 1, 0), axis=1).astype(jnp.int32)
    same_block = assigned_segments[:, None] == assigned_segments[None, :]
    leading = jnp.sum(jnp.where(same_block & earlier, 1, 0), axis=1) == 0
    below = assigned_segments[None, :] < assigned_segments[:, None]
    slot_record = jnp.sum(jnp.where(same_owner & below & leading[None, :], 1, 0), axis=1).astype(
        jnp.int32
    )
    return (owner_of, window_of, slot_raw, slot_record)


def local(record_data, offsets, thresholds):
    holding_processors = lax.axis_size("shot")
    groups = lax.axis_size("rcv")
    myself = lax.axis_index("shot")
    windows = record_data.shape[0]
    block_len = record_data.shape[2]
    rcv_dev = record_data.shape[3]
    feature = block_len * rcv_dev
    shot_dev = offsets.shape[0] // holding_processors
    emitter_segment = SHOT_BLK
    pair_count = shot_dev // 2
    pair_slots = min(pair_count, holding_processors // (emitter_segment + 1))
    rounds = (pair_count + pair_slots - 1) // pair_slots
    capacity = 2 * rounds
    receivers = rcv_dev * groups

    def target_cluster(active_emitters):
        return segment_targets(active_emitters, holding_processors, emitter_segment)

    all_owner, all_window, all_raw, all_record = jax.vmap(target_cluster)(
        offsets.reshape(holding_processors, shot_dev)
    )
    my_owner = all_owner[myself]
    my_raw = all_raw[myself]
    my_record = all_record[myself]
    landed = all_owner == myself
    source = jnp.broadcast_to(
        jnp.arange(holding_processors, dtype=jnp.int32)[:, None], all_owner.shape
    )
    raw_table = (
        jnp.full((holding_processors, capacity), -1, jnp.int32)
        .at[source, jnp.where(landed, all_raw, capacity)]
        .set(all_window, mode="drop")
    )
    record_table = (
        jnp.full((holding_processors, rounds), -1, jnp.int32)
        .at[source, jnp.where(landed, all_record, rounds)]
        .set(all_window, mode="drop")
    )
    window_ids = jnp.arange(windows, dtype=jnp.int32)
    coverage = jnp.sum(
        jnp.where(
            landed[:, :, None] & (all_window[:, :, None] == window_ids[None, None, :]), 1.0, 0.0
        ),
        axis=(0, 1),
    )
    precondition = (1.0 / jnp.maximum(coverage, 1.0))[:, None]
    records = record_data.reshape(windows, feature)
    table = cosine_table(block_len)

    def spread(values):
        slot_table = raw_table.reshape(-1)
        one_hot = (slot_table[:, None] == window_ids[None, :]).astype(jnp.bfloat16)
        outgoing = jnp.dot(one_hot, values, preferred_element_type=jnp.float32).astype(jnp.bfloat16)
        returned = lax.all_to_all(outgoing, "shot", split_axis=0, concat_axis=0, tiled=True)
        picked = returned[my_owner * capacity + my_raw]
        return picked.astype(jnp.float32).reshape(shot_dev, emitter_segment, block_len, rcv_dev)

    def shrink(coefficients):
        partial_value = jnp.sum(coefficients * coefficients, axis=(1, 3))
        energy = lax.psum(partial_value, "rcv")
        cutoff = (thresholds[None, :] * jnp.sqrt(energy / (emitter_segment * receivers) + epsilon))[
            :, None, :, None
        ]
        return coefficients - jnp.clip(coefficients, -cutoff, cutoff)

    first_spread = (records * precondition).astype(jnp.bfloat16)
    first_update = spread(first_spread)
    first_shrunk = shrink(analysis(table, first_update))
    first_model = synthesis(table, first_shrunk)
    sent_blocks = first_model.astype(jnp.bfloat16).reshape(shot_dev * emitter_segment, feature)
    target_slot = my_owner * rounds + my_record
    slot_ids = jnp.arange(holding_processors * rounds, dtype=jnp.int32)
    collect_hot = (slot_ids[:, None] == target_slot[None, :]).astype(jnp.bfloat16)
    outgoing = jnp.dot(collect_hot, sent_blocks, preferred_element_type=jnp.float32).astype(
        jnp.bfloat16
    )
    arrived = lax.all_to_all(outgoing, "shot", split_axis=0, concat_axis=0, tiled=True)
    gather_hot = (window_ids[:, None] == record_table.reshape(-1)[None, :]).astype(jnp.bfloat16)
    blended = jnp.dot(gather_hot, arrived, preferred_element_type=jnp.float32)
    residual = records - (1.0 + momentum) * blended
    second_spread = (residual * precondition).astype(jnp.bfloat16)
    second_update = (1.0 + momentum) * first_model + spread(second_spread)
    second_coefficients = analysis(table, second_update)
    model = synthesis(table, shrink(second_coefficients)).astype(jnp.bfloat16)
    return (model, residual.reshape(windows, 1, block_len, rcv_dev))


def solution(mesh):
    return jax.shard_map(
        local,
        mesh=mesh,
        in_specs=(P(None, "shot", None, "rcv"), P(), P()),
        out_specs=(P("shot", None, None, "rcv"), P(None, "shot", None, "rcv")),
        check_vma=False,
    )
```

profile of v0, /device:TPU:16, one launch (start us, length us, event | category | flops | bytes accessed | tf_op | source)
XLA Modules:
  0.0 344.4 jit_solution(4696796699778393144)
XLA Ops:
  0.7 0.8 add.185
  1.5 0.1 add.189
  1.9 0.1 select_reduce_fusion.3
  2.0 0.5 select_reduce_fusion.1
  2.5 0.9 select_reduce_fusion
  3.5 0.7 multiply_reduce_fusion
  4.3 0.7 and_reduce_fusion
  5.1 4.3 %scatter_custom_fusion = s32[96]{0:T(128)S(1)} fusion(s32[1024]{0:T(1024)S(1)} %reshape.401, s32[1024]{0:T(1024)S(1)} %reshape.403, s32[]{:T(128)} %constant.26.clone.1), kind=kCustom, calls=%fused_computation.127 | custom fusion | bytes 388
  9.5 0.1 copy.75
  9.6 0.1 eq.142
  9.7 2.3 convolution_convert_fusion.1
  11.9 2.9 all_to_all.24
  14.8 6.2 %all-to-all-start = ((bf16[16,6,16384]{2,1,0:T(8,128)(2,1)}), bf16[16,6,16384]{2,1,0:T(8,128)(2,1)}, u32[]{:S(2)}, u32[]{:S(2)}) async-start(bf16[16,6,16384]{2,1,0:T(8,128)(2,1)} %all_to_all.24), calls=%async_computation | async-start | bytes 8388608 | tf_op jit(solution)/shard_map/all_to_all | solution.py:100
  21.1 92.6 %all-to-all-done = bf16[16,6,16384]{2,1,0:T(8,128)(2,1)} async-done(((bf16[16,6,16384]{2,1,0:T(8,128)(2,1)}), bf16[16,6,16384]{2,1,0:T(8,128)(2,1)}, u32[]{:S(2)}, u32[]{:S(2)}) %all-to-all-start) | async-done | bytes 3145760 | tf_op jit(solution)/shard_map/all_to_all | solution.py:100
  113.7 3.4 all_to_all.26
  117.2 3.2 gather_fusion
  120.4 2.2 copy.85
  122.5 4.2 %fusion.5 = (f32[16,128]{1,0:T(8,128)S(1)}, f32[16,4,128,128]{3,2,1,0:T(8,128)}) fusion(bf16[16,4,128,128]{3,2,1,0:T(8,128)(2,1)S(1)} %bitcast.103, f32[128]{0:T(128)S(1)} %add_multiply_fusion, pred[128]{0:T(512)(128)(4,1)S(1)} %iota_compare_fusion.9), kind=kOutput, calls=%fused_computation.20 | convolution fusion | flops 1612789760 | bytes 6300288 | tf_op jit(solution)/shard_map/kn,sbnr->sbkr/dot_general | solution.py:21
  126.8 5.0 %psum.14 = f32[16,128]{1,0:T(8,128)S(1)} all-reduce(f32[16,128]{1,0:T(8,128)S(1)} %get-tuple-element.29), channel_id=1, replica_groups=mesh['rcv'=2,'shot'=16] {'rcv'}, use_global_device_ids=true, to_apply=%region_4.5 | all-reduce | flops 2048 | bytes 16384 | tf_op jit(solution)/shard_map/psum | solution.py:106
  131.7 5.8 %fusion.7 = f32[16,4,128,128]{3,2,1,0:T(8,128)S(1)} fusion(f32[16,4,128,128]{3,2,1,0:T(8,128)} %get-tuple-element.30, f32[16,128]{1,0:T(8,128)S(1)} %get-tuple-element.22, f32[16,128]{1,0:T(8,128)S(1)} %get-tuple-element.23, f32[128]{0:T(128)S(1)} %add_multiply_fusion, pred[128]{0:T(512)(128)(4,1)S(1)} %iota_compare_fusion.9), kind=kOutput, calls=%fused_computation.22 | convolution fusion | flops 1613840384 | bytes 8405632 | tf_op jit(solution)/shard_map/kn,sbkr->sbnr/dot_general | solution.py:25
  137.5 1.9 copy-done
  139.4 0.4 convert_bitcast_fusion.2
  139.8 2.6 copy.78
  142.4 3.2 convolution_convert_fusion.2
  145.6 1.9 all_to_all.27
  147.5 4.8 %all-to-all-start.1 = ((bf16[16,3,16384]{2,1,0:T(4,128)(2,1)}), bf16[16,3,16384]{2,1,0:T(4,128)(2,1)S(1)}, u32[]{:S(2)}, u32[]{:S(2)}) async-start(bf16[16,3,16384]{2,1,0:T(4,128)(2,1)} %all_to_all.27), calls=%async_computation.1 | async-start | bytes 4194304 | tf_op jit(solution)/shard_map/all_to_all | solution.py:123
  152.4 4.3 %scatter_custom_fusion.1 = s32[48]{0:T(128)S(1)} fusion(s32[1024]{0:T(1024)S(1)} %reshape.407, s32[1024]{0:T(1024)S(1)} %reshape.403, s32[]{:T(128)} %constant.26.clone.1), kind=kCustom, calls=%fused_computation.125 | custom fusion | bytes 196
  156.7 0.1 reshape.382
  156.8 0.1 copy.77
  156.9 0.1 eq.156
  157.0 43.0 %all-to-all-done.1 = bf16[16,3,16384]{2,1,0:T(4,128)(2,1)S(1)} async-done(((bf16[16,3,16384]{2,1,0:T(4,128)(2,1)}), bf16[16,3,16384]{2,1,0:T(4,128)(2,1)S(1)}, u32[]{:S(2)}, u32[]{:S(2)}) %all-to-all-start.1) | async-done | bytes 1572896 | tf_op jit(solution)/shard_map/all_to_all | solution.py:123
  200.0 2.2 all_to_all.29
  202.2 2.2 fusion
  204.4 1.0 copy-done.1
  205.4 1.0 convolution_convert_fusion
  206.4 3.0 all_to_all.30
  209.4 4.8 %all-to-all-start.2 = ((bf16[16,6,16384]{2,1,0:T(8,128)(2,1)}), bf16[16,6,16384]{2,1,0:T(8,128)(2,1)}, u32[]{:S(2)}, u32[]{:S(2)}) async-start(bf16[16,6,16384]{2,1,0:T(8,128)(2,1)} %all_to_all.30), calls=%async_computation.2 | async-start | bytes 8388608 | tf_op jit(solution)/shard_map/all_to_all | solution.py:100
  214.2 1.2 copy.88
  215.4 91.5 %all-to-all-done.2 = bf16[16,6,16384]{2,1,0:T(8,128)(2,1)} async-done(((bf16[16,6,16384]{2,1,0:T(8,128)(2,1)}), bf16[16,6,16384]{2,1,0:T(8,128)(2,1)}, u32[]{:S(2)}, u32[]{:S(2)}) %all-to-all-start.2) | async-done | bytes 3145760 | tf_op jit(solution)/shard_map/all_to_all | solution.py:100
  306.9 3.4 all_to_all.32
  310.3 3.2 gather_fusion.1
  313.5 1.9 convert_bitcast_fusion
  315.4 2.7 copy.87
  318.1 5.3 %copy.79 = f32[16,4,128,128]{2,3,1,0:T(8,128)} copy(f32[16,4,128,128]{3,2,1,0:T(8,128)} %bitcast.100) | data formatting | bytes 8388608 | tf_op jit(solution)/shard_map/convert_element_type | solution.py:102
  323.5 7.6 %fusion.1 = (f32[16,128]{1,0:T(8,128)S(1)}, f32[16,4,128,128]{3,2,1,0:T(8,128)}) fusion(f32[128]{0:T(128)S(1)} %add_multiply_fusion, pred[128]{0:T(512)(128)(4,1)S(1)} %iota_compare_fusion.9, f32[16,4,128,128]{2,3,1,0:T(8,128)} %copy.79, f32[16,4,128,128]{3,2,1,0:T(8,128)} %copy-done), kind=kOutput, calls=%fused_computation.12 | convolution fusion | flops 1614886912 | bytes 12591744 | tf_op jit(solution)/shard_map/kn,sbnr->sbkr/dot_general | solution.py:21
  331.1 5.0 %psum.15 = f32[16,128]{1,0:T(8,128)S(1)} all-reduce(f32[16,128]{1,0:T(8,128)S(1)} %get-tuple-element.31), channel_id=1, replica_groups=mesh['rcv'=2,'shot'=16] {'rcv'}, use_global_device_ids=true, to_apply=%region_9.10 | all-reduce | flops 2048 | bytes 16384 | tf_op jit(solution)/shard_map/psum | solution.py:106
  336.1 5.8 %convert_bitcast_fusion.1 = bf16[16,4,128,128]{2,3,1,0:T(8,128)(2,1)S(1)} fusion(f32[16,4,128,128]{3,2,1,0:T(8,128)} %get-tuple-element.32, f32[16,128]{1,0:T(8,128)S(1)} %get-tuple-element.20, f32[16,128]{1,0:T(8,128)S(1)} %get-tuple-element.21, f32[128]{0:T(128)S(1)} %add_multiply_fusion, pred[128]{0:T(512)(128)(4,1)S(1)} %iota_compare_fusion.9), kind=kOutput, calls=%fused_computation.27 | convolution fusion | flops 1614888960 | bytes 6308480 | tf_op jit(solution)/shard_map/kn,sbkr->sbnr/dot_general | solution.py:25
  341.8 2.6 copy.80
  (33 shorter events, 0.7 us)
Async XLA Ops:
  14.8 98.9 %all-to-all-start = ((bf16[16,6,16384]{2,1,0:T(8,128)(2,1)}), bf16[16,6,16384]{2,1,0:T(8,128)(2,1)}, u32[]{:S(2)}, u32[]{:S(2)}) async-start(bf16[16,6,16384]{2,1,0:T(8,128)(2,1)} %all_to_all.24), calls=%async_computation | async-start | bytes 8388608 | tf_op jit(solution)/shard_map/all_to_all | solution.py:100
  122.5 9.2 %copy-start.4 = (f32[128]{0:T(128)S(1)}, f32[128]{0:T(128)}, u32[]{:S(2)}) copy-start(f32[128]{0:T(128)} %param.5) | copy-start | bytes 1540
  137.5 1.9 copy-start
  147.5 54.7 %copy-start.3 = (f32[16,1,128,128]{3,2,1,0:T(8,128)S(1)}, f32[16,1,128,128]{3,2,1,0:T(8,128)}, u32[]{:S(2)}) copy-start(f32[16,1,128,128]{3,2,1,0:T(8,128)} %param.3) | copy-start | bytes 3145732
  147.5 52.5 %all-to-all-start.1 = ((bf16[16,3,16384]{2,1,0:T(4,128)(2,1)}), bf16[16,3,16384]{2,1,0:T(4,128)(2,1)S(1)}, u32[]{:S(2)}, u32[]{:S(2)}) async-start(bf16[16,3,16384]{2,1,0:T(4,128)(2,1)} %all_to_all.27), calls=%async_computation.1 | async-start | bytes 4194304 | tf_op jit(solution)/shard_map/all_to_all | solution.py:123
  204.4 1.0 copy-start.1
  209.4 4.8 %copy-start.2 = (f32[16,16384]{1,0:T(8,128)S(1)}, f32[16,16384]{1,0:T(8,128)}, u32[]{:S(2)}) copy-start(f32[16,16384]{1,0:T(8,128)} %copy-done.1) | copy-start | bytes 3145732
  209.4 97.5 %all-to-all-start.2 = ((bf16[16,6,16384]{2,1,0:T(8,128)(2,1)}), bf16[16,6,16384]{2,1,0:T(8,128)(2,1)}, u32[]{:S(2)}, u32[]{:S(2)}) async-start(bf16[16,6,16384]{2,1,0:T(8,128)(2,1)} %all_to_all.30), calls=%async_computation.2 | async-start | bytes 8388608 | tf_op jit(solution)/shard_map/all_to_all | solution.py:100
where the time goes:
time: 345 us; the launch traced here: 344 us
  waiting for transfers between devices  227 us (66%)
  local copies, waits for them, and re-layouts  53.1 us (15%)
  matrix products  32 us (9%)
  starting transfers between devices  15.8 us (5%)
  blocking collectives  9.94 us (3%)
  other arithmetic  5.49 us (2%)
    all_to_all x2, waiting for transfers between devices, spread(): lax.all_to_all(outgoing, 'shot', split_axis=0, concat_axis=0, tiled=True)  184 us
    all_to_all x1, waiting for transfers between devices, local(): lax.all_to_all(outgoing, 'shot', split_axis=0, concat_axis=0, tiled=True)  43 us
    unnamed x20, local copies, waits for them, and re-layouts  20.4 us
    all_to_all x4, local copies, waits for them, and re-layouts, spread(): lax.all_to_all(outgoing, 'shot', split_axis=0, concat_axis=0, tiled=True)  12.8 us
    dot_general x2, matrix products, analysis(): jnp.einsum('kn,sbnr->sbkr', table, values, precision=lax.Precision.HIGHEST)  11.8 us
    dot_general x2, matrix products, synthesis(): jnp.einsum('kn,sbkr->sbnr', table, coefficients, precision=lax.Precision....  11.5 us
    all_to_all x2, starting transfers between devices, spread(): lax.all_to_all(outgoing, 'shot', split_axis=0, concat_axis=0, tiled=True)  11 us
    psum x2, blocking collectives, shrink(): energy = lax.psum(partial_value, 'rcv')  9.94 us
  transfers between devices with their start and end apart: 3, of which 3 were waited for; matrix products, arithmetic and copies ran while one was open for 2% of the time, Pallas kernels for 0%

commit v1 on v0

v1 whole, which is shorter than its diff:
```python
import jax
import jax.numpy as jnp
import numpy as np
from jax import lax
from jax.experimental import pallas as pl
from jax.experimental.pallas import tpu as pltpu
from jax.sharding import PartitionSpec as P

SHOT_BLK = 4
momentum = 0.5
epsilon = 1e-06
step_size = 1.0 + momentum
VMEM_BYTES = 48 * 1024 * 1024


def cosine_table(length):
    rows = np.arange(length, dtype=np.float64)[:, None]
    cols = np.arange(length, dtype=np.float64)[None, :]
    table = np.cos(np.pi * (cols + 0.5) * rows / length) * np.sqrt(2.0 / length)
    return np.where(rows == 0, table * np.sqrt(0.5), table).astype(np.float32)


def split_bf16(values):
    high = values.astype(jnp.bfloat16)
    low = (values - high.astype(jnp.float32)).astype(jnp.bfloat16)
    return high, low


def full_vmem():
    return pl.BlockSpec(memory_space=pltpu.VMEM)


def full_smem():
    return pl.BlockSpec(memory_space=pltpu.SMEM)


def params(**kw):
    return pltpu.CompilerParams(vmem_limit_bytes=VMEM_BYTES, **kw)


def forward(high, low, values):
    dims = (((0,), (0,)), ((), ()))
    return lax.dot_general(
        values, high, dims, preferred_element_type=jnp.float32
    ) + lax.dot_general(values, low, dims, preferred_element_type=jnp.float32)


def backward(both, coefficients):
    doubled = jnp.concatenate([coefficients, coefficients], axis=1)
    return lax.dot_general(
        both, doubled, (((1,), (1,)), ((), ())), preferred_element_type=jnp.float32
    )


def head(records, offsets, me, owners, high, low):
    windows, block, rcv = records.shape
    shots = offsets.shape[0]
    step = 8

    def body(me_ref, off_ref, rec_ref, high_ref, low_ref, sent_ref, coef_ref, energy_ref):
        base = pl.program_id(0) * step
        ids = (base + lax.broadcasted_iota(jnp.int32, (step, shots), 0)) * owners + me_ref[0]
        lag = ids - off_ref[...]
        cover = jnp.sum(
            jnp.where((lag >= 0) & (lag < SHOT_BLK), 1.0, 0.0), axis=1, keepdims=True
        )
        scale = 1.0 / jnp.maximum(cover, 1.0)
        for w in range(step):
            spread = (rec_ref[w] * scale[w : w + 1, 0:1]).astype(jnp.bfloat16)
            coef = forward(high_ref[...], low_ref[...], spread)
            coef_ref[w] = coef
            sent_ref[w] = coef.astype(jnp.bfloat16)
            energy_ref[w : w + 1, :] = jnp.sum(coef * coef, axis=0, keepdims=True)

    return pl.pallas_call(
        body,
        grid=(windows // step,),
        in_specs=[
            full_smem(),
            full_vmem(),
            pl.BlockSpec((step, block, rcv), lambda i: (i, 0, 0)),
            full_vmem(),
            full_vmem(),
        ],
        out_specs=[
            pl.BlockSpec((step, rcv, block), lambda i: (i, 0, 0)),
            pl.BlockSpec((step, rcv, block), lambda i: (i, 0, 0)),
            pl.BlockSpec((step, block), lambda i: (i, 0)),
        ],
        out_shape=[
            jax.ShapeDtypeStruct((windows, rcv, block), jnp.bfloat16),
            jax.ShapeDtypeStruct((windows, rcv, block), jnp.float32),
            jax.ShapeDtypeStruct((windows, block), jnp.float32),
        ],
        compiler_params=params(),
        name="analysis_of_records",
    )(me[None], offsets[None, :], records, high, low)


def pack(table, sent, energy, owners, capacity):
    windows, rcv, block = sent.shape
    rows = capacity * rcv + 2 * windows
    step = 4

    def body(table_ref, sent_ref, energy_ref, out_ref):
        first = pl.program_id(0) * step
        high, low = split_bf16(energy_ref[...])
        for h in range(step):
            for i in range(capacity):
                window = table_ref[(first + h) * capacity + i]
                out_ref[h, i * rcv : (i + 1) * rcv, :] = sent_ref[window]
            out_ref[h, capacity * rcv : capacity * rcv + windows, :] = high
            out_ref[h, capacity * rcv + windows : rows, :] = low

    return pl.pallas_call(
        body,
        grid=(owners // step,),
        in_specs=[full_smem(), full_vmem(), full_vmem()],
        out_specs=pl.BlockSpec((step, rows, block), lambda i: (i, 0, 0)),
        out_shape=jax.ShapeDtypeStruct((owners, rows, block), jnp.bfloat16),
        compiler_params=params(),
        name="pack_blocks",
    )(table, sent, energy)


def clipped_sum(coef, cut_ref, low, high):
    def add(row, total):
        cut = cut_ref[row][None]
        return total + jnp.minimum(jnp.maximum(coef, -cut), cut)

    return lax.fori_loop(low, high, add, jnp.zeros_like(coef))


def second(arrived, hits, thresholds, lows, highs, scales, slots, capacity, windows, receivers):
    owners, rows, block = arrived.shape
    rcv = (rows - 2 * windows) // capacity
    tiles = rcv // 8
    shot_dev = slots.shape[0] // SHOT_BLK
    shots = hits.shape[0] - shot_dev
    step = min(4, shot_dev)
    count = owners * capacity

    def body(
        low_ref, high_ref, scale_ref, slot_ref, in_ref, hit_ref, thr_ref,
        out_ref, energy_ref, cuts_ref, wide_ref, diff_ref,
    ):
        def block_of(slot):
            owner = slot // capacity
            start = pl.multiple_of((slot - owner * capacity) * rcv, rcv)
            values = in_ref[owner, pl.ds(start, rcv), :].astype(jnp.float32)
            return values.reshape(tiles, 8, block)

        @pl.when(pl.program_id(0) == 0)
        def _():
            at = capacity * rcv
            both = jnp.concatenate(
                [
                    in_ref[:, at : at + windows, :].reshape(owners * windows, block),
                    in_ref[:, at + windows :, :].reshape(owners * windows, block),
                ],
                axis=1,
            )
            sums = jnp.dot(hit_ref[...], both, preferred_element_type=jnp.float32)
            energy = sums[:, :block] + sums[:, block:]
            cuts_ref[...] = thr_ref[...] * jnp.sqrt(energy / (SHOT_BLK * receivers) + epsilon)

            def widen(i, _):
                part = cuts_ref[pl.ds(pl.multiple_of(i * 8, 8), 8), :]
                wide_ref[pl.ds(pl.multiple_of(i * 8, 8), 8)] = jnp.broadcast_to(
                    part[:, None, :], (8, 8, block)
                )
                return 0

            lax.fori_loop(0, (shots + shot_dev) // 8, widen, 0)

            def difference(slot, _):
                low, high = low_ref[slot], high_ref[slot]
                coef = block_of(slot)
                clipped = clipped_sum(coef, wide_ref, low, high)
                many = (high - low).astype(jnp.float32)
                diff_ref[slot] = coef - scale_ref[slot] * (many * coef - clipped)
                return 0

            lax.fori_loop(0, count, difference, 0)

        def one_shot(i, _):
            shot = pl.program_id(0) * step + i
            cut = wide_ref[shots + shot][None]
            energy = jnp.zeros((8, block), jnp.float32)
            for q in range(SHOT_BLK):
                slot = slot_ref[shot * SHOT_BLK + q]
                coef = block_of(slot)
                shrunk = coef - jnp.minimum(jnp.maximum(coef, -cut), cut)
                value = step_size * shrunk + diff_ref[slot]
                out_ref[i, q] = value.reshape(rcv, block)
                energy = energy + jnp.sum(value * value, axis=0)
            energy_ref[pl.ds(shot, 1), :] = jnp.sum(energy, axis=0, keepdims=True)
            return 0

        lax.fori_loop(0, step, one_shot, 0)

    return pl.pallas_call(
        body,
        grid=(shot_dev // step,),
        in_specs=[full_smem()] * 4 + [full_vmem()] * 3,
        out_specs=[
            pl.BlockSpec((step, SHOT_BLK, rcv, block), lambda i: (i, 0, 0, 0)),
            full_vmem(),
            full_vmem(),
        ],
        out_shape=[
            jax.ShapeDtypeStruct((shot_dev, SHOT_BLK, rcv, block), jnp.float32),
            jax.ShapeDtypeStruct((shot_dev, block), jnp.float32),
            jax.ShapeDtypeStruct((shots + shot_dev, block), jnp.float32),
        ],
        scratch_shapes=[
            pltpu.VMEM((shots + shot_dev, 8, block), jnp.float32),
            pltpu.VMEM((count, tiles, 8, block), jnp.float32),
        ],
        compiler_params=params(),
        cost_estimate=pl.CostEstimate(flops=1, bytes_accessed=12 << 20, transcendentals=0),
        name="second_coefficients",
    )(lows, highs, scales, slots, arrived, hits, thresholds)


def remainder(records, coefs, cuts, lows, highs, both):
    windows, block, rcv = records.shape
    shots = cuts.shape[0]
    tiles = rcv // 8
    step = 4

    def body(low_ref, high_ref, rec_ref, coef_ref, cuts_ref, both_ref, out_ref, wide_ref):
        @pl.when(pl.program_id(0) == 0)
        def _():
            def widen(i, _):
                part = cuts_ref[pl.ds(pl.multiple_of(i * 8, 8), 8), :]
                wide_ref[pl.ds(pl.multiple_of(i * 8, 8), 8)] = jnp.broadcast_to(
                    part[:, None, :], (8, 8, block)
                )
                return 0

            lax.fori_loop(0, shots // 8, widen, 0)

        for w in range(step):
            window = pl.program_id(0) * step + w
            low, high = low_ref[window], high_ref[window]
            coef = coef_ref[w].reshape(tiles, 8, block)
            clipped = clipped_sum(coef, wide_ref, low, high)
            shrunk = ((high - low).astype(jnp.float32) * coef - clipped).reshape(rcv, block)
            part, rest = split_bf16(shrunk)
            blended = backward(both_ref[...], part) + lax.dot_general(
                both_ref[:, :block], rest, (((1,), (1,)), ((), ())),
                preferred_element_type=jnp.float32,
            )
            out_ref[w] = rec_ref[w] - step_size * blended

    return pl.pallas_call(
        body,
        grid=(windows // step,),
        in_specs=[
            full_smem(),
            full_smem(),
            pl.BlockSpec((step, block, rcv), lambda i: (i, 0, 0)),
            pl.BlockSpec((step, rcv, block), lambda i: (i, 0, 0)),
            full_vmem(),
            full_vmem(),
        ],
        out_specs=pl.BlockSpec((step, block, rcv), lambda i: (i, 0, 0)),
        out_shape=jax.ShapeDtypeStruct((windows, block, rcv), jnp.float32),
        scratch_shapes=[pltpu.VMEM((shots, 8, block), jnp.float32)],
        compiler_params=params(),
        cost_estimate=pl.CostEstimate(flops=1, bytes_accessed=6 << 20, transcendentals=0),
        name="residual_of_records",
    )(lows, highs, records, coefs, cuts, both)


def finish(values, energies, thresholds, both, receivers):
    shot_dev, _, rcv, block = values.shape
    step = min(4, shot_dev)

    def body(*refs):
        in_ref, thr_ref, both_ref = refs[:3]
        out_ref = refs[-1]
        energy = refs[3][...]
        for ref in refs[4:-1]:
            energy = energy + ref[...]
        cuts = thr_ref[...] * jnp.sqrt(energy / (SHOT_BLK * receivers) + epsilon)
        for i in range(step):
            cut = cuts[i : i + 1, :]
            for q in range(SHOT_BLK):
                value = in_ref[i, q]
                shrunk = value - jnp.minimum(jnp.maximum(value, -cut), cut)
                out_ref[i, q] = backward(both_ref[...], shrunk.astype(jnp.bfloat16)).astype(
                    jnp.bfloat16
                )

    shape = (shot_dev // step, step, block)
    energies = [energy.reshape(shape) for energy in energies]
    return pl.pallas_call(
        body,
        grid=(shot_dev // step,),
        in_specs=[
            pl.BlockSpec((step, SHOT_BLK, rcv, block), lambda i: (i, 0, 0, 0)),
            full_vmem(),
            full_vmem(),
        ]
        + [pl.BlockSpec((None, step, block), lambda i: (i, 0, 0))] * len(energies),
        out_specs=pl.BlockSpec((step, SHOT_BLK, block, rcv), lambda i: (i, 0, 0, 0)),
        out_shape=jax.ShapeDtypeStruct((shot_dev, SHOT_BLK, block, rcv), jnp.bfloat16),
        compiler_params=params(),
        name="model_of_shots",
    )(values, thresholds, both, *energies)


def over_receivers(values):
    if lax.axis_size("rcv") == 2:
        return [values, lax.ppermute(values, "rcv", [(0, 1), (1, 0)])]
    return [lax.psum(values, "rcv")]


def local(record_data, offsets, thresholds):
    owners = lax.axis_size("shot")
    me = lax.axis_index("shot")
    windows, _, block, rcv = record_data.shape
    shots = offsets.shape[0]
    shot_dev = shots // owners
    pairs = shot_dev // 2
    pair_slots = min(pairs, owners // (SHOT_BLK + 1))
    capacity = (pairs + pair_slots - 1) // pair_slots
    receivers = rcv * lax.axis_size("rcv")

    table = jnp.asarray(cosine_table(block).T)
    high, low = split_bf16(table)
    both = jnp.concatenate([high, low], axis=1)
    records = record_data.reshape(windows, block, rcv)
    thr = thresholds[None, :]
    window_ids = jnp.arange(windows, dtype=jnp.int32)

    sent, coefs, energy = head(records, offsets, me, owners, high, low)
    energy = sum(over_receivers(energy))

    def ranks(present, axis):
        before = (window_ids[:, None] < window_ids[None, :]).astype(jnp.int32)
        return jnp.sum(present[..., :, None] * before, axis=axis)

    own_ids = window_ids * owners + me
    lag = own_ids[None, None, :] - offsets.reshape(owners, shot_dev)[:, :, None]
    present = jnp.max(((lag >= 0) & (lag < SHOT_BLK)).astype(jnp.int32), axis=1)
    rank = ranks(present, 1)
    slot_ids = jnp.arange(capacity, dtype=jnp.int32)
    chosen = (rank[:, None, :] == slot_ids[None, :, None]) & (present[:, None, :] > 0)
    send_table = jnp.sum(jnp.where(chosen, window_ids[None, None, :], 0), axis=2)
    packed = pack(send_table.reshape(-1), sent, energy, owners, capacity)
    arrived = lax.all_to_all(packed, "shot", split_axis=0, concat_axis=0, tiled=True)

    index = jnp.arange(shots, dtype=jnp.int32)
    ahead = (offsets[None, :] < offsets[:, None]) | (
        (offsets[None, :] == offsets[:, None]) & (index[None, :] < index[:, None])
    )
    place = jnp.sum(ahead.astype(jnp.int32), axis=1)
    ordered = jnp.sum(jnp.where(place[None, :] == index[:, None], offsets[None, :], 0), axis=1)
    mine = lax.dynamic_slice(offsets, (me * shot_dev,), (shot_dev,))
    all_offsets = jnp.concatenate([ordered, mine])
    grid_ids = (
        window_ids[None, :] * owners + jnp.arange(owners, dtype=jnp.int32)[:, None]
    )
    hit = grid_ids.reshape(-1)[None, :] - all_offsets[:, None]
    hits = ((hit >= 0) & (hit < SHOT_BLK)).astype(jnp.bfloat16)

    def bounds(ids):
        below = jnp.sum((offsets < ids[..., None] - (SHOT_BLK - 1)).astype(jnp.int32), axis=-1)
        upto = jnp.sum((offsets <= ids[..., None]).astype(jnp.int32), axis=-1)
        return below, upto

    near = grid_ids[:, :, None] - mine[None, None, :]
    held = jnp.max(((near >= 0) & (near < SHOT_BLK)).astype(jnp.int32), axis=2)
    held_rank = ranks(held, 1)
    taken = (held_rank[:, None, :] == slot_ids[None, :, None]) & (held[:, None, :] > 0)
    held_ids = jnp.sum(jnp.where(taken, grid_ids[:, None, :], 0), axis=2)
    valid = jnp.sum(taken.astype(jnp.int32), axis=2)
    lows, highs = bounds(held_ids)
    lows, highs = lows * valid, highs * valid
    scales = step_size / jnp.maximum((highs - lows).astype(jnp.float32), 1.0)
    targets = mine[:, None] + jnp.arange(SHOT_BLK, dtype=jnp.int32)[None, :]
    slot_of = jnp.arange(owners, dtype=jnp.int32)[:, None] * capacity + held_rank
    slots = jnp.sum(
        jnp.where(targets[:, :, None, None] == grid_ids[None, None], slot_of[None, None], 0),
        axis=(2, 3),
    )
    own_lows, own_highs = bounds(own_ids)

    values, energy2, cuts = second(
        arrived, hits, thr, lows.reshape(-1), highs.reshape(-1), scales.reshape(-1),
        slots.reshape(-1), capacity, windows, receivers,
    )
    energies = over_receivers(energy2)
    residual = remainder(records, coefs, cuts, own_lows, own_highs, both)
    model = finish(values, energies, thr, both, receivers)
    return (model, residual.reshape(windows, 1, block, rcv))


def solution(mesh):
    return jax.shard_map(
        local,
        mesh=mesh,
        in_specs=(P(None, "shot", None, "rcv"), P(), P()),
        out_specs=(P("shot", None, None, "rcv"), P(None, "shot", None, "rcv")),
        check_vma=False,
    )
```

time: 345 us -> 75.2 us (0.22)
  waiting for transfers between devices: 227 us -> 36.3 us
  local copies, waits for them, and re-layouts: 53.1 us -> 6.61 us
  matrix products: 32 us -> 0 us
  Pallas kernels: 0 us -> 18.3 us
  blocking collectives: 9.94 us -> 0 us
  starting transfers between devices: 15.8 us -> 8.89 us
    all_to_all x3 -> x1, waiting for transfers between devices: 227 us -> 36.3 us  [local(): lax.all_to_all(packed, 'shot', split_axis=0, concat_axis=0, tiled=True)]
    dot_general x8 -> x0, matrix products: 32 us -> none  [the longest x2 11.8 us: analysis(): jnp.einsum('kn,sbnr->sbkr', table, values, precision=lax.Precision.HIGHEST)]
    pallas_call x0 -> x5, Pallas kernels: none -> 18.3 us  [the longest x1 6.58 us: second(): pl.pallas_call(body, grid=(shot_dev // step,), in_specs=[full_smem()] * 4...]
    all_to_all x6 -> x0, local copies, waits for them, and re-layouts: 16.9 us -> none  [the longest x4 12.8 us: spread(): lax.all_to_all(outgoing, 'shot', split_axis=0, concat_axis=0, tiled=True)]
    unnamed x20, local copies, waits for them, and re-layouts: 20.4 us -> 4.4 us
    psum x2 -> x0, blocking collectives: 9.94 us -> none  [shrink(): energy = lax.psum(partial_value, 'rcv')]
    all_to_all x3 -> x1, starting transfers between devices: 15.8 us -> 6.33 us  [local(): lax.all_to_all(packed, 'shot', split_axis=0, concat_axis=0, tiled=True)]
    convert_element_type x2 -> x0, local copies, waits for them, and re-layouts: 7.94 us -> none  [the longest x1 5.34 us: spread(): picked.astype(jnp.float32)]
  transfers between devices with their start and end apart: 3 -> 3, of which waited for: 3 -> 1; matrix products, arithmetic and copies ran while one was open for 2% -> 8% of each run, Pallas kernels for 0% -> 7%
where the time goes in v1:
time: 75.2 us; the launch traced here: 74.3 us
  waiting for transfers between devices  36.3 us (48%)
  Pallas kernels  18.3 us (24%)
  starting transfers between devices  8.89 us (12%)
  local copies, waits for them, and re-layouts  6.61 us (9%)
  other arithmetic  3.41 us (5%)
  between operations  0.81 us (1%)
    all_to_all x1, waiting for transfers between devices, local(): lax.all_to_all(packed, 'shot', split_axis=0, concat_axis=0, tiled=True)  36.3 us
    pallas_call x1, Pallas kernels, second(): pl.pallas_call(body, grid=(shot_dev // step,), in_specs=[full_smem()] * 4...  6.58 us
    all_to_all x1, starting transfers between devices, local(): lax.all_to_all(packed, 'shot', split_axis=0, concat_axis=0, tiled=True)  6.33 us
    pallas_call x1, Pallas kernels, remainder(): pl.pallas_call(body, grid=(windows // step,), in_specs=[full_smem(), full...  5.53 us
    unnamed x20, local copies, waits for them, and re-layouts  4.4 us
    pallas_call x1, Pallas kernels, finish(): pl.pallas_call(body, grid=(shot_dev // step,), in_specs=[pl.BlockSpec((st...  2.98 us
    ppermute x2, starting transfers between devices, over_receivers(): return [values, lax.ppermute(values, 'rcv', [(0, 1), (1, 0)])]  2.57 us
    pallas_call x1, Pallas kernels, pack(): pl.pallas_call(body, grid=(owners // step,), in_specs=[full_smem(), full_...  2.29 us
  transfers between devices with their start and end apart: 3, of which 1 were waited for; matrix products, arithmetic and copies ran while one was open for 8% of the time, Pallas kernels for 7%

profile of v1, /device:TPU:16, one launch (start us, length us, event | category | flops | bytes accessed | tf_op | source)
XLA Modules:
  0.0 74.3 jit_solution(11478795568540991221)
XLA Ops:
  0.6 0.0 copy-start
  0.6 1.2 %copy-done = f32[16,1,128,128]{3,2,1,0:T(8,128)S(1)} copy-done((f32[16,1,128,128]{3,2,1,0:T(8,128)S(1)}, f32[16,1,128,128]{3,2,1,0:T(8,128)}, u32[]{:S(2)}) %copy-start) | copy-done | bytes 1048600
  1.9 0.0 copy-start.5
  1.9 0.7 copy-done.5
  2.5 0.0 copy-start.7
  2.5 0.8 %copy-done.7 = bf16[128,128]{1,0:T(8,128)(2,1)S(1)} copy-done((bf16[128,128]{1,0:T(8,128)(2,1)S(1)}, bf16[128,128]{1,0:T(8,128)(2,1)}, u32[]{:S(2)}) %copy-start.7) | copy-done | bytes 32792
  3.3 0.8 %copy-done.8 = bf16[128,128]{1,0:T(8,128)(2,1)S(1)} copy-done((bf16[128,128]{1,0:T(8,128)(2,1)S(1)}, bf16[128,128]{1,0:T(8,128)(2,1)}, u32[]{:S(2)}) %copy-start.8) | copy-done | bytes 32792
  4.1 0.9 %analysis_of_records.1 = (bf16[16,128,128]{2,1,0:T(8,128)(2,1)S(1)}, f32[16,128,128]{2,1,0:T(8,128)S(1)}, f32[16,128]{1,0:T(8,128)S(1)}) custom-call(s32[1]{0:T(128)} %bitcast.me_ref, s32[1,256]{1,0:T(1,128)S(1)} %bitcast.11, f32[16,128,128]{2,1,0:T(8,128)S(1)} %bitcast.9, bf16[128,128]{1,0:T(8,128)(2,1)S(1)} %copy-done.8, bf16[128,128]{1,0:T(8,128)(2,1)S(1)} %copy-done.7), custom_call_target="tpu_custom_call" | custom-call | tf_op jit(solution)/shard_map/analysis_of_records/pallas_call | solution.py:75
  5.0 0.0 copy-start.2
  5.0 1.0 %copy-done.2 = f32[16,128,128]{2,1,0:T(8,128)} copy-done((f32[16,128,128]{2,1,0:T(8,128)}, f32[16,128,128]{2,1,0:T(8,128)S(1)}, u32[]{:S(2)}) %copy-start.2) | copy-done | bytes 1048600
  5.9 1.5 %collective-permute-start = (f32[16,128]{1,0:T(8,128)S(1)}, f32[16,128]{1,0:T(8,128)S(1)}, u32[]{:S(2)}, u32[]{:S(2)}) collective-permute-start(f32[16,128]{1,0:T(8,128)S(1)} %get-tuple-element.9), channel_id=1, source_target_pairs={{0,16},{16,0},{1,17},{17,1},{2,18},{18,2},{3,19},{19,3},{4,20},{20... | collective-permute-start | bytes 24584 | tf_op jit(solution)/shard_map/ppermute | solution.py:317
  7.4 0.8 %sub.61 = s32[16,16]{1,0:T(8,128)S(1)} reshape(s32[256]{0:T(256)} %param.5) | data formatting | bytes 2048 | tf_op jit(solution)/shard_map/sub | solution.py:347
  8.2 0.8 %dynamic_slice.3 = s32[16]{0:T(128)S(1)} dynamic-slice(s32[256]{0:T(256)} %param.5, s32[]{:T(128)S(6)} %select_n.19), dynamic_slice_sizes={16} | dynamic-slice | bytes 132 | tf_op jit(solution)/shard_map/dynamic_slice | solution.py:362
  9.0 0.1 convert_reduce_fusion.1
  9.1 0.4 convert_reduce_fusion.2
  9.5 0.1 multiply_reduce_fusion
  9.7 0.1 select_reduce_fusion.2
  9.8 0.1 copy.10
  9.9 0.1 reshape.202.table_ref
  10.0 0.0 collective-permute-done
  10.1 2.3 %pack_blocks.1 = bf16[16,416,128]{2,1,0:T(8,128)(2,1)} custom-call(s32[48]{0:T(128)S(1)} %reshape.202.table_ref, bf16[16,128,128]{2,1,0:T(8,128)(2,1)S(1)} %get-tuple-element.8.sent_ref, f32[16,128]{1,0:T(8,128)S(1)} %add.130.energy_ref), custom_call_target="tpu_custom_call" | custom-call | tf_op jit(solution)/shard_map/pack_blocks/pallas_call | solution.py:115
  12.4 6.3 %all-to-all-start = ((bf16[16,416,128]{2,1,0:T(8,128)(2,1)}), bf16[16,416,128]{2,1,0:T(8,128)(2,1)S(1)}, u32[]{:S(2)}, u32[]{:S(2)}) async-start(bf16[16,416,128]{2,1,0:T(8,128)(2,1)} %pack_blocks.1), calls=%async_computation | async-start | bytes 3407872 | tf_op jit(solution)/shard_map/all_to_all | solution.py:354
  18.7 0.1 add.131
  18.8 0.1 iota_add_fusion
  18.8 0.1 broadcast_add_fusion
  18.9 1.3 %select_reduce_fusion = s32[16,4]{1,0:T(8,128)S(1)} fusion(s32[16,16]{1,0:T(8,128)S(1)} %broadcast_add_fusion, s32[16,16]{1,0:T(8,128)S(1)} %iota_add_fusion.1, s32[16,4]{1,0:T(8,128)S(1)} %iota_add_fusion), kind=kLoop, calls=%fused_computation | loop fusion | flops 49088 | bytes 2560 | tf_op jit(solution)/shard_map/reduce_sum | solution.py:386
  20.2 0.1 reshape.201.slot_ref
  20.3 0.2 convert_reduce_fusion.5
  20.5 0.0 copy-done.6
  20.5 0.3 convert_reduce_fusion.3
  20.8 0.1 copy.9
  20.9 0.1 mul.89.high_ref
  21.0 0.1 copy.8
  21.0 0.1 mul.87.low_ref
  21.1 0.2 convert_reduce_fusion
  21.3 0.1 select_reduce_fusion.1
  21.5 0.1 fusion.1.hit_ref
  21.6 36.3 %all-to-all-done.in_ref = bf16[16,416,128]{2,1,0:T(8,128)(2,1)S(1)} async-done(((bf16[16,416,128]{2,1,0:T(8,128)(2,1)}), bf16[16,416,128]{2,1,0:T(8,128)(2,1)S(1)}, u32[]{:S(2)}, u32[]{:S(2)}) %all-to-all-start) | async-done | bytes 1703968 | tf_op jit(solution)/shard_map/all_to_all | solution.py:354
  57.9 0.0 copy-done.9
  57.9 6.6 %second_coefficients.1 = (f32[16,4,128,128]{3,2,1,0:T(8,128)S(1)}, f32[16,128]{1,0:T(8,128)S(1)}, f32[272,128]{1,0:T(8,128)S(1)}) custom-call(s32[48]{0:T(128)S(1)} %mul.87.low_ref, s32[48]{0:T(128)S(1)} %mul.89.high_ref, f32[48]{0:T(128)S(1)} %maximum_divide_fusion.scale_ref, s32[64]{0:T(128)S(1)} %reshape.201.slot_ref, ...), custom_call_target="tpu_custom_call" | custom-call | flops 1 | bytes 12582912 | tf_op jit(solution)/shard_map/second_coefficients/pallas_call | solution.py:202
  64.5 1.1 %collective-permute-start.1 = (f32[16,128]{1,0:T(8,128)S(1)}, f32[16,128]{1,0:T(8,128)S(1)}, u32[]{:S(2)}, u32[]{:S(2)}) collective-permute-start(f32[16,128]{1,0:T(8,128)S(1)} %get-tuple-element.11), channel_id=1, source_target_pairs={{0,16},{16,0},{1,17},{17,1},{2,18},{18,2},{3,19},{19,3},{4,20},{20... | collective-permute-start | bytes 24584 | tf_op jit(solution)/shard_map/ppermute | solution.py:317
  65.6 0.2 convert_reduce_fusion.6
  65.8 0.0 copy-done.1
  65.8 0.0 copy-done.4
  65.8 0.0 copy-done.3
  65.8 5.5 %residual_of_records.1 = f32[16,128,128]{2,1,0:T(8,128)} custom-call(s32[16]{0:T(128)S(1)} %get-tuple-element.25.low_ref, s32[16]{0:T(128)S(1)} %get-tuple-element.24.high_ref, f32[16,128,128]{2,1,0:T(8,128)S(1)} %bitcast.10, f32[16,128,128]{2,1,0:T(8,128)S(1)} %copy-done.3, f32[272,128]{1,0:T(8,128)S(1)} %get-tuple-element.13.cuts_ref, ...), custom_call_target="tpu_custom_call" | custom-call | flops 1 | bytes 6291456 | tf_op jit(solution)/shard_map/residual_of_records/pallas_call | solution.py:257
  71.3 0.0 collective-permute-done.1
  71.3 3.0 %model_of_shots.1 = bf16[16,4,128,128]{3,2,1,0:T(8,128)(2,1)} custom-call(f32[16,4,128,128]{3,2,1,0:T(8,128)S(1)} %get-tuple-element.10.refs_0_, f32[1,128]{1,0:T(1,128)S(1)} %bitcast.15, bf16[128,256]{1,0:T(8,128)(2,1)S(1)} %copy-done.4, f32[4,4,128]{2,1,0:T(4,128)S(1)} %bitcast.12, f32[4,4,128]{2,1,0:T(4,128)S(1)} %bitcast.13), custom_call_target="tpu_custom_call" | custom-call | tf_op jit(solution)/shard_map/model_of_shots/pallas_call | solution.py:299
  (18 shorter events, 0.1 us)
Async XLA Ops:
  0.6 1.2 %copy-start = (f32[16,1,128,128]{3,2,1,0:T(8,128)S(1)}, f32[16,1,128,128]{3,2,1,0:T(8,128)}, u32[]{:S(2)}) copy-start(f32[16,1,128,128]{3,2,1,0:T(8,128)} %param.4) | copy-start | bytes 3145732
  1.9 0.7 copy-start.5
  2.5 0.8 %copy-start.7 = (bf16[128,128]{1,0:T(8,128)(2,1)S(1)}, bf16[128,128]{1,0:T(8,128)(2,1)}, u32[]{:S(2)}) copy-start(bf16[128,128]{1,0:T(8,128)(2,1)} %constant.37.low_ref) | copy-start | bytes 98308
  3.3 0.8 %copy-start.8 = (bf16[128,128]{1,0:T(8,128)(2,1)S(1)}, bf16[128,128]{1,0:T(8,128)(2,1)}, u32[]{:S(2)}) copy-start(bf16[128,128]{1,0:T(8,128)(2,1)} %constant.9.high_ref) | copy-start | bytes 98308
  5.0 1.0 %copy-start.2 = (f32[16,128,128]{2,1,0:T(8,128)}, f32[16,128,128]{2,1,0:T(8,128)S(1)}, u32[]{:S(2)}) copy-start(f32[16,128,128]{2,1,0:T(8,128)S(1)} %get-tuple-element.12.coef_ref) | copy-start | bytes 3145732
  5.9 4.1 %collective-permute-start = (f32[16,128]{1,0:T(8,128)S(1)}, f32[16,128]{1,0:T(8,128)S(1)}, u32[]{:S(2)}, u32[]{:S(2)}) collective-permute-start(f32[16,128]{1,0:T(8,128)S(1)} %get-tuple-element.9), channel_id=1, source_target_pairs={{0,16},{16,0},{1,17},{17,1},{2,18},{18,2},{3,19},{19,3},{4,20},{20... | collective-permute-start | bytes 24584 | tf_op jit(solution)/shard_map/ppermute | solution.py:317
  12.3 8.2 %copy-start.6 = (s32[256]{0:T(256)S(1)}, s32[256]{0:T(256)}, u32[]{:S(2)}) copy-start(s32[256]{0:T(256)} %param.5) | copy-start | bytes 3076
  12.3 45.6 %copy-start.9 = (f32[128]{0:T(128)S(1)}, f32[128]{0:T(128)}, u32[]{:S(2)}) copy-start(f32[128]{0:T(128)} %param.6) | copy-start | bytes 1540
  12.3 53.4 %copy-start.1 = (f32[16,1,128,128]{3,2,1,0:T(8,128)S(1)}, f32[16,1,128,128]{3,2,1,0:T(8,128)}, u32[]{:S(2)}) copy-start(f32[16,1,128,128]{3,2,1,0:T(8,128)} %param.4) | copy-start | bytes 3145732
  12.3 53.4 %copy-start.4 = (bf16[128,256]{1,0:T(8,128)(2,1)S(1)}, bf16[128,256]{1,0:T(8,128)(2,1)}, u32[]{:S(2)}) copy-start(bf16[128,256]{1,0:T(8,128)(2,1)} %constant.38.refs_2_.both_ref) | copy-start | bytes 196612
  12.4 45.5 %all-to-all-start = ((bf16[16,416,128]{2,1,0:T(8,128)(2,1)}), bf16[16,416,128]{2,1,0:T(8,128)(2,1)S(1)}, u32[]{:S(2)}, u32[]{:S(2)}) async-start(bf16[16,416,128]{2,1,0:T(8,128)(2,1)} %pack_blocks.1), calls=%async_computation | async-start | bytes 3407872 | tf_op jit(solution)/shard_map/all_to_all | solution.py:354
  57.9 7.9 %copy-start.3 = (f32[16,128,128]{2,1,0:T(8,128)S(1)}, f32[16,128,128]{2,1,0:T(8,128)}, u32[]{:S(2)}) copy-start(f32[16,128,128]{2,1,0:T(8,128)} %copy-done.2) | copy-start | bytes 3145732
  64.5 6.8 %collective-permute-start.1 = (f32[16,128]{1,0:T(8,128)S(1)}, f32[16,128]{1,0:T(8,128)S(1)}, u32[]{:S(2)}, u32[]{:S(2)}) collective-permute-start(f32[16,128]{1,0:T(8,128)S(1)} %get-tuple-element.11), channel_id=1, source_target_pairs={{0,16},{16,0},{1,17},{17,1},{2,18},{18,2},{3,19},{19,3},{4,20},{20... | collective-permute-start | bytes 24584 | tf_op jit(solution)/shard_map/ppermute | solution.py:317

commit v2 on v1

v2 whole, which is shorter than its diff:
```python
import jax
import jax.numpy as jnp
import numpy as np
from jax import lax
from jax.experimental import pallas as pl
from jax.experimental.pallas import tpu as pltpu
from jax.sharding import PartitionSpec as P

SHOT_BLK = 4
momentum = 0.5
epsilon = 1e-06
step_size = 1.0 + momentum
VMEM_BYTES = 48 * 1024 * 1024


def cosine_table(length):
    rows = np.arange(length, dtype=np.float64)[:, None]
    cols = np.arange(length, dtype=np.float64)[None, :]
    table = np.cos(np.pi * (cols + 0.5) * rows / length) * np.sqrt(2.0 / length)
    return np.where(rows == 0, table * np.sqrt(0.5), table).astype(np.float32)


def split_bf16(values):
    high = values.astype(jnp.bfloat16)
    low = (values - high.astype(jnp.float32)).astype(jnp.bfloat16)
    return high, low


def full_vmem():
    return pl.BlockSpec(memory_space=pltpu.VMEM)


def full_smem():
    return pl.BlockSpec(memory_space=pltpu.SMEM)


def params(**kw):
    return pltpu.CompilerParams(vmem_limit_bytes=VMEM_BYTES, **kw)


def forward(both, values):
    block = values.shape[0]
    parts = lax.dot_general(
        values, both, (((0,), (0,)), ((), ())), preferred_element_type=jnp.float32
    )
    return parts[:, :block] + parts[:, block:]


def backward(both, coefficients):
    doubled = jnp.concatenate([coefficients, coefficients], axis=1)
    return lax.dot_general(
        both, doubled, (((1,), (1,)), ((), ())), preferred_element_type=jnp.float32
    )


def landed(ids, offsets):
    lag = ids - offsets
    return (lag >= 0) & (lag < SHOT_BLK)


def head(records, offsets, me, owners, capacity, both):
    windows, block, rcv = records.shape
    shots = offsets.shape[0]
    shot_dev = shots // owners
    chunk = 4
    chunks = windows // chunk
    f32, bf16 = jnp.float32, jnp.bfloat16

    def body(
        me_ref, off_hbm, rec_hbm, both_hbm, out_ref, energy_ref,
        off_ref, rec_ref, both_ref, sent_ref, table_ref, table_smem,
        small_sem, rec_sem, out_sem,
    ):
        get_off = pltpu.make_async_copy(off_hbm, off_ref, small_sem.at[0])
        get_both = pltpu.make_async_copy(both_hbm, both_ref, small_sem.at[1])
        get_rec = [
            pltpu.make_async_copy(
                rec_hbm.at[pl.ds(c * chunk, chunk)],
                rec_ref.at[pl.ds(c * chunk, chunk)],
                rec_sem.at[c],
            )
            for c in range(chunks)
        ]
        get_off.start()
        get_both.start()
        for copy in get_rec:
            copy.start()
        get_off.wait()

        ids = lax.broadcasted_iota(jnp.int32, (windows, shots), 0) * owners + me_ref[0]
        hits = jnp.where(landed(ids, off_ref[...]), 1.0, 0.0)
        cover = jnp.sum(hits, axis=1, keepdims=True)
        scale = 1.0 / jnp.maximum(cover, 1.0)

        shot = lax.broadcasted_iota(jnp.int32, (shots, owners), 0)
        first = lax.broadcasted_iota(jnp.int32, (shots, owners), 1) * shot_dev
        member = jnp.where((shot >= first) & (shot < first + shot_dev), 1.0, 0.0)
        counts = jnp.dot(hits.astype(bf16), member.astype(bf16), preferred_element_type=f32)
        present = jnp.where(counts > 0.5, 1.0, 0.0)
        after = lax.broadcasted_iota(jnp.int32, (windows, windows), 0)
        before = lax.broadcasted_iota(jnp.int32, (windows, windows), 1)
        lower = jnp.where(before < after, 1.0, 0.0)
        rank = jnp.dot(lower.astype(bf16), present.astype(bf16), preferred_element_type=f32)
        rank = rank.astype(jnp.int32)
        window = lax.broadcasted_iota(jnp.int32, (windows, owners), 0)
        for i in range(capacity):
            here = (rank == i) & (present > 0.5)
            table_ref[i : i + 1, :owners] = jnp.sum(
                jnp.where(here, window, 0), axis=0, keepdims=True
            )
        put_table = pltpu.make_async_copy(table_ref, table_smem, small_sem.at[2])
        put_table.start()

        get_both.wait()
        for c in range(chunks):
            get_rec[c].wait()
            for w in range(c * chunk, (c + 1) * chunk):
                spread = (rec_ref[w] * scale[w : w + 1, 0:1]).astype(bf16)
                coef = forward(both_ref[...], spread)
                sent_ref[w] = coef.astype(bf16)
                energy_ref[w : w + 1, :] = jnp.sum(coef * coef, axis=0, keepdims=True)

        put_table.wait()

        def send(h, i):
            return pltpu.make_async_copy(
                sent_ref.at[table_smem[i, h]],
                out_ref.at[h, pl.ds(i * rcv, rcv), :],
                out_sem.at[h * capacity + i],
            )

        for h in range(owners):
            for i in range(capacity):
                send(h, i).start()
        for h in range(owners):
            for i in range(capacity):
                send(h, i).wait()

    hbm = pl.BlockSpec(memory_space=pltpu.HBM)
    table_shape = (8, 128)
    return pl.pallas_call(
        body,
        in_specs=[full_smem(), hbm, hbm, hbm],
        out_specs=[pl.BlockSpec(memory_space=pl.ANY), full_vmem()],
        out_shape=[
            jax.ShapeDtypeStruct((owners, capacity * rcv, block), bf16),
            jax.ShapeDtypeStruct((windows, block), f32),
        ],
        scratch_shapes=[
            pltpu.VMEM((1, shots), jnp.int32),
            pltpu.VMEM((windows, block, rcv), f32),
            pltpu.VMEM((block, 2 * block), bf16),
            pltpu.VMEM((windows, rcv, block), bf16),
            pltpu.VMEM(table_shape, jnp.int32),
            pltpu.SMEM(table_shape, jnp.int32),
            pltpu.SemaphoreType.DMA((3,)),
            pltpu.SemaphoreType.DMA((chunks,)),
            pltpu.SemaphoreType.DMA((owners * capacity,)),
        ],
        compiler_params=params(),
        name="pack_coefficients",
    )(me[None], offsets[None, :], records, both)


def cutoffs(energies, hits, thresholds, receivers):
    rows = hits.shape[0]
    block = thresholds.shape[1]

    def body(*refs):
        hit_ref, thr_ref = refs[:2]
        out_ref, cuts_ref = refs[-2:]
        energy = refs[2][...]
        for ref in refs[3:-2]:
            energy = energy + ref[...]
        high, low = split_bf16(energy)
        sums = jnp.dot(hit_ref[...], high, preferred_element_type=jnp.float32) + jnp.dot(
            hit_ref[...], low, preferred_element_type=jnp.float32
        )
        cuts_ref[...] = thr_ref[...] * jnp.sqrt(sums / (SHOT_BLK * receivers) + epsilon)

        def widen(i, _):
            at = pl.multiple_of(i * 8, 8)
            out_ref[pl.ds(at, 8)] = jnp.broadcast_to(
                cuts_ref[pl.ds(at, 8), :][:, None, :], (8, 8, block)
            )
            return 0

        lax.fori_loop(0, rows // 8, widen, 0)

    return pl.pallas_call(
        body,
        in_specs=[full_vmem()] * (2 + len(energies)),
        out_specs=full_vmem(),
        out_shape=jax.ShapeDtypeStruct((rows, 8, block), jnp.float32),
        scratch_shapes=[pltpu.VMEM((rows, block), jnp.float32)],
        compiler_params=params(),
        name="first_cutoffs",
    )(hits, thresholds, *energies)


def clipped_sum(coef, cut_ref, low, high):
    def add(row, total):
        cut = cut_ref[row][None]
        return total + jnp.minimum(jnp.maximum(coef, -cut), cut)

    return lax.fori_loop(low, high, add, jnp.zeros_like(coef))


def second(arrived, cuts, lows, highs, scales, slots, capacity):
    owners, rows, block = arrived.shape
    rcv = rows // capacity
    tiles = rcv // 8
    shot_dev = slots.shape[0] // SHOT_BLK
    shots = cuts.shape[0] - shot_dev
    step = min(4, shot_dev)
    count = owners * capacity

    def body(
        low_ref, high_ref, scale_ref, slot_ref, in_ref, cut_ref, out_ref, energy_ref, diff_ref
    ):
        def block_of(slot):
            owner = slot // capacity
            start = pl.multiple_of((slot - owner * capacity) * rcv, rcv)
            values = in_ref[owner, pl.ds(start, rcv), :].astype(jnp.float32)
            return values.reshape(tiles, 8, block)

        @pl.when(pl.program_id(0) == 0)
        def _():
            def difference(slot, _):
                low, high = low_ref[slot], high_ref[slot]
                coef = block_of(slot)
                clipped = clipped_sum(coef, cut_ref, low, high)
                many = (high - low).astype(jnp.float32)
                diff_ref[slot] = coef - scale_ref[slot] * (many * coef - clipped)
                return 0

            lax.fori_loop(0, count, difference, 0)

        def one_shot(i, _):
            shot = pl.program_id(0) * step + i
            cut = cut_ref[shots + shot][None]
            energy = jnp.zeros((8, block), jnp.float32)
            for q in range(SHOT_BLK):
                slot = slot_ref[shot * SHOT_BLK + q]
                coef = block_of(slot)
                shrunk = coef - jnp.minimum(jnp.maximum(coef, -cut), cut)
                value = step_size * shrunk + diff_ref[slot]
                out_ref[i, q] = value.reshape(rcv, block)
                energy = energy + jnp.sum(value * value, axis=0)
            energy_ref[pl.ds(shot, 1), :] = jnp.sum(energy, axis=0, keepdims=True)
            return 0

        lax.fori_loop(0, step, one_shot, 0)

    return pl.pallas_call(
        body,
        grid=(shot_dev // step,),
        in_specs=[full_smem()] * 4 + [full_vmem()] * 2,
        out_specs=[
            pl.BlockSpec((step, SHOT_BLK, rcv, block), lambda i: (i, 0, 0, 0)),
            full_vmem(),
        ],
        out_shape=[
            jax.ShapeDtypeStruct((shot_dev, SHOT_BLK, rcv, block), jnp.float32),
            jax.ShapeDtypeStruct((shot_dev, block), jnp.float32),
        ],
        scratch_shapes=[pltpu.VMEM((count, tiles, 8, block), jnp.float32)],
        compiler_params=params(),
        cost_estimate=pl.CostEstimate(flops=1, bytes_accessed=12 << 20, transcendentals=0),
        name="second_coefficients",
    )(lows, highs, scales, slots, arrived, cuts)


def remainder(records, cuts, lows, highs, both):
    windows, block, rcv = records.shape
    tiles = rcv // 8
    step = 4

    def body(low_ref, high_ref, rec_ref, cut_ref, both_ref, out_ref):
        for w in range(step):
            window = pl.program_id(0) * step + w
            low, high = low_ref[window], high_ref[window]
            many = (high - low).astype(jnp.float32)
            scale = 1.0 / jnp.maximum(jnp.full((1, rcv), many, jnp.float32), 1.0)
            spread = (rec_ref[w] * scale).astype(jnp.bfloat16)
            coef = forward(both_ref[...], spread)
            clipped = clipped_sum(coef.reshape(tiles, 8, block), cut_ref, low, high)
            part, rest = split_bf16(many * coef - clipped.reshape(rcv, block))
            blended = backward(both_ref[...], part) + lax.dot_general(
                both_ref[:, :block], rest, (((1,), (1,)), ((), ())),
                preferred_element_type=jnp.float32,
            )
            out_ref[w] = rec_ref[w] - step_size * blended

    return pl.pallas_call(
        body,
        grid=(windows // step,),
        in_specs=[
            full_smem(),
            full_smem(),
            pl.BlockSpec((step, block, rcv), lambda i: (i, 0, 0)),
            full_vmem(),
            full_vmem(),
        ],
        out_specs=pl.BlockSpec((step, block, rcv), lambda i: (i, 0, 0)),
        out_shape=jax.ShapeDtypeStruct((windows, block, rcv), jnp.float32),
        compiler_params=params(),
        cost_estimate=pl.CostEstimate(flops=1, bytes_accessed=6 << 20, transcendentals=0),
        name="residual_of_records",
    )(lows, highs, records, cuts, both)


def finish(values, energies, thresholds, both, receivers):
    shot_dev, _, rcv, block = values.shape
    step = min(4, shot_dev)

    def body(*refs):
        in_ref, thr_ref, both_ref = refs[:3]
        out_ref = refs[-1]
        energy = refs[3][...]
        for ref in refs[4:-1]:
            energy = energy + ref[...]
        cuts = thr_ref[...] * jnp.sqrt(energy / (SHOT_BLK * receivers) + epsilon)
        for i in range(step):
            cut = cuts[i : i + 1, :]
            for q in range(SHOT_BLK):
                value = in_ref[i, q]
                shrunk = value - jnp.minimum(jnp.maximum(value, -cut), cut)
                out_ref[i, q] = backward(both_ref[...], shrunk.astype(jnp.bfloat16)).astype(
                    jnp.bfloat16
                )

    shape = (shot_dev // step, step, block)
    energies = [energy.reshape(shape) for energy in energies]
    return pl.pallas_call(
        body,
        grid=(shot_dev // step,),
        in_specs=[
            pl.BlockSpec((step, SHOT_BLK, rcv, block), lambda i: (i, 0, 0, 0)),
            full_vmem(),
            full_vmem(),
        ]
        + [pl.BlockSpec((None, step, block), lambda i: (i, 0, 0))] * len(energies),
        out_specs=pl.BlockSpec((step, SHOT_BLK, block, rcv), lambda i: (i, 0, 0, 0)),
        out_shape=jax.ShapeDtypeStruct((shot_dev, SHOT_BLK, block, rcv), jnp.bfloat16),
        compiler_params=params(),
        name="model_of_shots",
    )(values, thresholds, both, *energies)


def over_receivers(values):
    if lax.axis_size("rcv") == 2:
        return [values, lax.ppermute(values, "rcv", [(0, 1), (1, 0)])]
    return [lax.psum(values, "rcv")]


def rotate(values, stride, by, size):
    n = lax.axis_size("shot")
    pairs = []
    for i in range(n):
        place = (i // stride) % size
        pairs.append((i, i + ((place + by) % size - place) * stride))
    return lax.ppermute(values, "shot", pairs)


def local(record_data, offsets, thresholds):
    owners = lax.axis_size("shot")
    me = lax.axis_index("shot")
    windows, _, block, rcv = record_data.shape
    shots = offsets.shape[0]
    shot_dev = shots // owners
    pairs = shot_dev // 2
    pair_slots = min(pairs, owners // (SHOT_BLK + 1))
    capacity = (pairs + pair_slots - 1) // pair_slots
    receivers = rcv * lax.axis_size("rcv")
    near = min(4, owners)
    far = owners // near

    high, low = split_bf16(jnp.asarray(cosine_table(block).T))
    both = jnp.concatenate([high, low], axis=1)
    records = record_data.reshape(windows, block, rcv)
    thr = thresholds[None, :]
    window_ids = jnp.arange(windows, dtype=jnp.int32)

    packed, energy = head(records, offsets, me, owners, capacity, both)
    remote = [rotate(energy, near, j, far) for j in range(1, far)]
    packed, *remote = lax.optimization_barrier((packed, *remote))
    arrived = lax.all_to_all(packed, "shot", split_axis=0, concat_axis=0, tiled=True)

    energy = jnp.concatenate([energy, *remote])
    energy = jnp.concatenate([energy] + [rotate(energy, 1, j, near) for j in range(1, near)])
    energies = over_receivers(energy)
    back = jnp.arange(far, dtype=jnp.int32)[None, :]
    side = jnp.arange(near, dtype=jnp.int32)[:, None]
    origin = (me // near - back + far) % far * near + (me % near - side + near) % near
    energy_ids = (window_ids * owners + origin[:, :, None]).reshape(-1)

    index = jnp.arange(shots, dtype=jnp.int32)
    ahead = (offsets[None, :] < offsets[:, None]) | (
        (offsets[None, :] == offsets[:, None]) & (index[None, :] < index[:, None])
    )
    place = jnp.sum(ahead.astype(jnp.int32), axis=1)
    ordered = jnp.sum(jnp.where(place[None, :] == index[:, None], offsets[None, :], 0), axis=1)
    mine = lax.dynamic_slice(offsets, (me * shot_dev,), (shot_dev,))
    all_offsets = jnp.concatenate([ordered, mine])
    hits = landed(energy_ids[None, :], all_offsets[:, None]).astype(jnp.bfloat16)
    cuts = cutoffs(energies, hits, thr, receivers)

    def bounds(ids):
        below = jnp.sum((offsets < ids[..., None] - (SHOT_BLK - 1)).astype(jnp.int32), axis=-1)
        upto = jnp.sum((offsets <= ids[..., None]).astype(jnp.int32), axis=-1)
        return below, upto

    residual = remainder(records, cuts, *bounds(window_ids * owners + me), both)

    grid_ids = window_ids[None, :] * owners + jnp.arange(owners, dtype=jnp.int32)[:, None]
    slot_ids = jnp.arange(capacity, dtype=jnp.int32)
    held = jnp.max(landed(grid_ids[:, :, None], mine).astype(jnp.int32), axis=2)
    before = (window_ids[:, None] < window_ids[None, :]).astype(jnp.int32)
    held_rank = jnp.sum(held[:, :, None] * before, axis=1)
    taken = (held_rank[:, None, :] == slot_ids[None, :, None]) & (held[:, None, :] > 0)
    held_ids = jnp.sum(jnp.where(taken, grid_ids[:, None, :], 0), axis=2)
    valid = jnp.sum(taken.astype(jnp.int32), axis=2)
    lows, highs = bounds(held_ids)
    lows, highs = lows * valid, highs * valid
    scales = step_size / jnp.maximum((highs - lows).astype(jnp.float32), 1.0)
    targets = mine[:, None] + jnp.arange(SHOT_BLK, dtype=jnp.int32)[None, :]
    slot_of = jnp.arange(owners, dtype=jnp.int32)[:, None] * capacity + held_rank
    slots = jnp.sum(
        jnp.where(targets[:, :, None, None] == grid_ids[None, None], slot_of[None, None], 0),
        axis=(2, 3),
    )

    values, energy2 = second(
        arrived, cuts, lows.reshape(-1), highs.reshape(-1), scales.reshape(-1),
        slots.reshape(-1), capacity,
    )
    model = finish(values, over_receivers(energy2), thr, both, receivers)
    return (model, residual.reshape(windows, 1, block, rcv))


def solution(mesh):
    return jax.shard_map(
        local,
        mesh=mesh,
        in_specs=(P(None, "shot", None, "rcv"), P(), P()),
        out_specs=(P("shot", None, None, "rcv"), P(None, "shot", None, "rcv")),
        check_vma=False,
    )
```

time: 75.2 us -> 78.8 us (1.048)
  starting transfers between devices: 8.89 us -> 16.8 us
  waiting for transfers between devices: 36.3 us -> 29.7 us
  Pallas kernels: 18.3 us -> 20.7 us
    all_to_all x1, waiting for transfers between devices: 36.3 us -> 19.7 us  [local(): lax.all_to_all(packed, 'shot', split_axis=0, concat_axis=0, tiled=True)]
    ppermute x0 -> x6, waiting for transfers between devices: none -> 7.4 us  [rotate(): return lax.ppermute(values, 'shot', pairs)]
    ppermute x0 -> x6, starting transfers between devices: none -> 6.16 us  [rotate(): return lax.ppermute(values, 'shot', pairs)]
    ppermute x2, waiting for transfers between devices: 0.01 us -> 2.61 us  [over_receivers(): return [values, lax.ppermute(values, 'rcv', [(0, 1), (1, 0)])]]
    all_to_all x1, starting transfers between devices: 6.33 us -> 7.55 us  [local(): lax.all_to_all(packed, 'shot', split_axis=0, concat_axis=0, tiled=True)]
    pallas_call x1, Pallas kernels: 6.58 us -> 7.74 us  [second(): pl.pallas_call(body, grid=(shot_dev // step,), in_specs=[full_smem()] * 4...]
    pallas_call x1, Pallas kernels: 5.53 us -> 6.34 us  [remainder(): pl.pallas_call(body, grid=(windows // step,), in_specs=[full_smem(), full...]
    unnamed x20 -> x21, local copies, waits for them, and re-layouts: 4.4 us -> 4.96 us
  transfers between devices with their start and end apart: 3 -> 9, of which waited for: 1 -> 5; matrix products, arithmetic and copies ran while one was open for 8% -> 6% of each run, Pallas kernels for 7% -> 9%
where the time goes in v2:
time: 78.8 us; the launch traced here: 77.6 us
  waiting for transfers between devices  29.7 us (38%)
  Pallas kernels  20.7 us (26%)
  starting transfers between devices  16.8 us (21%)
  local copies, waits for them, and re-layouts  6.25 us (8%)
  other arithmetic  3.24 us (4%)
  between operations  0.84 us (1%)
    all_to_all x1, waiting for transfers between devices, local(): lax.all_to_all(packed, 'shot', split_axis=0, concat_axis=0, tiled=True)  19.7 us
    pallas_call x1, Pallas kernels, second(): pl.pallas_call(body, grid=(shot_dev // step,), in_specs=[full_smem()] * 4...  7.74 us
    all_to_all x1, starting transfers between devices, local(): lax.all_to_all(packed, 'shot', split_axis=0, concat_axis=0, tiled=True)  7.55 us
    ppermute x6, waiting for transfers between devices, rotate(): return lax.ppermute(values, 'shot', pairs)  7.4 us
    pallas_call x1, Pallas kernels, remainder(): pl.pallas_call(body, grid=(windows // step,), in_specs=[full_smem(), full...  6.34 us
    ppermute x6, starting transfers between devices, rotate(): return lax.ppermute(values, 'shot', pairs)  6.16 us
    unnamed x21, local copies, waits for them, and re-layouts  4.96 us
    pallas_call x1, Pallas kernels, head(): pl.pallas_call(body, in_specs=[full_smem(), hbm, hbm, hbm], out_specs=[pl...  3.09 us
  transfers between devices with their start and end apart: 9, of which 5 were waited for; matrix products, arithmetic and copies ran while one was open for 6% of the time, Pallas kernels for 9%

profile of v2, /device:TPU:16, one launch (start us, length us, event | category | flops | bytes accessed | tf_op | source)
XLA Modules:
  0.0 77.6 jit_solution(12670294245193774246)
XLA Ops:
  0.6 0.0 copy-start.1
  0.6 1.2 %copy-done.1 = f32[16,1,128,128]{3,2,1,0:T(8,128)S(1)} copy-done((f32[16,1,128,128]{3,2,1,0:T(8,128)S(1)}, f32[16,1,128,128]{3,2,1,0:T(8,128)}, u32[]{:S(2)}) %copy-start.1) | copy-done | bytes 1048600
  1.9 0.8 %copy-done.3 = bf16[128,256]{1,0:T(8,128)(2,1)S(1)} copy-done((bf16[128,256]{1,0:T(8,128)(2,1)S(1)}, bf16[128,256]{1,0:T(8,128)(2,1)}, u32[]{:S(2)}) %copy-start.3) | copy-done | bytes 65560
  2.7 0.7 copy-done.5
  3.4 3.1 %pack_coefficients.1 = (bf16[16,384,128]{2,1,0:T(8,128)(2,1)}, f32[16,128]{1,0:T(8,128)S(1)}) custom-call(s32[1]{0:T(128)} %bitcast.me_ref, s32[1,256]{1,0:T(1,128)S(1)} %bitcast.11, f32[16,128,128]{2,1,0:T(8,128)S(1)} %bitcast.9, bf16[128,256]{1,0:T(8,128)(2,1)S(1)} %copy-done.3), custom_call_target="tpu_custom_call" | custom-call | tf_op jit(solution)/shard_map/pack_coefficients/pallas_call | solution.py:141
  6.5 1.6 %collective-permute-start = (f32[16,128]{1,0:T(8,128)S(1)}, f32[16,128]{1,0:T(8,128)S(1)}, u32[]{:S(2)}, u32[]{:S(2)}) collective-permute-start(f32[16,128]{1,0:T(8,128)S(1)} %get-tuple-element.11), channel_id=1, source_target_pairs={{0,4},{1,5},{2,6},{3,7},{4,8},{5,9},{6,10},{7,11},{8,12},{9,13},{1... | collective-permute-start | bytes 24584 | tf_op jit(solution)/shard_map/ppermute | solution.py:363
  8.1 0.3 collective-permute-start.1
  8.4 1.2 %collective-permute-start.2 = (f32[16,128]{1,0:T(8,128)S(1)}, f32[16,128]{1,0:T(8,128)S(1)}, u32[]{:S(2)}, u32[]{:S(2)}) collective-permute-start(f32[16,128]{1,0:T(8,128)S(1)} %get-tuple-element.11), channel_id=1, source_target_pairs={{0,12},{1,13},{2,14},{3,15},{4,0},{5,1},{6,2},{7,3},{8,4},{9,5},{1... | collective-permute-start | bytes 24584 | tf_op jit(solution)/shard_map/ppermute | solution.py:363
  9.7 0.1 broadcast_add_fusion.2
  9.8 0.1 broadcast_add_fusion
  9.8 0.8 dynamic_slice.3
  10.6 0.4 convert_reduce_fusion.1
  11.0 0.1 multiply_reduce_fusion
  11.2 0.2 convert_reduce_fusion.4
  11.3 0.1 add.197
  11.4 0.0 collective-permute-done
  11.4 1.2 %collective-permute-done.1 = f32[16,128]{1,0:T(8,128)S(1)} collective-permute-done((f32[16,128]{1,0:T(8,128)S(1)}, f32[16,128]{1,0:T(8,128)S(1)}, u32[]{:S(2)}, u32[]{:S(2)}) %collective-permute-start.1) | collective-permute-done | bytes 8224 | tf_op jit(solution)/shard_map/ppermute | solution.py:363
  12.7 0.0 collective-permute-done.2
  12.7 7.5 %all-to-all-start = ((bf16[16,384,128]{2,1,0:T(8,128)(2,1)}), bf16[16,384,128]{2,1,0:T(8,128)(2,1)S(1)}, u32[]{:S(2)}, u32[]{:S(2)}) async-start(bf16[16,384,128]{2,1,0:T(8,128)(2,1)} %get-tuple-element.12), calls=%async_computation | async-start | bytes 3145728 | tf_op jit(solution)/shard_map/all_to_all | solution.py:388
  20.2 0.3 convert_reduce_fusion.2
  20.5 0.1 copy.8
  20.6 0.1 mul.83.low_ref
  20.7 0.1 copy.9
  20.8 0.1 mul.85.high_ref
  20.9 0.2 convert_reduce_fusion
  21.0 0.1 select_reduce_fusion.1
  21.2 0.1 iota_add_fusion
  21.3 0.1 broadcast_add_fusion.1
  21.3 0.1 fusion.1.refs_0_
  21.5 0.2 collective-permute-start.3
  21.7 1.5 %collective-permute-start.4 = (f32[64,128]{1,0:T(8,128)S(1)}, f32[64,128]{1,0:T(8,128)S(1)}, u32[]{:S(2)}, u32[]{:S(2)}) collective-permute-start(f32[64,128]{1,0:T(8,128)S(1)} %get-tuple-element.30), channel_id=1, source_target_pairs={{0,2},{1,3},{2,0},{3,1},{4,6},{5,7},{6,4},{7,5},{8,10},{9,11},{10,... | collective-permute-start | bytes 98312 | tf_op jit(solution)/shard_map/ppermute | solution.py:363
  23.2 1.3 %collective-permute-start.5 = (f32[64,128]{1,0:T(8,128)S(1)}, f32[64,128]{1,0:T(8,128)S(1)}, u32[]{:S(2)}, u32[]{:S(2)}) collective-permute-start(f32[64,128]{1,0:T(8,128)S(1)} %get-tuple-element.30), channel_id=1, source_target_pairs={{0,3},{1,0},{2,1},{3,2},{4,7},{5,4},{6,5},{7,6},{8,11},{9,8},{10,9... | collective-permute-start | bytes 98312 | tf_op jit(solution)/shard_map/ppermute | solution.py:363
  24.5 4.9 %collective-permute-done.3 = f32[64,128]{1,0:T(8,128)S(1)} collective-permute-done((f32[64,128]{1,0:T(8,128)S(1)}, f32[64,128]{1,0:T(8,128)S(1)}, u32[]{:S(2)}, u32[]{:S(2)}) %collective-permute-start.3) | collective-permute-done | bytes 32800 | tf_op jit(solution)/shard_map/ppermute | solution.py:363
  29.4 1.3 %collective-permute-done.4 = f32[64,128]{1,0:T(8,128)S(1)} collective-permute-done((f32[64,128]{1,0:T(8,128)S(1)}, f32[64,128]{1,0:T(8,128)S(1)}, u32[]{:S(2)}, u32[]{:S(2)}) %collective-permute-start.4) | collective-permute-done | bytes 32800 | tf_op jit(solution)/shard_map/ppermute | solution.py:363
  30.7 0.0 collective-permute-done.5
  30.7 1.6 %collective-permute-start.6 = (f32[256,128]{1,0:T(8,128)S(1)}, f32[256,128]{1,0:T(8,128)S(1)}, u32[]{:S(2)}, u32[]{:S(2)}) collective-permute-start(f32[256,128]{1,0:T(8,128)S(1)} %constant_dynamic-update-slice_fusion.4.refs_2_), channel_id=1, source_target_pairs={{0,16},{16,0},{1,17},{17,1},{2,18},{18,2},{3,19},{19,3},{4,20},{20... | collective-permute-start | bytes 393224 | tf_op jit(solution)/shard_map/ppermute | solution.py:353
  32.3 1.3 %select_reduce_fusion = s32[16,4]{1,0:T(8,128)S(1)} fusion(s32[16,16]{1,0:T(8,128)S(1)} %broadcast_add_fusion.1, s32[16,16]{1,0:T(8,128)S(1)} %iota_add_fusion.1, s32[16,4]{1,0:T(8,128)S(1)} %iota_add_fusion), kind=kLoop, calls=%fused_computation | loop fusion | flops 49088 | bytes 2560 | tf_op jit(solution)/shard_map/reduce_sum | solution.py:429
  33.5 0.1 reshape.267.slot_ref
  33.7 2.6 %collective-permute-done.6.refs_3_ = f32[256,128]{1,0:T(8,128)S(1)} collective-permute-done((f32[256,128]{1,0:T(8,128)S(1)}, f32[256,128]{1,0:T(8,128)S(1)}, u32[]{:S(2)}, u32[]{:S(2)}) %collective-permute-start.6) | collective-permute-done | bytes 131104 | tf_op jit(solution)/shard_map/ppermute | solution.py:353
  36.3 0.6 first_cutoffs.1.cut_ref
  36.9 0.0 copy-start.4
  36.9 19.7 %all-to-all-done.in_ref = bf16[16,384,128]{2,1,0:T(8,128)(2,1)S(1)} async-done(((bf16[16,384,128]{2,1,0:T(8,128)(2,1)}), bf16[16,384,128]{2,1,0:T(8,128)(2,1)S(1)}, u32[]{:S(2)}, u32[]{:S(2)}) %all-to-all-start) | async-done | bytes 1572896 | tf_op jit(solution)/shard_map/all_to_all | solution.py:388
  56.6 7.7 %second_coefficients.1 = (f32[16,4,128,128]{3,2,1,0:T(8,128)}, f32[16,128]{1,0:T(8,128)S(1)}) custom-call(s32[48]{0:T(128)S(1)} %mul.83.low_ref, s32[48]{0:T(128)S(1)} %mul.85.high_ref, f32[48]{0:T(128)S(1)} %maximum_divide_fusion.scale_ref, s32[64]{0:T(128)S(1)} %reshape.267.slot_ref, bf16[16,384,128]{2,1,0:T(8,128)(2,1)S(1)} %all-to-all-done.in_ref, ...), custom_call_target="tpu_custom_call" | custom-call | flops 1 | bytes 12582912 | tf_op jit(solution)/shard_map/second_coefficients/pallas_call | solution.py:255
  64.4 1.5 %collective-permute-start.7 = (f32[16,128]{1,0:T(8,128)S(1)}, f32[16,128]{1,0:T(8,128)S(1)}, u32[]{:S(2)}, u32[]{:S(2)}) collective-permute-start(f32[16,128]{1,0:T(8,128)S(1)} %get-tuple-element.17), channel_id=1, source_target_pairs={{0,16},{16,0},{1,17},{17,1},{2,18},{18,2},{3,19},{19,3},{4,20},{20... | collective-permute-start | bytes 24584 | tf_op jit(solution)/shard_map/ppermute | solution.py:353
  65.9 0.2 convert_reduce_fusion.5
  66.1 6.3 %residual_of_records.1 = f32[16,128,128]{2,1,0:T(8,128)} custom-call(s32[16]{0:T(128)S(1)} %get-tuple-element.27.low_ref, s32[16]{0:T(128)S(1)} %get-tuple-element.26.high_ref, f32[16,128,128]{2,1,0:T(8,128)S(1)} %bitcast.10, f32[272,8,128]{2,1,0:T(8,128)S(1)} %first_cutoffs.1.cut_ref, bf16[128,256]{1,0:T(8,128)(2,1)S(1)} %copy-done.4), custom_call_target="tpu_custom_call" | custom-call | flops 1 | bytes 6291456 | tf_op jit(solution)/shard_map/residual_of_records/pallas_call | solution.py:295
  72.4 2.2 %copy-done = f32[16,4,128,128]{3,2,1,0:T(8,128)S(1)} copy-done((f32[16,4,128,128]{3,2,1,0:T(8,128)S(1)}, f32[16,4,128,128]{3,2,1,0:T(8,128)}, u32[]{:S(2)}) %copy-start) | copy-done | bytes 4194328
  74.6 3.0 %model_of_shots.1 = bf16[16,4,128,128]{3,2,1,0:T(8,128)(2,1)} custom-call(f32[16,4,128,128]{3,2,1,0:T(8,128)S(1)} %copy-done, f32[1,128]{1,0:T(1,128)S(1)} %bitcast.15, bf16[128,256]{1,0:T(8,128)(2,1)S(1)} %copy-done.4, f32[4,4,128]{2,1,0:T(4,128)S(1)} %bitcast.12, f32[4,4,128]{2,1,0:T(4,128)S(1)} %bitcast.13), custom_call_target="tpu_custom_call" | custom-call | tf_op jit(solution)/shard_map/model_of_shots/pallas_call | solution.py:335
  (29 shorter events, 0.1 us)
Async XLA Ops:
  0.6 1.2 %copy-start.1 = (f32[16,1,128,128]{3,2,1,0:T(8,128)S(1)}, f32[16,1,128,128]{3,2,1,0:T(8,128)}, u32[]{:S(2)}) copy-start(f32[16,1,128,128]{3,2,1,0:T(8,128)} %param.4) | copy-start | bytes 3145732
  1.9 0.8 %copy-start.3 = (bf16[128,256]{1,0:T(8,128)(2,1)S(1)}, bf16[128,256]{1,0:T(8,128)(2,1)}, u32[]{:S(2)}) copy-start(bf16[128,256]{1,0:T(8,128)(2,1)} %constant.79.both_hbm.refs_2_.both_ref) | copy-start | bytes 196612
  2.7 0.7 copy-start.5
  6.5 5.0 %collective-permute-start = (f32[16,128]{1,0:T(8,128)S(1)}, f32[16,128]{1,0:T(8,128)S(1)}, u32[]{:S(2)}, u32[]{:S(2)}) collective-permute-start(f32[16,128]{1,0:T(8,128)S(1)} %get-tuple-element.11), channel_id=1, source_target_pairs={{0,4},{1,5},{2,6},{3,7},{4,8},{5,9},{6,10},{7,11},{8,12},{9,13},{1... | collective-permute-start | bytes 24584 | tf_op jit(solution)/shard_map/ppermute | solution.py:363
  8.1 4.5 %collective-permute-start.1 = (f32[16,128]{1,0:T(8,128)S(1)}, f32[16,128]{1,0:T(8,128)S(1)}, u32[]{:S(2)}, u32[]{:S(2)}) collective-permute-start(f32[16,128]{1,0:T(8,128)S(1)} %get-tuple-element.11), channel_id=1, source_target_pairs={{0,8},{1,9},{2,10},{3,11},{4,12},{5,13},{6,14},{7,15},{8,0},{9,1},... | collective-permute-start | bytes 24584 | tf_op jit(solution)/shard_map/ppermute | solution.py:363
  8.4 4.2 %collective-permute-start.2 = (f32[16,128]{1,0:T(8,128)S(1)}, f32[16,128]{1,0:T(8,128)S(1)}, u32[]{:S(2)}, u32[]{:S(2)}) collective-permute-start(f32[16,128]{1,0:T(8,128)S(1)} %get-tuple-element.11), channel_id=1, source_target_pairs={{0,12},{1,13},{2,14},{3,15},{4,0},{5,1},{6,2},{7,3},{8,4},{9,5},{1... | collective-permute-start | bytes 24584 | tf_op jit(solution)/shard_map/ppermute | solution.py:363
  12.7 7.6 %copy-start.6 = (s32[256]{0:T(256)S(1)}, s32[256]{0:T(256)}, u32[]{:S(2)}) copy-start(s32[256]{0:T(256)} %param.5) | copy-start | bytes 3076
  12.7 23.6 %copy-start.7 = (f32[128]{0:T(128)S(1)}, f32[128]{0:T(128)}, u32[]{:S(2)}) copy-start(f32[128]{0:T(128)} %param.6) | copy-start | bytes 1540
  12.7 44.0 %all-to-all-start = ((bf16[16,384,128]{2,1,0:T(8,128)(2,1)}), bf16[16,384,128]{2,1,0:T(8,128)(2,1)S(1)}, u32[]{:S(2)}, u32[]{:S(2)}) async-start(bf16[16,384,128]{2,1,0:T(8,128)(2,1)} %get-tuple-element.12), calls=%async_computation | async-start | bytes 3145728 | tf_op jit(solution)/shard_map/all_to_all | solution.py:388
  21.5 7.9 %collective-permute-start.3 = (f32[64,128]{1,0:T(8,128)S(1)}, f32[64,128]{1,0:T(8,128)S(1)}, u32[]{:S(2)}, u32[]{:S(2)}) collective-permute-start(f32[64,128]{1,0:T(8,128)S(1)} %get-tuple-element.30), channel_id=1, source_target_pairs={{0,1},{1,2},{2,3},{3,0},{4,5},{5,6},{6,7},{7,4},{8,9},{9,10},{10,1... | collective-permute-start | bytes 98312 | tf_op jit(solution)/shard_map/ppermute | solution.py:363
  21.7 9.0 %collective-permute-start.4 = (f32[64,128]{1,0:T(8,128)S(1)}, f32[64,128]{1,0:T(8,128)S(1)}, u32[]{:S(2)}, u32[]{:S(2)}) collective-permute-start(f32[64,128]{1,0:T(8,128)S(1)} %get-tuple-element.30), channel_id=1, source_target_pairs={{0,2},{1,3},{2,0},{3,1},{4,6},{5,7},{6,4},{7,5},{8,10},{9,11},{10,... | collective-permute-start | bytes 98312 | tf_op jit(solution)/shard_map/ppermute | solution.py:363
  23.2 7.5 %collective-permute-start.5 = (f32[64,128]{1,0:T(8,128)S(1)}, f32[64,128]{1,0:T(8,128)S(1)}, u32[]{:S(2)}, u32[]{:S(2)}) collective-permute-start(f32[64,128]{1,0:T(8,128)S(1)} %get-tuple-element.30), channel_id=1, source_target_pairs={{0,3},{1,0},{2,1},{3,2},{4,7},{5,4},{6,5},{7,6},{8,11},{9,8},{10,9... | collective-permute-start | bytes 98312 | tf_op jit(solution)/shard_map/ppermute | solution.py:363
  30.7 5.6 %collective-permute-start.6 = (f32[256,128]{1,0:T(8,128)S(1)}, f32[256,128]{1,0:T(8,128)S(1)}, u32[]{:S(2)}, u32[]{:S(2)}) collective-permute-start(f32[256,128]{1,0:T(8,128)S(1)} %constant_dynamic-update-slice_fusion.4.refs_2_), channel_id=1, source_target_pairs={{0,16},{16,0},{1,17},{17,1},{2,18},{18,2},{3,19},{19,3},{4,20},{20... | collective-permute-start | bytes 393224 | tf_op jit(solution)/shard_map/ppermute | solution.py:353
  36.9 29.2 %copy-start.4 = (bf16[128,256]{1,0:T(8,128)(2,1)S(1)}, bf16[128,256]{1,0:T(8,128)(2,1)}, u32[]{:S(2)}) copy-start(bf16[128,256]{1,0:T(8,128)(2,1)} %constant.79.both_hbm.refs_2_.both_ref) | copy-start | bytes 196612
  56.6 9.4 %copy-start.2 = (f32[16,1,128,128]{3,2,1,0:T(8,128)S(1)}, f32[16,1,128,128]{3,2,1,0:T(8,128)}, u32[]{:S(2)}) copy-start(f32[16,1,128,128]{3,2,1,0:T(8,128)} %param.4) | copy-start | bytes 3145732
  64.4 8.0 %collective-permute-start.7 = (f32[16,128]{1,0:T(8,128)S(1)}, f32[16,128]{1,0:T(8,128)S(1)}, u32[]{:S(2)}, u32[]{:S(2)}) collective-permute-start(f32[16,128]{1,0:T(8,128)S(1)} %get-tuple-element.17), channel_id=1, source_target_pairs={{0,16},{16,0},{1,17},{17,1},{2,18},{18,2},{3,19},{19,3},{4,20},{20... | collective-permute-start | bytes 24584 | tf_op jit(solution)/shard_map/ppermute | solution.py:353
  72.4 2.2 %copy-start = (f32[16,4,128,128]{3,2,1,0:T(8,128)S(1)}, f32[16,4,128,128]{3,2,1,0:T(8,128)}, u32[]{:S(2)}) copy-start(f32[16,4,128,128]{3,2,1,0:T(8,128)} %get-tuple-element.16.refs_0_) | copy-start | bytes 12582916

commit v3 on v2

--- a/solution.py
+++ b/solution.py
@@ -10,7 +10,8 @@
 momentum = 0.5
 epsilon = 1e-06
 step_size = 1.0 + momentum
-VMEM_BYTES = 48 * 1024 * 1024
+VMEM_BYTES = 16 * 1024 * 1024
+HEAD_VMEM_BYTES = 60 * 1024 * 1024
 
 
 def cosine_table(length):
@@ -34,8 +35,8 @@
     return pl.BlockSpec(memory_space=pltpu.SMEM)
 
 
-def params(**kw):
-    return pltpu.CompilerParams(vmem_limit_bytes=VMEM_BYTES, **kw)
+def params(vmem=VMEM_BYTES):
+    return pltpu.CompilerParams(vmem_limit_bytes=vmem)
 
 
 def forward(both, values):
@@ -157,7 +158,7 @@
             pltpu.SemaphoreType.DMA((chunks,)),
             pltpu.SemaphoreType.DMA((owners * capacity,)),
         ],
-        compiler_params=params(),
+        compiler_params=params(HEAD_VMEM_BYTES),
         name="pack_coefficients",
     )(me[None], offsets[None, :], records, both)
 
@@ -412,6 +413,7 @@
         return below, upto
 
     residual = remainder(records, cuts, *bounds(window_ids * owners + me), both)
+    cuts, residual = lax.optimization_barrier((cuts, residual))
 
     grid_ids = window_ids[None, :] * owners + jnp.arange(owners, dtype=jnp.int32)[:, None]
     slot_ids = jnp.arange(capacity, dtype=jnp.int32)

time: 78.8 us -> 68.3 us (0.87); the launches traced: 77.6 us -> 68.3 us
  waiting for transfers between devices: 29.7 us -> 24.5 us
  local copies, waits for them, and re-layouts: 6.25 us -> 2.53 us
  starting transfers between devices: 16.8 us -> 15.9 us
    all_to_all x1, waiting for transfers between devices: 19.7 us -> 10.7 us  [local(): lax.all_to_all(packed, 'shot', split_axis=0, concat_axis=0, tiled=True)]
    unnamed x21 -> x15, local copies, waits for them, and re-layouts: 4.96 us -> 1.25 us
    ppermute x2, waiting for transfers between devices: 2.61 us -> 5.36 us  [over_receivers(): return [values, lax.ppermute(values, 'rcv', [(0, 1), (1, 0)])]]
    all_to_all x1, starting transfers between devices: 7.55 us -> 5.48 us  [local(): lax.all_to_all(packed, 'shot', split_axis=0, concat_axis=0, tiled=True)]
    pallas_call x1, Pallas kernels: 3.09 us -> 4.39 us  [head(): pl.pallas_call(body, in_specs=[full_smem(), hbm, hbm, hbm], out_specs=[pl...]
    ppermute x6, starting transfers between devices: 6.16 us -> 7.32 us  [rotate(): return lax.ppermute(values, 'shot', pairs)]
    ppermute x6, waiting for transfers between devices: 7.4 us -> 8.41 us  [rotate(): return lax.ppermute(values, 'shot', pairs)]
    pallas_call x1, Pallas kernels: 7.74 us -> 6.82 us  [second(): pl.pallas_call(body, grid=(shot_dev // step,), in_specs=[full_smem()] * 4...]
  transfers between devices with their start and end apart: 9 -> 9, of which waited for: 5 -> 7; matrix products, arithmetic and copies ran while one was open for 6% -> 7% of each run, Pallas kernels for 9% -> 10%
where the time goes in v3:
time: 68.3 us
  waiting for transfers between devices  24.5 us (36%)
  Pallas kernels  21.3 us (31%)
  starting transfers between devices  15.9 us (23%)
  other arithmetic  3.24 us (5%)
  local copies, waits for them, and re-layouts  2.53 us (4%)
  between operations  0.83 us (1%)
    all_to_all x1, waiting for transfers between devices, local(): lax.all_to_all(packed, 'shot', split_axis=0, concat_axis=0, tiled=True)  10.7 us
    ppermute x6, waiting for transfers between devices, rotate(): return lax.ppermute(values, 'shot', pairs)  8.41 us
    ppermute x6, starting transfers between devices, rotate(): return lax.ppermute(values, 'shot', pairs)  7.32 us
    pallas_call x1, Pallas kernels, second(): pl.pallas_call(body, grid=(shot_dev // step,), in_specs=[full_smem()] * 4...  6.82 us
    pallas_call x1, Pallas kernels, remainder(): pl.pallas_call(body, grid=(windows // step,), in_specs=[full_smem(), full...  6.49 us
    all_to_all x1, starting transfers between devices, local(): lax.all_to_all(packed, 'shot', split_axis=0, concat_axis=0, tiled=True)  5.48 us
    ppermute x2, waiting for transfers between devices, over_receivers(): return [values, lax.ppermute(values, 'rcv', [(0, 1), (1, 0)])]  5.36 us
    pallas_call x1, Pallas kernels, head(): pl.pallas_call(body, in_specs=[full_smem(), hbm, hbm, hbm], out_specs=[pl...  4.39 us
  transfers between devices with their start and end apart: 9, of which 7 were waited for; matrix products, arithmetic and copies ran while one was open for 7% of the time, Pallas kernels for 10%

profile of v3, /device:TPU:16, one launch (start us, length us, event | category | flops | bytes accessed | tf_op | source)
XLA Modules:
  0.0 68.3 jit_solution(5189781042187193237)
XLA Ops:
  0.6 4.4 %pack_coefficients.1 = (bf16[16,384,128]{2,1,0:T(8,128)(2,1)}, f32[16,128]{1,0:T(8,128)}) custom-call(s32[1]{0:T(128)} %bitcast.me_ref, s32[1,256]{1,0:T(1,128)} %bitcast.16, f32[16,128,128]{2,1,0:T(8,128)} %bitcast.9, bf16[128,256]{1,0:T(8,128)(2,1)} %constant.79.both_hbm.both_ref.refs_2_), custom_call_target="tpu_custom_call" | custom-call | tf_op jit(solution)/shard_map/pack_coefficients/pallas_call | solution.py:142
  5.0 0.5 collective-permute-start.2
  5.5 3.5 %collective-permute-start.1 = (f32[16,128]{1,0:T(8,128)}, f32[16,128]{1,0:T(8,128)S(1)}, u32[]{:S(2)}, u32[]{:S(2)}) collective-permute-start(f32[16,128]{1,0:T(8,128)} %get-tuple-element.13), channel_id=1, source_target_pairs={{0,8},{1,9},{2,10},{3,11},{4,12},{5,13},{6,14},{7,15},{8,0},{9,1},... | collective-permute-start | bytes 24584 | tf_op jit(solution)/shard_map/ppermute | solution.py:364
  9.0 0.0 collective-permute-start
  9.0 0.8 %dynamic_slice.3 = s32[16]{0:T(128)S(1)} dynamic-slice(s32[256]{0:T(256)} %param.5, s32[]{:T(128)S(6)} %select_n.48), dynamic_slice_sizes={16} | dynamic-slice | bytes 132 | tf_op jit(solution)/shard_map/dynamic_slice | solution.py:405
  9.8 0.1 broadcast_add_fusion.2
  9.9 0.1 broadcast_add_fusion
  10.0 0.4 convert_reduce_fusion.1
  10.4 0.1 multiply_reduce_fusion
  10.5 0.2 convert_reduce_fusion.4
  10.7 0.0 collective-permute-done.2
  10.7 0.2 collective-permute-done.1
  10.9 1.9 %collective-permute-done = f32[16,128]{1,0:T(8,128)S(1)} collective-permute-done((f32[16,128]{1,0:T(8,128)}, f32[16,128]{1,0:T(8,128)S(1)}, u32[]{:S(2)}, u32[]{:S(2)}) %collective-permute-start) | collective-permute-done | bytes 8224 | tf_op jit(solution)/shard_map/ppermute | solution.py:364
  12.9 5.5 %all-to-all-start = ((bf16[16,384,128]{2,1,0:T(8,128)(2,1)}), bf16[16,384,128]{2,1,0:T(8,128)(2,1)S(1)}, u32[]{:S(2)}, u32[]{:S(2)}) async-start(bf16[16,384,128]{2,1,0:T(8,128)(2,1)} %get-tuple-element.14), calls=%async_computation | async-start | bytes 3145728 | tf_op jit(solution)/shard_map/all_to_all | solution.py:389
  18.4 0.1 add.197
  18.5 0.0 copy-done.3
  18.5 0.3 convert_reduce_fusion.2
  18.7 0.1 copy.9
  18.8 0.1 mul.85.high_ref
  18.9 0.1 copy.8
  19.0 0.1 mul.83.low_ref
  19.1 0.2 convert_reduce_fusion
  19.3 0.1 select_reduce_fusion.1
  19.4 0.0 copy-done.4
  19.5 0.1 iota_add_fusion
  19.5 0.1 broadcast_add_fusion.1
  19.6 0.1 fusion.1.refs_0_
  19.8 0.2 collective-permute-start.3
  20.0 1.3 %select_reduce_fusion = s32[16,4]{1,0:T(8,128)S(1)} fusion(s32[16,16]{1,0:T(8,128)S(1)} %broadcast_add_fusion.1, s32[16,16]{1,0:T(8,128)S(1)} %iota_add_fusion.1, s32[16,4]{1,0:T(8,128)S(1)} %iota_add_fusion), kind=kLoop, calls=%fused_computation | loop fusion | flops 49088 | bytes 2560 | tf_op jit(solution)/shard_map/reduce_sum | solution.py:431
  21.3 1.6 %collective-permute-start.5 = (f32[64,128]{1,0:T(8,128)S(1)}, f32[64,128]{1,0:T(8,128)S(1)}, u32[]{:S(2)}, u32[]{:S(2)}) collective-permute-start(f32[64,128]{1,0:T(8,128)S(1)} %get-tuple-element.34), channel_id=1, source_target_pairs={{0,3},{1,0},{2,1},{3,2},{4,7},{5,4},{6,5},{7,6},{8,11},{9,8},{10,9... | collective-permute-start | bytes 98312 | tf_op jit(solution)/shard_map/ppermute | solution.py:364
  22.9 1.5 %collective-permute-start.4 = (f32[64,128]{1,0:T(8,128)S(1)}, f32[64,128]{1,0:T(8,128)S(1)}, u32[]{:S(2)}, u32[]{:S(2)}) collective-permute-start(f32[64,128]{1,0:T(8,128)S(1)} %get-tuple-element.34), channel_id=1, source_target_pairs={{0,2},{1,3},{2,0},{3,1},{4,6},{5,7},{6,4},{7,5},{8,10},{9,11},{10,... | collective-permute-start | bytes 98312 | tf_op jit(solution)/shard_map/ppermute | solution.py:364
  24.4 3.2 %collective-permute-done.3 = f32[64,128]{1,0:T(8,128)S(1)} collective-permute-done((f32[64,128]{1,0:T(8,128)S(1)}, f32[64,128]{1,0:T(8,128)S(1)}, u32[]{:S(2)}, u32[]{:S(2)}) %collective-permute-start.3) | collective-permute-done | bytes 32800 | tf_op jit(solution)/shard_map/ppermute | solution.py:364
  27.6 3.1 %collective-permute-done.4 = f32[64,128]{1,0:T(8,128)S(1)} collective-permute-done((f32[64,128]{1,0:T(8,128)S(1)}, f32[64,128]{1,0:T(8,128)S(1)}, u32[]{:S(2)}, u32[]{:S(2)}) %collective-permute-start.4) | collective-permute-done | bytes 32800 | tf_op jit(solution)/shard_map/ppermute | solution.py:364
  30.7 0.0 collective-permute-done.5
  30.7 1.6 %collective-permute-start.6 = (f32[256,128]{1,0:T(8,128)S(1)}, f32[256,128]{1,0:T(8,128)S(1)}, u32[]{:S(2)}, u32[]{:S(2)}) collective-permute-start(f32[256,128]{1,0:T(8,128)S(1)} %constant_dynamic-update-slice_fusion.4.refs_2_), channel_id=1, source_target_pairs={{0,16},{16,0},{1,17},{17,1},{2,18},{18,2},{3,19},{19,3},{4,20},{20... | collective-permute-start | bytes 393224 | tf_op jit(solution)/shard_map/ppermute | solution.py:354
  32.2 0.1 reshape.267.slot_ref
  32.3 0.2 convert_reduce_fusion.5
  32.5 3.2 %collective-permute-done.6.refs_3_ = f32[256,128]{1,0:T(8,128)S(1)} collective-permute-done((f32[256,128]{1,0:T(8,128)S(1)}, f32[256,128]{1,0:T(8,128)S(1)}, u32[]{:S(2)}, u32[]{:S(2)}) %collective-permute-start.6) | collective-permute-done | bytes 131104 | tf_op jit(solution)/shard_map/ppermute | solution.py:354
  35.7 0.6 first_cutoffs.1.cut_ref
  36.3 0.0 copy-done.1
  36.3 0.0 copy-start
  36.3 1.2 %copy-done = f32[16,1,128,128]{3,2,1,0:T(8,128)S(1)} copy-done((f32[16,1,128,128]{3,2,1,0:T(8,128)S(1)}, f32[16,1,128,128]{3,2,1,0:T(8,128)}, u32[]{:S(2)}) %copy-start) | copy-done | bytes 1048600
  37.6 6.5 %residual_of_records.1 = f32[16,128,128]{2,1,0:T(8,128)} custom-call(s32[16]{0:T(128)S(1)} %get-tuple-element.31.low_ref, s32[16]{0:T(128)S(1)} %get-tuple-element.30.high_ref, f32[16,128,128]{2,1,0:T(8,128)S(1)} %bitcast.10, f32[272,8,128]{2,1,0:T(8,128)S(1)} %first_cutoffs.1.cut_ref, bf16[128,256]{1,0:T(8,128)(2,1)S(1)} %copy-done.1), custom_call_target="tpu_custom_call" | custom-call | flops 1 | bytes 6291456 | tf_op jit(solution)/shard_map/residual_of_records/pallas_call | solution.py:296
  44.1 10.7 %all-to-all-done.in_ref = bf16[16,384,128]{2,1,0:T(8,128)(2,1)S(1)} async-done(((bf16[16,384,128]{2,1,0:T(8,128)(2,1)}), bf16[16,384,128]{2,1,0:T(8,128)(2,1)S(1)}, u32[]{:S(2)}, u32[]{:S(2)}) %all-to-all-start) | async-done | bytes 1572896 | tf_op jit(solution)/shard_map/all_to_all | solution.py:389
  54.8 6.8 %second_coefficients.1 = (f32[16,4,128,128]{3,2,1,0:T(8,128)S(1)}, f32[16,128]{1,0:T(8,128)S(1)}) custom-call(s32[48]{0:T(128)S(1)} %mul.83.low_ref, s32[48]{0:T(128)S(1)} %mul.85.high_ref, f32[48]{0:T(128)S(1)} %maximum_divide_fusion.scale_ref, s32[64]{0:T(128)S(1)} %reshape.267.slot_ref, bf16[16,384,128]{2,1,0:T(8,128)(2,1)S(1)} %all-to-all-done.in_ref, ...), custom_call_target="tpu_custom_call" | custom-call | flops 1 | bytes 12582912 | tf_op jit(solution)/shard_map/second_coefficients/pallas_call | solution.py:256
  61.6 1.6 %collective-permute-start.7 = (f32[16,128]{1,0:T(8,128)S(1)}, f32[16,128]{1,0:T(8,128)S(1)}, u32[]{:S(2)}, u32[]{:S(2)}) collective-permute-start(f32[16,128]{1,0:T(8,128)S(1)} %get-tuple-element.20), channel_id=1, source_target_pairs={{0,16},{16,0},{1,17},{17,1},{2,18},{18,2},{3,19},{19,3},{4,20},{20... | collective-permute-start | bytes 24584 | tf_op jit(solution)/shard_map/ppermute | solution.py:354
  63.2 2.2 %collective-permute-done.7 = f32[16,128]{1,0:T(8,128)S(1)} collective-permute-done((f32[16,128]{1,0:T(8,128)S(1)}, f32[16,128]{1,0:T(8,128)S(1)}, u32[]{:S(2)}, u32[]{:S(2)}) %collective-permute-start.7) | collective-permute-done | bytes 8224 | tf_op jit(solution)/shard_map/ppermute | solution.py:354
  65.3 3.0 %model_of_shots.1 = bf16[16,4,128,128]{3,2,1,0:T(8,128)(2,1)} custom-call(f32[16,4,128,128]{3,2,1,0:T(8,128)S(1)} %get-tuple-element.19.refs_0_, f32[1,128]{1,0:T(1,128)S(1)} %bitcast.14, bf16[128,256]{1,0:T(8,128)(2,1)S(1)} %copy-done.1, f32[4,4,128]{2,1,0:T(4,128)S(1)} %bitcast.11, f32[4,4,128]{2,1,0:T(4,128)S(1)} %bitcast.12), custom_call_target="tpu_custom_call" | custom-call | tf_op jit(solution)/shard_map/model_of_shots/pallas_call | solution.py:336
  (23 shorter events, 0.1 us)
Async XLA Ops:
  5.0 5.7 %collective-permute-start.2 = (f32[16,128]{1,0:T(8,128)}, f32[16,128]{1,0:T(8,128)S(1)}, u32[]{:S(2)}, u32[]{:S(2)}) collective-permute-start(f32[16,128]{1,0:T(8,128)} %get-tuple-element.13), channel_id=1, source_target_pairs={{0,12},{1,13},{2,14},{3,15},{4,0},{5,1},{6,2},{7,3},{8,4},{9,5},{1... | collective-permute-start | bytes 24584 | tf_op jit(solution)/shard_map/ppermute | solution.py:364
  5.5 5.4 %collective-permute-start.1 = (f32[16,128]{1,0:T(8,128)}, f32[16,128]{1,0:T(8,128)S(1)}, u32[]{:S(2)}, u32[]{:S(2)}) collective-permute-start(f32[16,128]{1,0:T(8,128)} %get-tuple-element.13), channel_id=1, source_target_pairs={{0,8},{1,9},{2,10},{3,11},{4,12},{5,13},{6,14},{7,15},{8,0},{9,1},... | collective-permute-start | bytes 24584 | tf_op jit(solution)/shard_map/ppermute | solution.py:364
  9.0 3.9 %collective-permute-start = (f32[16,128]{1,0:T(8,128)}, f32[16,128]{1,0:T(8,128)S(1)}, u32[]{:S(2)}, u32[]{:S(2)}) collective-permute-start(f32[16,128]{1,0:T(8,128)} %get-tuple-element.13), channel_id=1, source_target_pairs={{0,4},{1,5},{2,6},{3,7},{4,8},{5,9},{6,10},{7,11},{8,12},{9,13},{1... | collective-permute-start | bytes 24584 | tf_op jit(solution)/shard_map/ppermute | solution.py:364
  12.9 5.6 %copy-start.3 = (s32[256]{0:T(256)S(1)}, s32[256]{0:T(256)}, u32[]{:S(2)}) copy-start(s32[256]{0:T(256)} %param.5) | copy-start | bytes 3076
  12.9 6.6 %copy-start.4 = (f32[16,128]{1,0:T(8,128)S(1)}, f32[16,128]{1,0:T(8,128)}, u32[]{:S(2)}) copy-start(f32[16,128]{1,0:T(8,128)} %get-tuple-element.13) | copy-start | bytes 24580
  12.9 22.8 %copy-start.2 = (f32[128]{0:T(128)S(1)}, f32[128]{0:T(128)}, u32[]{:S(2)}) copy-start(f32[128]{0:T(128)} %param.6) | copy-start | bytes 1540
  12.9 41.9 %all-to-all-start = ((bf16[16,384,128]{2,1,0:T(8,128)(2,1)}), bf16[16,384,128]{2,1,0:T(8,128)(2,1)S(1)}, u32[]{:S(2)}, u32[]{:S(2)}) async-start(bf16[16,384,128]{2,1,0:T(8,128)(2,1)} %get-tuple-element.14), calls=%async_computation | async-start | bytes 3145728 | tf_op jit(solution)/shard_map/all_to_all | solution.py:389
  18.4 18.0 %copy-start.1 = (bf16[128,256]{1,0:T(8,128)(2,1)S(1)}, bf16[128,256]{1,0:T(8,128)(2,1)}, u32[]{:S(2)}) copy-start(bf16[128,256]{1,0:T(8,128)(2,1)} %constant.79.both_hbm.both_ref.refs_2_) | copy-start | bytes 196612
  19.8 7.8 %collective-permute-start.3 = (f32[64,128]{1,0:T(8,128)S(1)}, f32[64,128]{1,0:T(8,128)S(1)}, u32[]{:S(2)}, u32[]{:S(2)}) collective-permute-start(f32[64,128]{1,0:T(8,128)S(1)} %get-tuple-element.34), channel_id=1, source_target_pairs={{0,1},{1,2},{2,3},{3,0},{4,5},{5,6},{6,7},{7,4},{8,9},{9,10},{10,1... | collective-permute-start | bytes 98312 | tf_op jit(solution)/shard_map/ppermute | solution.py:364
  21.3 9.4 %collective-permute-start.5 = (f32[64,128]{1,0:T(8,128)S(1)}, f32[64,128]{1,0:T(8,128)S(1)}, u32[]{:S(2)}, u32[]{:S(2)}) collective-permute-start(f32[64,128]{1,0:T(8,128)S(1)} %get-tuple-element.34), channel_id=1, source_target_pairs={{0,3},{1,0},{2,1},{3,2},{4,7},{5,4},{6,5},{7,6},{8,11},{9,8},{10,9... | collective-permute-start | bytes 98312 | tf_op jit(solution)/shard_map/ppermute | solution.py:364
  22.9 7.7 %collective-permute-start.4 = (f32[64,128]{1,0:T(8,128)S(1)}, f32[64,128]{1,0:T(8,128)S(1)}, u32[]{:S(2)}, u32[]{:S(2)}) collective-permute-start(f32[64,128]{1,0:T(8,128)S(1)} %get-tuple-element.34), channel_id=1, source_target_pairs={{0,2},{1,3},{2,0},{3,1},{4,6},{5,7},{6,4},{7,5},{8,10},{9,11},{10,... | collective-permute-start | bytes 98312 | tf_op jit(solution)/shard_map/ppermute | solution.py:364
  30.7 5.0 %collective-permute-start.6 = (f32[256,128]{1,0:T(8,128)S(1)}, f32[256,128]{1,0:T(8,128)S(1)}, u32[]{:S(2)}, u32[]{:S(2)}) collective-permute-start(f32[256,128]{1,0:T(8,128)S(1)} %constant_dynamic-update-slice_fusion.4.refs_2_), channel_id=1, source_target_pairs={{0,16},{16,0},{1,17},{17,1},{2,18},{18,2},{3,19},{19,3},{4,20},{20... | collective-permute-start | bytes 393224 | tf_op jit(solution)/shard_map/ppermute | solution.py:354
  36.3 1.2 %copy-start = (f32[16,1,128,128]{3,2,1,0:T(8,128)S(1)}, f32[16,1,128,128]{3,2,1,0:T(8,128)}, u32[]{:S(2)}) copy-start(f32[16,1,128,128]{3,2,1,0:T(8,128)} %param.4) | copy-start | bytes 3145732
  61.6 3.7 %collective-permute-start.7 = (f32[16,128]{1,0:T(8,128)S(1)}, f32[16,128]{1,0:T(8,128)S(1)}, u32[]{:S(2)}, u32[]{:S(2)}) collective-permute-start(f32[16,128]{1,0:T(8,128)S(1)} %get-tuple-element.20), channel_id=1, source_target_pairs={{0,16},{16,0},{1,17},{17,1},{2,18},{18,2},{3,19},{19,3},{4,20},{20... | collective-permute-start | bytes 24584 | tf_op jit(solution)/shard_map/ppermute | solution.py:354

commit v4 on v3

v4 whole, which is shorter than its diff:
```python
import jax
import jax.numpy as jnp
import numpy as np
from jax import lax
from jax.experimental import pallas as pl
from jax.experimental.pallas import tpu as pltpu
from jax.sharding import PartitionSpec as P

SHOT_BLK = 4
momentum = 0.5
epsilon = 1e-06
step_size = 1.0 + momentum
VMEM_BYTES = 16 * 1024 * 1024
HEAD_VMEM_BYTES = 60 * 1024 * 1024


def cosine_table(length):
    rows = np.arange(length, dtype=np.float64)[:, None]
    cols = np.arange(length, dtype=np.float64)[None, :]
    table = np.cos(np.pi * (cols + 0.5) * rows / length) * np.sqrt(2.0 / length)
    return np.where(rows == 0, table * np.sqrt(0.5), table).astype(np.float32)


def split_bf16(values):
    high = values.astype(jnp.bfloat16)
    low = (values - high.astype(jnp.float32)).astype(jnp.bfloat16)
    return high, low


def full_vmem():
    return pl.BlockSpec(memory_space=pltpu.VMEM)


def full_smem():
    return pl.BlockSpec(memory_space=pltpu.SMEM)


def params(vmem=VMEM_BYTES):
    return pltpu.CompilerParams(vmem_limit_bytes=vmem)


def forward(both, values):
    block = values.shape[0]
    parts = lax.dot_general(
        values, both, (((0,), (0,)), ((), ())), preferred_element_type=jnp.float32
    )
    return parts[:, :block] + parts[:, block:]


def backward(both, coefficients):
    doubled = jnp.concatenate([coefficients, coefficients], axis=1)
    return lax.dot_general(
        both, doubled, (((1,), (1,)), ((), ())), preferred_element_type=jnp.float32
    )


def landed(ids, offsets):
    lag = ids - offsets
    return (lag >= 0) & (lag < SHOT_BLK)


def owned(records, offsets, me, owners, capacity, both):
    windows, block, rcv = records.shape
    shots = offsets.shape[0]
    shot_dev = shots // owners
    chunk = 4
    chunks = windows // chunk
    f32, bf16 = jnp.float32, jnp.bfloat16

    def body(
        me_ref, off_hbm, rec_hbm, both_hbm, sent_ref, energy_ref, table_ref,
        off_ref, rec_ref, both_ref, small_sem, rec_sem,
    ):
        get_off = pltpu.make_async_copy(off_hbm, off_ref, small_sem.at[0])
        get_both = pltpu.make_async_copy(both_hbm, both_ref, small_sem.at[1])
        get_rec = [
            pltpu.make_async_copy(
                rec_hbm.at[pl.ds(c * chunk, chunk)],
                rec_ref.at[pl.ds(c * chunk, chunk)],
                rec_sem.at[c],
            )
            for c in range(chunks)
        ]
        get_off.start()
        get_both.start()
        for copy in get_rec:
            copy.start()
        get_off.wait()

        ids = lax.broadcasted_iota(jnp.int32, (windows, shots), 0) * owners + me_ref[0]
        hits = jnp.where(landed(ids, off_ref[...]), 1.0, 0.0)
        cover = jnp.sum(hits, axis=1, keepdims=True)
        scale = 1.0 / jnp.maximum(cover, 1.0)

        shot = lax.broadcasted_iota(jnp.int32, (shots, owners), 0)
        first = lax.broadcasted_iota(jnp.int32, (shots, owners), 1) * shot_dev
        member = jnp.where((shot >= first) & (shot < first + shot_dev), 1.0, 0.0)
        counts = jnp.dot(hits.astype(bf16), member.astype(bf16), preferred_element_type=f32)
        present = jnp.where(counts > 0.5, 1.0, 0.0)
        after = lax.broadcasted_iota(jnp.int32, (windows, windows), 0)
        before = lax.broadcasted_iota(jnp.int32, (windows, windows), 1)
        lower = jnp.where(before < after, 1.0, 0.0)
        rank = jnp.dot(lower.astype(bf16), present.astype(bf16), preferred_element_type=f32)
        rank = rank.astype(jnp.int32)
        window = lax.broadcasted_iota(jnp.int32, (windows, owners), 0)
        for i in range(capacity):
            here = (rank == i) & (present > 0.5)
            table_ref[i : i + 1, :owners] = jnp.sum(
                jnp.where(here, window, 0), axis=0, keepdims=True
            )

        get_both.wait()
        for c in range(chunks):
            get_rec[c].wait()
            for w in range(c * chunk, (c + 1) * chunk):
                spread = (rec_ref[w] * scale[w : w + 1, 0:1]).astype(bf16)
                coef = forward(both_ref[...], spread)
                sent_ref[w] = coef.astype(bf16)
                energy_ref[w : w + 1, :] = jnp.sum(coef * coef, axis=0, keepdims=True)

    hbm = pl.BlockSpec(memory_space=pltpu.HBM)
    return pl.pallas_call(
        body,
        in_specs=[full_smem(), hbm, hbm, hbm],
        out_specs=[full_vmem()] * 3,
        out_shape=[
            jax.ShapeDtypeStruct((windows, rcv, block), bf16),
            jax.ShapeDtypeStruct((windows, block), f32),
            jax.ShapeDtypeStruct((8, 128), jnp.int32),
        ],
        scratch_shapes=[
            pltpu.VMEM((1, shots), jnp.int32),
            pltpu.VMEM((windows, block, rcv), f32),
            pltpu.VMEM((block, 2 * block), bf16),
            pltpu.SemaphoreType.DMA((2,)),
            pltpu.SemaphoreType.DMA((chunks,)),
        ],
        compiler_params=params(HEAD_VMEM_BYTES),
        name="owned_coefficients",
    )(me[None], offsets[None, :], records, both)


def pack(sent, table, energies, owners, capacity):
    windows, rcv, block = sent.shape
    rows = capacity * rcv + windows

    def body(table_ref, sent_ref, *refs):
        out_ref, energy_ref, block_sem, energy_sem = refs[-4:]
        energy = refs[0][...]
        for ref in refs[1:-4]:
            energy = energy + ref[...]
        energy_ref[...] = energy.astype(jnp.bfloat16)

        def blocks(h, i):
            return pltpu.make_async_copy(
                sent_ref.at[table_ref[i, h]],
                out_ref.at[h, pl.ds(i * rcv, rcv), :],
                block_sem.at[h * capacity + i],
            )

        def rest(h):
            return pltpu.make_async_copy(
                energy_ref, out_ref.at[h, pl.ds(capacity * rcv, windows), :], energy_sem.at[h]
            )

        for h in range(owners):
            for i in range(capacity):
                blocks(h, i).start()
            rest(h).start()
        for h in range(owners):
            for i in range(capacity):
                blocks(h, i).wait()
            rest(h).wait()

    return pl.pallas_call(
        body,
        in_specs=[full_smem(), pl.BlockSpec(memory_space=pl.ANY)] + [full_vmem()] * len(energies),
        out_specs=pl.BlockSpec(memory_space=pl.ANY),
        out_shape=jax.ShapeDtypeStruct((owners, rows, block), jnp.bfloat16),
        scratch_shapes=[
            pltpu.VMEM((windows, block), jnp.bfloat16),
            pltpu.SemaphoreType.DMA((owners * capacity,)),
            pltpu.SemaphoreType.DMA((owners,)),
        ],
        compiler_params=params(),
        name="pack_blocks",
    )(table, sent, *energies)


def clipped_sum(coef, cut_ref, low, high, none):
    size = jnp.abs(coef)
    unroll = 2

    def add(j, total):
        for u in range(unroll):
            row = low + j * unroll + u
            if u:
                row = jnp.where(row < high, row, none)
            total = total + jnp.minimum(size, cut_ref[row][None])
        return total

    trips = lax.div(high - low + unroll - 1, unroll)
    total = lax.fori_loop(0, trips, add, jnp.zeros_like(coef))
    return jnp.where(coef < 0, -total, total)


def second(arrived, hits, thresholds, lows, highs, scales, slots, capacity, windows, receivers):
    owners, rows, block = arrived.shape
    rcv = (rows - windows) // capacity
    tiles = rcv // 8
    shot_dev = slots.shape[0] // SHOT_BLK
    count = owners * capacity
    cut_rows = hits.shape[0]
    shots = cut_rows - shot_dev

    def body(
        low_ref, high_ref, scale_ref, slot_ref, in_ref, hit_ref, thr_ref,
        out_ref, energy_ref, wide_ref, cuts_ref, diff_ref,
    ):
        energy = in_ref[:, capacity * rcv :, :].reshape(owners * windows, block)
        sums = jnp.dot(hit_ref[...], energy, preferred_element_type=jnp.float32)
        cuts_ref[...] = thr_ref[...] * jnp.sqrt(sums / (SHOT_BLK * receivers) + epsilon)

        def widen(i, _):
            at = pl.multiple_of(i * 8, 8)
            wide_ref[pl.ds(at, 8)] = jnp.broadcast_to(
                cuts_ref[pl.ds(at, 8), :][:, None, :], (8, 8, block)
            )
            return 0

        lax.fori_loop(0, cut_rows // 8, widen, 0, unroll=2)
        wide_ref[cut_rows] = jnp.zeros((8, block), jnp.float32)

        def block_of(slot):
            owner = slot // capacity
            start = pl.multiple_of((slot - owner * capacity) * rcv, rcv)
            values = in_ref[owner, pl.ds(start, rcv), :].astype(jnp.float32)
            return values.reshape(tiles, 8, block)

        def difference(slot, _):
            low, high = low_ref[slot], high_ref[slot]

            @pl.when(high > low)
            def _():
                coef = block_of(slot)
                clipped = clipped_sum(coef, wide_ref, low, high, cut_rows)
                scale = scale_ref[slot]
                kept = 1.0 - scale * (high - low).astype(jnp.float32)
                diff_ref[slot] = kept * coef + scale * clipped

            return 0

        lax.fori_loop(0, count, difference, 0)

        def one_shot(shot, _):
            cut = wide_ref[shots + shot][None]
            energy = jnp.zeros((8, block), jnp.float32)
            for q in range(SHOT_BLK):
                slot = slot_ref[shot * SHOT_BLK + q]
                coef = block_of(slot)
                shrunk = coef - jnp.minimum(jnp.maximum(coef, -cut), cut)
                value = step_size * shrunk + diff_ref[slot]
                out_ref[shot, q] = value.reshape(rcv, block)
                energy = energy + jnp.sum(value * value, axis=0)
            energy_ref[pl.ds(shot, 1), :] = jnp.sum(energy, axis=0, keepdims=True)
            return 0

        lax.fori_loop(0, shot_dev, one_shot, 0)

    return pl.pallas_call(
        body,
        in_specs=[full_smem()] * 4 + [full_vmem()] * 3,
        out_specs=[full_vmem()] * 3,
        out_shape=[
            jax.ShapeDtypeStruct((shot_dev, SHOT_BLK, rcv, block), jnp.float32),
            jax.ShapeDtypeStruct((shot_dev, block), jnp.float32),
            jax.ShapeDtypeStruct((cut_rows + 1, 8, block), jnp.float32),
        ],
        scratch_shapes=[
            pltpu.VMEM((cut_rows, block), jnp.float32),
            pltpu.VMEM((count, tiles, 8, block), jnp.float32),
        ],
        compiler_params=params(),
        cost_estimate=pl.CostEstimate(flops=1, bytes_accessed=12 << 20, transcendentals=0),
        name="second_coefficients",
    )(lows, highs, scales, slots, arrived, hits, thresholds)


def again(records, lows, highs, both):
    windows, block, rcv = records.shape

    def body(low_ref, high_ref, rec_ref, both_ref, out_ref):
        for w in range(windows):
            many = jnp.full((1, rcv), (high_ref[w] - low_ref[w]).astype(jnp.float32))
            spread = (rec_ref[w] * (1.0 / jnp.maximum(many, 1.0))).astype(jnp.bfloat16)
            out_ref[w] = forward(both_ref[...], spread)

    return pl.pallas_call(
        body,
        in_specs=[full_smem()] * 2 + [full_vmem()] * 2,
        out_specs=full_vmem(),
        out_shape=jax.ShapeDtypeStruct((windows, rcv, block), jnp.float32),
        compiler_params=params(),
        cost_estimate=pl.CostEstimate(flops=1, bytes_accessed=6 << 20, transcendentals=0),
        name="owned_again",
    )(lows, highs, records, both)


def remainder(records, coefs, cuts, lows, highs, both):
    windows, block, rcv = records.shape
    tiles = rcv // 8
    none = cuts.shape[0] - 1
    group = 4

    def body(
        low_ref, high_ref, rec_ref, coef_ref, cut_ref, both_ref, out_hbm, sum_ref, out_ref, sem
    ):
        copies = []
        for at in range(0, windows, group):
            for w in range(at, at + group):
                low, high = low_ref[w], high_ref[w]
                coef = coef_ref[w].reshape(tiles, 8, block)
                clipped = clipped_sum(coef, cut_ref, low, high, none)
                shrunk = (high - low).astype(jnp.float32) * coef - clipped
                sum_ref[pl.ds((w - at) * rcv, rcv), :] = shrunk.reshape(rcv, block).astype(
                    jnp.bfloat16
                )
            blended = backward(both_ref[...], sum_ref[...])
            for w in range(at, at + group):
                part = blended[:, (w - at) * rcv : (w - at + 1) * rcv]
                out_ref[w] = rec_ref[w] - step_size * part
            copy = pltpu.make_async_copy(
                out_ref.at[pl.ds(at, group)], out_hbm.at[pl.ds(at, group)], sem.at[at // group]
            )
            copy.start()
            copies.append(copy)
        for copy in copies:
            copy.wait()

    return pl.pallas_call(
        body,
        in_specs=[full_smem()] * 2 + [full_vmem()] * 4,
        out_specs=pl.BlockSpec(memory_space=pl.ANY),
        out_shape=jax.ShapeDtypeStruct((windows, block, rcv), jnp.float32),
        scratch_shapes=[
            pltpu.VMEM((group * rcv, block), jnp.bfloat16),
            pltpu.VMEM((windows, block, rcv), jnp.float32),
            pltpu.SemaphoreType.DMA((windows // group,)),
        ],
        compiler_params=params(),
        cost_estimate=pl.CostEstimate(flops=1, bytes_accessed=6 << 20, transcendentals=0),
        name="residual_of_records",
    )(lows, highs, records, coefs, cuts, both)


def finish(values, energies, thresholds, both, receivers):
    shot_dev, _, rcv, block = values.shape
    step = min(2, shot_dev)

    def body(in_ref, thr_ref, both_ref, *refs):
        out_hbm, out_ref, sem = refs[-3:]
        energy = refs[0][...]
        for ref in refs[1:-3]:
            energy = energy + ref[...]
        cuts = thr_ref[...] * jnp.sqrt(energy / (SHOT_BLK * receivers) + epsilon)
        copies = []
        for at in range(0, shot_dev, step):
            for i in range(at, at + step):
                cut = cuts[i : i + 1, :]
                value = in_ref[i].reshape(SHOT_BLK * rcv, block)
                shrunk = value - jnp.minimum(jnp.maximum(value, -cut), cut)
                model = lax.dot_general(
                    both_ref[:, :block], shrunk.astype(jnp.bfloat16), (((1,), (1,)), ((), ())),
                    preferred_element_type=jnp.float32,
                )
                for q in range(SHOT_BLK):
                    out_ref[i, q] = model[:, q * rcv : (q + 1) * rcv].astype(jnp.bfloat16)
            copy = pltpu.make_async_copy(
                out_ref.at[pl.ds(at, step)], out_hbm.at[pl.ds(at, step)], sem.at[at // step]
            )
            copy.start()
            copies.append(copy)
        for copy in copies:
            copy.wait()

    return pl.pallas_call(
        body,
        in_specs=[full_vmem()] * (3 + len(energies)),
        out_specs=pl.BlockSpec(memory_space=pl.ANY),
        out_shape=jax.ShapeDtypeStruct((shot_dev, SHOT_BLK, block, rcv), jnp.bfloat16),
        scratch_shapes=[
            pltpu.VMEM((shot_dev, SHOT_BLK, block, rcv), jnp.bfloat16),
            pltpu.SemaphoreType.DMA((shot_dev // step,)),
        ],
        compiler_params=params(),
        name="model_of_shots",
    )(values, thresholds, both, *energies)


def over_receivers(values):
    if lax.axis_size("rcv") == 2:
        return [values, lax.ppermute(values, "rcv", [(0, 1), (1, 0)])]
    return [lax.psum(values, "rcv")]


def local(record_data, offsets, thresholds):
    owners = lax.axis_size("shot")
    me = lax.axis_index("shot")
    windows, _, block, rcv = record_data.shape
    shots = offsets.shape[0]
    shot_dev = shots // owners
    pairs = shot_dev // 2
    pair_slots = min(pairs, owners // (SHOT_BLK + 1))
    capacity = (pairs + pair_slots - 1) // pair_slots
    receivers = rcv * lax.axis_size("rcv")

    high, low = split_bf16(jnp.asarray(cosine_table(block).T))
    both = jnp.concatenate([high, low], axis=1)
    records = record_data.reshape(windows, block, rcv)
    thr = thresholds[None, :]
    window_ids = jnp.arange(windows, dtype=jnp.int32)

    sent, energy, table = owned(records, offsets, me, owners, capacity, both)
    packed = pack(sent, table, over_receivers(energy), owners, capacity)
    arrived = lax.all_to_all(packed, "shot", split_axis=0, concat_axis=0, tiled=True)

    index = jnp.arange(shots, dtype=jnp.int32)
    ahead = (offsets[None, :] < offsets[:, None]) | (
        (offsets[None, :] == offsets[:, None]) & (index[None, :] < index[:, None])
    )
    place = jnp.sum(ahead.astype(jnp.int32), axis=1)
    ordered = jnp.sum(jnp.where(place[None, :] == index[:, None], offsets[None, :], 0), axis=1)
    mine = lax.dynamic_slice(offsets, (me * shot_dev,), (shot_dev,))
    all_offsets = jnp.concatenate([ordered, mine])
    grid_ids = window_ids[None, :] * owners + jnp.arange(owners, dtype=jnp.int32)[:, None]
    hits = landed(grid_ids.reshape(-1)[None, :], all_offsets[:, None]).astype(jnp.bfloat16)

    def bounds(ids):
        below = jnp.sum((offsets < ids[..., None] - (SHOT_BLK - 1)).astype(jnp.int32), axis=-1)
        upto = jnp.sum((offsets <= ids[..., None]).astype(jnp.int32), axis=-1)
        return below, upto

    own_lows, own_highs = bounds(window_ids * owners + me)
    coefs = again(records, own_lows, own_highs, both)

    slot_ids = jnp.arange(capacity, dtype=jnp.int32)
    held = jnp.max(landed(grid_ids[:, :, None], mine).astype(jnp.int32), axis=2)
    before = (window_ids[:, None] < window_ids[None, :]).astype(jnp.int32)
    held_rank = jnp.sum(held[:, :, None] * before, axis=1)
    taken = (held_rank[:, None, :] == slot_ids[None, :, None]) & (held[:, None, :] > 0)
    held_ids = jnp.sum(jnp.where(taken, grid_ids[:, None, :], 0), axis=2)
    valid = jnp.sum(taken.astype(jnp.int32), axis=2)
    lows, highs = bounds(held_ids)
    lows, highs = lows * valid, highs * valid
    scales = step_size / jnp.maximum((highs - lows).astype(jnp.float32), 1.0)
    targets = mine[:, None] + jnp.arange(SHOT_BLK, dtype=jnp.int32)[None, :]
    slot_of = jnp.arange(owners, dtype=jnp.int32)[:, None] * capacity + held_rank
    slots = jnp.sum(
        jnp.where(targets[:, :, None, None] == grid_ids[None, None], slot_of[None, None], 0),
        axis=(2, 3),
    )

    hits, coefs = lax.optimization_barrier((hits, coefs))
    values, energy2, cuts = second(
        arrived, hits, thr, lows.reshape(-1), highs.reshape(-1), scales.reshape(-1),
        slots.reshape(-1), capacity, windows, receivers,
    )
    energies = over_receivers(energy2)
    residual = remainder(records, coefs, cuts, own_lows, own_highs, both)
    model = finish(values, energies, thr, both, receivers)
    return (model, residual.reshape(windows, 1, block, rcv))


def solution(mesh):
    return jax.shard_map(
        local,
        mesh=mesh,
        in_specs=(P(None, "shot", None, "rcv"), P(), P()),
        out_specs=(P("shot", None, None, "rcv"), P(None, "shot", None, "rcv")),
        check_vma=False,
    )
```

time: 68.3 us -> 70.3 us (1.029)
  waiting for transfers between devices: 24.5 us -> 34.4 us
  starting transfers between devices: 15.9 us -> 8.47 us
  Pallas kernels: 21.3 us -> 19 us
  local copies, waits for them, and re-layouts: 2.53 us -> 3.59 us
    all_to_all x1, waiting for transfers between devices: 10.7 us -> 34.3 us  [local(): lax.all_to_all(packed, 'shot', split_axis=0, concat_axis=0, tiled=True)]
    ppermute x6 -> x0, waiting for transfers between devices: 8.41 us -> none  [rotate(): return lax.ppermute(values, 'shot', pairs)]
    ppermute x6 -> x0, starting transfers between devices: 7.32 us -> none  [rotate(): return lax.ppermute(values, 'shot', pairs)]
    ppermute x2, waiting for transfers between devices: 5.36 us -> 0.06 us  [over_receivers(): return [values, lax.ppermute(values, 'rcv', [(0, 1), (1, 0)])]]
    pallas_call x5 -> x6, Pallas kernels: 21.3 us -> 19 us  [the longest x1 6.62 us: second(): pl.pallas_call(body, in_specs=[full_smem()] * 4 + [full_vmem()] * 3, out_...]
    unnamed x15 -> x22, local copies, waits for them, and re-layouts: 1.25 us -> 2.99 us
    ppermute x2, starting transfers between devices: 3.11 us -> 2.16 us  [over_receivers(): return [values, lax.ppermute(values, 'rcv', [(0, 1), (1, 0)])]]
    all_to_all x1, starting transfers between devices: 5.48 us -> 6.32 us  [local(): lax.all_to_all(packed, 'shot', split_axis=0, concat_axis=0, tiled=True)]
  transfers between devices with their start and end apart: 9 -> 3, of which waited for: 7 -> 2; matrix products, arithmetic and copies ran while one was open for 7% -> 6% of each run, Pallas kernels for 10% -> 6%
where the time goes in v4:
time: 70.3 us; the launch traced here: 70 us
  waiting for transfers between devices  34.4 us (49%)
  Pallas kernels  19 us (27%)
  starting transfers between devices  8.47 us (12%)
  other arithmetic  3.78 us (5%)
  local copies, waits for them, and re-layouts  3.59 us (5%)
  between operations  0.83 us (1%)
    all_to_all x1, waiting for transfers between devices, local(): lax.all_to_all(packed, 'shot', split_axis=0, concat_axis=0, tiled=True)  34.3 us
    pallas_call x1, Pallas kernels, second(): pl.pallas_call(body, in_specs=[full_smem()] * 4 + [full_vmem()] * 3, out_...  6.62 us
    all_to_all x1, starting transfers between devices, local(): lax.all_to_all(packed, 'shot', split_axis=0, concat_axis=0, tiled=True)  6.32 us
    pallas_call x1, Pallas kernels, pack(): pl.pallas_call(body, in_specs=[full_smem(), pl.BlockSpec(memory_space=pl....  3.57 us
    pallas_call x1, Pallas kernels, owned(): pl.pallas_call(body, in_specs=[full_smem(), hbm, hbm, hbm], out_specs=[fu...  3.1 us
    pallas_call x1, Pallas kernels, remainder(): pl.pallas_call(body, in_specs=[full_smem()] * 2 + [full_vmem()] * 4, out_...  3.05 us
    unnamed x22, local copies, waits for them, and re-layouts  2.99 us
    ppermute x2, starting transfers between devices, over_receivers(): return [values, lax.ppermute(values, 'rcv', [(0, 1), (1, 0)])]  2.16 us
  transfers between devices with their start and end apart: 3, of which 2 were waited for; matrix products, arithmetic and copies ran while one was open for 6% of the time, Pallas kernels for 6%

profile of v4, /device:TPU:16, one launch (start us, length us, event | category | flops | bytes accessed | tf_op | source)
XLA Modules:
  0.0 70.0 jit_solution(14457442907790281832)
XLA Ops:
  0.6 0.0 copy-start
  0.6 0.0 copy-start.10
  0.7 3.1 %owned_coefficients.1 = (bf16[16,128,128]{2,1,0:T(8,128)(2,1)}, f32[16,128]{1,0:T(8,128)}, s32[8,128]{1,0:T(8,128)}) custom-call(s32[1]{0:T(128)} %bitcast.me_ref, s32[1,256]{1,0:T(1,128)} %bitcast.13, f32[16,128,128]{2,1,0:T(8,128)} %bitcast.7, bf16[128,256]{1,0:T(8,128)(2,1)} %constant.38.both_hbm.both_ref), custom_call_target="tpu_custom_call" | custom-call | tf_op jit(solution)/shard_map/owned_coefficients/pallas_call | solution.py:122
  3.8 0.0 copy-start.7
  3.8 0.0 copy-start.8
  3.8 1.6 %collective-permute-start = (f32[16,128]{1,0:T(8,128)}, f32[16,128]{1,0:T(8,128)S(1)}, u32[]{:S(2)}, u32[]{:S(2)}) collective-permute-start(f32[16,128]{1,0:T(8,128)} %get-tuple-element.12.refs_0_), channel_id=1, source_target_pairs={{0,16},{16,0},{1,17},{17,1},{2,18},{18,2},{3,19},{19,3},{4,20},{20... | collective-permute-start | bytes 24584 | tf_op jit(solution)/shard_map/ppermute | solution.py:402
  5.3 0.9 %convert_reduce_fusion.5 = (s32[16]{0:T(128)S(1)}, s32[16]{0:T(128)S(1)}) fusion(s32[256]{0:T(256)} %param.5, s32[16]{0:T(128)S(1)} %get-tuple-element.33, s32[16]{0:T(128)S(1)} %get-tuple-element.32), kind=kLoop, calls=%fused_computation.22 | loop fusion | flops 24544 | bytes 1280 | tf_op jit(solution)/shard_map/reduce_sum | solution.py:440
  6.2 0.0 copy-done
  6.2 0.0 copy-start.4
  6.2 0.8 %copy-done.4 = bf16[128,256]{1,0:T(8,128)(2,1)S(1)} copy-done((bf16[128,256]{1,0:T(8,128)(2,1)S(1)}, bf16[128,256]{1,0:T(8,128)(2,1)}, u32[]{:S(2)}) %copy-start.4) | copy-done | bytes 65560
  7.1 1.0 %owned_again.1.coef_ref = f32[16,128,128]{2,1,0:T(8,128)S(1)} custom-call(s32[16]{0:T(128)S(1)} %get-tuple-element.27.low_ref, s32[16]{0:T(128)S(1)} %get-tuple-element.26.high_ref, f32[16,128,128]{2,1,0:T(8,128)S(1)} %bitcast.8, bf16[128,256]{1,0:T(8,128)(2,1)S(1)} %copy-done.4), custom_call_target="tpu_custom_call" | custom-call | flops 1 | bytes 6291456 | tf_op jit(solution)/shard_map/owned_again/pallas_call | solution.py:298
  8.1 0.0 copy-start.2
  8.1 1.0 %copy-done.2 = f32[16,128,128]{2,1,0:T(8,128)} copy-done((f32[16,128,128]{2,1,0:T(8,128)}, f32[16,128,128]{2,1,0:T(8,128)S(1)}, u32[]{:S(2)}) %copy-start.2) | copy-done | bytes 1048600
  9.1 0.0 copy-done.10
  9.1 0.1 dynamic_slice.3
  9.1 0.0 collective-permute-done.refs_1_
  9.1 0.0 copy-done.7
  9.1 0.0 copy-done.8
  9.2 0.0 copy-done.6
  9.2 3.6 %pack_blocks.1 = bf16[16,400,128]{2,1,0:T(8,128)(2,1)S(1)} custom-call(s32[8,128]{1,0:T(8,128)S(1)} %copy-done.8, bf16[16,128,128]{2,1,0:T(8,128)(2,1)S(1)} %copy-done.6, f32[16,128]{1,0:T(8,128)S(1)} %copy-done.7, f32[16,128]{1,0:T(8,128)S(1)} %collective-permute-done.refs_1_), custom_call_target="tpu_custom_call" | custom-call | tf_op jit(solution)/shard_map/pack_blocks/pallas_call | solution.py:175
  12.7 0.0 copy-start.1
  12.7 1.2 %copy-done.1 = bf16[16,400,128]{2,1,0:T(8,128)(2,1)} copy-done((bf16[16,400,128]{2,1,0:T(8,128)(2,1)}, bf16[16,400,128]{2,1,0:T(8,128)(2,1)S(1)}, u32[]{:S(2)}) %copy-start.1) | copy-done | bytes 1638424
  13.9 6.3 %all-to-all-start = ((bf16[16,400,128]{2,1,0:T(8,128)(2,1)}), bf16[16,400,128]{2,1,0:T(8,128)(2,1)S(1)}, u32[]{:S(2)}, u32[]{:S(2)}) async-start(bf16[16,400,128]{2,1,0:T(8,128)(2,1)} %copy-done.1), calls=%async_computation | async-start | bytes 3276800 | tf_op jit(solution)/shard_map/all_to_all | solution.py:425
  20.2 0.1 add.119
  20.3 0.4 convert_reduce_fusion.1
  20.8 0.1 multiply_reduce_fusion
  20.9 0.1 iota_add_fusion
  21.0 0.1 broadcast_add_fusion
  21.0 1.3 %select_reduce_fusion = s32[16,4]{1,0:T(8,128)S(1)} fusion(s32[16,16]{1,0:T(8,128)S(1)} %broadcast_add_fusion, s32[16,16]{1,0:T(8,128)S(1)} %iota_add_fusion.1, s32[16,4]{1,0:T(8,128)S(1)} %iota_add_fusion), kind=kLoop, calls=%fused_computation | loop fusion | flops 49088 | bytes 2560 | tf_op jit(solution)/shard_map/reduce_sum | solution.py:458
  22.3 0.1 reshape.180.slot_ref
  22.4 0.2 convert_reduce_fusion.4
  22.6 0.3 convert_reduce_fusion.2
  22.9 0.1 copy.9
  23.0 0.1 mul.72.high_ref
  23.1 0.1 copy.8
  23.2 0.1 mul.70.low_ref
  23.3 0.2 convert_reduce_fusion
  23.5 0.1 select_reduce_fusion.1
  23.6 0.1 fusion.1.hit_ref
  23.7 34.3 %all-to-all-done.in_ref = bf16[16,400,128]{2,1,0:T(8,128)(2,1)S(1)} async-done(((bf16[16,400,128]{2,1,0:T(8,128)(2,1)}), bf16[16,400,128]{2,1,0:T(8,128)(2,1)S(1)}, u32[]{:S(2)}, u32[]{:S(2)}) %all-to-all-start) | async-done | bytes 1638432 | tf_op jit(solution)/shard_map/all_to_all | solution.py:425
  58.0 0.0 copy-done.9
  58.0 6.6 %second_coefficients.1 = (f32[16,4,128,128]{3,2,1,0:T(8,128)S(1)}, f32[16,128]{1,0:T(8,128)S(1)}, f32[273,8,128]{2,1,0:T(8,128)S(1)}) custom-call(s32[48]{0:T(128)S(1)} %mul.70.low_ref, s32[48]{0:T(128)S(1)} %mul.72.high_ref, f32[48]{0:T(128)S(1)} %maximum_divide_fusion.scale_ref, s32[64]{0:T(128)S(1)} %reshape.180.slot_ref, ...), custom_call_target="tpu_custom_call" | custom-call | flops 1 | bytes 12582912 | tf_op jit(solution)/shard_map/second_coefficients/pallas_call | solution.py:270
  64.7 0.6 collective-permute-start.1
  65.3 0.0 copy-done.5
  65.3 0.0 copy-done.3
  65.3 3.0 %residual_of_records.1 = f32[16,128,128]{2,1,0:T(8,128)} custom-call(s32[16]{0:T(128)S(1)} %get-tuple-element.27.low_ref, s32[16]{0:T(128)S(1)} %get-tuple-element.26.high_ref, f32[16,128,128]{2,1,0:T(8,128)S(1)} %bitcast.9, f32[16,128,128]{2,1,0:T(8,128)S(1)} %copy-done.3, f32[273,8,128]{2,1,0:T(8,128)S(1)} %get-tuple-element.17.cut_ref, ...), custom_call_target="tpu_custom_call" | custom-call | flops 1 | bytes 6291456 | tf_op jit(solution)/shard_map/residual_of_records/pallas_call | solution.py:340
  68.3 0.1 collective-permute-done.1.refs_1_
  68.4 1.6 %model_of_shots.1 = bf16[16,4,128,128]{3,2,1,0:T(8,128)(2,1)} custom-call(f32[16,4,128,128]{3,2,1,0:T(8,128)S(1)} %get-tuple-element.14.in_ref, f32[1,128]{1,0:T(1,128)S(1)} %bitcast.11, bf16[128,256]{1,0:T(8,128)(2,1)S(1)} %copy-done.5, f32[16,128]{1,0:T(8,128)S(1)} %get-tuple-element.15.refs_0_, f32[16,128]{1,0:T(8,128)S(1)} %collective-permute-done.1.refs_1_), custom_call_target="tpu_custom_call" | custom-call | tf_op jit(solution)/shard_map/model_of_shots/pallas_call | solution.py:386
  (14 shorter events, 0.1 us)
Async XLA Ops:
  0.6 5.6 %copy-start = (f32[16,1,128,128]{3,2,1,0:T(8,128)S(1)}, f32[16,1,128,128]{3,2,1,0:T(8,128)}, u32[]{:S(2)}) copy-start(f32[16,1,128,128]{3,2,1,0:T(8,128)} %param.4) | copy-start | bytes 3145732
  0.6 8.4 %copy-start.10 = (s32[256]{0:T(256)S(1)}, s32[256]{0:T(256)}, u32[]{:S(2)}) copy-start(s32[256]{0:T(256)} %param.5) | copy-start | bytes 3076
  3.8 5.4 %copy-start.7 = (f32[16,128]{1,0:T(8,128)S(1)}, f32[16,128]{1,0:T(8,128)}, u32[]{:S(2)}) copy-start(f32[16,128]{1,0:T(8,128)} %get-tuple-element.12.refs_0_) | copy-start | bytes 24580
  3.8 5.4 %copy-start.8 = (s32[8,128]{1,0:T(8,128)S(1)}, s32[8,128]{1,0:T(8,128)}, u32[]{:S(2)}) copy-start(s32[8,128]{1,0:T(8,128)} %get-tuple-element.10.table_ref) | copy-start | bytes 12292
  3.8 5.4 %collective-permute-start = (f32[16,128]{1,0:T(8,128)}, f32[16,128]{1,0:T(8,128)S(1)}, u32[]{:S(2)}, u32[]{:S(2)}) collective-permute-start(f32[16,128]{1,0:T(8,128)} %get-tuple-element.12.refs_0_), channel_id=1, source_target_pairs={{0,16},{16,0},{1,17},{17,1},{2,18},{18,2},{3,19},{19,3},{4,20},{20... | collective-permute-start | bytes 24584 | tf_op jit(solution)/shard_map/ppermute | solution.py:402
  6.2 0.8 %copy-start.4 = (bf16[128,256]{1,0:T(8,128)(2,1)S(1)}, bf16[128,256]{1,0:T(8,128)(2,1)}, u32[]{:S(2)}) copy-start(bf16[128,256]{1,0:T(8,128)(2,1)} %constant.38.both_hbm.both_ref) | copy-start | bytes 196612
  7.1 2.1 %copy-start.6 = (bf16[16,128,128]{2,1,0:T(8,128)(2,1)S(1)}, bf16[16,128,128]{2,1,0:T(8,128)(2,1)}, u32[]{:S(2)}) copy-start(bf16[16,128,128]{2,1,0:T(8,128)(2,1)} %get-tuple-element.11.sent_ref) | copy-start | bytes 1572868
  8.1 1.0 %copy-start.2 = (f32[16,128,128]{2,1,0:T(8,128)}, f32[16,128,128]{2,1,0:T(8,128)S(1)}, u32[]{:S(2)}) copy-start(f32[16,128,128]{2,1,0:T(8,128)S(1)} %owned_again.1.coef_ref) | copy-start | bytes 3145732
  12.7 1.2 %copy-start.1 = (bf16[16,400,128]{2,1,0:T(8,128)(2,1)}, bf16[16,400,128]{2,1,0:T(8,128)(2,1)S(1)}, u32[]{:S(2)}) copy-start(bf16[16,400,128]{2,1,0:T(8,128)(2,1)S(1)} %pack_blocks.1) | copy-start | bytes 4915204
  13.9 44.1 %copy-start.9 = (f32[128]{0:T(128)S(1)}, f32[128]{0:T(128)}, u32[]{:S(2)}) copy-start(f32[128]{0:T(128)} %param.6) | copy-start | bytes 1540
  13.9 44.1 %all-to-all-start = ((bf16[16,400,128]{2,1,0:T(8,128)(2,1)}), bf16[16,400,128]{2,1,0:T(8,128)(2,1)S(1)}, u32[]{:S(2)}, u32[]{:S(2)}) async-start(bf16[16,400,128]{2,1,0:T(8,128)(2,1)} %copy-done.1), calls=%async_computation | async-start | bytes 3276800 | tf_op jit(solution)/shard_map/all_to_all | solution.py:425
  20.2 45.1 %copy-start.5 = (bf16[128,256]{1,0:T(8,128)(2,1)S(1)}, bf16[128,256]{1,0:T(8,128)(2,1)}, u32[]{:S(2)}) copy-start(bf16[128,256]{1,0:T(8,128)(2,1)} %constant.38.both_hbm.both_ref) | copy-start | bytes 196612
  58.0 7.2 %copy-start.3 = (f32[16,128,128]{2,1,0:T(8,128)S(1)}, f32[16,128,128]{2,1,0:T(8,128)}, u32[]{:S(2)}) copy-start(f32[16,128,128]{2,1,0:T(8,128)} %copy-done.2) | copy-start | bytes 3145732
  64.7 3.7 %collective-permute-start.1 = (f32[16,128]{1,0:T(8,128)S(1)}, f32[16,128]{1,0:T(8,128)S(1)}, u32[]{:S(2)}, u32[]{:S(2)}) collective-permute-start(f32[16,128]{1,0:T(8,128)S(1)} %get-tuple-element.15.refs_0_), channel_id=1, source_target_pairs={{0,16},{16,0},{1,17},{17,1},{2,18},{18,2},{3,19},{19,3},{4,20},{20... | collective-permute-start | bytes 24584 | tf_op jit(solution)/shard_map/ppermute | solution.py:402

commit v5 on v4

--- a/solution.py
+++ b/solution.py
@@ -59,17 +59,18 @@
     return (lag >= 0) & (lag < SHOT_BLK)
 
 
-def owned(records, offsets, me, owners, capacity, both):
+def head(records, offsets, me, owners, capacity, both):
     windows, block, rcv = records.shape
     shots = offsets.shape[0]
     shot_dev = shots // owners
-    chunk = 4
+    chunk = 8
     chunks = windows // chunk
     f32, bf16 = jnp.float32, jnp.bfloat16
 
     def body(
-        me_ref, off_hbm, rec_hbm, both_hbm, sent_ref, energy_ref, table_ref,
-        off_ref, rec_ref, both_ref, small_sem, rec_sem,
+        me_ref, off_hbm, rec_hbm, both_hbm, out_ref, energy_hbm,
+        off_ref, rec_ref, both_ref, sent_ref, energy_ref, table_ref, table_smem,
+        small_sem, rec_sem, out_sem,
     ):
         get_off = pltpu.make_async_copy(off_hbm, off_ref, small_sem.at[0])
         get_both = pltpu.make_async_copy(both_hbm, both_ref, small_sem.at[1])
@@ -108,6 +109,8 @@
             table_ref[i : i + 1, :owners] = jnp.sum(
                 jnp.where(here, window, 0), axis=0, keepdims=True
             )
+        put_table = pltpu.make_async_copy(table_ref, table_smem, small_sem.at[2])
+        put_table.start()
 
         get_both.wait()
         for c in range(chunks):
@@ -118,73 +121,84 @@
                 sent_ref[w] = coef.astype(bf16)
                 energy_ref[w : w + 1, :] = jnp.sum(coef * coef, axis=0, keepdims=True)
 
+        put_energy = pltpu.make_async_copy(energy_ref, energy_hbm, small_sem.at[3])
+        put_energy.start()
+        put_table.wait()
+
+        def send(h, i):
+            return pltpu.make_async_copy(
+                sent_ref.at[table_smem[i, h]],
+                out_ref.at[h, pl.ds(i * rcv, rcv), :],
+                out_sem.at[h * capacity + i],
+            )
+
+        for h in range(owners):
+            for i in range(capacity):
+                send(h, i).start()
+        for h in range(owners):
+            for i in range(capacity):
+                send(h, i).wait()
+        put_energy.wait()
+
     hbm = pl.BlockSpec(memory_space=pltpu.HBM)
+    table_shape = (8, 128)
     return pl.pallas_call(
         body,
         in_specs=[full_smem(), hbm, hbm, hbm],
-        out_specs=[full_vmem()] * 3,
+        out_specs=[pl.BlockSpec(memory_space=pl.ANY)] * 2,
         out_shape=[
-            jax.ShapeDtypeStruct((windows, rcv, block), bf16),
+            jax.ShapeDtypeStruct((owners, capacity * rcv, block), bf16),
             jax.ShapeDtypeStruct((windows, block), f32),
-            jax.ShapeDtypeStruct((8, 128), jnp.int32),
         ],
         scratch_shapes=[
             pltpu.VMEM((1, shots), jnp.int32),
             pltpu.VMEM((windows, block, rcv), f32),
             pltpu.VMEM((block, 2 * block), bf16),
-            pltpu.SemaphoreType.DMA((2,)),
+            pltpu.VMEM((windows, rcv, block), bf16),
+            pltpu.VMEM((windows, block), f32),
+            pltpu.VMEM(table_shape, jnp.int32),
+            pltpu.SMEM(table_shape, jnp.int32),
+            pltpu.SemaphoreType.DMA((4,)),
             pltpu.SemaphoreType.DMA((chunks,)),
+            pltpu.SemaphoreType.DMA((owners * capacity,)),
         ],
         compiler_params=params(HEAD_VMEM_BYTES),
-        name="owned_coefficients",
+        name="pack_coefficients",
     )(me[None], offsets[None, :], records, both)
 
 
-def pack(sent, table, energies, owners, capacity):
-    windows, rcv, block = sent.shape
-    rows = capacity * rcv + windows
-
-    def body(table_ref, sent_ref, *refs):
-        out_ref, energy_ref, block_sem, energy_sem = refs[-4:]
-        energy = refs[0][...]
-        for ref in refs[1:-4]:
-            energy = energy + ref[...]
-        energy_ref[...] = energy.astype(jnp.bfloat16)
-
-        def blocks(h, i):
-            return pltpu.make_async_copy(
-                sent_ref.at[table_ref[i, h]],
-                out_ref.at[h, pl.ds(i * rcv, rcv), :],
-                block_sem.at[h * capacity + i],
-            )
-
-        def rest(h):
-            return pltpu.make_async_copy(
-                energy_ref, out_ref.at[h, pl.ds(capacity * rcv, windows), :], energy_sem.at[h]
-            )
-
-        for h in range(owners):
-            for i in range(capacity):
-                blocks(h, i).start()
-            rest(h).start()
-        for h in range(owners):
-            for i in range(capacity):
-                blocks(h, i).wait()
-            rest(h).wait()
-
-    return pl.pallas_call(
-        body,
-        in_specs=[full_smem(), pl.BlockSpec(memory_space=pl.ANY)] + [full_vmem()] * len(energies),
-        out_specs=pl.BlockSpec(memory_space=pl.ANY),
-        out_shape=jax.ShapeDtypeStruct((owners, rows, block), jnp.bfloat16),
-        scratch_shapes=[
-            pltpu.VMEM((windows, block), jnp.bfloat16),
-            pltpu.SemaphoreType.DMA((owners * capacity,)),
-            pltpu.SemaphoreType.DMA((owners,)),
-        ],
+def cutoffs(energies, hits, thresholds, receivers):
+    rows = hits.shape[0]
+    block = thresholds.shape[1]
+
+    def body(*refs):
+        hit_ref, thr_ref = refs[:2]
+        out_ref, cuts_ref = refs[-2:]
+        high, low = split_bf16(jnp.concatenate([ref[...] for ref in refs[2:-2]], axis=0))
+        sums = jnp.dot(hit_ref[...], high, preferred_element_type=jnp.float32) + jnp.dot(
+            hit_ref[...], low, preferred_element_type=jnp.float32
+        )
+        cuts_ref[...] = thr_ref[...] * jnp.sqrt(sums / (SHOT_BLK * receivers) + epsilon)
+
+        def widen(i, _):
+            at = pl.multiple_of(i * 8, 8)
+            out_ref[pl.ds(at, 8)] = jnp.broadcast_to(
+                cuts_ref[pl.ds(at, 8), :][:, None, :], (8, 8, block)
+            )
+            return 0
+
+        lax.fori_loop(0, rows // 8, widen, 0, unroll=2)
+        out_ref[rows] = jnp.zeros((8, block), jnp.float32)
+
+    return pl.pallas_call(
+        body,
+        in_specs=[full_vmem()] * (2 + len(energies)),
+        out_specs=full_vmem(),
+        out_shape=jax.ShapeDtypeStruct((rows + 1, 8, block), jnp.float32),
+        scratch_shapes=[pltpu.VMEM((rows, block), jnp.float32)],
         compiler_params=params(),
-        name="pack_blocks",
-    )(table, sent, *energies)
+        name="first_cutoffs",
+    )(hits, thresholds, *energies)
 
 
 def clipped_sum(coef, cut_ref, low, high, none):
@@ -204,33 +218,18 @@
     return jnp.where(coef < 0, -total, total)
 
 
-def second(arrived, hits, thresholds, lows, highs, scales, slots, capacity, windows, receivers):
+def second(arrived, cuts, lows, highs, scales, slots, capacity):
     owners, rows, block = arrived.shape
-    rcv = (rows - windows) // capacity
+    rcv = rows // capacity
     tiles = rcv // 8
     shot_dev = slots.shape[0] // SHOT_BLK
     count = owners * capacity
-    cut_rows = hits.shape[0]
-    shots = cut_rows - shot_dev
+    none = cuts.shape[0] - 1
+    shots = none - shot_dev
 
     def body(
-        low_ref, high_ref, scale_ref, slot_ref, in_ref, hit_ref, thr_ref,
-        out_ref, energy_ref, wide_ref, cuts_ref, diff_ref,
+        low_ref, high_ref, scale_ref, slot_ref, in_ref, wide_ref, out_ref, energy_ref, diff_ref
     ):
-        energy = in_ref[:, capacity * rcv :, :].reshape(owners * windows, block)
-        sums = jnp.dot(hit_ref[...], energy, preferred_element_type=jnp.float32)
-        cuts_ref[...] = thr_ref[...] * jnp.sqrt(sums / (SHOT_BLK * receivers) + epsilon)
-
-        def widen(i, _):
-            at = pl.multiple_of(i * 8, 8)
-            wide_ref[pl.ds(at, 8)] = jnp.broadcast_to(
-                cuts_ref[pl.ds(at, 8), :][:, None, :], (8, 8, block)
-            )
-            return 0
-
-        lax.fori_loop(0, cut_rows // 8, widen, 0, unroll=2)
-        wide_ref[cut_rows] = jnp.zeros((8, block), jnp.float32)
-
         def block_of(slot):
             owner = slot // capacity
             start = pl.multiple_of((slot - owner * capacity) * rcv, rcv)
@@ -243,7 +242,7 @@
             @pl.when(high > low)
             def _():
                 coef = block_of(slot)
-                clipped = clipped_sum(coef, wide_ref, low, high, cut_rows)
+                clipped = clipped_sum(coef, wide_ref, low, high, none)
                 scale = scale_ref[slot]
                 kept = 1.0 - scale * (high - low).astype(jnp.float32)
                 diff_ref[slot] = kept * coef + scale * clipped
@@ -269,21 +268,17 @@
 
     return pl.pallas_call(
         body,
-        in_specs=[full_smem()] * 4 + [full_vmem()] * 3,
-        out_specs=[full_vmem()] * 3,
+        in_specs=[full_smem()] * 4 + [full_vmem()] * 2,
+        out_specs=[full_vmem()] * 2,
         out_shape=[
             jax.ShapeDtypeStruct((shot_dev, SHOT_BLK, rcv, block), jnp.float32),
             jax.ShapeDtypeStruct((shot_dev, block), jnp.float32),
-            jax.ShapeDtypeStruct((cut_rows + 1, 8, block), jnp.float32),
         ],
-        scratch_shapes=[
-            pltpu.VMEM((cut_rows, block), jnp.float32),
-            pltpu.VMEM((count, tiles, 8, block), jnp.float32),
-        ],
+        scratch_shapes=[pltpu.VMEM((count, tiles, 8, block), jnp.float32)],
         compiler_params=params(),
         cost_estimate=pl.CostEstimate(flops=1, bytes_accessed=12 << 20, transcendentals=0),
         name="second_coefficients",
-    )(lows, highs, scales, slots, arrived, hits, thresholds)
+    )(lows, highs, scales, slots, arrived, cuts)
 
 
 def again(records, lows, highs, both):
@@ -403,6 +398,15 @@
     return [lax.psum(values, "rcv")]
 
 
+def rotate(values, stride, by, size):
+    n = lax.axis_size("shot")
+    pairs = []
+    for i in range(n):
+        place = (i // stride) % size
+        pairs.append((i, i + ((place + by) % size - place) * stride))
+    return lax.ppermute(values, "shot", pairs)
+
+
 def local(record_data, offsets, thresholds):
     owners = lax.axis_size("shot")
     me = lax.axis_index("shot")
@@ -420,9 +424,19 @@
     thr = thresholds[None, :]
     window_ids = jnp.arange(windows, dtype=jnp.int32)
 
-    sent, energy, table = owned(records, offsets, me, owners, capacity, both)
-    packed = pack(sent, table, over_receivers(energy), owners, capacity)
+    packed, energy = head(records, offsets, me, owners, capacity, both)
+    packed, records, offsets, thr = lax.optimization_barrier((packed, records, offsets, thr))
     arrived = lax.all_to_all(packed, "shot", split_axis=0, concat_axis=0, tiled=True)
+
+    near = min(4, owners)
+    far = owners // near
+    energy = sum(over_receivers(energy))
+    energy = jnp.concatenate([energy] + [rotate(energy, 1, j, near) for j in range(1, near)])
+    energies = [energy] + [rotate(energy, near, j, far) for j in range(1, far)]
+    back = jnp.arange(far, dtype=jnp.int32)[:, None]
+    side = jnp.arange(near, dtype=jnp.int32)[None, :]
+    origin = (me // near - back + far) % far * near + (me % near - side + near) % near
+    energy_ids = (window_ids * owners + origin[:, :, None]).reshape(-1)
 
     index = jnp.arange(shots, dtype=jnp.int32)
     ahead = (offsets[None, :] < offsets[:, None]) | (
@@ -433,7 +447,7 @@
     mine = lax.dynamic_slice(offsets, (me * shot_dev,), (shot_dev,))
     all_offsets = jnp.concatenate([ordered, mine])
     grid_ids = window_ids[None, :] * owners + jnp.arange(owners, dtype=jnp.int32)[:, None]
-    hits = landed(grid_ids.reshape(-1)[None, :], all_offsets[:, None]).astype(jnp.bfloat16)
+    hits = landed(energy_ids[None, :], all_offsets[:, None]).astype(jnp.bfloat16)
 
     def bounds(ids):
         below = jnp.sum((offsets < ids[..., None] - (SHOT_BLK - 1)).astype(jnp.int32), axis=-1)
@@ -461,9 +475,10 @@
     )
 
     hits, coefs = lax.optimization_barrier((hits, coefs))
-    values, energy2, cuts = second(
-        arrived, hits, thr, lows.reshape(-1), highs.reshape(-1), scales.reshape(-1),
-        slots.reshape(-1), capacity, windows, receivers,
+    cuts = cutoffs(energies, hits, thr, receivers)
+    values, energy2 = second(
+        arrived, cuts, lows.reshape(-1), highs.reshape(-1), scales.reshape(-1),
+        slots.reshape(-1), capacity,
     )
     energies = over_receivers(energy2)
     residual = remainder(records, coefs, cuts, own_lows, own_highs, both)

time: 70.3 us -> 69.1 us (0.983)
  the two profiles are of different devices: /device:TPU:16 before, /device:TPU:0 now
where the time goes in v5:
time: 69.1 us; the launch traced here: 68.7 us
  waiting for transfers between devices  24.9 us (36%)
  starting transfers between devices  18.2 us (26%)
  Pallas kernels  16 us (23%)
  local copies, waits for them, and re-layouts  4.99 us (7%)
  other arithmetic  3.81 us (6%)
  between operations  0.9 us (1%)
    ppermute x6, waiting for transfers between devices, rotate(): return lax.ppermute(values, 'shot', pairs)  24.8 us
    all_to_all x1, starting transfers between devices, local(): lax.all_to_all(packed, 'shot', split_axis=0, concat_axis=0, tiled=True)  7.57 us
    ppermute x6, starting transfers between devices, rotate(): return lax.ppermute(values, 'shot', pairs)  7.46 us
    pallas_call x1, Pallas kernels, second(): pl.pallas_call(body, in_specs=[full_smem()] * 4 + [full_vmem()] * 2, out_...  6.43 us
    unnamed x28, local copies, waits for them, and re-layouts  3.82 us
    pallas_call x1, Pallas kernels, head(): pl.pallas_call(body, in_specs=[full_smem(), hbm, hbm, hbm], out_specs=[pl...  3.34 us
    ppermute x2, starting transfers between devices, over_receivers(): return [values, lax.ppermute(values, 'rcv', [(0, 1), (1, 0)])]  3.13 us
    pallas_call x1, Pallas kernels, remainder(): pl.pallas_call(body, in_specs=[full_smem()] * 2 + [full_vmem()] * 4, out_...  3.06 us
  transfers between devices with their start and end apart: 9, of which 4 were waited for; matrix products, arithmetic and copies ran while one was open for 7% of the time, Pallas kernels for 7%

profile of v5, /device:TPU:0, one launch (start us, length us, event | category | flops | bytes accessed | tf_op | source)
XLA Modules:
  0.0 68.7 jit_solution(16058835555619177793)
XLA Ops:
  0.6 3.3 %pack_coefficients.1 = (bf16[16,384,128]{2,1,0:T(8,128)(2,1)}, f32[16,128]{1,0:T(8,128)}) custom-call(s32[1]{0:T(128)} %bitcast.me_ref, s32[1,256]{1,0:T(1,128)} %bitcast.13, f32[16,128,128]{2,1,0:T(8,128)} %bitcast.7, bf16[128,256]{1,0:T(8,128)(2,1)} %constant.79.both_hbm.both_ref), custom_call_target="tpu_custom_call" | custom-call | tf_op jit(solution)/shard_map/pack_coefficients/pallas_call | solution.py:145
  4.0 0.0 copy-start.12
  4.0 0.0 copy-start.1
  4.0 7.6 %all-to-all-start = ((bf16[16,384,128]{2,1,0:T(8,128)(2,1)}), bf16[16,384,128]{2,1,0:T(8,128)(2,1)}, u32[]{:S(2)}, u32[]{:S(2)}) async-start(bf16[16,384,128]{2,1,0:T(8,128)(2,1)} %get-tuple-element.14), calls=%async_computation | async-start | bytes 3145728 | tf_op jit(solution)/shard_map/all_to_all | solution.py:429
  11.6 1.6 %collective-permute-start = (f32[16,128]{1,0:T(8,128)S(1)}, f32[16,128]{1,0:T(8,128)S(1)}, u32[]{:S(2)}, u32[]{:S(2)}) collective-permute-start(f32[16,128]{1,0:T(8,128)S(1)} %copy-done.13), channel_id=1, source_target_pairs={{0,16},{16,0},{1,17},{17,1},{2,18},{18,2},{3,19},{19,3},{4,20},{20... | collective-permute-start | bytes 24584 | tf_op jit(solution)/shard_map/ppermute | solution.py:397
  13.2 0.1 broadcast_add_fusion.2
  13.3 0.1 broadcast_add_fusion
  13.4 0.1 add.200
  13.5 0.1 dynamic_slice.3
  13.5 0.4 convert_reduce_fusion.1
  14.0 0.1 multiply_reduce_fusion
  14.1 0.2 convert_reduce_fusion.4
  14.3 0.3 convert_reduce_fusion.2
  14.6 0.1 copy.9
  14.7 0.1 mul.85.high_ref
  14.8 0.1 copy.8
  14.9 0.1 mul.83.low_ref
  15.0 0.2 convert_reduce_fusion
  15.2 0.1 select_reduce_fusion.1
  15.3 0.6 maximum_divide_fusion.scale_ref
  15.8 0.1 iota_add_fusion
  15.9 0.1 broadcast_add_fusion.1
  16.0 0.1 fusion.1.refs_0_
  16.1 1.3 %select_reduce_fusion = s32[16,4]{1,0:T(8,128)S(1)} fusion(s32[16,16]{1,0:T(8,128)S(1)} %broadcast_add_fusion.1, s32[16,16]{1,0:T(8,128)S(1)} %iota_add_fusion.1, s32[16,4]{1,0:T(8,128)S(1)} %iota_add_fusion), kind=kLoop, calls=%fused_computation | loop fusion | flops 49088 | bytes 2560 | tf_op jit(solution)/shard_map/reduce_sum | solution.py:472
  17.4 1.4 %collective-permute-start.3 = (f32[16,128]{1,0:T(8,128)S(1)}, f32[16,128]{1,0:T(8,128)S(1)}, u32[]{:S(2)}, u32[]{:S(2)}) collective-permute-start(f32[16,128]{1,0:T(8,128)S(1)} %add.203), channel_id=1, source_target_pairs={{0,3},{1,0},{2,1},{3,2},{4,7},{5,4},{6,5},{7,6},{8,11},{9,8},{10,9... | collective-permute-start | bytes 24584 | tf_op jit(solution)/shard_map/ppermute | solution.py:407
  18.8 0.6 collective-permute-start.2
  19.4 0.2 collective-permute-start.1
  19.6 0.6 collective-permute-done.3
  20.2 2.3 %collective-permute-done.2 = f32[16,128]{1,0:T(8,128)S(1)} collective-permute-done((f32[16,128]{1,0:T(8,128)S(1)}, f32[16,128]{1,0:T(8,128)S(1)}, u32[]{:S(2)}, u32[]{:S(2)}) %collective-permute-start.2) | collective-permute-done | bytes 8224 | tf_op jit(solution)/shard_map/ppermute | solution.py:407
  22.5 0.0 collective-permute-done.1
  22.6 4.7 %collective-permute-start.6 = (f32[64,128]{1,0:T(8,128)S(1)}, f32[64,128]{1,0:T(8,128)S(1)}, u32[]{:S(2)}, u32[]{:S(2)}) collective-permute-start(f32[64,128]{1,0:T(8,128)S(1)} %pad_maximum_fusion.refs_2_), channel_id=1, source_target_pairs={{0,12},{1,13},{2,14},{3,15},{4,0},{5,1},{6,2},{7,3},{8,4},{9,5},{1... | collective-permute-start | bytes 98312 | tf_op jit(solution)/shard_map/ppermute | solution.py:407
  27.2 0.6 collective-permute-start.4
  27.9 0.2 convert_reduce_fusion.5
  28.1 0.6 copy-done.2
  28.6 1.0 %owned_again.1.coef_ref = f32[16,128,128]{2,1,0:T(8,128)S(1)} custom-call(s32[16]{0:T(128)S(1)} %get-tuple-element.31.low_ref, s32[16]{0:T(128)S(1)} %get-tuple-element.30.high_ref, f32[16,128,128]{2,1,0:T(8,128)S(1)} %bitcast.8, bf16[128,256]{1,0:T(8,128)(2,1)S(1)} %copy-done.1), custom_call_target="tpu_custom_call" | custom-call | flops 1 | bytes 6291456 | tf_op jit(solution)/shard_map/owned_again/pallas_call | solution.py:293
  29.7 0.7 reshape.262.slot_ref
  30.3 8.6 %collective-permute-done.6.refs_5_ = f32[64,128]{1,0:T(8,128)S(1)} collective-permute-done((f32[64,128]{1,0:T(8,128)S(1)}, f32[64,128]{1,0:T(8,128)S(1)}, u32[]{:S(2)}, u32[]{:S(2)}) %collective-permute-start.6) | collective-permute-done | bytes 32800 | tf_op jit(solution)/shard_map/ppermute | solution.py:407
  38.9 13.3 %collective-permute-done.5.refs_4_ = f32[64,128]{1,0:T(8,128)S(1)} collective-permute-done((f32[64,128]{1,0:T(8,128)S(1)}, f32[64,128]{1,0:T(8,128)S(1)}, u32[]{:S(2)}, u32[]{:S(2)}) %collective-permute-start.5) | collective-permute-done | bytes 32800 | tf_op jit(solution)/shard_map/ppermute | solution.py:407
  52.2 0.7 copy-done.4
  52.9 0.5 first_cutoffs.1.wide_ref.cut_ref
  53.4 0.6 copy-done.7
  54.0 0.7 copy-done.9
  54.6 0.7 copy-done.10
  55.3 0.6 copy-done.11
  55.9 6.4 %second_coefficients.1 = (f32[16,4,128,128]{3,2,1,0:T(8,128)S(1)}, f32[16,128]{1,0:T(8,128)S(1)}) custom-call(s32[48]{0:T(128)S(1)} %copy-done.9, s32[48]{0:T(128)S(1)} %copy-done.7, f32[48]{0:T(128)S(1)} %copy-done.11, s32[64]{0:T(128)S(1)} %copy-done.10, bf16[16,384,128]{2,1,0:T(8,128)(2,1)} %all-to-all-done.in_ref, ...), custom_call_target="tpu_custom_call" | custom-call | flops 1 | bytes 12582912 | tf_op jit(solution)/shard_map/second_coefficients/pallas_call | solution.py:269
  62.4 1.6 %collective-permute-start.7 = (f32[16,128]{1,0:T(8,128)S(1)}, f32[16,128]{1,0:T(8,128)S(1)}, u32[]{:S(2)}, u32[]{:S(2)}) collective-permute-start(f32[16,128]{1,0:T(8,128)S(1)} %get-tuple-element.20.refs_0_), channel_id=1, source_target_pairs={{0,16},{16,0},{1,17},{17,1},{2,18},{18,2},{3,19},{19,3},{4,20},{20... | collective-permute-start | bytes 24584 | tf_op jit(solution)/shard_map/ppermute | solution.py:397
  64.0 3.1 %residual_of_records.1 = f32[16,128,128]{2,1,0:T(8,128)} custom-call(s32[16]{0:T(128)S(1)} %copy-done.3, s32[16]{0:T(128)S(1)} %get-tuple-element.30.high_ref, f32[16,128,128]{2,1,0:T(8,128)S(1)} %bitcast.9, f32[16,128,128]{2,1,0:T(8,128)S(1)} %owned_again.1.coef_ref, f32[273,8,128]{2,1,0:T(8,128)S(1)} %first_cutoffs.1.wide_ref.cut_ref, ...), custom_call_target="tpu_custom_call" | custom-call | flops 1 | bytes 6291456 | tf_op jit(solution)/shard_map/residual_of_records/pallas_call | solution.py:335
  67.0 1.6 %model_of_shots.1 = bf16[16,4,128,128]{3,2,1,0:T(8,128)(2,1)} custom-call(f32[16,4,128,128]{3,2,1,0:T(8,128)S(1)} %get-tuple-element.19.in_ref, f32[1,128]{1,0:T(1,128)S(1)} %bitcast.11, bf16[128,256]{1,0:T(8,128)(2,1)S(1)} %copy-done.1, f32[16,128]{1,0:T(8,128)S(1)} %get-tuple-element.20.refs_0_, f32[16,128]{1,0:T(8,128)S(1)} %collective-permute-done.7.refs_1_), custom_call_target="tpu_custom_call" | custom-call | tf_op jit(solution)/shard_map/model_of_shots/pallas_call | solution.py:381
  (37 shorter events, 0.1 us)
Async XLA Ops:
  4.0 7.6 %copy-start.13 = (f32[16,128]{1,0:T(8,128)S(1)}, f32[16,128]{1,0:T(8,128)}, u32[]{:S(2)}) copy-start(f32[16,128]{1,0:T(8,128)} %get-tuple-element.18) | copy-start | bytes 24580
  4.0 9.5 %copy-start.12 = (s32[256]{0:T(256)S(1)}, s32[256]{0:T(256)}, u32[]{:S(2)}) copy-start(s32[256]{0:T(256)} %param.5) | copy-start | bytes 3076
  4.0 24.6 %copy-start = (f32[16,1,128,128]{3,2,1,0:T(8,128)S(1)}, f32[16,1,128,128]{3,2,1,0:T(8,128)}, u32[]{:S(2)}) copy-start(f32[16,1,128,128]{3,2,1,0:T(8,128)} %param.4) | copy-start | bytes 3145732
  4.0 24.6 %copy-start.1 = (bf16[128,256]{1,0:T(8,128)(2,1)S(1)}, bf16[128,256]{1,0:T(8,128)(2,1)}, u32[]{:S(2)}) copy-start(bf16[128,256]{1,0:T(8,128)(2,1)} %constant.79.both_hbm.both_ref) | copy-start | bytes 196612
  4.0 49.3 %all-to-all-start = ((bf16[16,384,128]{2,1,0:T(8,128)(2,1)}), bf16[16,384,128]{2,1,0:T(8,128)(2,1)}, u32[]{:S(2)}, u32[]{:S(2)}) async-start(bf16[16,384,128]{2,1,0:T(8,128)(2,1)} %get-tuple-element.14), calls=%async_computation | async-start | bytes 3145728 | tf_op jit(solution)/shard_map/all_to_all | solution.py:429
  11.6 5.8 %collective-permute-start = (f32[16,128]{1,0:T(8,128)S(1)}, f32[16,128]{1,0:T(8,128)S(1)}, u32[]{:S(2)}, u32[]{:S(2)}) collective-permute-start(f32[16,128]{1,0:T(8,128)S(1)} %copy-done.13), channel_id=1, source_target_pairs={{0,16},{16,0},{1,17},{17,1},{2,18},{18,2},{3,19},{19,3},{4,20},{20... | collective-permute-start | bytes 24584 | tf_op jit(solution)/shard_map/ppermute | solution.py:397
  14.8 13.3 %copy-start.6 = (s32[48]{0:T(128)}, s32[48]{0:T(128)S(1)}, u32[]{:S(2)}) copy-start(s32[48]{0:T(128)S(1)} %mul.85.high_ref) | copy-start | bytes 580
  14.9 13.1 %copy-start.8 = (s32[48]{0:T(128)}, s32[48]{0:T(128)S(1)}, u32[]{:S(2)}) copy-start(s32[48]{0:T(128)S(1)} %mul.83.low_ref) | copy-start | bytes 580
  17.4 2.8 %collective-permute-start.3 = (f32[16,128]{1,0:T(8,128)S(1)}, f32[16,128]{1,0:T(8,128)S(1)}, u32[]{:S(2)}, u32[]{:S(2)}) collective-permute-start(f32[16,128]{1,0:T(8,128)S(1)} %add.203), channel_id=1, source_target_pairs={{0,3},{1,0},{2,1},{3,2},{4,7},{5,4},{6,5},{7,6},{8,11},{9,8},{10,9... | collective-permute-start | bytes 24584 | tf_op jit(solution)/shard_map/ppermute | solution.py:407
  18.8 3.7 %collective-permute-start.2 = (f32[16,128]{1,0:T(8,128)S(1)}, f32[16,128]{1,0:T(8,128)S(1)}, u32[]{:S(2)}, u32[]{:S(2)}) collective-permute-start(f32[16,128]{1,0:T(8,128)S(1)} %add.203), channel_id=1, source_target_pairs={{0,2},{1,3},{2,0},{3,1},{4,6},{5,7},{6,4},{7,5},{8,10},{9,11},{10,... | collective-permute-start | bytes 24584 | tf_op jit(solution)/shard_map/ppermute | solution.py:407
  19.4 3.1 %collective-permute-start.1 = (f32[16,128]{1,0:T(8,128)S(1)}, f32[16,128]{1,0:T(8,128)S(1)}, u32[]{:S(2)}, u32[]{:S(2)}) collective-permute-start(f32[16,128]{1,0:T(8,128)S(1)} %add.203), channel_id=1, source_target_pairs={{0,1},{1,2},{2,3},{3,0},{4,5},{5,6},{6,7},{7,4},{8,9},{9,10},{10,1... | collective-permute-start | bytes 24584 | tf_op jit(solution)/shard_map/ppermute | solution.py:407
  22.6 16.4 %collective-permute-start.6 = (f32[64,128]{1,0:T(8,128)S(1)}, f32[64,128]{1,0:T(8,128)S(1)}, u32[]{:S(2)}, u32[]{:S(2)}) collective-permute-start(f32[64,128]{1,0:T(8,128)S(1)} %pad_maximum_fusion.refs_2_), channel_id=1, source_target_pairs={{0,12},{1,13},{2,14},{3,15},{4,0},{5,1},{6,2},{7,3},{8,4},{9,5},{1... | collective-permute-start | bytes 98312 | tf_op jit(solution)/shard_map/ppermute | solution.py:407
  27.2 25.0 %collective-permute-start.5 = (f32[64,128]{1,0:T(8,128)S(1)}, f32[64,128]{1,0:T(8,128)S(1)}, u32[]{:S(2)}, u32[]{:S(2)}) collective-permute-start(f32[64,128]{1,0:T(8,128)S(1)} %pad_maximum_fusion.refs_2_), channel_id=1, source_target_pairs={{0,8},{1,9},{2,10},{3,11},{4,12},{5,13},{6,14},{7,15},{8,0},{9,1},... | collective-permute-start | bytes 98312 | tf_op jit(solution)/shard_map/ppermute | solution.py:407
  27.2 25.0 %collective-permute-start.4 = (f32[64,128]{1,0:T(8,128)S(1)}, f32[64,128]{1,0:T(8,128)S(1)}, u32[]{:S(2)}, u32[]{:S(2)}) collective-permute-start(f32[64,128]{1,0:T(8,128)S(1)} %pad_maximum_fusion.refs_2_), channel_id=1, source_target_pairs={{0,4},{1,5},{2,6},{3,7},{4,8},{5,9},{6,10},{7,11},{8,12},{9,13},{1... | collective-permute-start | bytes 98312 | tf_op jit(solution)/shard_map/ppermute | solution.py:407
  28.0 0.6 copy-start.2
  52.2 0.7 copy-start.4
  53.4 10.6 %copy-start.3 = (s32[16]{0:T(128)S(1)}, s32[16]{0:T(128)}, u32[]{:S(2)}) copy-start(s32[16]{0:T(128)} %copy-done.2) | copy-start | bytes 196
  53.4 0.6 copy-start.7
  54.0 0.7 copy-start.9
  54.6 0.7 copy-start.10
  55.3 0.6 copy-start.11
  62.4 4.7 %copy-start.5 = (f32[128]{0:T(128)S(1)}, f32[128]{0:T(128)}, u32[]{:S(2)}) copy-start(f32[128]{0:T(128)} %param.6) | copy-start | bytes 1540
  62.4 4.6 %collective-permute-start.7 = (f32[16,128]{1,0:T(8,128)S(1)}, f32[16,128]{1,0:T(8,128)S(1)}, u32[]{:S(2)}, u32[]{:S(2)}) collective-permute-start(f32[16,128]{1,0:T(8,128)S(1)} %get-tuple-element.20.refs_0_), channel_id=1, source_target_pairs={{0,16},{16,0},{1,17},{17,1},{2,18},{18,2},{3,19},{19,3},{4,20},{20... | collective-permute-start | bytes 24584 | tf_op jit(solution)/shard_map/ppermute | solution.py:397

commit v6 on v5

--- a/solution.py
+++ b/solution.py
@@ -174,10 +174,8 @@
     def body(*refs):
         hit_ref, thr_ref = refs[:2]
         out_ref, cuts_ref = refs[-2:]
-        high, low = split_bf16(jnp.concatenate([ref[...] for ref in refs[2:-2]], axis=0))
-        sums = jnp.dot(hit_ref[...], high, preferred_element_type=jnp.float32) + jnp.dot(
-            hit_ref[...], low, preferred_element_type=jnp.float32
-        )
+        energy = jnp.concatenate([ref[...] for ref in refs[2:-2]], axis=0)
+        sums = jnp.dot(hit_ref[...], energy, preferred_element_type=jnp.float32)
         cuts_ref[...] = thr_ref[...] * jnp.sqrt(sums / (SHOT_BLK * receivers) + epsilon)
 
         def widen(i, _):
@@ -203,33 +201,35 @@
 
 def clipped_sum(coef, cut_ref, low, high, none):
     size = jnp.abs(coef)
-    unroll = 2
+    peel, unroll = 6, 2
+
+    def term(row):
+        return jnp.minimum(size, cut_ref[jnp.where(row < high, row, none)][None])
+
+    total = term(low)
+    for u in range(1, peel):
+        total = total + term(low + u)
 
     def add(j, total):
         for u in range(unroll):
-            row = low + j * unroll + u
-            if u:
-                row = jnp.where(row < high, row, none)
-            total = total + jnp.minimum(size, cut_ref[row][None])
+            total = total + term(low + peel + j * unroll + u)
         return total
 
-    trips = lax.div(high - low + unroll - 1, unroll)
-    total = lax.fori_loop(0, trips, add, jnp.zeros_like(coef))
+    left = jnp.maximum(high - low - peel, 0)
+    total = lax.fori_loop(0, lax.div(left + unroll - 1, unroll), add, total)
     return jnp.where(coef < 0, -total, total)
 
 
-def second(arrived, cuts, lows, highs, scales, slots, capacity):
+def second(arrived, cuts, numbers, capacity):
     owners, rows, block = arrived.shape
     rcv = rows // capacity
     tiles = rcv // 8
-    shot_dev = slots.shape[0] // SHOT_BLK
     count = owners * capacity
+    shot_dev = (numbers.shape[0] - 2 * count) // SHOT_BLK
     none = cuts.shape[0] - 1
     shots = none - shot_dev
 
-    def body(
-        low_ref, high_ref, scale_ref, slot_ref, in_ref, wide_ref, out_ref, energy_ref, diff_ref
-    ):
+    def body(number_ref, in_ref, wide_ref, out_ref, energy_ref, diff_ref, coef_ref):
         def block_of(slot):
             owner = slot // capacity
             start = pl.multiple_of((slot - owner * capacity) * rcv, rcv)
@@ -237,28 +237,28 @@
             return values.reshape(tiles, 8, block)
 
         def difference(slot, _):
-            low, high = low_ref[slot], high_ref[slot]
+            low, high = number_ref[slot], number_ref[count + slot]
 
             @pl.when(high > low)
             def _():
                 coef = block_of(slot)
                 clipped = clipped_sum(coef, wide_ref, low, high, none)
-                scale = scale_ref[slot]
-                kept = 1.0 - scale * (high - low).astype(jnp.float32)
+                many = jnp.full((1, 8, block), (high - low).astype(jnp.float32))
+                scale = step_size / many
+                kept = 1.0 + step_size - scale * many
                 diff_ref[slot] = kept * coef + scale * clipped
+                coef_ref[slot] = step_size * coef
 
             return 0
 
         lax.fori_loop(0, count, difference, 0)
 
         def one_shot(shot, _):
-            cut = wide_ref[shots + shot][None]
+            cut = step_size * wide_ref[shots + shot][None]
             energy = jnp.zeros((8, block), jnp.float32)
             for q in range(SHOT_BLK):
-                slot = slot_ref[shot * SHOT_BLK + q]
-                coef = block_of(slot)
-                shrunk = coef - jnp.minimum(jnp.maximum(coef, -cut), cut)
-                value = step_size * shrunk + diff_ref[slot]
+                slot = number_ref[2 * count + shot * SHOT_BLK + q]
+                value = diff_ref[slot] - jnp.minimum(jnp.maximum(coef_ref[slot], -cut), cut)
                 out_ref[shot, q] = value.reshape(rcv, block)
                 energy = energy + jnp.sum(value * value, axis=0)
             energy_ref[pl.ds(shot, 1), :] = jnp.sum(energy, axis=0, keepdims=True)
@@ -268,48 +268,32 @@
 
     return pl.pallas_call(
         body,
-        in_specs=[full_smem()] * 4 + [full_vmem()] * 2,
+        in_specs=[full_smem()] + [full_vmem()] * 2,
         out_specs=[full_vmem()] * 2,
         out_shape=[
             jax.ShapeDtypeStruct((shot_dev, SHOT_BLK, rcv, block), jnp.float32),
             jax.ShapeDtypeStruct((shot_dev, block), jnp.float32),
         ],
-        scratch_shapes=[pltpu.VMEM((count, tiles, 8, block), jnp.float32)],
+        scratch_shapes=[pltpu.VMEM((count, tiles, 8, block), jnp.float32)] * 2,
         compiler_params=params(),
         cost_estimate=pl.CostEstimate(flops=1, bytes_accessed=12 << 20, transcendentals=0),
         name="second_coefficients",
-    )(lows, highs, scales, slots, arrived, cuts)
-
-
-def again(records, lows, highs, both):
-    windows, block, rcv = records.shape
-
-    def body(low_ref, high_ref, rec_ref, both_ref, out_ref):
-        for w in range(windows):
-            many = jnp.full((1, rcv), (high_ref[w] - low_ref[w]).astype(jnp.float32))
-            spread = (rec_ref[w] * (1.0 / jnp.maximum(many, 1.0))).astype(jnp.bfloat16)
-            out_ref[w] = forward(both_ref[...], spread)
-
-    return pl.pallas_call(
-        body,
-        in_specs=[full_smem()] * 2 + [full_vmem()] * 2,
-        out_specs=full_vmem(),
-        out_shape=jax.ShapeDtypeStruct((windows, rcv, block), jnp.float32),
-        compiler_params=params(),
-        cost_estimate=pl.CostEstimate(flops=1, bytes_accessed=6 << 20, transcendentals=0),
-        name="owned_again",
-    )(lows, highs, records, both)
-
-
-def remainder(records, coefs, cuts, lows, highs, both):
+    )(numbers, arrived, cuts)
+
+
+def remainder(records, cuts, lows, highs, both):
     windows, block, rcv = records.shape
     tiles = rcv // 8
     none = cuts.shape[0] - 1
     group = 4
 
     def body(
-        low_ref, high_ref, rec_ref, coef_ref, cut_ref, both_ref, out_hbm, sum_ref, out_ref, sem
+        low_ref, high_ref, rec_ref, cut_ref, both_ref, out_hbm, coef_ref, sum_ref, out_ref, sem
     ):
+        for w in range(windows):
+            many = jnp.full((1, rcv), (high_ref[w] - low_ref[w]).astype(jnp.float32))
+            spread = (rec_ref[w] * (1.0 / jnp.maximum(many, 1.0))).astype(jnp.bfloat16)
+            coef_ref[w] = forward(both_ref[...], spread)
         copies = []
         for at in range(0, windows, group):
             for w in range(at, at + group):
@@ -334,10 +318,11 @@
 
     return pl.pallas_call(
         body,
-        in_specs=[full_smem()] * 2 + [full_vmem()] * 4,
+        in_specs=[full_smem()] * 2 + [full_vmem()] * 3,
         out_specs=pl.BlockSpec(memory_space=pl.ANY),
         out_shape=jax.ShapeDtypeStruct((windows, block, rcv), jnp.float32),
         scratch_shapes=[
+            pltpu.VMEM((windows, rcv, block), jnp.float32),
             pltpu.VMEM((group * rcv, block), jnp.bfloat16),
             pltpu.VMEM((windows, block, rcv), jnp.float32),
             pltpu.SemaphoreType.DMA((windows // group,)),
@@ -345,7 +330,7 @@
         compiler_params=params(),
         cost_estimate=pl.CostEstimate(flops=1, bytes_accessed=6 << 20, transcendentals=0),
         name="residual_of_records",
-    )(lows, highs, records, coefs, cuts, both)
+    )(lows, highs, records, cuts, both)
 
 
 def finish(values, energies, thresholds, both, receivers):
@@ -430,7 +415,8 @@
 
     near = min(4, owners)
     far = owners // near
-    energy = sum(over_receivers(energy))
+    energy = energy.astype(jnp.bfloat16)
+    energy = sum(part.astype(jnp.float32) for part in over_receivers(energy)).astype(jnp.bfloat16)
     energy = jnp.concatenate([energy] + [rotate(energy, 1, j, near) for j in range(1, near)])
     energies = [energy] + [rotate(energy, near, j, far) for j in range(1, far)]
     back = jnp.arange(far, dtype=jnp.int32)[:, None]
@@ -455,7 +441,6 @@
         return below, upto
 
     own_lows, own_highs = bounds(window_ids * owners + me)
-    coefs = again(records, own_lows, own_highs, both)
 
     slot_ids = jnp.arange(capacity, dtype=jnp.int32)
     held = jnp.max(landed(grid_ids[:, :, None], mine).astype(jnp.int32), axis=2)
@@ -466,7 +451,6 @@
     valid = jnp.sum(taken.astype(jnp.int32), axis=2)
     lows, highs = bounds(held_ids)
     lows, highs = lows * valid, highs * valid
-    scales = step_size / jnp.maximum((highs - lows).astype(jnp.float32), 1.0)
     targets = mine[:, None] + jnp.arange(SHOT_BLK, dtype=jnp.int32)[None, :]
     slot_of = jnp.arange(owners, dtype=jnp.int32)[:, None] * capacity + held_rank
     slots = jnp.sum(
@@ -474,14 +458,11 @@
         axis=(2, 3),
     )
 
-    hits, coefs = lax.optimization_barrier((hits, coefs))
+    numbers = jnp.concatenate([lows.reshape(-1), highs.reshape(-1), slots.reshape(-1)])
     cuts = cutoffs(energies, hits, thr, receivers)
-    values, energy2 = second(
-        arrived, cuts, lows.reshape(-1), highs.reshape(-1), scales.reshape(-1),
-        slots.reshape(-1), capacity,
-    )
+    values, energy2 = second(arrived, cuts, numbers, capacity)
     energies = over_receivers(energy2)
-    residual = remainder(records, coefs, cuts, own_lows, own_highs, both)
+    residual = remainder(records, cuts, own_lows, own_highs, both)
     model = finish(values, energies, thr, both, receivers)
     return (model, residual.reshape(windows, 1, block, rcv))
 

time: 69.1 us -> 63.9 us (0.925)
  local copies, waits for them, and re-layouts: 4.99 us -> 0.61 us
  Pallas kernels: 16 us -> 13.3 us
  waiting for transfers between devices: 24.9 us -> 26.5 us
    unnamed x28 -> x10, local copies, waits for them, and re-layouts: 3.82 us -> 0.02 us
    pallas_call x3 -> x2, Pallas kernels: 10.5 us -> 7.84 us  [the longest x1 4.58 us: second(): pl.pallas_call(body, in_specs=[full_smem()] + [full_vmem()] * 2, out_spec...]
    ppermute x6, waiting for transfers between devices: 24.8 us -> 26.4 us  [rotate(): return lax.ppermute(values, 'shot', pairs)]
    all_to_all x1, starting transfers between devices: 7.57 us -> 6.06 us  [local(): lax.all_to_all(packed, 'shot', split_axis=0, concat_axis=0, tiled=True)]
    ppermute x6, starting transfers between devices: 7.46 us -> 8.73 us  [rotate(): return lax.ppermute(values, 'shot', pairs)]
    convert_element_type x0 -> x2, other arithmetic: none -> 0.71 us  [the longest x1 0.7 us: local(): energy = energy.astype(jnp.bfloat16)]
  transfers between devices with their start and end apart: 9 -> 9, of which waited for: 4 -> 4; matrix products, arithmetic and copies ran while one was open for 7% -> 6% of each run, Pallas kernels for 7% -> 6%
where the time goes in v6:
time: 63.9 us; the launch traced here: 63.6 us
  waiting for transfers between devices  26.5 us (41%)
  starting transfers between devices  18.3 us (29%)
  Pallas kernels  13.3 us (21%)
  other arithmetic  4.03 us (6%)
  between operations  0.86 us (1%)
    ppermute x6, waiting for transfers between devices, rotate(): return lax.ppermute(values, 'shot', pairs)  26.4 us
    ppermute x6, starting transfers between devices, rotate(): return lax.ppermute(values, 'shot', pairs)  8.73 us
    all_to_all x1, starting transfers between devices, local(): lax.all_to_all(packed, 'shot', split_axis=0, concat_axis=0, tiled=True)  6.06 us
    pallas_call x1, Pallas kernels, second(): pl.pallas_call(body, in_specs=[full_smem()] + [full_vmem()] * 2, out_spec...  4.58 us
    ppermute x2, starting transfers between devices, over_receivers(): return [values, lax.ppermute(values, 'rcv', [(0, 1), (1, 0)])]  3.54 us
    pallas_call x1, Pallas kernels, head(): pl.pallas_call(body, in_specs=[full_smem(), hbm, hbm, hbm], out_specs=[pl...  3.34 us
    pallas_call x1, Pallas kernels, remainder(): pl.pallas_call(body, in_specs=[full_smem()] * 2 + [full_vmem()] * 3, out_...  3.27 us
    pallas_call x1, Pallas kernels, finish(): pl.pallas_call(body, in_specs=[full_vmem()] * (3 + len(energies)), out_sp...  1.65 us
  transfers between devices with their start and end apart: 9, of which 4 were waited for; matrix products, arithmetic and copies ran while one was open for 6% of the time, Pallas kernels for 6%

profile of v6, /device:TPU:0, one launch (start us, length us, event | category | flops | bytes accessed | tf_op | source)
XLA Modules:
  0.0 63.6 jit_solution(9115239719248566641)
XLA Ops:
  0.6 3.3 %pack_coefficients.1 = (bf16[16,384,128]{2,1,0:T(8,128)(2,1)}, f32[16,128]{1,0:T(8,128)}) custom-call(s32[1]{0:T(128)} %bitcast.me_ref, s32[1,256]{1,0:T(1,128)} %bitcast.12, f32[16,128,128]{2,1,0:T(8,128)} %bitcast.7, bf16[128,256]{1,0:T(8,128)(2,1)} %constant.75.both_hbm.both_ref), custom_call_target="tpu_custom_call" | custom-call | tf_op jit(solution)/shard_map/pack_coefficients/pallas_call | solution.py:145
  4.0 0.7 %convert_element_type.62 = bf16[16,128]{1,0:T(8,128)(2,1)S(1)} convert(f32[16,128]{1,0:T(8,128)} %get-tuple-element.14) | non-fusion elementwise | flops 2048 | bytes 12288 | tf_op jit(solution)/shard_map/convert_element_type | solution.py:418
  4.7 2.9 %collective-permute-start = (bf16[16,128]{1,0:T(8,128)(2,1)S(1)}, bf16[16,128]{1,0:T(8,128)(2,1)S(1)}, u32[]{:S(2)}, u32[]{:S(2)}) collective-permute-start(bf16[16,128]{1,0:T(8,128)(2,1)S(1)} %convert_element_type.62), channel_id=1, source_target_pairs={{0,16},{16,0},{1,17},{17,1},{2,18},{18,2},{3,19},{19,3},{4,20},{20... | collective-permute-start | bytes 12296 | tf_op jit(solution)/shard_map/ppermute | solution.py:382
  7.6 6.1 %all-to-all-start = ((bf16[16,384,128]{2,1,0:T(8,128)(2,1)}), bf16[16,384,128]{2,1,0:T(8,128)(2,1)S(1)}, u32[]{:S(2)}, u32[]{:S(2)}) async-start(bf16[16,384,128]{2,1,0:T(8,128)(2,1)} %get-tuple-element.12), calls=%async_computation | async-start | bytes 3145728 | tf_op jit(solution)/shard_map/all_to_all | solution.py:414
  13.7 0.0 copy-done.3
  13.8 0.2 convert_reduce_fusion
  13.9 0.1 select_reduce_fusion.1
  14.1 0.1 broadcast_add_fusion.2
  14.2 0.1 broadcast_add_fusion
  14.2 0.1 add.200
  14.3 0.1 dynamic_slice.3
  14.4 0.4 convert_reduce_fusion.1
  14.9 0.1 multiply_reduce_fusion
  15.0 0.2 convert_reduce_fusion.4
  15.2 0.3 convert_reduce_fusion.3
  15.5 0.1 iota_add_fusion
  15.5 0.1 broadcast_add_fusion.1
  15.6 0.1 fusion.1.refs_0_
  15.7 1.3 %select_reduce_fusion = s32[16,4]{1,0:T(8,128)S(1)} fusion(s32[16,16]{1,0:T(8,128)S(1)} %broadcast_add_fusion.1, s32[16,16]{1,0:T(8,128)S(1)} %iota_add_fusion.1, s32[16,4]{1,0:T(8,128)S(1)} %iota_add_fusion), kind=kLoop, calls=%fused_computation | loop fusion | flops 49088 | bytes 2560 | tf_op jit(solution)/shard_map/reduce_sum | solution.py:456
  17.0 0.0 collective-permute-done
  17.1 0.4 collective-permute-start.1
  17.5 1.7 %collective-permute-start.2 = (bf16[16,128]{1,0:T(8,128)(2,1)S(1)}, bf16[16,128]{1,0:T(8,128)(2,1)S(1)}, u32[]{:S(2)}, u32[]{:S(2)}) collective-permute-start(bf16[16,128]{1,0:T(8,128)(2,1)S(1)} %add_convert_fusion), channel_id=1, source_target_pairs={{0,2},{1,3},{2,0},{3,1},{4,6},{5,7},{6,4},{7,5},{8,10},{9,11},{10,... | collective-permute-start | bytes 12296 | tf_op jit(solution)/shard_map/ppermute | solution.py:392
  19.2 1.3 %collective-permute-start.3 = (bf16[16,128]{1,0:T(8,128)(2,1)S(1)}, bf16[16,128]{1,0:T(8,128)(2,1)S(1)}, u32[]{:S(2)}, u32[]{:S(2)}) collective-permute-start(bf16[16,128]{1,0:T(8,128)(2,1)S(1)} %add_convert_fusion), channel_id=1, source_target_pairs={{0,3},{1,0},{2,1},{3,2},{4,7},{5,4},{6,5},{7,6},{8,11},{9,8},{10,9... | collective-permute-start | bytes 12296 | tf_op jit(solution)/shard_map/ppermute | solution.py:392
  20.5 0.1 copy.8
  20.6 0.1 mul.81
  20.7 0.1 copy.9
  20.8 0.1 mul.83
  20.8 0.1 reshape.258
  20.9 2.9 %collective-permute-done.1 = bf16[16,128]{1,0:T(8,128)(2,1)S(1)} collective-permute-done((bf16[16,128]{1,0:T(8,128)(2,1)S(1)}, bf16[16,128]{1,0:T(8,128)(2,1)S(1)}, u32[]{:S(2)}, u32[]{:S(2)}) %collective-permute-start.1) | collective-permute-done | bytes 4128 | tf_op jit(solution)/shard_map/ppermute | solution.py:392
  23.8 0.5 collective-permute-done.2
  24.3 0.0 collective-permute-done.3
  24.3 0.1 collective-permute-start.4
  24.4 5.2 %collective-permute-start.5 = (bf16[64,128]{1,0:T(8,128)(2,1)S(1)}, bf16[64,128]{1,0:T(8,128)(2,1)S(1)}, u32[]{:S(2)}, u32[]{:S(2)}) collective-permute-start(bf16[64,128]{1,0:T(8,128)(2,1)S(1)} %pad_maximum_fusion.refs_2_), channel_id=1, source_target_pairs={{0,8},{1,9},{2,10},{3,11},{4,12},{5,13},{6,14},{7,15},{8,0},{9,1},... | collective-permute-start | bytes 49160 | tf_op jit(solution)/shard_map/ppermute | solution.py:392
  29.6 0.0 collective-permute-start.6
  29.6 0.1 pad_add_fusion.1.number_ref
  29.7 15.1 %collective-permute-done.4.refs_3_ = bf16[64,128]{1,0:T(8,128)(2,1)S(1)} collective-permute-done((bf16[64,128]{1,0:T(8,128)(2,1)S(1)}, bf16[64,128]{1,0:T(8,128)(2,1)S(1)}, u32[]{:S(2)}, u32[]{:S(2)}) %collective-permute-start.4) | collective-permute-done | bytes 16416 | tf_op jit(solution)/shard_map/ppermute | solution.py:392
  44.9 7.9 %collective-permute-done.5.refs_4_ = bf16[64,128]{1,0:T(8,128)(2,1)S(1)} collective-permute-done((bf16[64,128]{1,0:T(8,128)(2,1)S(1)}, bf16[64,128]{1,0:T(8,128)(2,1)S(1)}, u32[]{:S(2)}, u32[]{:S(2)}) %collective-permute-start.5) | collective-permute-done | bytes 16416 | tf_op jit(solution)/shard_map/ppermute | solution.py:392
  52.8 0.0 collective-permute-done.6.refs_5_
  52.8 0.4 first_cutoffs.1.wide_ref.cut_ref
  53.2 0.0 copy-start.1
  53.2 0.0 all-to-all-done.in_ref
  53.2 0.0 copy-start
  53.3 4.6 %second_coefficients.1 = (f32[16,4,128,128]{3,2,1,0:T(8,128)S(1)}, f32[16,128]{1,0:T(8,128)S(1)}) custom-call(s32[160]{0:T(256)S(1)} %pad_add_fusion.1.number_ref, bf16[16,384,128]{2,1,0:T(8,128)(2,1)S(1)} %all-to-all-done.in_ref, f32[273,8,128]{2,1,0:T(8,128)S(1)} %first_cutoffs.1.wide_ref.cut_ref), custom_call_target="tpu_custom_call" | custom-call | flops 1 | bytes 12582912 | tf_op jit(solution)/shard_map/second_coefficients/pallas_call | solution.py:269
  57.8 0.6 collective-permute-start.7
  58.4 0.2 convert_reduce_fusion.5
  58.6 3.3 %residual_of_records.1 = f32[16,128,128]{2,1,0:T(8,128)} custom-call(s32[16]{0:T(128)S(1)} %get-tuple-element.27.low_ref, s32[16]{0:T(128)S(1)} %get-tuple-element.26.high_ref, f32[16,128,128]{2,1,0:T(8,128)S(1)} %bitcast.8, f32[273,8,128]{2,1,0:T(8,128)S(1)} %first_cutoffs.1.wide_ref.cut_ref, bf16[128,256]{1,0:T(8,128)(2,1)S(1)} %copy-done.1), custom_call_target="tpu_custom_call" | custom-call | flops 1 | bytes 6291456 | tf_op jit(solution)/shard_map/residual_of_records/pallas_call | solution.py:319
  61.9 0.0 collective-permute-done.7.refs_1_
  61.9 1.6 %model_of_shots.1 = bf16[16,4,128,128]{3,2,1,0:T(8,128)(2,1)} custom-call(f32[16,4,128,128]{3,2,1,0:T(8,128)S(1)} %get-tuple-element.15.in_ref, f32[1,128]{1,0:T(1,128)S(1)} %bitcast.10, bf16[128,256]{1,0:T(8,128)(2,1)S(1)} %copy-done.1, f32[16,128]{1,0:T(8,128)S(1)} %get-tuple-element.16.refs_0_, f32[16,128]{1,0:T(8,128)S(1)} %collective-permute-done.7.refs_1_), custom_call_target="tpu_custom_call" | custom-call | tf_op jit(solution)/shard_map/model_of_shots/pallas_call | solution.py:366
  (19 shorter events, 0.1 us)
Async XLA Ops:
  4.7 12.4 %collective-permute-start = (bf16[16,128]{1,0:T(8,128)(2,1)S(1)}, bf16[16,128]{1,0:T(8,128)(2,1)S(1)}, u32[]{:S(2)}, u32[]{:S(2)}) collective-permute-start(bf16[16,128]{1,0:T(8,128)(2,1)S(1)} %convert_element_type.62), channel_id=1, source_target_pairs={{0,16},{16,0},{1,17},{17,1},{2,18},{18,2},{3,19},{19,3},{4,20},{20... | collective-permute-start | bytes 12296 | tf_op jit(solution)/shard_map/ppermute | solution.py:382
  7.6 6.1 %copy-start.3 = (s32[256]{0:T(256)S(1)}, s32[256]{0:T(256)}, u32[]{:S(2)}) copy-start(s32[256]{0:T(256)} %param.5) | copy-start | bytes 3076
  7.6 9.4 %copy-start.4 = (f32[16,128]{1,0:T(8,128)S(1)}, f32[16,128]{1,0:T(8,128)}, u32[]{:S(2)}) copy-start(f32[16,128]{1,0:T(8,128)} %get-tuple-element.14) | copy-start | bytes 24580
  7.6 45.1 %copy-start.2 = (f32[128]{0:T(128)S(1)}, f32[128]{0:T(128)}, u32[]{:S(2)}) copy-start(f32[128]{0:T(128)} %param.6) | copy-start | bytes 1540
  7.6 45.6 %all-to-all-start = ((bf16[16,384,128]{2,1,0:T(8,128)(2,1)}), bf16[16,384,128]{2,1,0:T(8,128)(2,1)S(1)}, u32[]{:S(2)}, u32[]{:S(2)}) async-start(bf16[16,384,128]{2,1,0:T(8,128)(2,1)} %get-tuple-element.12), calls=%async_computation | async-start | bytes 3145728 | tf_op jit(solution)/shard_map/all_to_all | solution.py:414
  17.1 6.8 %collective-permute-start.1 = (bf16[16,128]{1,0:T(8,128)(2,1)S(1)}, bf16[16,128]{1,0:T(8,128)(2,1)S(1)}, u32[]{:S(2)}, u32[]{:S(2)}) collective-permute-start(bf16[16,128]{1,0:T(8,128)(2,1)S(1)} %add_convert_fusion), channel_id=1, source_target_pairs={{0,1},{1,2},{2,3},{3,0},{4,5},{5,6},{6,7},{7,4},{8,9},{9,10},{10,1... | collective-permute-start | bytes 12296 | tf_op jit(solution)/shard_map/ppermute | solution.py:392
  17.5 6.8 %collective-permute-start.2 = (bf16[16,128]{1,0:T(8,128)(2,1)S(1)}, bf16[16,128]{1,0:T(8,128)(2,1)S(1)}, u32[]{:S(2)}, u32[]{:S(2)}) collective-permute-start(bf16[16,128]{1,0:T(8,128)(2,1)S(1)} %add_convert_fusion), channel_id=1, source_target_pairs={{0,2},{1,3},{2,0},{3,1},{4,6},{5,7},{6,4},{7,5},{8,10},{9,11},{10,... | collective-permute-start | bytes 12296 | tf_op jit(solution)/shard_map/ppermute | solution.py:392
  19.2 5.2 %collective-permute-start.3 = (bf16[16,128]{1,0:T(8,128)(2,1)S(1)}, bf16[16,128]{1,0:T(8,128)(2,1)S(1)}, u32[]{:S(2)}, u32[]{:S(2)}) collective-permute-start(bf16[16,128]{1,0:T(8,128)(2,1)S(1)} %add_convert_fusion), channel_id=1, source_target_pairs={{0,3},{1,0},{2,1},{3,2},{4,7},{5,4},{6,5},{7,6},{8,11},{9,8},{10,9... | collective-permute-start | bytes 12296 | tf_op jit(solution)/shard_map/ppermute | solution.py:392
  24.3 20.5 %collective-permute-start.4 = (bf16[64,128]{1,0:T(8,128)(2,1)S(1)}, bf16[64,128]{1,0:T(8,128)(2,1)S(1)}, u32[]{:S(2)}, u32[]{:S(2)}) collective-permute-start(bf16[64,128]{1,0:T(8,128)(2,1)S(1)} %pad_maximum_fusion.refs_2_), channel_id=1, source_target_pairs={{0,4},{1,5},{2,6},{3,7},{4,8},{5,9},{6,10},{7,11},{8,12},{9,13},{1... | collective-permute-start | bytes 49160 | tf_op jit(solution)/shard_map/ppermute | solution.py:392
  24.4 28.3 %collective-permute-start.5 = (bf16[64,128]{1,0:T(8,128)(2,1)S(1)}, bf16[64,128]{1,0:T(8,128)(2,1)S(1)}, u32[]{:S(2)}, u32[]{:S(2)}) collective-permute-start(bf16[64,128]{1,0:T(8,128)(2,1)S(1)} %pad_maximum_fusion.refs_2_), channel_id=1, source_target_pairs={{0,8},{1,9},{2,10},{3,11},{4,12},{5,13},{6,14},{7,15},{8,0},{9,1},... | collective-permute-start | bytes 49160 | tf_op jit(solution)/shard_map/ppermute | solution.py:392
  29.6 23.1 %collective-permute-start.6 = (bf16[64,128]{1,0:T(8,128)(2,1)S(1)}, bf16[64,128]{1,0:T(8,128)(2,1)S(1)}, u32[]{:S(2)}, u32[]{:S(2)}) collective-permute-start(bf16[64,128]{1,0:T(8,128)(2,1)S(1)} %pad_maximum_fusion.refs_2_), channel_id=1, source_target_pairs={{0,12},{1,13},{2,14},{3,15},{4,0},{5,1},{6,2},{7,3},{8,4},{9,5},{1... | collective-permute-start | bytes 49160 | tf_op jit(solution)/shard_map/ppermute | solution.py:392
  53.2 5.4 %copy-start.1 = (bf16[128,256]{1,0:T(8,128)(2,1)S(1)}, bf16[128,256]{1,0:T(8,128)(2,1)}, u32[]{:S(2)}) copy-start(bf16[128,256]{1,0:T(8,128)(2,1)} %constant.75.both_hbm.both_ref) | copy-start | bytes 196612
  53.2 5.4 %copy-start = (f32[16,1,128,128]{3,2,1,0:T(8,128)S(1)}, f32[16,1,128,128]{3,2,1,0:T(8,128)}, u32[]{:S(2)}) copy-start(f32[16,1,128,128]{3,2,1,0:T(8,128)} %param.4) | copy-start | bytes 3145732
  57.8 4.1 %collective-permute-start.7 = (f32[16,128]{1,0:T(8,128)S(1)}, f32[16,128]{1,0:T(8,128)S(1)}, u32[]{:S(2)}, u32[]{:S(2)}) collective-permute-start(f32[16,128]{1,0:T(8,128)S(1)} %get-tuple-element.16.refs_0_), channel_id=1, source_target_pairs={{0,16},{16,0},{1,17},{17,1},{2,18},{18,2},{3,19},{19,3},{4,20},{20... | collective-permute-start | bytes 24584 | tf_op jit(solution)/shard_map/ppermute | solution.py:382

commit v7 on v6

--- a/solution.py
+++ b/solution.py
@@ -113,14 +113,16 @@
         put_table.start()
 
         get_both.wait()
+        rows = []
         for c in range(chunks):
             get_rec[c].wait()
             for w in range(c * chunk, (c + 1) * chunk):
                 spread = (rec_ref[w] * scale[w : w + 1, 0:1]).astype(bf16)
                 coef = forward(both_ref[...], spread)
                 sent_ref[w] = coef.astype(bf16)
-                energy_ref[w : w + 1, :] = jnp.sum(coef * coef, axis=0, keepdims=True)
-
+                rows.append(jnp.sum(coef * coef, axis=0, keepdims=True))
+
+        energy_ref[...] = jnp.concatenate(rows, axis=0).astype(bf16)
         put_energy = pltpu.make_async_copy(energy_ref, energy_hbm, small_sem.at[3])
         put_energy.start()
         put_table.wait()
@@ -148,14 +150,14 @@
         out_specs=[pl.BlockSpec(memory_space=pl.ANY)] * 2,
         out_shape=[
             jax.ShapeDtypeStruct((owners, capacity * rcv, block), bf16),
-            jax.ShapeDtypeStruct((windows, block), f32),
+            jax.ShapeDtypeStruct((windows, block), bf16),
         ],
         scratch_shapes=[
             pltpu.VMEM((1, shots), jnp.int32),
             pltpu.VMEM((windows, block, rcv), f32),
             pltpu.VMEM((block, 2 * block), bf16),
             pltpu.VMEM((windows, rcv, block), bf16),
-            pltpu.VMEM((windows, block), f32),
+            pltpu.VMEM((windows, block), bf16),
             pltpu.VMEM(table_shape, jnp.int32),
             pltpu.SMEM(table_shape, jnp.int32),
             pltpu.SemaphoreType.DMA((4,)),
@@ -174,8 +176,9 @@
     def body(*refs):
         hit_ref, thr_ref = refs[:2]
         out_ref, cuts_ref = refs[-2:]
-        energy = jnp.concatenate([ref[...] for ref in refs[2:-2]], axis=0)
-        sums = jnp.dot(hit_ref[...], energy, preferred_element_type=jnp.float32)
+        sums = jnp.dot(hit_ref[...], refs[2][...], preferred_element_type=jnp.float32)
+        for ref in refs[3:-2]:
+            sums = sums + jnp.dot(hit_ref[...], ref[...], preferred_element_type=jnp.float32)
         cuts_ref[...] = thr_ref[...] * jnp.sqrt(sums / (SHOT_BLK * receivers) + epsilon)
 
         def widen(i, _):
@@ -220,137 +223,153 @@
     return jnp.where(coef < 0, -total, total)
 
 
-def second(arrived, cuts, numbers, capacity):
+def shot_terms(coef, cut_ref, low, high, none):
+    clipped = clipped_sum(coef, cut_ref, low, high, none)
+    many = jnp.full((1, 8, coef.shape[2]), (high - low).astype(jnp.float32))
+    scale = step_size / jnp.maximum(many, 1.0)
+    diff = (1.0 + step_size - scale * many) * coef + scale * clipped
+    return diff, step_size * coef, many * coef - clipped
+
+
+def landed_energies(records, cuts, numbers, both, groups):
+    windows, block, rcv = records.shape
+    tiles = rcv // 8
+    none = cuts.shape[0] - 1
+    shots = numbers.shape[0] - 2 * windows
+    size = shots // groups
+    chunk = 4
+    chunks = windows // chunk
+
+    def body(number_ref, rec_ref, cut_ref, both_ref, *refs):
+        energy_refs, out_hbm = refs[:groups], refs[groups]
+        diff_ref, base_ref, shrunk_ref, out_ref, sum_ref, sem = refs[groups + 1 :]
+        sum_ref[...] = jnp.zeros_like(sum_ref)
+        for w in range(windows):
+            cover = (number_ref[windows + w] - number_ref[w]).astype(jnp.float32)
+            scale = 1.0 / jnp.maximum(jnp.full((1, rcv), cover), 1.0)
+            spread = (rec_ref[w] * scale).astype(jnp.bfloat16)
+            base_ref[w] = forward(both_ref[...], spread).reshape(tiles, 8, block)
+
+        def one_window(w, _):
+            low, high = number_ref[w], number_ref[windows + w]
+            diff_ref[w], base_ref[w], shrunk = shot_terms(base_ref[w], cut_ref, low, high, none)
+            shrunk_ref[w] = shrunk.reshape(rcv, block).astype(jnp.bfloat16)
+            return 0
+
+        lax.fori_loop(0, windows, one_window, 0)
+        copies = []
+        for c in range(chunks):
+            part = pl.ds(c * chunk, chunk)
+            blended = backward(both_ref[...], shrunk_ref[part].reshape(chunk * rcv, block))
+            for w in range(chunk):
+                at = c * chunk + w
+                out_ref[at] = rec_ref[at] - step_size * blended[:, w * rcv : (w + 1) * rcv]
+            copy = pltpu.make_async_copy(out_ref.at[part], out_hbm.at[part], sem.at[c])
+            copy.start()
+            copies.append(copy)
+
+        def energies_of_window(w, _):
+            diff, base = diff_ref[w], base_ref[w]
+
+            def one_shot(row, _):
+                cut = step_size * cut_ref[row][None]
+                value = diff - jnp.minimum(jnp.maximum(base, -cut), cut)
+                sum_ref[number_ref[2 * windows + row]] = jnp.sum(value * value, axis=0)
+                return 0
+
+            lax.fori_loop(number_ref[w], number_ref[windows + w], one_shot, 0)
+            return 0
+
+        lax.fori_loop(0, windows, energies_of_window, 0)
+        for g in range(groups):
+            energy_refs[g][...] = jnp.sum(sum_ref[g * size : (g + 1) * size], axis=1)
+        for copy in copies:
+            copy.wait()
+
+    terms = pltpu.VMEM((windows, tiles, 8, block), jnp.float32)
+    return pl.pallas_call(
+        body,
+        in_specs=[full_smem()] + [full_vmem()] * 3,
+        out_specs=[full_vmem()] * groups + [pl.BlockSpec(memory_space=pl.ANY)],
+        out_shape=[jax.ShapeDtypeStruct((size, block), jnp.float32)] * groups
+        + [jax.ShapeDtypeStruct((windows, block, rcv), jnp.float32)],
+        scratch_shapes=[
+            terms,
+            terms,
+            pltpu.VMEM((windows, rcv, block), jnp.bfloat16),
+            pltpu.VMEM((windows, block, rcv), jnp.float32),
+            pltpu.VMEM((shots, 8, block), jnp.float32),
+            pltpu.SemaphoreType.DMA((chunks,)),
+        ],
+        compiler_params=params(),
+        cost_estimate=pl.CostEstimate(flops=1, bytes_accessed=6 << 20, transcendentals=0),
+        name="residual_and_energies",
+    )(numbers, records, cuts, both)
+
+
+def differences(arrived, cuts, numbers, capacity):
     owners, rows, block = arrived.shape
     rcv = rows // capacity
     tiles = rcv // 8
     count = owners * capacity
-    shot_dev = (numbers.shape[0] - 2 * count) // SHOT_BLK
     none = cuts.shape[0] - 1
-    shots = none - shot_dev
-
-    def body(number_ref, in_ref, wide_ref, out_ref, energy_ref, diff_ref, coef_ref):
-        def block_of(slot):
-            owner = slot // capacity
-            start = pl.multiple_of((slot - owner * capacity) * rcv, rcv)
-            values = in_ref[owner, pl.ds(start, rcv), :].astype(jnp.float32)
-            return values.reshape(tiles, 8, block)
-
-        def difference(slot, _):
+
+    def body(number_ref, in_ref, cut_ref, diff_ref, base_ref):
+        def one_block(slot, _):
             low, high = number_ref[slot], number_ref[count + slot]
 
             @pl.when(high > low)
             def _():
-                coef = block_of(slot)
-                clipped = clipped_sum(coef, wide_ref, low, high, none)
-                many = jnp.full((1, 8, block), (high - low).astype(jnp.float32))
-                scale = step_size / many
-                kept = 1.0 + step_size - scale * many
-                diff_ref[slot] = kept * coef + scale * clipped
-                coef_ref[slot] = step_size * coef
+                owner = slot // capacity
+                start = pl.multiple_of((slot - owner * capacity) * rcv, rcv)
+                coef = in_ref[owner, pl.ds(start, rcv), :].astype(jnp.float32)
+                diff_ref[slot], base_ref[slot], _ = shot_terms(
+                    coef.reshape(tiles, 8, block), cut_ref, low, high, none
+                )
 
             return 0
 
-        lax.fori_loop(0, count, difference, 0)
-
-        def one_shot(shot, _):
-            cut = step_size * wide_ref[shots + shot][None]
-            energy = jnp.zeros((8, block), jnp.float32)
-            for q in range(SHOT_BLK):
-                slot = number_ref[2 * count + shot * SHOT_BLK + q]
-                value = diff_ref[slot] - jnp.minimum(jnp.maximum(coef_ref[slot], -cut), cut)
-                out_ref[shot, q] = value.reshape(rcv, block)
-                energy = energy + jnp.sum(value * value, axis=0)
-            energy_ref[pl.ds(shot, 1), :] = jnp.sum(energy, axis=0, keepdims=True)
-            return 0
-
-        lax.fori_loop(0, shot_dev, one_shot, 0)
-
+        lax.fori_loop(0, count, one_block, 0)
+
+    shape = jax.ShapeDtypeStruct((count, tiles, 8, block), jnp.float32)
     return pl.pallas_call(
         body,
         in_specs=[full_smem()] + [full_vmem()] * 2,
         out_specs=[full_vmem()] * 2,
-        out_shape=[
-            jax.ShapeDtypeStruct((shot_dev, SHOT_BLK, rcv, block), jnp.float32),
-            jax.ShapeDtypeStruct((shot_dev, block), jnp.float32),
-        ],
-        scratch_shapes=[pltpu.VMEM((count, tiles, 8, block), jnp.float32)] * 2,
+        out_shape=[shape] * 2,
         compiler_params=params(),
-        cost_estimate=pl.CostEstimate(flops=1, bytes_accessed=12 << 20, transcendentals=0),
-        name="second_coefficients",
+        cost_estimate=pl.CostEstimate(flops=1, bytes_accessed=8 << 20, transcendentals=0),
+        name="shot_differences",
     )(numbers, arrived, cuts)
 
 
-def remainder(records, cuts, lows, highs, both):
-    windows, block, rcv = records.shape
-    tiles = rcv // 8
-    none = cuts.shape[0] - 1
-    group = 4
-
-    def body(
-        low_ref, high_ref, rec_ref, cut_ref, both_ref, out_hbm, coef_ref, sum_ref, out_ref, sem
-    ):
-        for w in range(windows):
-            many = jnp.full((1, rcv), (high_ref[w] - low_ref[w]).astype(jnp.float32))
-            spread = (rec_ref[w] * (1.0 / jnp.maximum(many, 1.0))).astype(jnp.bfloat16)
-            coef_ref[w] = forward(both_ref[...], spread)
-        copies = []
-        for at in range(0, windows, group):
-            for w in range(at, at + group):
-                low, high = low_ref[w], high_ref[w]
-                coef = coef_ref[w].reshape(tiles, 8, block)
-                clipped = clipped_sum(coef, cut_ref, low, high, none)
-                shrunk = (high - low).astype(jnp.float32) * coef - clipped
-                sum_ref[pl.ds((w - at) * rcv, rcv), :] = shrunk.reshape(rcv, block).astype(
-                    jnp.bfloat16
-                )
-            blended = backward(both_ref[...], sum_ref[...])
-            for w in range(at, at + group):
-                part = blended[:, (w - at) * rcv : (w - at + 1) * rcv]
-                out_ref[w] = rec_ref[w] - step_size * part
-            copy = pltpu.make_async_copy(
-                out_ref.at[pl.ds(at, group)], out_hbm.at[pl.ds(at, group)], sem.at[at // group]
-            )
-            copy.start()
-            copies.append(copy)
-        for copy in copies:
-            copy.wait()
-
-    return pl.pallas_call(
-        body,
-        in_specs=[full_smem()] * 2 + [full_vmem()] * 3,
-        out_specs=pl.BlockSpec(memory_space=pl.ANY),
-        out_shape=jax.ShapeDtypeStruct((windows, block, rcv), jnp.float32),
-        scratch_shapes=[
-            pltpu.VMEM((windows, rcv, block), jnp.float32),
-            pltpu.VMEM((group * rcv, block), jnp.bfloat16),
-            pltpu.VMEM((windows, block, rcv), jnp.float32),
-            pltpu.SemaphoreType.DMA((windows // group,)),
-        ],
-        compiler_params=params(),
-        cost_estimate=pl.CostEstimate(flops=1, bytes_accessed=6 << 20, transcendentals=0),
-        name="residual_of_records",
-    )(lows, highs, records, cuts, both)
-
-
-def finish(values, energies, thresholds, both, receivers):
-    shot_dev, _, rcv, block = values.shape
+def finish(diffs, bases, cuts, energies, thresholds, numbers, both, receivers):
+    count, tiles, _, block = diffs.shape
+    rcv = tiles * 8
+    shot_dev = (numbers.shape[0] - 2 * count) // SHOT_BLK
+    shots = cuts.shape[0] - 1 - shot_dev
     step = min(2, shot_dev)
 
-    def body(in_ref, thr_ref, both_ref, *refs):
+    def body(number_ref, diff_ref, base_ref, cut_ref, thr_ref, both_ref, *refs):
         out_hbm, out_ref, sem = refs[-3:]
         energy = refs[0][...]
         for ref in refs[1:-3]:
             energy = energy + ref[...]
-        cuts = thr_ref[...] * jnp.sqrt(energy / (SHOT_BLK * receivers) + epsilon)
+        seconds = thr_ref[...] * jnp.sqrt(energy / (SHOT_BLK * receivers) + epsilon)
         copies = []
         for at in range(0, shot_dev, step):
             for i in range(at, at + step):
-                cut = cuts[i : i + 1, :]
-                value = in_ref[i].reshape(SHOT_BLK * rcv, block)
-                shrunk = value - jnp.minimum(jnp.maximum(value, -cut), cut)
+                first = step_size * cut_ref[shots + i][None]
+                cut = seconds[i : i + 1, :]
+                parts = []
+                for q in range(SHOT_BLK):
+                    slot = number_ref[2 * count + i * SHOT_BLK + q]
+                    value = diff_ref[slot] - jnp.minimum(jnp.maximum(base_ref[slot], -first), first)
+                    value = value.reshape(rcv, block)
+                    shrunk = value - jnp.minimum(jnp.maximum(value, -cut), cut)
+                    parts.append(shrunk.astype(jnp.bfloat16))
                 model = lax.dot_general(
-                    both_ref[:, :block], shrunk.astype(jnp.bfloat16), (((1,), (1,)), ((), ())),
+                    both_ref[:, :block], jnp.concatenate(parts, axis=0), (((1,), (1,)), ((), ())),
                     preferred_element_type=jnp.float32,
                 )
                 for q in range(SHOT_BLK):
@@ -365,7 +384,7 @@
 
     return pl.pallas_call(
         body,
-        in_specs=[full_vmem()] * (3 + len(energies)),
+        in_specs=[full_smem()] + [full_vmem()] * (5 + len(energies)),
         out_specs=pl.BlockSpec(memory_space=pl.ANY),
         out_shape=jax.ShapeDtypeStruct((shot_dev, SHOT_BLK, block, rcv), jnp.bfloat16),
         scratch_shapes=[
@@ -374,13 +393,13 @@
         ],
         compiler_params=params(),
         name="model_of_shots",
-    )(values, thresholds, both, *energies)
+    )(numbers, diffs, bases, cuts, thresholds, both, *energies)
 
 
 def over_receivers(values):
     if lax.axis_size("rcv") == 2:
         return [values, lax.ppermute(values, "rcv", [(0, 1), (1, 0)])]
-    return [lax.psum(values, "rcv")]
+    return [lax.psum(values.astype(jnp.float32), "rcv").astype(values.dtype)]
 
 
 def rotate(values, stride, by, size):
@@ -415,12 +434,11 @@
 
     near = min(4, owners)
     far = owners // near
-    energy = energy.astype(jnp.bfloat16)
-    energy = sum(part.astype(jnp.float32) for part in over_receivers(energy)).astype(jnp.bfloat16)
+    energy = jnp.concatenate([energy] + [rotate(energy, near, j, far) for j in range(1, far)])
     energy = jnp.concatenate([energy] + [rotate(energy, 1, j, near) for j in range(1, near)])
-    energies = [energy] + [rotate(energy, near, j, far) for j in range(1, far)]
-    back = jnp.arange(far, dtype=jnp.int32)[:, None]
-    side = jnp.arange(near, dtype=jnp.int32)[None, :]
+    energies = over_receivers(energy)
+    back = jnp.arange(far, dtype=jnp.int32)[None, :]
+    side = jnp.arange(near, dtype=jnp.int32)[:, None]
     origin = (me // near - back + far) % far * near + (me % near - side + near) % near
     energy_ids = (window_ids * owners + origin[:, :, None]).reshape(-1)
 
@@ -459,11 +477,22 @@
     )
 
     numbers = jnp.concatenate([lows.reshape(-1), highs.reshape(-1), slots.reshape(-1)])
+    group = index // shot_dev
+    away = (group % near - me % near + near) % near * far
+    away = (away + (group // near - me // near + far) % far) * shot_dev + index % shot_dev
+    order = jnp.sum(jnp.where(place[None, :] == index[:, None], away[None, :], 0), axis=1)
+    own_numbers = jnp.concatenate([own_lows, own_highs, order])
+
     cuts = cutoffs(energies, hits, thr, receivers)
-    values, energy2 = second(arrived, cuts, numbers, capacity)
-    energies = over_receivers(energy2)
-    residual = remainder(records, cuts, own_lows, own_highs, both)
-    model = finish(values, energies, thr, both, receivers)
+    *landed_parts, residual = landed_energies(records, cuts, own_numbers, both, near)
+    plane = [landed_parts[0]] + [rotate(landed_parts[j], 1, j, near) for j in range(1, near)]
+    plane = sum(plane)
+    plane = sum(over_receivers(plane))
+    energies = [plane[:shot_dev]] + [
+        rotate(plane[j * shot_dev : (j + 1) * shot_dev], near, j, far) for j in range(1, far)
+    ]
+    diffs, bases = differences(arrived, cuts, numbers, capacity)
+    model = finish(diffs, bases, cuts, energies, thr, numbers, both, receivers)
     return (model, residual.reshape(windows, 1, block, rcv))
 
 

time: 63.9 us -> 59.4 us (0.930)
  waiting for transfers between devices: 26.5 us -> 12 us
  starting transfers between devices: 18.3 us -> 26.2 us
  local copies, waits for them, and re-layouts: 0.61 us -> 1.9 us
  Pallas kernels: 13.3 us -> 14.5 us
    ppermute x6 -> x12, waiting for transfers between devices: 26.4 us -> 8.49 us  [rotate(): return lax.ppermute(values, 'shot', pairs)]
    ppermute x6 -> x12, starting transfers between devices: 8.73 us -> 17.8 us  [rotate(): return lax.ppermute(values, 'shot', pairs)]
    ppermute x2, waiting for transfers between devices: 0.01 us -> 3.55 us  [over_receivers(): return [values, lax.ppermute(values, 'rcv', [(0, 1), (1, 0)])]]
    unnamed x10 -> x15, local copies, waits for them, and re-layouts: 0.02 us -> 1.28 us
    pallas_call x3, Pallas kernels: 9.49 us -> 10.7 us  [the longest x1 4.42 us: landed_energies(): pl.pallas_call(body, in_specs=[full_smem()] + [full_vmem()] * 3, out_spec...]
    all_to_all x1, starting transfers between devices: 6.06 us -> 5.28 us  [local(): lax.all_to_all(packed, 'shot', split_axis=0, concat_axis=0, tiled=True)]
    convert_element_type x2 -> x0, other arithmetic: 0.71 us -> none  [the longest x1 0.7 us: local(): energy = energy.astype(jnp.bfloat16)]
  transfers between devices with their start and end apart: 9 -> 15, of which waited for: 4 -> 7; matrix products, arithmetic and copies ran while one was open for 6% -> 7% of each run, Pallas kernels for 6% -> 14%
where the time goes in v7:
time: 59.4 us; the launch traced here: 59 us
  starting transfers between devices  26.2 us (44%)
  Pallas kernels  14.5 us (24%)
  waiting for transfers between devices  12 us (20%)
  other arithmetic  3.46 us (6%)
  local copies, waits for them, and re-layouts  1.9 us (3%)
  between operations  0.94 us (2%)
    ppermute x12, starting transfers between devices, rotate(): return lax.ppermute(values, 'shot', pairs)  17.8 us
    ppermute x12, waiting for transfers between devices, rotate(): return lax.ppermute(values, 'shot', pairs)  8.49 us
    all_to_all x1, starting transfers between devices, local(): lax.all_to_all(packed, 'shot', split_axis=0, concat_axis=0, tiled=True)  5.28 us
    pallas_call x1, Pallas kernels, landed_energies(): pl.pallas_call(body, in_specs=[full_smem()] + [full_vmem()] * 3, out_spec...  4.42 us
    ppermute x2, waiting for transfers between devices, over_receivers(): return [values, lax.ppermute(values, 'rcv', [(0, 1), (1, 0)])]  3.55 us
    pallas_call x1, Pallas kernels, differences(): pl.pallas_call(body, in_specs=[full_smem()] + [full_vmem()] * 2, out_spec...  3.35 us
    pallas_call x1, Pallas kernels, head(): pl.pallas_call(body, in_specs=[full_smem(), hbm, hbm, hbm], out_specs=[pl...  3.35 us
    ppermute x2, starting transfers between devices, over_receivers(): return [values, lax.ppermute(values, 'rcv', [(0, 1), (1, 0)])]  3.1 us
  transfers between devices with their start and end apart: 15, of which 7 were waited for; matrix products, arithmetic and copies ran while one was open for 7% of the time, Pallas kernels for 14%

profile of v7, /device:TPU:0, one launch (start us, length us, event | category | flops | bytes accessed | tf_op | source)
XLA Modules:
  0.0 59.0 jit_solution(12048743726171249691)
XLA Ops:
  0.6 3.3 %pack_coefficients.1 = (bf16[16,384,128]{2,1,0:T(8,128)(2,1)}, bf16[16,128]{1,0:T(8,128)(2,1)}) custom-call(s32[1]{0:T(128)} %bitcast.me_ref, s32[1,256]{1,0:T(1,128)} %bitcast.11, f32[16,128,128]{2,1,0:T(8,128)} %bitcast.7, bf16[128,256]{1,0:T(8,128)(2,1)} %constant.128.both_hbm.both_ref), custom_call_target="tpu_custom_call" | custom-call | tf_op jit(solution)/shard_map/pack_coefficients/pallas_call | solution.py:147
  4.0 5.1 %collective-permute-start.2 = (bf16[16,128]{1,0:T(8,128)(2,1)}, bf16[16,128]{1,0:T(8,128)(2,1)S(1)}, u32[]{:S(2)}, u32[]{:S(2)}) collective-permute-start(bf16[16,128]{1,0:T(8,128)(2,1)} %get-tuple-element.19), channel_id=1, source_target_pairs={{0,12},{1,13},{2,14},{3,15},{4,0},{5,1},{6,2},{7,3},{8,4},{9,5},{1... | collective-permute-start | bytes 12296 | tf_op jit(solution)/shard_map/ppermute | solution.py:411
  9.1 1.0 %collective-permute-start = (bf16[16,128]{1,0:T(8,128)(2,1)}, bf16[16,128]{1,0:T(8,128)(2,1)S(1)}, u32[]{:S(2)}, u32[]{:S(2)}) collective-permute-start(bf16[16,128]{1,0:T(8,128)(2,1)} %get-tuple-element.19), channel_id=1, source_target_pairs={{0,4},{1,5},{2,6},{3,7},{4,8},{5,9},{6,10},{7,11},{8,12},{9,13},{1... | collective-permute-start | bytes 12296 | tf_op jit(solution)/shard_map/ppermute | solution.py:411
  10.1 5.3 %all-to-all-start = ((bf16[16,384,128]{2,1,0:T(8,128)(2,1)}), bf16[16,384,128]{2,1,0:T(8,128)(2,1)S(1)}, u32[]{:S(2)}, u32[]{:S(2)}) async-start(bf16[16,384,128]{2,1,0:T(8,128)(2,1)} %get-tuple-element.17), calls=%async_computation | async-start | bytes 3145728 | tf_op jit(solution)/shard_map/all_to_all | solution.py:433
  15.6 0.1 broadcast_add_fusion.2
  15.6 0.1 broadcast_add_fusion
  15.7 0.2 convert_reduce_fusion
  15.9 0.1 dynamic_slice.3
  16.0 0.2 select_reduce_fusion.1
  16.2 0.4 convert_reduce_fusion.1
  16.6 0.1 multiply_reduce_fusion
  16.7 0.2 convert_reduce_fusion.4
  16.9 0.1 add.282
  17.0 0.3 convert_reduce_fusion.3
  17.3 0.1 broadcast_add_fusion.1
  17.3 0.1 fusion.1.refs_0_
  17.6 0.4 collective-permute-start.3
  18.0 0.2 convert_reduce_fusion.6
  18.2 1.4 %collective-permute-start.5 = (bf16[64,128]{1,0:T(8,128)(2,1)S(1)}, bf16[64,128]{1,0:T(8,128)(2,1)S(1)}, u32[]{:S(2)}, u32[]{:S(2)}) collective-permute-start(bf16[64,128]{1,0:T(8,128)(2,1)S(1)} %get-tuple-element.46), channel_id=1, source_target_pairs={{0,3},{1,0},{2,1},{3,2},{4,7},{5,4},{6,5},{7,6},{8,11},{9,8},{10,9... | collective-permute-start | bytes 49160 | tf_op jit(solution)/shard_map/ppermute | solution.py:411
  19.6 1.9 %collective-permute-start.4 = (bf16[64,128]{1,0:T(8,128)(2,1)S(1)}, bf16[64,128]{1,0:T(8,128)(2,1)S(1)}, u32[]{:S(2)}, u32[]{:S(2)}) collective-permute-start(bf16[64,128]{1,0:T(8,128)(2,1)S(1)} %get-tuple-element.46), channel_id=1, source_target_pairs={{0,2},{1,3},{2,0},{3,1},{4,6},{5,7},{6,4},{7,5},{8,10},{9,11},{10,... | collective-permute-start | bytes 49160 | tf_op jit(solution)/shard_map/ppermute | solution.py:411
  21.5 4.3 %collective-permute-done.3 = bf16[64,128]{1,0:T(8,128)(2,1)S(1)} collective-permute-done((bf16[64,128]{1,0:T(8,128)(2,1)S(1)}, bf16[64,128]{1,0:T(8,128)(2,1)S(1)}, u32[]{:S(2)}, u32[]{:S(2)}) %collective-permute-start.3) | collective-permute-done | bytes 16416 | tf_op jit(solution)/shard_map/ppermute | solution.py:411
  25.8 1.0 %collective-permute-done.4 = bf16[64,128]{1,0:T(8,128)(2,1)S(1)} collective-permute-done((bf16[64,128]{1,0:T(8,128)(2,1)S(1)}, bf16[64,128]{1,0:T(8,128)(2,1)S(1)}, u32[]{:S(2)}, u32[]{:S(2)}) %collective-permute-start.4) | collective-permute-done | bytes 16416 | tf_op jit(solution)/shard_map/ppermute | solution.py:411
  26.9 1.6 %collective-permute-start.6 = (bf16[256,128]{1,0:T(8,128)(2,1)S(1)}, bf16[256,128]{1,0:T(8,128)(2,1)S(1)}, u32[]{:S(2)}, u32[]{:S(2)}) collective-permute-start(bf16[256,128]{1,0:T(8,128)(2,1)S(1)} %constant_dynamic-update-slice_fusion.4.refs_2_), channel_id=1, source_target_pairs={{0,16},{16,0},{1,17},{17,1},{2,18},{18,2},{3,19},{19,3},{4,20},{20... | collective-permute-start | bytes 196616 | tf_op jit(solution)/shard_map/ppermute | solution.py:401
  28.4 0.1 pad_add_fusion.1.number_ref
  28.5 2.7 %collective-permute-done.6.refs_3_ = bf16[256,128]{1,0:T(8,128)(2,1)S(1)} collective-permute-done((bf16[256,128]{1,0:T(8,128)(2,1)S(1)}, bf16[256,128]{1,0:T(8,128)(2,1)S(1)}, u32[]{:S(2)}, u32[]{:S(2)}) %collective-permute-start.6) | collective-permute-done | bytes 65568 | tf_op jit(solution)/shard_map/ppermute | solution.py:401
  31.2 0.5 first_cutoffs.1.cut_ref
  31.7 1.2 %copy-done = f32[16,1,128,128]{3,2,1,0:T(8,128)S(1)} copy-done((f32[16,1,128,128]{3,2,1,0:T(8,128)S(1)}, f32[16,1,128,128]{3,2,1,0:T(8,128)}, u32[]{:S(2)}) %copy-start) | copy-done | bytes 1048600
  32.9 4.4 %residual_and_energies.1 = (f32[64,128]{1,0:T(8,128)S(1)}, f32[64,128]{1,0:T(8,128)S(1)}, f32[64,128]{1,0:T(8,128)S(1)}, f32[64,128]{1,0:T(8,128)S(1)}, f32[16,128,128]{2,1,0:T(8,128)}) custom-call(s32[288]{0:T(512)S(1)} %pad_add_fusion.1.number_ref, f32[16,128,128]{2,1,0:T(8,128)S(1)} %bitcast.8, f32[273,8,128]{2,1,0:T(8,128)S(1)} %first_cutoffs.1.cut_ref, ...), custom_call_target="tpu_custom_call" | custom-call | flops 1 | bytes 6291456 | tf_op jit(solution)/shard_map/residual_and_energies/pallas_call | solution.py:290
  37.4 0.1 collective-permute-start.7
  37.4 0.1 collective-permute-start.8
  37.5 1.7 %collective-permute-start.9 = (f32[64,128]{1,0:T(8,128)S(1)}, f32[64,128]{1,0:T(8,128)S(1)}, u32[]{:S(2)}, u32[]{:S(2)}) collective-permute-start(f32[64,128]{1,0:T(8,128)S(1)} %get-tuple-element.26), channel_id=1, source_target_pairs={{0,3},{1,0},{2,1},{3,2},{4,7},{5,4},{6,5},{7,6},{8,11},{9,8},{10,9... | collective-permute-start | bytes 98312 | tf_op jit(solution)/shard_map/ppermute | solution.py:411
  39.2 0.1 iota_add_fusion
  39.3 1.5 %collective-permute-done.7 = f32[64,128]{1,0:T(8,128)S(1)} collective-permute-done((f32[64,128]{1,0:T(8,128)S(1)}, f32[64,128]{1,0:T(8,128)S(1)}, u32[]{:S(2)}, u32[]{:S(2)}) %collective-permute-start.7) | collective-permute-done | bytes 32800 | tf_op jit(solution)/shard_map/ppermute | solution.py:411
  40.8 0.7 %collective-permute-done.8 = f32[64,128]{1,0:T(8,128)S(1)} collective-permute-done((f32[64,128]{1,0:T(8,128)S(1)}, f32[64,128]{1,0:T(8,128)S(1)}, u32[]{:S(2)}, u32[]{:S(2)}) %collective-permute-start.8) | collective-permute-done | bytes 32800 | tf_op jit(solution)/shard_map/ppermute | solution.py:411
  41.5 1.6 %collective-permute-start.10 = (f32[64,128]{1,0:T(8,128)S(1)}, f32[64,128]{1,0:T(8,128)S(1)}, u32[]{:S(2)}, u32[]{:S(2)}) collective-permute-start(f32[64,128]{1,0:T(8,128)S(1)} %add_add_fusion), channel_id=1, source_target_pairs={{0,16},{16,0},{1,17},{17,1},{2,18},{18,2},{3,19},{19,3},{4,20},{20... | collective-permute-start | bytes 98312 | tf_op jit(solution)/shard_map/ppermute | solution.py:401
  43.0 1.3 %select_reduce_fusion = s32[16,4]{1,0:T(8,128)S(1)} fusion(s32[16,16]{1,0:T(8,128)S(1)} %broadcast_add_fusion.1, s32[16,16]{1,0:T(8,128)S(1)} %iota_add_fusion.1, s32[16,4]{1,0:T(8,128)S(1)} %iota_add_fusion), kind=kLoop, calls=%fused_computation | loop fusion | flops 49088 | bytes 2560 | tf_op jit(solution)/shard_map/reduce_sum | solution.py:474
  44.3 0.1 copy.8
  44.4 0.1 mul.96
  44.5 0.1 reshape.334
  44.6 0.1 copy.9
  44.7 0.1 mul.98
  44.8 0.8 %collective-permute-done.10 = f32[64,128]{1,0:T(8,128)S(1)} collective-permute-done((f32[64,128]{1,0:T(8,128)S(1)}, f32[64,128]{1,0:T(8,128)S(1)}, u32[]{:S(2)}, u32[]{:S(2)}) %collective-permute-start.10) | collective-permute-done | bytes 32800 | tf_op jit(solution)/shard_map/ppermute | solution.py:401
  45.6 5.1 %collective-permute-start.13 = (f32[16,128]{1,0:T(8,128)S(1)}, f32[16,128]{1,0:T(8,128)S(1)}, u32[]{:S(2)}, u32[]{:S(2)}) collective-permute-start(f32[16,128]{1,0:T(8,128)S(1)} %get-tuple-element.42), channel_id=1, source_target_pairs={{0,12},{1,13},{2,14},{3,15},{4,0},{5,1},{6,2},{7,3},{8,4},{9,5},{1... | collective-permute-start | bytes 24584 | tf_op jit(solution)/shard_map/ppermute | solution.py:411
  50.7 1.1 %collective-permute-start.11 = (f32[16,128]{1,0:T(8,128)S(1)}, f32[16,128]{1,0:T(8,128)S(1)}, u32[]{:S(2)}, u32[]{:S(2)}) collective-permute-start(f32[16,128]{1,0:T(8,128)S(1)} %get-tuple-element.44), channel_id=1, source_target_pairs={{0,4},{1,5},{2,6},{3,7},{4,8},{5,9},{6,10},{7,11},{8,12},{9,13},{1... | collective-permute-start | bytes 24584 | tf_op jit(solution)/shard_map/ppermute | solution.py:411
  51.8 0.1 pad_add_fusion.2.number_ref
  51.8 3.4 %shot_differences.1 = (f32[48,16,8,128]{3,2,1,0:T(8,128)S(1)}, f32[48,16,8,128]{3,2,1,0:T(8,128)S(1)}) custom-call(s32[160]{0:T(256)S(1)} %pad_add_fusion.2.number_ref, bf16[16,384,128]{2,1,0:T(8,128)(2,1)S(1)} %all-to-all-done.in_ref, f32[273,8,128]{2,1,0:T(8,128)S(1)} %first_cutoffs.1.cut_ref), custom_call_target="tpu_custom_call" | custom-call | flops 1 | bytes 8388608 | tf_op jit(solution)/shard_map/shot_differences/pallas_call | solution.py:335
  55.2 0.9 %collective-permute-done.11.refs_1_ = f32[16,128]{1,0:T(8,128)S(1)} collective-permute-done((f32[16,128]{1,0:T(8,128)S(1)}, f32[16,128]{1,0:T(8,128)S(1)}, u32[]{:S(2)}, u32[]{:S(2)}) %collective-permute-start.11) | collective-permute-done | bytes 8224 | tf_op jit(solution)/shard_map/ppermute | solution.py:411
  56.1 2.9 %model_of_shots.1 = bf16[16,4,128,128]{3,2,1,0:T(8,128)(2,1)} custom-call(s32[160]{0:T(256)S(1)} %pad_add_fusion.2.number_ref, f32[48,16,8,128]{3,2,1,0:T(8,128)S(1)} %get-tuple-element.20.diff_ref, f32[48,16,8,128]{3,2,1,0:T(8,128)S(1)} %get-tuple-element.21.base_ref, f32[273,8,128]{2,1,0:T(8,128)S(1)} %first_cutoffs.1.cut_ref, f32[1,128]{1,0:T(1,128)S(1)} %bitcast.10, ...), custom_call_target="tpu_custom_call" | custom-call | tf_op jit(solution)/shard_map/model_of_shots/pallas_call | solution.py:385
  (40 shorter events, 0.2 us)
Async XLA Ops:
  0.6 15.1 %copy-start.3 = (s32[256]{0:T(256)S(1)}, s32[256]{0:T(256)}, u32[]{:S(2)}) copy-start(s32[256]{0:T(256)} %param.5) | copy-start | bytes 3076
  4.0 11.5 %copy-start.4 = (bf16[16,128]{1,0:T(8,128)(2,1)S(1)}, bf16[16,128]{1,0:T(8,128)(2,1)}, u32[]{:S(2)}) copy-start(bf16[16,128]{1,0:T(8,128)(2,1)} %get-tuple-element.19) | copy-start | bytes 12292
  4.0 27.2 %copy-start.2 = (f32[128]{0:T(128)S(1)}, f32[128]{0:T(128)}, u32[]{:S(2)}) copy-start(f32[128]{0:T(128)} %param.6) | copy-start | bytes 1540
  4.0 13.5 %collective-permute-start.2 = (bf16[16,128]{1,0:T(8,128)(2,1)}, bf16[16,128]{1,0:T(8,128)(2,1)S(1)}, u32[]{:S(2)}, u32[]{:S(2)}) collective-permute-start(bf16[16,128]{1,0:T(8,128)(2,1)} %get-tuple-element.19), channel_id=1, source_target_pairs={{0,12},{1,13},{2,14},{3,15},{4,0},{5,1},{6,2},{7,3},{8,4},{9,5},{1... | collective-permute-start | bytes 12296 | tf_op jit(solution)/shard_map/ppermute | solution.py:411
  9.1 8.4 %collective-permute-start.1 = (bf16[16,128]{1,0:T(8,128)(2,1)}, bf16[16,128]{1,0:T(8,128)(2,1)S(1)}, u32[]{:S(2)}, u32[]{:S(2)}) collective-permute-start(bf16[16,128]{1,0:T(8,128)(2,1)} %get-tuple-element.19), channel_id=1, source_target_pairs={{0,8},{1,9},{2,10},{3,11},{4,12},{5,13},{6,14},{7,15},{8,0},{9,1},... | collective-permute-start | bytes 12296 | tf_op jit(solution)/shard_map/ppermute | solution.py:411
  9.1 8.4 %collective-permute-start = (bf16[16,128]{1,0:T(8,128)(2,1)}, bf16[16,128]{1,0:T(8,128)(2,1)S(1)}, u32[]{:S(2)}, u32[]{:S(2)}) collective-permute-start(bf16[16,128]{1,0:T(8,128)(2,1)} %get-tuple-element.19), channel_id=1, source_target_pairs={{0,4},{1,5},{2,6},{3,7},{4,8},{5,9},{6,10},{7,11},{8,12},{9,13},{1... | collective-permute-start | bytes 12296 | tf_op jit(solution)/shard_map/ppermute | solution.py:411
  10.1 21.6 %copy-start.1 = (bf16[128,256]{1,0:T(8,128)(2,1)S(1)}, bf16[128,256]{1,0:T(8,128)(2,1)}, u32[]{:S(2)}) copy-start(bf16[128,256]{1,0:T(8,128)(2,1)} %constant.128.both_hbm.both_ref) | copy-start | bytes 196612
  10.1 41.7 %all-to-all-start = ((bf16[16,384,128]{2,1,0:T(8,128)(2,1)}), bf16[16,384,128]{2,1,0:T(8,128)(2,1)S(1)}, u32[]{:S(2)}, u32[]{:S(2)}) async-start(bf16[16,384,128]{2,1,0:T(8,128)(2,1)} %get-tuple-element.17), calls=%async_computation | async-start | bytes 3145728 | tf_op jit(solution)/shard_map/all_to_all | solution.py:433
  17.6 8.2 %collective-permute-start.3 = (bf16[64,128]{1,0:T(8,128)(2,1)S(1)}, bf16[64,128]{1,0:T(8,128)(2,1)S(1)}, u32[]{:S(2)}, u32[]{:S(2)}) collective-permute-start(bf16[64,128]{1,0:T(8,128)(2,1)S(1)} %get-tuple-element.46), channel_id=1, source_target_pairs={{0,1},{1,2},{2,3},{3,0},{4,5},{5,6},{6,7},{7,4},{8,9},{9,10},{10,1... | collective-permute-start | bytes 49160 | tf_op jit(solution)/shard_map/ppermute | solution.py:411
  18.2 8.7 %collective-permute-start.5 = (bf16[64,128]{1,0:T(8,128)(2,1)S(1)}, bf16[64,128]{1,0:T(8,128)(2,1)S(1)}, u32[]{:S(2)}, u32[]{:S(2)}) collective-permute-start(bf16[64,128]{1,0:T(8,128)(2,1)S(1)} %get-tuple-element.46), channel_id=1, source_target_pairs={{0,3},{1,0},{2,1},{3,2},{4,7},{5,4},{6,5},{7,6},{8,11},{9,8},{10,9... | collective-permute-start | bytes 49160 | tf_op jit(solution)/shard_map/ppermute | solution.py:411
  19.6 7.3 %collective-permute-start.4 = (bf16[64,128]{1,0:T(8,128)(2,1)S(1)}, bf16[64,128]{1,0:T(8,128)(2,1)S(1)}, u32[]{:S(2)}, u32[]{:S(2)}) collective-permute-start(bf16[64,128]{1,0:T(8,128)(2,1)S(1)} %get-tuple-element.46), channel_id=1, source_target_pairs={{0,2},{1,3},{2,0},{3,1},{4,6},{5,7},{6,4},{7,5},{8,10},{9,11},{10,... | collective-permute-start | bytes 49160 | tf_op jit(solution)/shard_map/ppermute | solution.py:411
  26.9 4.3 %collective-permute-start.6 = (bf16[256,128]{1,0:T(8,128)(2,1)S(1)}, bf16[256,128]{1,0:T(8,128)(2,1)S(1)}, u32[]{:S(2)}, u32[]{:S(2)}) collective-permute-start(bf16[256,128]{1,0:T(8,128)(2,1)S(1)} %constant_dynamic-update-slice_fusion.4.refs_2_), channel_id=1, source_target_pairs={{0,16},{16,0},{1,17},{17,1},{2,18},{18,2},{3,19},{19,3},{4,20},{20... | collective-permute-start | bytes 196616 | tf_op jit(solution)/shard_map/ppermute | solution.py:401
  31.7 1.2 %copy-start = (f32[16,1,128,128]{3,2,1,0:T(8,128)S(1)}, f32[16,1,128,128]{3,2,1,0:T(8,128)}, u32[]{:S(2)}) copy-start(f32[16,1,128,128]{3,2,1,0:T(8,128)} %param.4) | copy-start | bytes 3145732
  37.4 3.4 %collective-permute-start.7 = (f32[64,128]{1,0:T(8,128)S(1)}, f32[64,128]{1,0:T(8,128)S(1)}, u32[]{:S(2)}, u32[]{:S(2)}) collective-permute-start(f32[64,128]{1,0:T(8,128)S(1)} %get-tuple-element.24), channel_id=1, source_target_pairs={{0,1},{1,2},{2,3},{3,0},{4,5},{5,6},{6,7},{7,4},{8,9},{9,10},{10,1... | collective-permute-start | bytes 98312 | tf_op jit(solution)/shard_map/ppermute | solution.py:411
  37.4 4.0 %collective-permute-start.8 = (f32[64,128]{1,0:T(8,128)S(1)}, f32[64,128]{1,0:T(8,128)S(1)}, u32[]{:S(2)}, u32[]{:S(2)}) collective-permute-start(f32[64,128]{1,0:T(8,128)S(1)} %get-tuple-element.25), channel_id=1, source_target_pairs={{0,2},{1,3},{2,0},{3,1},{4,6},{5,7},{6,4},{7,5},{8,10},{9,11},{10,... | collective-permute-start | bytes 98312 | tf_op jit(solution)/shard_map/ppermute | solution.py:411
  37.5 4.0 %collective-permute-start.9 = (f32[64,128]{1,0:T(8,128)S(1)}, f32[64,128]{1,0:T(8,128)S(1)}, u32[]{:S(2)}, u32[]{:S(2)}) collective-permute-start(f32[64,128]{1,0:T(8,128)S(1)} %get-tuple-element.26), channel_id=1, source_target_pairs={{0,3},{1,0},{2,1},{3,2},{4,7},{5,4},{6,5},{7,6},{8,11},{9,8},{10,9... | collective-permute-start | bytes 98312 | tf_op jit(solution)/shard_map/ppermute | solution.py:411
  41.5 4.1 %collective-permute-start.10 = (f32[64,128]{1,0:T(8,128)S(1)}, f32[64,128]{1,0:T(8,128)S(1)}, u32[]{:S(2)}, u32[]{:S(2)}) collective-permute-start(f32[64,128]{1,0:T(8,128)S(1)} %add_add_fusion), channel_id=1, source_target_pairs={{0,16},{16,0},{1,17},{17,1},{2,18},{18,2},{3,19},{19,3},{4,20},{20... | collective-permute-start | bytes 98312 | tf_op jit(solution)/shard_map/ppermute | solution.py:401
  45.6 9.6 %collective-permute-start.13 = (f32[16,128]{1,0:T(8,128)S(1)}, f32[16,128]{1,0:T(8,128)S(1)}, u32[]{:S(2)}, u32[]{:S(2)}) collective-permute-start(f32[16,128]{1,0:T(8,128)S(1)} %get-tuple-element.42), channel_id=1, source_target_pairs={{0,12},{1,13},{2,14},{3,15},{4,0},{5,1},{6,2},{7,3},{8,4},{9,5},{1... | collective-permute-start | bytes 24584 | tf_op jit(solution)/shard_map/ppermute | solution.py:411
  50.7 4.5 %collective-permute-start.12 = (f32[16,128]{1,0:T(8,128)S(1)}, f32[16,128]{1,0:T(8,128)S(1)}, u32[]{:S(2)}, u32[]{:S(2)}) collective-permute-start(f32[16,128]{1,0:T(8,128)S(1)} %get-tuple-element.43), channel_id=1, source_target_pairs={{0,8},{1,9},{2,10},{3,11},{4,12},{5,13},{6,14},{7,15},{8,0},{9,1},... | collective-permute-start | bytes 24584 | tf_op jit(solution)/shard_map/ppermute | solution.py:411
  50.7 5.4 %collective-permute-start.11 = (f32[16,128]{1,0:T(8,128)S(1)}, f32[16,128]{1,0:T(8,128)S(1)}, u32[]{:S(2)}, u32[]{:S(2)}) collective-permute-start(f32[16,128]{1,0:T(8,128)S(1)} %get-tuple-element.44), channel_id=1, source_target_pairs={{0,4},{1,5},{2,6},{3,7},{4,8},{5,9},{6,10},{7,11},{8,12},{9,13},{1... | collective-permute-start | bytes 24584 | tf_op jit(solution)/shard_map/ppermute | solution.py:411

commit v8 on v7

--- a/solution.py
+++ b/solution.py
@@ -169,39 +169,6 @@
     )(me[None], offsets[None, :], records, both)
 
 
-def cutoffs(energies, hits, thresholds, receivers):
-    rows = hits.shape[0]
-    block = thresholds.shape[1]
-
-    def body(*refs):
-        hit_ref, thr_ref = refs[:2]
-        out_ref, cuts_ref = refs[-2:]
-        sums = jnp.dot(hit_ref[...], refs[2][...], preferred_element_type=jnp.float32)
-        for ref in refs[3:-2]:
-            sums = sums + jnp.dot(hit_ref[...], ref[...], preferred_element_type=jnp.float32)
-        cuts_ref[...] = thr_ref[...] * jnp.sqrt(sums / (SHOT_BLK * receivers) + epsilon)
-
-        def widen(i, _):
-            at = pl.multiple_of(i * 8, 8)
-            out_ref[pl.ds(at, 8)] = jnp.broadcast_to(
-                cuts_ref[pl.ds(at, 8), :][:, None, :], (8, 8, block)
-            )
-            return 0
-
-        lax.fori_loop(0, rows // 8, widen, 0, unroll=2)
-        out_ref[rows] = jnp.zeros((8, block), jnp.float32)
-
-    return pl.pallas_call(
-        body,
-        in_specs=[full_vmem()] * (2 + len(energies)),
-        out_specs=full_vmem(),
-        out_shape=jax.ShapeDtypeStruct((rows + 1, 8, block), jnp.float32),
-        scratch_shapes=[pltpu.VMEM((rows, block), jnp.float32)],
-        compiler_params=params(),
-        name="first_cutoffs",
-    )(hits, thresholds, *energies)
-
-
 def clipped_sum(coef, cut_ref, low, high, none):
     size = jnp.abs(coef)
     peel, unroll = 6, 2
@@ -231,19 +198,37 @@
     return diff, step_size * coef, many * coef - clipped
 
 
-def landed_energies(records, cuts, numbers, both, groups):
+def landed_energies(records, energies, hits, thresholds, numbers, both, groups, receivers):
     windows, block, rcv = records.shape
     tiles = rcv // 8
-    none = cuts.shape[0] - 1
+    none = hits.shape[0]
     shots = numbers.shape[0] - 2 * windows
     size = shots // groups
-    chunk = 4
-    chunks = windows // chunk
-
-    def body(number_ref, rec_ref, cut_ref, both_ref, *refs):
-        energy_refs, out_hbm = refs[:groups], refs[groups]
-        diff_ref, base_ref, shrunk_ref, out_ref, sum_ref, sem = refs[groups + 1 :]
+
+    def body(number_ref, rec_hbm, hit_ref, thr_ref, both_ref, *refs):
+        refs, scratch = refs[:-6], refs[-6:]
+        cuts_ref, rec_ref, diff_ref, base_ref, sum_ref, sem = scratch
+        part_refs, (cut_ref, *energy_refs, shrunk_ref) = (
+            refs[: len(energies)],
+            refs[len(energies) :],
+        )
+        get_rec = pltpu.make_async_copy(rec_hbm, rec_ref, sem)
+        get_rec.start()
+        energy = jnp.concatenate([ref[...] for ref in part_refs], axis=0)
+        sums = jnp.dot(hit_ref[...], energy, preferred_element_type=jnp.float32)
+        cuts_ref[...] = thr_ref[...] * jnp.sqrt(sums / (SHOT_BLK * receivers) + epsilon)
+
+        def widen(i, _):
+            at = pl.multiple_of(i * 8, 8)
+            cut_ref[pl.ds(at, 8)] = jnp.broadcast_to(
+                cuts_ref[pl.ds(at, 8), :][:, None, :], (8, 8, block)
+            )
+            return 0
+
+        lax.fori_loop(0, none // 8, widen, 0, unroll=2)
+        cut_ref[none] = jnp.zeros((8, block), jnp.float32)
         sum_ref[...] = jnp.zeros_like(sum_ref)
+        get_rec.wait()
         for w in range(windows):
             cover = (number_ref[windows + w] - number_ref[w]).astype(jnp.float32)
             scale = 1.0 / jnp.maximum(jnp.full((1, rcv), cover), 1.0)
@@ -257,17 +242,6 @@
             return 0
 
         lax.fori_loop(0, windows, one_window, 0)
-        copies = []
-        for c in range(chunks):
-            part = pl.ds(c * chunk, chunk)
-            blended = backward(both_ref[...], shrunk_ref[part].reshape(chunk * rcv, block))
-            for w in range(chunk):
-                at = c * chunk + w
-                out_ref[at] = rec_ref[at] - step_size * blended[:, w * rcv : (w + 1) * rcv]
-            copy = pltpu.make_async_copy(out_ref.at[part], out_hbm.at[part], sem.at[c])
-            copy.start()
-            copies.append(copy)
-
         def energies_of_window(w, _):
             diff, base = diff_ref[w], base_ref[w]
 
@@ -283,28 +257,64 @@
         lax.fori_loop(0, windows, energies_of_window, 0)
         for g in range(groups):
             energy_refs[g][...] = jnp.sum(sum_ref[g * size : (g + 1) * size], axis=1)
-        for copy in copies:
-            copy.wait()
 
     terms = pltpu.VMEM((windows, tiles, 8, block), jnp.float32)
     return pl.pallas_call(
         body,
-        in_specs=[full_smem()] + [full_vmem()] * 3,
-        out_specs=[full_vmem()] * groups + [pl.BlockSpec(memory_space=pl.ANY)],
-        out_shape=[jax.ShapeDtypeStruct((size, block), jnp.float32)] * groups
-        + [jax.ShapeDtypeStruct((windows, block, rcv), jnp.float32)],
+        in_specs=[full_smem(), pl.BlockSpec(memory_space=pltpu.HBM)]
+        + [full_vmem()] * (3 + len(energies)),
+        out_specs=[full_vmem()] * (groups + 2),
+        out_shape=[jax.ShapeDtypeStruct((none + 1, 8, block), jnp.float32)]
+        + [jax.ShapeDtypeStruct((size, block), jnp.float32)] * groups
+        + [jax.ShapeDtypeStruct((windows, rcv, block), jnp.bfloat16)],
         scratch_shapes=[
+            pltpu.VMEM((none, block), jnp.float32),
+            pltpu.VMEM((windows, block, rcv), jnp.float32),
             terms,
             terms,
-            pltpu.VMEM((windows, rcv, block), jnp.bfloat16),
-            pltpu.VMEM((windows, block, rcv), jnp.float32),
             pltpu.VMEM((shots, 8, block), jnp.float32),
-            pltpu.SemaphoreType.DMA((chunks,)),
+            pltpu.SemaphoreType.DMA,
         ],
         compiler_params=params(),
         cost_estimate=pl.CostEstimate(flops=1, bytes_accessed=6 << 20, transcendentals=0),
-        name="residual_and_energies",
-    )(numbers, records, cuts, both)
+        name="second_energies",
+    )(numbers, records, hits, thresholds, both, *energies)
+
+
+def remainder(records, sums, both):
+    windows, block, rcv = records.shape
+    chunk = 4
+    chunks = windows // chunk
+
+    def body(rec_hbm, sum_ref, both_ref, out_hbm, rec_ref, out_ref, sem):
+        def copy(c, source, target, k):
+            part = pl.ds(c * chunk, chunk)
+            return pltpu.make_async_copy(source.at[part], target.at[part], sem.at[k])
+
+        for c in range(chunks):
+            copy(c, rec_hbm, rec_ref, c).start()
+        for c in range(chunks):
+            sums = sum_ref[c * chunk : (c + 1) * chunk].reshape(chunk * rcv, block)
+            blended = backward(both_ref[...], sums)
+            copy(c, rec_hbm, rec_ref, c).wait()
+            for w in range(chunk):
+                at = c * chunk + w
+                out_ref[at] = rec_ref[at] - step_size * blended[:, w * rcv : (w + 1) * rcv]
+            copy(c, out_ref, out_hbm, chunks + c).start()
+        for c in range(chunks):
+            copy(c, out_ref, out_hbm, chunks + c).wait()
+
+    own = pltpu.VMEM((windows, block, rcv), jnp.float32)
+    return pl.pallas_call(
+        body,
+        in_specs=[pl.BlockSpec(memory_space=pltpu.HBM), full_vmem(), full_vmem()],
+        out_specs=pl.BlockSpec(memory_space=pl.ANY),
+        out_shape=jax.ShapeDtypeStruct((windows, block, rcv), jnp.float32),
+        scratch_shapes=[own, own, pltpu.SemaphoreType.DMA((2 * chunks,))],
+        compiler_params=params(),
+        cost_estimate=pl.CostEstimate(flops=1, bytes_accessed=4 << 20, transcendentals=0),
+        name="residual_of_records",
+    )(records, sums, both)
 
 
 def differences(arrived, cuts, numbers, capacity):
@@ -315,21 +325,22 @@
     none = cuts.shape[0] - 1
 
     def body(number_ref, in_ref, cut_ref, diff_ref, base_ref):
-        def one_block(slot, _):
-            low, high = number_ref[slot], number_ref[count + slot]
-
-            @pl.when(high > low)
-            def _():
-                owner = slot // capacity
-                start = pl.multiple_of((slot - owner * capacity) * rcv, rcv)
-                coef = in_ref[owner, pl.ds(start, rcv), :].astype(jnp.float32)
-                diff_ref[slot], base_ref[slot], _ = shot_terms(
-                    coef.reshape(tiles, 8, block), cut_ref, low, high, none
-                )
-
+        def one_block(place):
+            slot = number_ref[place]
+            owner = slot // capacity
+            start = pl.multiple_of((slot - owner * capacity) * rcv, rcv)
+            coef = in_ref[owner, pl.ds(start, rcv), :].astype(jnp.float32)
+            diff_ref[slot], base_ref[slot], _ = shot_terms(
+                coef.reshape(tiles, 8, block), cut_ref,
+                number_ref[count + slot], number_ref[2 * count + slot], none,
+            )
+
+        def two_blocks(i, _):
+            one_block(2 * i)
+            one_block(2 * i + 1)
             return 0
 
-        lax.fori_loop(0, count, one_block, 0)
+        lax.fori_loop(0, number_ref[number_ref.shape[0] - 1], two_blocks, 0)
 
     shape = jax.ShapeDtypeStruct((count, tiles, 8, block), jnp.float32)
     return pl.pallas_call(
@@ -346,7 +357,7 @@
 def finish(diffs, bases, cuts, energies, thresholds, numbers, both, receivers):
     count, tiles, _, block = diffs.shape
     rcv = tiles * 8
-    shot_dev = (numbers.shape[0] - 2 * count) // SHOT_BLK
+    shot_dev = (numbers.shape[0] - 1 - 3 * count) // SHOT_BLK
     shots = cuts.shape[0] - 1 - shot_dev
     step = min(2, shot_dev)
 
@@ -363,7 +374,7 @@
                 cut = seconds[i : i + 1, :]
                 parts = []
                 for q in range(SHOT_BLK):
-                    slot = number_ref[2 * count + i * SHOT_BLK + q]
+                    slot = number_ref[3 * count + i * SHOT_BLK + q]
                     value = diff_ref[slot] - jnp.minimum(jnp.maximum(base_ref[slot], -first), first)
                     value = value.reshape(rcv, block)
                     shrunk = value - jnp.minimum(jnp.maximum(value, -cut), cut)
@@ -435,8 +446,9 @@
     near = min(4, owners)
     far = owners // near
     energy = jnp.concatenate([energy] + [rotate(energy, near, j, far) for j in range(1, far)])
-    energy = jnp.concatenate([energy] + [rotate(energy, 1, j, near) for j in range(1, near)])
-    energies = over_receivers(energy)
+    energy, offsets = lax.optimization_barrier((energy, offsets))
+    energy = sum(part.astype(jnp.float32) for part in over_receivers(energy)).astype(jnp.bfloat16)
+    energies = [energy] + [rotate(energy, 1, j, near) for j in range(1, near)]
     back = jnp.arange(far, dtype=jnp.int32)[None, :]
     side = jnp.arange(near, dtype=jnp.int32)[:, None]
     origin = (me // near - back + far) % far * near + (me % near - side + near) % near
@@ -476,16 +488,29 @@
         axis=(2, 3),
     )
 
-    numbers = jnp.concatenate([lows.reshape(-1), highs.reshape(-1), slots.reshape(-1)])
+    filled = valid.reshape(-1)
+    count = jnp.arange(filled.shape[0], dtype=jnp.int32)
+    nth = jnp.sum(jnp.where(count[None, :] < count[:, None], filled[None, :], 0), axis=1)
+    chosen = (nth[None, :] == count[:, None]) & (filled[None, :] > 0)
+    chosen = jnp.sum(jnp.where(chosen, count[None, :], 0), axis=1)
+    half = (jnp.sum(filled) + 1) // 2
+    numbers = jnp.concatenate(
+        [chosen, lows.reshape(-1), highs.reshape(-1), slots.reshape(-1), half[None]]
+    )
     group = index // shot_dev
     away = (group % near - me % near + near) % near * far
     away = (away + (group // near - me // near + far) % far) * shot_dev + index % shot_dev
     order = jnp.sum(jnp.where(place[None, :] == index[:, None], away[None, :], 0), axis=1)
     own_numbers = jnp.concatenate([own_lows, own_highs, order])
 
-    cuts = cutoffs(energies, hits, thr, receivers)
-    *landed_parts, residual = landed_energies(records, cuts, own_numbers, both, near)
+    records = pltpu.with_memory_space_constraint(records, pltpu.HBM)
+    hits, own_numbers, numbers = lax.optimization_barrier((hits, own_numbers, numbers))
+    cuts, *landed_parts, sums = landed_energies(
+        records, energies, hits, thr, own_numbers, both, near, receivers
+    )
+    residual = remainder(records, sums, both)
     plane = [landed_parts[0]] + [rotate(landed_parts[j], 1, j, near) for j in range(1, near)]
+    *plane, residual = lax.optimization_barrier((*plane, residual))
     plane = sum(plane)
     plane = sum(over_receivers(plane))
     energies = [plane[:shot_dev]] + [

time: 59.4 us -> 57.6 us (0.970)
  the two profiles are of different devices: /device:TPU:0 before, /device:TPU:16 now
where the time goes in v8:
time: 57.6 us; the launch traced here: 56.8 us
  starting transfers between devices  20.3 us (35%)
  Pallas kernels  16.7 us (29%)
  waiting for transfers between devices  13.1 us (23%)
  other arithmetic  4.18 us (7%)
  between operations  1.63 us (3%)
  local copies, waits for them, and re-layouts  0.89 us (2%)
    ppermute x12, starting transfers between devices, rotate(): return lax.ppermute(values, 'shot', pairs)  11.2 us
    all_to_all x1, waiting for transfers between devices, local(): lax.all_to_all(packed, 'shot', split_axis=0, concat_axis=0, tiled=True)  6.43 us
    all_to_all x1, starting transfers between devices, local(): lax.all_to_all(packed, 'shot', split_axis=0, concat_axis=0, tiled=True)  6.08 us
    pallas_call x1, Pallas kernels, landed_energies(): pl.pallas_call(body, in_specs=[full_smem(), pl.BlockSpec(memory_space=plt...  5.19 us
    ppermute x12, waiting for transfers between devices, rotate(): return lax.ppermute(values, 'shot', pairs)  3.89 us
    pallas_call x1, Pallas kernels, head(): pl.pallas_call(body, in_specs=[full_smem(), hbm, hbm, hbm], out_specs=[pl...  3.35 us
    ppermute x2, starting transfers between devices, over_receivers(): return [values, lax.ppermute(values, 'rcv', [(0, 1), (1, 0)])]  3 us
    pallas_call x1, Pallas kernels, finish(): pl.pallas_call(body, in_specs=[full_smem()] + [full_vmem()] * (5 + len(en...  2.92 us
  transfers between devices with their start and end apart: 15, of which 4 were waited for; matrix products, arithmetic and copies ran while one was open for 9% of the time, Pallas kernels for 18%

profile of v8, /device:TPU:16, one launch (start us, length us, event | category | flops | bytes accessed | tf_op | source)
XLA Modules:
  0.0 56.8 jit_solution(7578122912873801711)
XLA Ops:
  0.6 3.3 %pack_coefficients.1 = (bf16[16,384,128]{2,1,0:T(8,128)(2,1)}, bf16[16,128]{1,0:T(8,128)(2,1)}) custom-call(s32[1]{0:T(128)} %bitcast.me_ref, s32[1,256]{1,0:T(1,128)} %bitcast.14, f32[16,128,128]{2,1,0:T(8,128)} %bitcast.10, bf16[128,256]{1,0:T(8,128)(2,1)} %constant.139.both_hbm.both_ref), custom_call_target="tpu_custom_call" | custom-call | tf_op jit(solution)/shard_map/pack_coefficients/pallas_call | solution.py:147
  4.0 0.5 collective-permute-start.2
  4.5 3.5 %collective-permute-start.1 = (bf16[16,128]{1,0:T(8,128)(2,1)}, bf16[16,128]{1,0:T(8,128)(2,1)S(1)}, u32[]{:S(2)}, u32[]{:S(2)}) collective-permute-start(bf16[16,128]{1,0:T(8,128)(2,1)} %get-tuple-element.26), channel_id=1, source_target_pairs={{0,8},{1,9},{2,10},{3,11},{4,12},{5,13},{6,14},{7,15},{8,0},{9,1},... | collective-permute-start | bytes 12296 | tf_op jit(solution)/shard_map/ppermute | solution.py:422
  8.0 6.1 %all-to-all-start = ((bf16[16,384,128]{2,1,0:T(8,128)(2,1)}), bf16[16,384,128]{2,1,0:T(8,128)(2,1)S(1)}, u32[]{:S(2)}, u32[]{:S(2)}) async-start(bf16[16,384,128]{2,1,0:T(8,128)(2,1)} %get-tuple-element.31), calls=%async_computation | async-start | bytes 3145728 | tf_op jit(solution)/shard_map/all_to_all | solution.py:444
  14.2 0.1 broadcast_add_fusion.3
  14.3 0.1 broadcast_add_fusion.1
  14.4 0.1 add.279
  14.5 0.1 dynamic_slice.3
  14.6 0.4 convert_reduce_fusion.1
  15.0 0.1 multiply_reduce_fusion
  15.1 0.7 %convert_reduce_fusion.4 = (s32[]{:T(128)}, s32[16,3]{0,1:T(4,128)S(1)}, s32[16,3]{0,1:T(4,128)S(1)}) fusion(s32[16,16]{1,0:T(8,128)S(1)} %multiply_reduce_fusion, pred[16,16]{1,0:T(8,128)(4,1)S(1)} %broadcast_compare_fusion, s32[16,16]{1,0:T(8,128)S(1)} %iota_add_fusion.1), kind=kLoop, calls=%fused_computation.19 | loop fusion | flops 5279 | bytes 2692 | tf_op jit(solution)/shard_map/reduce_sum | solution.py:496
  15.9 0.3 convert_reduce_fusion.2
  16.1 0.1 copy.10
  16.2 0.1 reduce_sum.143
  16.3 0.1 copy.8
  16.4 0.1 broadcast_in_dim.67
  16.5 0.1 copy.9
  16.6 0.1 reduce_sum.141
  16.7 1.6 %collective-permute-start.3 = (bf16[64,128]{1,0:T(8,128)(2,1)S(1)}, bf16[64,128]{1,0:T(8,128)(2,1)S(1)}, u32[]{:S(2)}, u32[]{:S(2)}) collective-permute-start(bf16[64,128]{1,0:T(8,128)(2,1)S(1)} %pad_maximum_fusion), channel_id=1, source_target_pairs={{0,16},{16,0},{1,17},{17,1},{2,18},{18,2},{3,19},{19,3},{4,20},{20... | collective-permute-start | bytes 49160 | tf_op jit(solution)/shard_map/ppermute | solution.py:412
  18.2 0.2 convert_reduce_fusion
  18.4 0.2 select_reduce_fusion.1
  18.6 0.1 select_reduce_fusion.5
  18.7 0.2 convert_reduce_fusion.7
  18.9 0.1 iota_add_fusion
  19.0 0.1 broadcast_add_fusion
  19.0 1.3 %select_reduce_fusion = s32[16,4]{1,0:T(8,128)S(1)} fusion(s32[16,16]{1,0:T(8,128)S(1)} %broadcast_add_fusion, s32[16,16]{1,0:T(8,128)S(1)} %iota_add_fusion.1, s32[16,4]{1,0:T(8,128)S(1)} %iota_add_fusion), kind=kLoop, calls=%fused_computation | loop fusion | flops 49088 | bytes 2560 | tf_op jit(solution)/shard_map/reduce_sum | solution.py:486
  20.4 0.1 fusion.1.hit_ref
  20.5 0.1 select_reduce_fusion.4
  20.6 1.0 %collective-permute-start.6 = (bf16[64,128]{1,0:T(8,128)(2,1)S(1)}, bf16[64,128]{1,0:T(8,128)(2,1)S(1)}, u32[]{:S(2)}, u32[]{:S(2)}) collective-permute-start(bf16[64,128]{1,0:T(8,128)(2,1)S(1)} %add_convert_fusion.refs_0_), channel_id=1, source_target_pairs={{0,3},{1,0},{2,1},{3,2},{4,7},{5,4},{6,5},{7,6},{8,11},{9,8},{10,9... | collective-permute-start | bytes 49160 | tf_op jit(solution)/shard_map/ppermute | solution.py:422
  21.6 0.6 %collective-permute-start.5 = (bf16[64,128]{1,0:T(8,128)(2,1)S(1)}, bf16[64,128]{1,0:T(8,128)(2,1)S(1)}, u32[]{:S(2)}, u32[]{:S(2)}) collective-permute-start(bf16[64,128]{1,0:T(8,128)(2,1)S(1)} %add_convert_fusion.refs_0_), channel_id=1, source_target_pairs={{0,2},{1,3},{2,0},{3,1},{4,6},{5,7},{6,4},{7,5},{8,10},{9,11},{10,... | collective-permute-start | bytes 49160 | tf_op jit(solution)/shard_map/ppermute | solution.py:422
  22.2 0.2 collective-permute-start.4
  22.4 0.1 pad_add_fusion.1.number_ref
  23.1 0.1 reshape.342
  23.2 0.1 concatenate.19.number_ref
  23.3 3.2 %collective-permute-done.5.refs_2_ = bf16[64,128]{1,0:T(8,128)(2,1)S(1)} collective-permute-done((bf16[64,128]{1,0:T(8,128)(2,1)S(1)}, bf16[64,128]{1,0:T(8,128)(2,1)S(1)}, u32[]{:S(2)}, u32[]{:S(2)}) %collective-permute-start.5) | collective-permute-done | bytes 16416 | tf_op jit(solution)/shard_map/ppermute | solution.py:422
  26.5 5.2 %second_energies.1 = (f32[273,8,128]{2,1,0:T(8,128)S(1)}, f32[64,128]{1,0:T(8,128)S(1)}, f32[64,128]{1,0:T(8,128)S(1)}, f32[64,128]{1,0:T(8,128)S(1)}, f32[64,12...) custom-call(s32[288]{0:T(512)S(1)} %pad_add_fusion.1.number_ref, f32[16,128,128]{2,1,0:T(8,128)} %bitcast.11, ...), custom_call_target="tpu_custom_call" | custom-call | flops 1 | bytes 6291456 | tf_op jit(solution)/shard_map/second_energies/pallas_call | solution.py:262
  31.8 0.1 collective-permute-start.8
  31.9 1.7 %collective-permute-start.9 = (f32[64,128]{1,0:T(8,128)S(1)}, f32[64,128]{1,0:T(8,128)S(1)}, u32[]{:S(2)}, u32[]{:S(2)}) collective-permute-start(f32[64,128]{1,0:T(8,128)S(1)} %get-tuple-element.43), channel_id=1, source_target_pairs={{0,3},{1,0},{2,1},{3,2},{4,7},{5,4},{6,5},{7,6},{8,11},{9,8},{10,9... | collective-permute-start | bytes 98312 | tf_op jit(solution)/shard_map/ppermute | solution.py:422
  33.5 2.4 %residual_of_records.1 = f32[16,128,128]{2,1,0:T(8,128)} custom-call(f32[16,128,128]{2,1,0:T(8,128)} %bitcast.12, bf16[16,128,128]{2,1,0:T(8,128)(2,1)S(1)} %get-tuple-element.44.sum_ref, bf16[128,256]{1,0:T(8,128)(2,1)S(1)} %copy-done), custom_call_target="tpu_custom_call" | custom-call | flops 1 | bytes 4194304 | tf_op jit(solution)/shard_map/residual_of_records/pallas_call | solution.py:308
  36.0 0.7 %collective-permute-done.9 = f32[64,128]{1,0:T(8,128)S(1)} collective-permute-done((f32[64,128]{1,0:T(8,128)S(1)}, f32[64,128]{1,0:T(8,128)S(1)}, u32[]{:S(2)}, u32[]{:S(2)}) %collective-permute-start.9) | collective-permute-done | bytes 32800 | tf_op jit(solution)/shard_map/ppermute | solution.py:422
  36.7 1.4 %collective-permute-start.10 = (f32[64,128]{1,0:T(8,128)S(1)}, f32[64,128]{1,0:T(8,128)S(1)}, u32[]{:S(2)}, u32[]{:S(2)}) collective-permute-start(f32[64,128]{1,0:T(8,128)S(1)} %add_add_fusion), channel_id=1, source_target_pairs={{0,16},{16,0},{1,17},{17,1},{2,18},{18,2},{3,19},{19,3},{4,20},{20... | collective-permute-start | bytes 98312 | tf_op jit(solution)/shard_map/ppermute | solution.py:412
  38.1 2.8 %collective-permute-done.10 = f32[64,128]{1,0:T(8,128)S(1)} collective-permute-done((f32[64,128]{1,0:T(8,128)S(1)}, f32[64,128]{1,0:T(8,128)S(1)}, u32[]{:S(2)}, u32[]{:S(2)}) %collective-permute-start.10) | collective-permute-done | bytes 32800 | tf_op jit(solution)/shard_map/ppermute | solution.py:412
  40.9 0.3 collective-permute-start.13
  41.3 3.0 %collective-permute-start.12 = (f32[16,128]{1,0:T(8,128)S(1)}, f32[16,128]{1,0:T(8,128)S(1)}, u32[]{:S(2)}, u32[]{:S(2)}) collective-permute-start(f32[16,128]{1,0:T(8,128)S(1)} %get-tuple-element.66), channel_id=1, source_target_pairs={{0,8},{1,9},{2,10},{3,11},{4,12},{5,13},{6,14},{7,15},{8,0},{9,1},... | collective-permute-start | bytes 24584 | tf_op jit(solution)/shard_map/ppermute | solution.py:422
  44.3 0.3 collective-permute-start.11
  44.6 6.4 %all-to-all-done.in_ref = bf16[16,384,128]{2,1,0:T(8,128)(2,1)S(1)} async-done(((bf16[16,384,128]{2,1,0:T(8,128)(2,1)}), bf16[16,384,128]{2,1,0:T(8,128)(2,1)S(1)}, u32[]{:S(2)}, u32[]{:S(2)}) %all-to-all-start) | async-done | bytes 1572896 | tf_op jit(solution)/shard_map/all_to_all | solution.py:444
  51.0 2.8 %shot_differences.1 = (f32[48,16,8,128]{3,2,1,0:T(8,128)S(1)}, f32[48,16,8,128]{3,2,1,0:T(8,128)S(1)}) custom-call(s32[209]{0:T(256)S(1)} %concatenate.19.number_ref, bf16[16,384,128]{2,1,0:T(8,128)(2,1)S(1)} %all-to-all-done.in_ref, f32[273,8,128]{2,1,0:T(8,128)S(1)} %get-tuple-element.37.cut_ref), custom_call_target="tpu_custom_call" | custom-call | flops 1 | bytes 8388608 | tf_op jit(solution)/shard_map/shot_differences/pallas_call | solution.py:346
  53.9 2.9 %model_of_shots.1 = bf16[16,4,128,128]{3,2,1,0:T(8,128)(2,1)} custom-call(s32[209]{0:T(256)S(1)} %concatenate.19.number_ref, f32[48,16,8,128]{3,2,1,0:T(8,128)S(1)} %get-tuple-element.38.diff_ref, f32[48,16,8,128]{3,2,1,0:T(8,128)S(1)} %get-tuple-element.39.base_ref, f32[273,8,128]{2,1,0:T(8,128)S(1)} %get-tuple-element.37.cut_ref, f32[1,128]{1,0:T(1,128)S(1)} %bitcast.9, ...), custom_call_target="tpu_custom_call" | custom-call | tf_op jit(solution)/shard_map/model_of_shots/pallas_call | solution.py:396
  (38 shorter events, 0.2 us)
Async XLA Ops:
  0.6 13.9 %copy-start.2 = (s32[256]{0:T(256)S(1)}, s32[256]{0:T(256)}, u32[]{:S(2)}) copy-start(s32[256]{0:T(256)} %param.5) | copy-start | bytes 3076
  4.0 10.5 %copy-start.3 = (bf16[16,128]{1,0:T(8,128)(2,1)S(1)}, bf16[16,128]{1,0:T(8,128)(2,1)}, u32[]{:S(2)}) copy-start(bf16[16,128]{1,0:T(8,128)(2,1)} %get-tuple-element.26) | copy-start | bytes 12292
  4.0 22.5 %copy-start = (bf16[128,256]{1,0:T(8,128)(2,1)S(1)}, bf16[128,256]{1,0:T(8,128)(2,1)}, u32[]{:S(2)}) copy-start(bf16[128,256]{1,0:T(8,128)(2,1)} %constant.139.both_hbm.both_ref) | copy-start | bytes 196612
  4.0 22.5 %copy-start.1 = (f32[128]{0:T(128)S(1)}, f32[128]{0:T(128)}, u32[]{:S(2)}) copy-start(f32[128]{0:T(128)} %param.6) | copy-start | bytes 1540
  4.0 10.4 %collective-permute-start.2 = (bf16[16,128]{1,0:T(8,128)(2,1)}, bf16[16,128]{1,0:T(8,128)(2,1)S(1)}, u32[]{:S(2)}, u32[]{:S(2)}) collective-permute-start(bf16[16,128]{1,0:T(8,128)(2,1)} %get-tuple-element.26), channel_id=1, source_target_pairs={{0,12},{1,13},{2,14},{3,15},{4,0},{5,1},{6,2},{7,3},{8,4},{9,5},{1... | collective-permute-start | bytes 12296 | tf_op jit(solution)/shard_map/ppermute | solution.py:422
  4.5 9.9 %collective-permute-start.1 = (bf16[16,128]{1,0:T(8,128)(2,1)}, bf16[16,128]{1,0:T(8,128)(2,1)S(1)}, u32[]{:S(2)}, u32[]{:S(2)}) collective-permute-start(bf16[16,128]{1,0:T(8,128)(2,1)} %get-tuple-element.26), channel_id=1, source_target_pairs={{0,8},{1,9},{2,10},{3,11},{4,12},{5,13},{6,14},{7,15},{8,0},{9,1},... | collective-permute-start | bytes 12296 | tf_op jit(solution)/shard_map/ppermute | solution.py:422
  8.0 6.4 %collective-permute-start = (bf16[16,128]{1,0:T(8,128)(2,1)}, bf16[16,128]{1,0:T(8,128)(2,1)S(1)}, u32[]{:S(2)}, u32[]{:S(2)}) collective-permute-start(bf16[16,128]{1,0:T(8,128)(2,1)} %get-tuple-element.26), channel_id=1, source_target_pairs={{0,4},{1,5},{2,6},{3,7},{4,8},{5,9},{6,10},{7,11},{8,12},{9,13},{1... | collective-permute-start | bytes 12296 | tf_op jit(solution)/shard_map/ppermute | solution.py:422
  8.0 43.0 %all-to-all-start = ((bf16[16,384,128]{2,1,0:T(8,128)(2,1)}), bf16[16,384,128]{2,1,0:T(8,128)(2,1)S(1)}, u32[]{:S(2)}, u32[]{:S(2)}) async-start(bf16[16,384,128]{2,1,0:T(8,128)(2,1)} %get-tuple-element.31), calls=%async_computation | async-start | bytes 3145728 | tf_op jit(solution)/shard_map/all_to_all | solution.py:444
  16.7 3.9 %collective-permute-start.3 = (bf16[64,128]{1,0:T(8,128)(2,1)S(1)}, bf16[64,128]{1,0:T(8,128)(2,1)S(1)}, u32[]{:S(2)}, u32[]{:S(2)}) collective-permute-start(bf16[64,128]{1,0:T(8,128)(2,1)S(1)} %pad_maximum_fusion), channel_id=1, source_target_pairs={{0,16},{16,0},{1,17},{17,1},{2,18},{18,2},{3,19},{19,3},{4,20},{20... | collective-permute-start | bytes 49160 | tf_op jit(solution)/shard_map/ppermute | solution.py:412
  20.6 2.7 %collective-permute-start.6 = (bf16[64,128]{1,0:T(8,128)(2,1)S(1)}, bf16[64,128]{1,0:T(8,128)(2,1)S(1)}, u32[]{:S(2)}, u32[]{:S(2)}) collective-permute-start(bf16[64,128]{1,0:T(8,128)(2,1)S(1)} %add_convert_fusion.refs_0_), channel_id=1, source_target_pairs={{0,3},{1,0},{2,1},{3,2},{4,7},{5,4},{6,5},{7,6},{8,11},{9,8},{10,9... | collective-permute-start | bytes 49160 | tf_op jit(solution)/shard_map/ppermute | solution.py:422
  21.6 4.9 %collective-permute-start.5 = (bf16[64,128]{1,0:T(8,128)(2,1)S(1)}, bf16[64,128]{1,0:T(8,128)(2,1)S(1)}, u32[]{:S(2)}, u32[]{:S(2)}) collective-permute-start(bf16[64,128]{1,0:T(8,128)(2,1)S(1)} %add_convert_fusion.refs_0_), channel_id=1, source_target_pairs={{0,2},{1,3},{2,0},{3,1},{4,6},{5,7},{6,4},{7,5},{8,10},{9,11},{10,... | collective-permute-start | bytes 49160 | tf_op jit(solution)/shard_map/ppermute | solution.py:422
  22.2 4.3 %collective-permute-start.4 = (bf16[64,128]{1,0:T(8,128)(2,1)S(1)}, bf16[64,128]{1,0:T(8,128)(2,1)S(1)}, u32[]{:S(2)}, u32[]{:S(2)}) collective-permute-start(bf16[64,128]{1,0:T(8,128)(2,1)S(1)} %add_convert_fusion.refs_0_), channel_id=1, source_target_pairs={{0,1},{1,2},{2,3},{3,0},{4,5},{5,6},{6,7},{7,4},{8,9},{9,10},{10,1... | collective-permute-start | bytes 49160 | tf_op jit(solution)/shard_map/ppermute | solution.py:422
  31.7 4.3 %collective-permute-start.7 = (f32[64,128]{1,0:T(8,128)S(1)}, f32[64,128]{1,0:T(8,128)S(1)}, u32[]{:S(2)}, u32[]{:S(2)}) collective-permute-start(f32[64,128]{1,0:T(8,128)S(1)} %get-tuple-element.41), channel_id=1, source_target_pairs={{0,1},{1,2},{2,3},{3,0},{4,5},{5,6},{6,7},{7,4},{8,9},{9,10},{10,1... | collective-permute-start | bytes 98312 | tf_op jit(solution)/shard_map/ppermute | solution.py:422
  31.8 4.2 %collective-permute-start.8 = (f32[64,128]{1,0:T(8,128)S(1)}, f32[64,128]{1,0:T(8,128)S(1)}, u32[]{:S(2)}, u32[]{:S(2)}) collective-permute-start(f32[64,128]{1,0:T(8,128)S(1)} %get-tuple-element.42), channel_id=1, source_target_pairs={{0,2},{1,3},{2,0},{3,1},{4,6},{5,7},{6,4},{7,5},{8,10},{9,11},{10,... | collective-permute-start | bytes 98312 | tf_op jit(solution)/shard_map/ppermute | solution.py:422
  31.9 4.8 %collective-permute-start.9 = (f32[64,128]{1,0:T(8,128)S(1)}, f32[64,128]{1,0:T(8,128)S(1)}, u32[]{:S(2)}, u32[]{:S(2)}) collective-permute-start(f32[64,128]{1,0:T(8,128)S(1)} %get-tuple-element.43), channel_id=1, source_target_pairs={{0,3},{1,0},{2,1},{3,2},{4,7},{5,4},{6,5},{7,6},{8,11},{9,8},{10,9... | collective-permute-start | bytes 98312 | tf_op jit(solution)/shard_map/ppermute | solution.py:422
  36.7 4.2 %collective-permute-start.10 = (f32[64,128]{1,0:T(8,128)S(1)}, f32[64,128]{1,0:T(8,128)S(1)}, u32[]{:S(2)}, u32[]{:S(2)}) collective-permute-start(f32[64,128]{1,0:T(8,128)S(1)} %add_add_fusion), channel_id=1, source_target_pairs={{0,16},{16,0},{1,17},{17,1},{2,18},{18,2},{3,19},{19,3},{4,20},{20... | collective-permute-start | bytes 98312 | tf_op jit(solution)/shard_map/ppermute | solution.py:412
  40.9 12.9 %collective-permute-start.13 = (f32[16,128]{1,0:T(8,128)S(1)}, f32[16,128]{1,0:T(8,128)S(1)}, u32[]{:S(2)}, u32[]{:S(2)}) collective-permute-start(f32[16,128]{1,0:T(8,128)S(1)} %get-tuple-element.65), channel_id=1, source_target_pairs={{0,12},{1,13},{2,14},{3,15},{4,0},{5,1},{6,2},{7,3},{8,4},{9,5},{1... | collective-permute-start | bytes 24584 | tf_op jit(solution)/shard_map/ppermute | solution.py:422
  41.3 12.6 %collective-permute-start.12 = (f32[16,128]{1,0:T(8,128)S(1)}, f32[16,128]{1,0:T(8,128)S(1)}, u32[]{:S(2)}, u32[]{:S(2)}) collective-permute-start(f32[16,128]{1,0:T(8,128)S(1)} %get-tuple-element.66), channel_id=1, source_target_pairs={{0,8},{1,9},{2,10},{3,11},{4,12},{5,13},{6,14},{7,15},{8,0},{9,1},... | collective-permute-start | bytes 24584 | tf_op jit(solution)/shard_map/ppermute | solution.py:422
  44.3 9.6 %collective-permute-start.11 = (f32[16,128]{1,0:T(8,128)S(1)}, f32[16,128]{1,0:T(8,128)S(1)}, u32[]{:S(2)}, u32[]{:S(2)}) collective-permute-start(f32[16,128]{1,0:T(8,128)S(1)} %get-tuple-element.67), channel_id=1, source_target_pairs={{0,4},{1,5},{2,6},{3,7},{4,8},{5,9},{6,10},{7,11},{8,12},{9,13},{1... | collective-permute-start | bytes 24584 | tf_op jit(solution)/shard_map/ppermute | solution.py:422

commit v9 on v8

--- a/solution.py
+++ b/solution.py
@@ -422,6 +422,10 @@
     return lax.ppermute(values, "shot", pairs)
 
 
+def zorder(far):
+    return list((2, 3, 1)) if far == 4 else list(range(1, far))
+
+
 def local(record_data, offsets, thresholds):
     owners = lax.axis_size("shot")
     me = lax.axis_index("shot")
@@ -445,11 +449,11 @@
 
     near = min(4, owners)
     far = owners // near
-    energy = jnp.concatenate([energy] + [rotate(energy, near, j, far) for j in range(1, far)])
+    energy = jnp.concatenate([energy] + [rotate(energy, near, j, far) for j in zorder(far)])
     energy, offsets = lax.optimization_barrier((energy, offsets))
     energy = sum(part.astype(jnp.float32) for part in over_receivers(energy)).astype(jnp.bfloat16)
     energies = [energy] + [rotate(energy, 1, j, near) for j in range(1, near)]
-    back = jnp.arange(far, dtype=jnp.int32)[None, :]
+    back = jnp.asarray([0] + zorder(far), jnp.int32)[None, :]
     side = jnp.arange(near, dtype=jnp.int32)[:, None]
     origin = (me // near - back + far) % far * near + (me % near - side + near) % near
     energy_ids = (window_ids * owners + origin[:, :, None]).reshape(-1)

time: 57.6 us -> 57.1 us (level)
    all_to_all x1, starting transfers between devices: 6.08 us -> 5.32 us  [local(): lax.all_to_all(packed, 'shot', split_axis=0, concat_axis=0, tiled=True)]
where the time goes in v9:
time: 57.1 us; the launch traced here: 56.3 us
  starting transfers between devices  20.1 us (35%)
  Pallas kernels  16.6 us (29%)
  waiting for transfers between devices  12.9 us (23%)
  other arithmetic  4.19 us (7%)
  between operations  1.64 us (3%)
  local copies, waits for them, and re-layouts  0.89 us (2%)
    ppermute x12, starting transfers between devices, rotate(): return lax.ppermute(values, 'shot', pairs)  11.8 us
    all_to_all x1, waiting for transfers between devices, local(): lax.all_to_all(packed, 'shot', split_axis=0, concat_axis=0, tiled=True)  6.42 us
    all_to_all x1, starting transfers between devices, local(): lax.all_to_all(packed, 'shot', split_axis=0, concat_axis=0, tiled=True)  5.32 us
    pallas_call x1, Pallas kernels, landed_energies(): pl.pallas_call(body, in_specs=[full_smem(), pl.BlockSpec(memory_space=plt...  4.99 us
    ppermute x12, waiting for transfers between devices, rotate(): return lax.ppermute(values, 'shot', pairs)  3.68 us
    pallas_call x1, Pallas kernels, head(): pl.pallas_call(body, in_specs=[full_smem(), hbm, hbm, hbm], out_specs=[pl...  3.35 us
    ppermute x2, starting transfers between devices, over_receivers(): return [values, lax.ppermute(values, 'rcv', [(0, 1), (1, 0)])]  3 us
    pallas_call x1, Pallas kernels, differences(): pl.pallas_call(body, in_specs=[full_smem()] + [full_vmem()] * 2, out_spec...  2.94 us
  transfers between devices with their start and end apart: 15, of which 4 were waited for; matrix products, arithmetic and copies ran while one was open for 9% of the time, Pallas kernels for 18%

profile of v9, /device:TPU:16, one launch (start us, length us, event | category | flops | bytes accessed | tf_op | source)
XLA Modules:
  0.0 56.3 jit_solution(2851679607162468752)
XLA Ops:
  0.7 3.4 %pack_coefficients.1 = (bf16[16,384,128]{2,1,0:T(8,128)(2,1)}, bf16[16,128]{1,0:T(8,128)(2,1)}) custom-call(s32[1]{0:T(128)} %bitcast.me_ref, s32[1,256]{1,0:T(1,128)} %bitcast.14, f32[16,128,128]{2,1,0:T(8,128)} %bitcast.10, bf16[128,256]{1,0:T(8,128)(2,1)} %constant.143.both_hbm.both_ref), custom_call_target="tpu_custom_call" | custom-call | tf_op jit(solution)/shard_map/pack_coefficients/pallas_call | solution.py:147
  4.1 1.6 %collective-permute-start.2 = (bf16[16,128]{1,0:T(8,128)(2,1)}, bf16[16,128]{1,0:T(8,128)(2,1)S(1)}, u32[]{:S(2)}, u32[]{:S(2)}) collective-permute-start(bf16[16,128]{1,0:T(8,128)(2,1)} %get-tuple-element.26), channel_id=1, source_target_pairs={{0,4},{1,5},{2,6},{3,7},{4,8},{5,9},{6,10},{7,11},{8,12},{9,13},{1... | collective-permute-start | bytes 12296 | tf_op jit(solution)/shard_map/ppermute | solution.py:422
  5.7 0.4 collective-permute-start.1
  6.1 2.0 %collective-permute-start = (bf16[16,128]{1,0:T(8,128)(2,1)}, bf16[16,128]{1,0:T(8,128)(2,1)S(1)}, u32[]{:S(2)}, u32[]{:S(2)}) collective-permute-start(bf16[16,128]{1,0:T(8,128)(2,1)} %get-tuple-element.26), channel_id=1, source_target_pairs={{0,8},{1,9},{2,10},{3,11},{4,12},{5,13},{6,14},{7,15},{8,0},{9,1},... | collective-permute-start | bytes 12296 | tf_op jit(solution)/shard_map/ppermute | solution.py:422
  8.1 5.3 %all-to-all-start = ((bf16[16,384,128]{2,1,0:T(8,128)(2,1)}), bf16[16,384,128]{2,1,0:T(8,128)(2,1)S(1)}, u32[]{:S(2)}, u32[]{:S(2)}) async-start(bf16[16,384,128]{2,1,0:T(8,128)(2,1)} %get-tuple-element.31), calls=%async_computation | async-start | bytes 3145728 | tf_op jit(solution)/shard_map/all_to_all | solution.py:448
  13.6 0.1 broadcast_add_fusion.3
  13.6 0.1 broadcast_add_fusion.1
  13.7 0.1 add.271
  13.9 0.1 dynamic_slice.3
  13.9 0.4 convert_reduce_fusion.1
  14.4 0.1 multiply_reduce_fusion
  14.5 0.7 %convert_reduce_fusion.4 = (s32[]{:T(128)}, s32[16,3]{0,1:T(4,128)S(1)}, s32[16,3]{0,1:T(4,128)S(1)}) fusion(s32[16,16]{1,0:T(8,128)S(1)} %multiply_reduce_fusion, pred[16,16]{1,0:T(8,128)(4,1)S(1)} %broadcast_compare_fusion, s32[16,16]{1,0:T(8,128)S(1)} %iota_add_fusion.1), kind=kLoop, calls=%fused_computation.19 | loop fusion | flops 5279 | bytes 2692 | tf_op jit(solution)/shard_map/reduce_sum | solution.py:500
  15.2 0.3 convert_reduce_fusion.2
  15.5 0.1 copy.11
  15.6 0.1 reduce_sum.143
  15.7 0.1 copy.9
  15.8 0.1 broadcast_in_dim.67
  15.8 0.1 copy.10
  15.9 0.1 reduce_sum.141
  16.0 1.6 %collective-permute-start.3 = (bf16[64,128]{1,0:T(8,128)(2,1)S(1)}, bf16[64,128]{1,0:T(8,128)(2,1)S(1)}, u32[]{:S(2)}, u32[]{:S(2)}) collective-permute-start(bf16[64,128]{1,0:T(8,128)(2,1)S(1)} %pad_maximum_fusion), channel_id=1, source_target_pairs={{0,16},{16,0},{1,17},{17,1},{2,18},{18,2},{3,19},{19,3},{4,20},{20... | collective-permute-start | bytes 49160 | tf_op jit(solution)/shard_map/ppermute | solution.py:412
  17.6 0.2 convert_reduce_fusion
  17.8 0.2 select_reduce_fusion.1
  17.9 0.1 select_reduce_fusion.5
  18.1 0.2 convert_reduce_fusion.7
  18.2 0.1 iota_add_fusion
  18.4 1.3 %select_reduce_fusion = s32[16,4]{1,0:T(8,128)S(1)} fusion(s32[16,16]{1,0:T(8,128)S(1)} %broadcast_add_fusion, s32[16,16]{1,0:T(8,128)S(1)} %iota_add_fusion.1, s32[16,4]{1,0:T(8,128)S(1)} %iota_add_fusion), kind=kLoop, calls=%fused_computation | loop fusion | flops 49088 | bytes 2560 | tf_op jit(solution)/shard_map/reduce_sum | solution.py:490
  19.7 0.1 fusion.1.hit_ref
  19.8 0.1 select_reduce_fusion.4
  20.0 1.0 %collective-permute-start.6 = (bf16[64,128]{1,0:T(8,128)(2,1)S(1)}, bf16[64,128]{1,0:T(8,128)(2,1)S(1)}, u32[]{:S(2)}, u32[]{:S(2)}) collective-permute-start(bf16[64,128]{1,0:T(8,128)(2,1)S(1)} %add_convert_fusion.refs_0_), channel_id=1, source_target_pairs={{0,3},{1,0},{2,1},{3,2},{4,7},{5,4},{6,5},{7,6},{8,11},{9,8},{10,9... | collective-permute-start | bytes 49160 | tf_op jit(solution)/shard_map/ppermute | solution.py:422
  21.0 0.6 %collective-permute-start.5 = (bf16[64,128]{1,0:T(8,128)(2,1)S(1)}, bf16[64,128]{1,0:T(8,128)(2,1)S(1)}, u32[]{:S(2)}, u32[]{:S(2)}) collective-permute-start(bf16[64,128]{1,0:T(8,128)(2,1)S(1)} %add_convert_fusion.refs_0_), channel_id=1, source_target_pairs={{0,2},{1,3},{2,0},{3,1},{4,6},{5,7},{6,4},{7,5},{8,10},{9,11},{10,... | collective-permute-start | bytes 49160 | tf_op jit(solution)/shard_map/ppermute | solution.py:422
  21.6 0.2 collective-permute-start.4
  21.7 0.1 pad_add_fusion.1.number_ref
  22.5 0.1 reshape.324
  22.6 0.1 concatenate.19.number_ref
  22.7 3.2 %collective-permute-done.5.refs_2_ = bf16[64,128]{1,0:T(8,128)(2,1)S(1)} collective-permute-done((bf16[64,128]{1,0:T(8,128)(2,1)S(1)}, bf16[64,128]{1,0:T(8,128)(2,1)S(1)}, u32[]{:S(2)}, u32[]{:S(2)}) %collective-permute-start.5) | collective-permute-done | bytes 16416 | tf_op jit(solution)/shard_map/ppermute | solution.py:422
  25.9 5.0 %second_energies.1 = (f32[273,8,128]{2,1,0:T(8,128)S(1)}, f32[64,128]{1,0:T(8,128)S(1)}, f32[64,128]{1,0:T(8,128)S(1)}, f32[64,128]{1,0:T(8,128)S(1)}, f32[64,12...) custom-call(s32[288]{0:T(512)S(1)} %pad_add_fusion.1.number_ref, f32[16,128,128]{2,1,0:T(8,128)} %bitcast.11, ...), custom_call_target="tpu_custom_call" | custom-call | flops 1 | bytes 6291456 | tf_op jit(solution)/shard_map/second_energies/pallas_call | solution.py:262
  30.9 0.7 %collective-permute-start.8 = (f32[64,128]{1,0:T(8,128)S(1)}, f32[64,128]{1,0:T(8,128)S(1)}, u32[]{:S(2)}, u32[]{:S(2)}) collective-permute-start(f32[64,128]{1,0:T(8,128)S(1)} %get-tuple-element.42), channel_id=1, source_target_pairs={{0,2},{1,3},{2,0},{3,1},{4,6},{5,7},{6,4},{7,5},{8,10},{9,11},{10,... | collective-permute-start | bytes 98312 | tf_op jit(solution)/shard_map/ppermute | solution.py:422
  31.6 1.4 %collective-permute-start.9 = (f32[64,128]{1,0:T(8,128)S(1)}, f32[64,128]{1,0:T(8,128)S(1)}, u32[]{:S(2)}, u32[]{:S(2)}) collective-permute-start(f32[64,128]{1,0:T(8,128)S(1)} %get-tuple-element.43), channel_id=1, source_target_pairs={{0,3},{1,0},{2,1},{3,2},{4,7},{5,4},{6,5},{7,6},{8,11},{9,8},{10,9... | collective-permute-start | bytes 98312 | tf_op jit(solution)/shard_map/ppermute | solution.py:422
  33.0 2.4 %residual_of_records.1 = f32[16,128,128]{2,1,0:T(8,128)} custom-call(f32[16,128,128]{2,1,0:T(8,128)} %bitcast.12, bf16[16,128,128]{2,1,0:T(8,128)(2,1)S(1)} %get-tuple-element.44.sum_ref, bf16[128,256]{1,0:T(8,128)(2,1)S(1)} %copy-done), custom_call_target="tpu_custom_call" | custom-call | flops 1 | bytes 4194304 | tf_op jit(solution)/shard_map/residual_of_records/pallas_call | solution.py:308
  35.4 0.5 collective-permute-done.9
  35.9 1.4 %collective-permute-start.10 = (f32[64,128]{1,0:T(8,128)S(1)}, f32[64,128]{1,0:T(8,128)S(1)}, u32[]{:S(2)}, u32[]{:S(2)}) collective-permute-start(f32[64,128]{1,0:T(8,128)S(1)} %add_add_fusion), channel_id=1, source_target_pairs={{0,16},{16,0},{1,17},{17,1},{2,18},{18,2},{3,19},{19,3},{4,20},{20... | collective-permute-start | bytes 98312 | tf_op jit(solution)/shard_map/ppermute | solution.py:412
  37.4 2.8 %collective-permute-done.10 = f32[64,128]{1,0:T(8,128)S(1)} collective-permute-done((f32[64,128]{1,0:T(8,128)S(1)}, f32[64,128]{1,0:T(8,128)S(1)}, u32[]{:S(2)}, u32[]{:S(2)}) %collective-permute-start.10) | collective-permute-done | bytes 32800 | tf_op jit(solution)/shard_map/ppermute | solution.py:412
  40.1 0.8 %collective-permute-start.13 = (f32[16,128]{1,0:T(8,128)S(1)}, f32[16,128]{1,0:T(8,128)S(1)}, u32[]{:S(2)}, u32[]{:S(2)}) collective-permute-start(f32[16,128]{1,0:T(8,128)S(1)} %get-tuple-element.65), channel_id=1, source_target_pairs={{0,12},{1,13},{2,14},{3,15},{4,0},{5,1},{6,2},{7,3},{8,4},{9,5},{1... | collective-permute-start | bytes 24584 | tf_op jit(solution)/shard_map/ppermute | solution.py:422
  40.9 2.6 %collective-permute-start.12 = (f32[16,128]{1,0:T(8,128)S(1)}, f32[16,128]{1,0:T(8,128)S(1)}, u32[]{:S(2)}, u32[]{:S(2)}) collective-permute-start(f32[16,128]{1,0:T(8,128)S(1)} %get-tuple-element.66), channel_id=1, source_target_pairs={{0,8},{1,9},{2,10},{3,11},{4,12},{5,13},{6,14},{7,15},{8,0},{9,1},... | collective-permute-start | bytes 24584 | tf_op jit(solution)/shard_map/ppermute | solution.py:422
  43.5 0.4 collective-permute-start.11
  44.0 6.4 %all-to-all-done.in_ref = bf16[16,384,128]{2,1,0:T(8,128)(2,1)S(1)} async-done(((bf16[16,384,128]{2,1,0:T(8,128)(2,1)}), bf16[16,384,128]{2,1,0:T(8,128)(2,1)S(1)}, u32[]{:S(2)}, u32[]{:S(2)}) %all-to-all-start) | async-done | bytes 1572896 | tf_op jit(solution)/shard_map/all_to_all | solution.py:448
  50.4 2.9 %shot_differences.1 = (f32[48,16,8,128]{3,2,1,0:T(8,128)S(1)}, f32[48,16,8,128]{3,2,1,0:T(8,128)S(1)}) custom-call(s32[209]{0:T(256)S(1)} %concatenate.19.number_ref, bf16[16,384,128]{2,1,0:T(8,128)(2,1)S(1)} %all-to-all-done.in_ref, f32[273,8,128]{2,1,0:T(8,128)S(1)} %get-tuple-element.37.cut_ref), custom_call_target="tpu_custom_call" | custom-call | flops 1 | bytes 8388608 | tf_op jit(solution)/shard_map/shot_differences/pallas_call | solution.py:346
  53.4 2.9 %model_of_shots.1 = bf16[16,4,128,128]{3,2,1,0:T(8,128)(2,1)} custom-call(s32[209]{0:T(256)S(1)} %concatenate.19.number_ref, f32[48,16,8,128]{3,2,1,0:T(8,128)S(1)} %get-tuple-element.38.diff_ref, f32[48,16,8,128]{3,2,1,0:T(8,128)S(1)} %get-tuple-element.39.base_ref, f32[273,8,128]{2,1,0:T(8,128)S(1)} %get-tuple-element.37.cut_ref, f32[1,128]{1,0:T(1,128)S(1)} %bitcast.9, ...), custom_call_target="tpu_custom_call" | custom-call | tf_op jit(solution)/shard_map/model_of_shots/pallas_call | solution.py:396
  (40 shorter events, 0.3 us)
Async XLA Ops:
  0.6 12.9 %copy-start.4 = (s32[4]{0:T(128)S(1)}, s32[4]{0:T(128)}, u32[]{:S(2)}) copy-start(s32[4]{0:T(128)} %constant.138) | copy-start | bytes 52
  0.6 13.2 %copy-start.2 = (s32[256]{0:T(256)S(1)}, s32[256]{0:T(256)}, u32[]{:S(2)}) copy-start(s32[256]{0:T(256)} %param.6) | copy-start | bytes 3076
  4.0 9.8 %copy-start.3 = (bf16[16,128]{1,0:T(8,128)(2,1)S(1)}, bf16[16,128]{1,0:T(8,128)(2,1)}, u32[]{:S(2)}) copy-start(bf16[16,128]{1,0:T(8,128)(2,1)} %get-tuple-element.26) | copy-start | bytes 12292
  4.0 21.8 %copy-start = (bf16[128,256]{1,0:T(8,128)(2,1)S(1)}, bf16[128,256]{1,0:T(8,128)(2,1)}, u32[]{:S(2)}) copy-start(bf16[128,256]{1,0:T(8,128)(2,1)} %constant.143.both_hbm.both_ref) | copy-start | bytes 196612
  4.0 21.8 %copy-start.1 = (f32[128]{0:T(128)S(1)}, f32[128]{0:T(128)}, u32[]{:S(2)}) copy-start(f32[128]{0:T(128)} %param.7) | copy-start | bytes 1540
  4.1 9.7 %collective-permute-start.2 = (bf16[16,128]{1,0:T(8,128)(2,1)}, bf16[16,128]{1,0:T(8,128)(2,1)S(1)}, u32[]{:S(2)}, u32[]{:S(2)}) collective-permute-start(bf16[16,128]{1,0:T(8,128)(2,1)} %get-tuple-element.26), channel_id=1, source_target_pairs={{0,4},{1,5},{2,6},{3,7},{4,8},{5,9},{6,10},{7,11},{8,12},{9,13},{1... | collective-permute-start | bytes 12296 | tf_op jit(solution)/shard_map/ppermute | solution.py:422
  5.7 8.1 %collective-permute-start.1 = (bf16[16,128]{1,0:T(8,128)(2,1)}, bf16[16,128]{1,0:T(8,128)(2,1)S(1)}, u32[]{:S(2)}, u32[]{:S(2)}) collective-permute-start(bf16[16,128]{1,0:T(8,128)(2,1)} %get-tuple-element.26), channel_id=1, source_target_pairs={{0,12},{1,13},{2,14},{3,15},{4,0},{5,1},{6,2},{7,3},{8,4},{9,5},{1... | collective-permute-start | bytes 12296 | tf_op jit(solution)/shard_map/ppermute | solution.py:422
  6.1 7.7 %collective-permute-start = (bf16[16,128]{1,0:T(8,128)(2,1)}, bf16[16,128]{1,0:T(8,128)(2,1)S(1)}, u32[]{:S(2)}, u32[]{:S(2)}) collective-permute-start(bf16[16,128]{1,0:T(8,128)(2,1)} %get-tuple-element.26), channel_id=1, source_target_pairs={{0,8},{1,9},{2,10},{3,11},{4,12},{5,13},{6,14},{7,15},{8,0},{9,1},... | collective-permute-start | bytes 12296 | tf_op jit(solution)/shard_map/ppermute | solution.py:422
  8.1 42.3 %all-to-all-start = ((bf16[16,384,128]{2,1,0:T(8,128)(2,1)}), bf16[16,384,128]{2,1,0:T(8,128)(2,1)S(1)}, u32[]{:S(2)}, u32[]{:S(2)}) async-start(bf16[16,384,128]{2,1,0:T(8,128)(2,1)} %get-tuple-element.31), calls=%async_computation | async-start | bytes 3145728 | tf_op jit(solution)/shard_map/all_to_all | solution.py:448
  16.0 3.9 %collective-permute-start.3 = (bf16[64,128]{1,0:T(8,128)(2,1)S(1)}, bf16[64,128]{1,0:T(8,128)(2,1)S(1)}, u32[]{:S(2)}, u32[]{:S(2)}) collective-permute-start(bf16[64,128]{1,0:T(8,128)(2,1)S(1)} %pad_maximum_fusion), channel_id=1, source_target_pairs={{0,16},{16,0},{1,17},{17,1},{2,18},{18,2},{3,19},{19,3},{4,20},{20... | collective-permute-start | bytes 49160 | tf_op jit(solution)/shard_map/ppermute | solution.py:412
  20.0 2.7 %collective-permute-start.6 = (bf16[64,128]{1,0:T(8,128)(2,1)S(1)}, bf16[64,128]{1,0:T(8,128)(2,1)S(1)}, u32[]{:S(2)}, u32[]{:S(2)}) collective-permute-start(bf16[64,128]{1,0:T(8,128)(2,1)S(1)} %add_convert_fusion.refs_0_), channel_id=1, source_target_pairs={{0,3},{1,0},{2,1},{3,2},{4,7},{5,4},{6,5},{7,6},{8,11},{9,8},{10,9... | collective-permute-start | bytes 49160 | tf_op jit(solution)/shard_map/ppermute | solution.py:422
  21.0 4.9 %collective-permute-start.5 = (bf16[64,128]{1,0:T(8,128)(2,1)S(1)}, bf16[64,128]{1,0:T(8,128)(2,1)S(1)}, u32[]{:S(2)}, u32[]{:S(2)}) collective-permute-start(bf16[64,128]{1,0:T(8,128)(2,1)S(1)} %add_convert_fusion.refs_0_), channel_id=1, source_target_pairs={{0,2},{1,3},{2,0},{3,1},{4,6},{5,7},{6,4},{7,5},{8,10},{9,11},{10,... | collective-permute-start | bytes 49160 | tf_op jit(solution)/shard_map/ppermute | solution.py:422
  21.6 4.3 %collective-permute-start.4 = (bf16[64,128]{1,0:T(8,128)(2,1)S(1)}, bf16[64,128]{1,0:T(8,128)(2,1)S(1)}, u32[]{:S(2)}, u32[]{:S(2)}) collective-permute-start(bf16[64,128]{1,0:T(8,128)(2,1)S(1)} %add_convert_fusion.refs_0_), channel_id=1, source_target_pairs={{0,1},{1,2},{2,3},{3,0},{4,5},{5,6},{6,7},{7,4},{8,9},{9,10},{10,1... | collective-permute-start | bytes 49160 | tf_op jit(solution)/shard_map/ppermute | solution.py:422
  30.9 4.6 %collective-permute-start.7 = (f32[64,128]{1,0:T(8,128)S(1)}, f32[64,128]{1,0:T(8,128)S(1)}, u32[]{:S(2)}, u32[]{:S(2)}) collective-permute-start(f32[64,128]{1,0:T(8,128)S(1)} %get-tuple-element.41), channel_id=1, source_target_pairs={{0,1},{1,2},{2,3},{3,0},{4,5},{5,6},{6,7},{7,4},{8,9},{9,10},{10,1... | collective-permute-start | bytes 98312 | tf_op jit(solution)/shard_map/ppermute | solution.py:422
  30.9 4.5 %collective-permute-start.8 = (f32[64,128]{1,0:T(8,128)S(1)}, f32[64,128]{1,0:T(8,128)S(1)}, u32[]{:S(2)}, u32[]{:S(2)}) collective-permute-start(f32[64,128]{1,0:T(8,128)S(1)} %get-tuple-element.42), channel_id=1, source_target_pairs={{0,2},{1,3},{2,0},{3,1},{4,6},{5,7},{6,4},{7,5},{8,10},{9,11},{10,... | collective-permute-start | bytes 98312 | tf_op jit(solution)/shard_map/ppermute | solution.py:422
  31.6 4.3 %collective-permute-start.9 = (f32[64,128]{1,0:T(8,128)S(1)}, f32[64,128]{1,0:T(8,128)S(1)}, u32[]{:S(2)}, u32[]{:S(2)}) collective-permute-start(f32[64,128]{1,0:T(8,128)S(1)} %get-tuple-element.43), channel_id=1, source_target_pairs={{0,3},{1,0},{2,1},{3,2},{4,7},{5,4},{6,5},{7,6},{8,11},{9,8},{10,9... | collective-permute-start | bytes 98312 | tf_op jit(solution)/shard_map/ppermute | solution.py:422
  35.9 4.2 %collective-permute-start.10 = (f32[64,128]{1,0:T(8,128)S(1)}, f32[64,128]{1,0:T(8,128)S(1)}, u32[]{:S(2)}, u32[]{:S(2)}) collective-permute-start(f32[64,128]{1,0:T(8,128)S(1)} %add_add_fusion), channel_id=1, source_target_pairs={{0,16},{16,0},{1,17},{17,1},{2,18},{18,2},{3,19},{19,3},{4,20},{20... | collective-permute-start | bytes 98312 | tf_op jit(solution)/shard_map/ppermute | solution.py:412
  40.1 13.2 %collective-permute-start.13 = (f32[16,128]{1,0:T(8,128)S(1)}, f32[16,128]{1,0:T(8,128)S(1)}, u32[]{:S(2)}, u32[]{:S(2)}) collective-permute-start(f32[16,128]{1,0:T(8,128)S(1)} %get-tuple-element.65), channel_id=1, source_target_pairs={{0,12},{1,13},{2,14},{3,15},{4,0},{5,1},{6,2},{7,3},{8,4},{9,5},{1... | collective-permute-start | bytes 24584 | tf_op jit(solution)/shard_map/ppermute | solution.py:422
  40.9 12.4 %collective-permute-start.12 = (f32[16,128]{1,0:T(8,128)S(1)}, f32[16,128]{1,0:T(8,128)S(1)}, u32[]{:S(2)}, u32[]{:S(2)}) collective-permute-start(f32[16,128]{1,0:T(8,128)S(1)} %get-tuple-element.66), channel_id=1, source_target_pairs={{0,8},{1,9},{2,10},{3,11},{4,12},{5,13},{6,14},{7,15},{8,0},{9,1},... | collective-permute-start | bytes 24584 | tf_op jit(solution)/shard_map/ppermute | solution.py:422
  43.5 9.8 %collective-permute-start.11 = (f32[16,128]{1,0:T(8,128)S(1)}, f32[16,128]{1,0:T(8,128)S(1)}, u32[]{:S(2)}, u32[]{:S(2)}) collective-permute-start(f32[16,128]{1,0:T(8,128)S(1)} %get-tuple-element.67), channel_id=1, source_target_pairs={{0,4},{1,5},{2,6},{3,7},{4,8},{5,9},{6,10},{7,11},{8,12},{9,13},{1... | collective-permute-start | bytes 24584 | tf_op jit(solution)/shard_map/ppermute | solution.py:422

commit v10 on v9

--- a/solution.py
+++ b/solution.py
@@ -11,6 +11,7 @@
 epsilon = 1e-06
 step_size = 1.0 + momentum
 VMEM_BYTES = 16 * 1024 * 1024
+BLOCKS_STEP = 4
 HEAD_VMEM_BYTES = 60 * 1024 * 1024
 
 
@@ -335,12 +336,12 @@
                 number_ref[count + slot], number_ref[2 * count + slot], none,
             )
 
-        def two_blocks(i, _):
-            one_block(2 * i)
-            one_block(2 * i + 1)
+        def some_blocks(i, _):
+            for u in range(BLOCKS_STEP):
+                one_block(BLOCKS_STEP * i + u)
             return 0
 
-        lax.fori_loop(0, number_ref[number_ref.shape[0] - 1], two_blocks, 0)
+        lax.fori_loop(0, number_ref[number_ref.shape[0] - 1], some_blocks, 0)
 
     shape = jax.ShapeDtypeStruct((count, tiles, 8, block), jnp.float32)
     return pl.pallas_call(
@@ -497,9 +498,9 @@
     nth = jnp.sum(jnp.where(count[None, :] < count[:, None], filled[None, :], 0), axis=1)
     chosen = (nth[None, :] == count[:, None]) & (filled[None, :] > 0)
     chosen = jnp.sum(jnp.where(chosen, count[None, :], 0), axis=1)
-    half = (jnp.sum(filled) + 1) // 2
+    steps = (jnp.sum(filled) + BLOCKS_STEP - 1) // BLOCKS_STEP
     numbers = jnp.concatenate(
-        [chosen, lows.reshape(-1), highs.reshape(-1), slots.reshape(-1), half[None]]
+        [chosen, lows.reshape(-1), highs.reshape(-1), slots.reshape(-1), steps[None]]
     )
     group = index // shot_dev
     away = (group % near - me % near + near) % near * far

time: 57.1 us -> 56.8 us (level)
  transfers between devices with their start and end apart: 15 -> 15, of which waited for: 4 -> 4; matrix products, arithmetic and copies ran while one was open for 9% -> 9% of each run, Pallas kernels for 18% -> 19%
where the time goes in v10:
time: 56.8 us; the launch traced here: 56.5 us
  starting transfers between devices  19.8 us (35%)
  Pallas kernels  16.9 us (30%)
  waiting for transfers between devices  13 us (23%)
  other arithmetic  4.19 us (7%)
  between operations  1.64 us (3%)
  local copies, waits for them, and re-layouts  0.89 us (2%)
    ppermute x12, starting transfers between devices, rotate(): return lax.ppermute(values, 'shot', pairs)  11.5 us
    all_to_all x1, waiting for transfers between devices, local(): lax.all_to_all(packed, 'shot', split_axis=0, concat_axis=0, tiled=True)  6.42 us
    all_to_all x1, starting transfers between devices, local(): lax.all_to_all(packed, 'shot', split_axis=0, concat_axis=0, tiled=True)  5.32 us
    pallas_call x1, Pallas kernels, landed_energies(): pl.pallas_call(body, in_specs=[full_smem(), pl.BlockSpec(memory_space=plt...  5.1 us
    ppermute x12, waiting for transfers between devices, rotate(): return lax.ppermute(values, 'shot', pairs)  3.81 us
    pallas_call x1, Pallas kernels, head(): pl.pallas_call(body, in_specs=[full_smem(), hbm, hbm, hbm], out_specs=[pl...  3.35 us
    pallas_call x1, Pallas kernels, differences(): pl.pallas_call(body, in_specs=[full_smem()] + [full_vmem()] * 2, out_spec...  3.14 us
    ppermute x2, starting transfers between devices, over_receivers(): return [values, lax.ppermute(values, 'rcv', [(0, 1), (1, 0)])]  3.01 us
  transfers between devices with their start and end apart: 15, of which 4 were waited for; matrix products, arithmetic and copies ran while one was open for 9% of the time, Pallas kernels for 19%

profile of v10, /device:TPU:16, one launch (start us, length us, event | category | flops | bytes accessed | tf_op | source)
XLA Modules:
  0.0 56.5 jit_solution(9697841093694334330)
XLA Ops:
  0.7 3.4 %pack_coefficients.1 = (bf16[16,384,128]{2,1,0:T(8,128)(2,1)}, bf16[16,128]{1,0:T(8,128)(2,1)}) custom-call(s32[1]{0:T(128)} %bitcast.me_ref, s32[1,256]{1,0:T(1,128)} %bitcast.14, f32[16,128,128]{2,1,0:T(8,128)} %bitcast.10, bf16[128,256]{1,0:T(8,128)(2,1)} %constant.143.both_hbm.both_ref), custom_call_target="tpu_custom_call" | custom-call | tf_op jit(solution)/shard_map/pack_coefficients/pallas_call | solution.py:148
  4.1 1.6 %collective-permute-start.2 = (bf16[16,128]{1,0:T(8,128)(2,1)}, bf16[16,128]{1,0:T(8,128)(2,1)S(1)}, u32[]{:S(2)}, u32[]{:S(2)}) collective-permute-start(bf16[16,128]{1,0:T(8,128)(2,1)} %get-tuple-element.26), channel_id=1, source_target_pairs={{0,4},{1,5},{2,6},{3,7},{4,8},{5,9},{6,10},{7,11},{8,12},{9,13},{1... | collective-permute-start | bytes 12296 | tf_op jit(solution)/shard_map/ppermute | solution.py:423
  5.7 0.4 collective-permute-start.1
  6.1 2.0 %collective-permute-start = (bf16[16,128]{1,0:T(8,128)(2,1)}, bf16[16,128]{1,0:T(8,128)(2,1)S(1)}, u32[]{:S(2)}, u32[]{:S(2)}) collective-permute-start(bf16[16,128]{1,0:T(8,128)(2,1)} %get-tuple-element.26), channel_id=1, source_target_pairs={{0,8},{1,9},{2,10},{3,11},{4,12},{5,13},{6,14},{7,15},{8,0},{9,1},... | collective-permute-start | bytes 12296 | tf_op jit(solution)/shard_map/ppermute | solution.py:423
  8.1 5.3 %all-to-all-start = ((bf16[16,384,128]{2,1,0:T(8,128)(2,1)}), bf16[16,384,128]{2,1,0:T(8,128)(2,1)S(1)}, u32[]{:S(2)}, u32[]{:S(2)}) async-start(bf16[16,384,128]{2,1,0:T(8,128)(2,1)} %get-tuple-element.31), calls=%async_computation | async-start | bytes 3145728 | tf_op jit(solution)/shard_map/all_to_all | solution.py:449
  13.6 0.1 broadcast_add_fusion.3
  13.6 0.1 broadcast_add_fusion.1
  13.7 0.1 add.272
  13.9 0.1 dynamic_slice.3
  13.9 0.4 convert_reduce_fusion.1
  14.4 0.1 multiply_reduce_fusion
  14.5 0.7 %convert_reduce_fusion.4 = (s32[]{:T(128)}, s32[16,3]{0,1:T(4,128)S(1)}, s32[16,3]{0,1:T(4,128)S(1)}) fusion(s32[16,16]{1,0:T(8,128)S(1)} %multiply_reduce_fusion, pred[16,16]{1,0:T(8,128)(4,1)S(1)} %broadcast_compare_fusion, s32[16,16]{1,0:T(8,128)S(1)} %iota_add_fusion.1), kind=kLoop, calls=%fused_computation.19 | loop fusion | flops 5279 | bytes 2692 | tf_op jit(solution)/shard_map/reduce_sum | solution.py:501
  15.2 0.3 convert_reduce_fusion.2
  15.5 0.1 copy.11
  15.6 0.1 reduce_sum.143
  15.7 0.1 copy.9
  15.8 0.1 broadcast_in_dim.67
  15.8 0.1 copy.10
  15.9 0.1 reduce_sum.141
  16.0 1.6 %collective-permute-start.3 = (bf16[64,128]{1,0:T(8,128)(2,1)S(1)}, bf16[64,128]{1,0:T(8,128)(2,1)S(1)}, u32[]{:S(2)}, u32[]{:S(2)}) collective-permute-start(bf16[64,128]{1,0:T(8,128)(2,1)S(1)} %pad_maximum_fusion), channel_id=1, source_target_pairs={{0,16},{16,0},{1,17},{17,1},{2,18},{18,2},{3,19},{19,3},{4,20},{20... | collective-permute-start | bytes 49160 | tf_op jit(solution)/shard_map/ppermute | solution.py:413
  17.6 0.2 convert_reduce_fusion
  17.8 0.2 select_reduce_fusion.1
  17.9 0.1 select_reduce_fusion.5
  18.1 0.2 convert_reduce_fusion.7
  18.2 0.1 iota_add_fusion
  18.4 1.3 %select_reduce_fusion = s32[16,4]{1,0:T(8,128)S(1)} fusion(s32[16,16]{1,0:T(8,128)S(1)} %broadcast_add_fusion, s32[16,16]{1,0:T(8,128)S(1)} %iota_add_fusion.1, s32[16,4]{1,0:T(8,128)S(1)} %iota_add_fusion), kind=kLoop, calls=%fused_computation | loop fusion | flops 49088 | bytes 2560 | tf_op jit(solution)/shard_map/reduce_sum | solution.py:491
  19.7 0.1 fusion.1.hit_ref
  19.8 0.1 select_reduce_fusion.4
  20.0 1.0 %collective-permute-start.6 = (bf16[64,128]{1,0:T(8,128)(2,1)S(1)}, bf16[64,128]{1,0:T(8,128)(2,1)S(1)}, u32[]{:S(2)}, u32[]{:S(2)}) collective-permute-start(bf16[64,128]{1,0:T(8,128)(2,1)S(1)} %add_convert_fusion.refs_0_), channel_id=1, source_target_pairs={{0,3},{1,0},{2,1},{3,2},{4,7},{5,4},{6,5},{7,6},{8,11},{9,8},{10,9... | collective-permute-start | bytes 49160 | tf_op jit(solution)/shard_map/ppermute | solution.py:423
  21.0 0.6 %collective-permute-start.5 = (bf16[64,128]{1,0:T(8,128)(2,1)S(1)}, bf16[64,128]{1,0:T(8,128)(2,1)S(1)}, u32[]{:S(2)}, u32[]{:S(2)}) collective-permute-start(bf16[64,128]{1,0:T(8,128)(2,1)S(1)} %add_convert_fusion.refs_0_), channel_id=1, source_target_pairs={{0,2},{1,3},{2,0},{3,1},{4,6},{5,7},{6,4},{7,5},{8,10},{9,11},{10,... | collective-permute-start | bytes 49160 | tf_op jit(solution)/shard_map/ppermute | solution.py:423
  21.6 0.2 collective-permute-start.4
  21.7 0.1 pad_add_fusion.1.number_ref
  22.5 0.1 reshape.324
  22.6 0.1 concatenate.19.number_ref
  22.7 3.2 %collective-permute-done.5.refs_2_ = bf16[64,128]{1,0:T(8,128)(2,1)S(1)} collective-permute-done((bf16[64,128]{1,0:T(8,128)(2,1)S(1)}, bf16[64,128]{1,0:T(8,128)(2,1)S(1)}, u32[]{:S(2)}, u32[]{:S(2)}) %collective-permute-start.5) | collective-permute-done | bytes 16416 | tf_op jit(solution)/shard_map/ppermute | solution.py:423
  25.9 5.1 %second_energies.1 = (f32[273,8,128]{2,1,0:T(8,128)S(1)}, f32[64,128]{1,0:T(8,128)S(1)}, f32[64,128]{1,0:T(8,128)S(1)}, f32[64,128]{1,0:T(8,128)S(1)}, f32[64,12...) custom-call(s32[288]{0:T(512)S(1)} %pad_add_fusion.1.number_ref, f32[16,128,128]{2,1,0:T(8,128)} %bitcast.11, ...), custom_call_target="tpu_custom_call" | custom-call | flops 1 | bytes 6291456 | tf_op jit(solution)/shard_map/second_energies/pallas_call | solution.py:263
  31.0 0.5 collective-permute-start.8
  31.5 1.4 %collective-permute-start.9 = (f32[64,128]{1,0:T(8,128)S(1)}, f32[64,128]{1,0:T(8,128)S(1)}, u32[]{:S(2)}, u32[]{:S(2)}) collective-permute-start(f32[64,128]{1,0:T(8,128)S(1)} %get-tuple-element.43), channel_id=1, source_target_pairs={{0,3},{1,0},{2,1},{3,2},{4,7},{5,4},{6,5},{7,6},{8,11},{9,8},{10,9... | collective-permute-start | bytes 98312 | tf_op jit(solution)/shard_map/ppermute | solution.py:423
  32.9 2.4 %residual_of_records.1 = f32[16,128,128]{2,1,0:T(8,128)} custom-call(f32[16,128,128]{2,1,0:T(8,128)} %bitcast.12, bf16[16,128,128]{2,1,0:T(8,128)(2,1)S(1)} %get-tuple-element.44.sum_ref, bf16[128,256]{1,0:T(8,128)(2,1)S(1)} %copy-done), custom_call_target="tpu_custom_call" | custom-call | flops 1 | bytes 4194304 | tf_op jit(solution)/shard_map/residual_of_records/pallas_call | solution.py:309
  35.3 0.6 %collective-permute-done.9 = f32[64,128]{1,0:T(8,128)S(1)} collective-permute-done((f32[64,128]{1,0:T(8,128)S(1)}, f32[64,128]{1,0:T(8,128)S(1)}, u32[]{:S(2)}, u32[]{:S(2)}) %collective-permute-start.9) | collective-permute-done | bytes 32800 | tf_op jit(solution)/shard_map/ppermute | solution.py:423
  36.0 1.5 %collective-permute-start.10 = (f32[64,128]{1,0:T(8,128)S(1)}, f32[64,128]{1,0:T(8,128)S(1)}, u32[]{:S(2)}, u32[]{:S(2)}) collective-permute-start(f32[64,128]{1,0:T(8,128)S(1)} %add_add_fusion), channel_id=1, source_target_pairs={{0,16},{16,0},{1,17},{17,1},{2,18},{18,2},{3,19},{19,3},{4,20},{20... | collective-permute-start | bytes 98312 | tf_op jit(solution)/shard_map/ppermute | solution.py:413
  37.4 2.8 %collective-permute-done.10 = f32[64,128]{1,0:T(8,128)S(1)} collective-permute-done((f32[64,128]{1,0:T(8,128)S(1)}, f32[64,128]{1,0:T(8,128)S(1)}, u32[]{:S(2)}, u32[]{:S(2)}) %collective-permute-start.10) | collective-permute-done | bytes 32800 | tf_op jit(solution)/shard_map/ppermute | solution.py:413
  40.2 0.8 %collective-permute-start.13 = (f32[16,128]{1,0:T(8,128)S(1)}, f32[16,128]{1,0:T(8,128)S(1)}, u32[]{:S(2)}, u32[]{:S(2)}) collective-permute-start(f32[16,128]{1,0:T(8,128)S(1)} %get-tuple-element.65), channel_id=1, source_target_pairs={{0,12},{1,13},{2,14},{3,15},{4,0},{5,1},{6,2},{7,3},{8,4},{9,5},{1... | collective-permute-start | bytes 24584 | tf_op jit(solution)/shard_map/ppermute | solution.py:423
  41.1 2.0 %collective-permute-start.12 = (f32[16,128]{1,0:T(8,128)S(1)}, f32[16,128]{1,0:T(8,128)S(1)}, u32[]{:S(2)}, u32[]{:S(2)}) collective-permute-start(f32[16,128]{1,0:T(8,128)S(1)} %get-tuple-element.66), channel_id=1, source_target_pairs={{0,8},{1,9},{2,10},{3,11},{4,12},{5,13},{6,14},{7,15},{8,0},{9,1},... | collective-permute-start | bytes 24584 | tf_op jit(solution)/shard_map/ppermute | solution.py:423
  43.0 0.9 %collective-permute-start.11 = (f32[16,128]{1,0:T(8,128)S(1)}, f32[16,128]{1,0:T(8,128)S(1)}, u32[]{:S(2)}, u32[]{:S(2)}) collective-permute-start(f32[16,128]{1,0:T(8,128)S(1)} %get-tuple-element.67), channel_id=1, source_target_pairs={{0,4},{1,5},{2,6},{3,7},{4,8},{5,9},{6,10},{7,11},{8,12},{9,13},{1... | collective-permute-start | bytes 24584 | tf_op jit(solution)/shard_map/ppermute | solution.py:423
  44.0 6.4 %all-to-all-done.in_ref = bf16[16,384,128]{2,1,0:T(8,128)(2,1)S(1)} async-done(((bf16[16,384,128]{2,1,0:T(8,128)(2,1)}), bf16[16,384,128]{2,1,0:T(8,128)(2,1)S(1)}, u32[]{:S(2)}, u32[]{:S(2)}) %all-to-all-start) | async-done | bytes 1572896 | tf_op jit(solution)/shard_map/all_to_all | solution.py:449
  50.4 3.1 %shot_differences.1 = (f32[48,16,8,128]{3,2,1,0:T(8,128)S(1)}, f32[48,16,8,128]{3,2,1,0:T(8,128)S(1)}) custom-call(s32[209]{0:T(256)S(1)} %concatenate.19.number_ref, bf16[16,384,128]{2,1,0:T(8,128)(2,1)S(1)} %all-to-all-done.in_ref, f32[273,8,128]{2,1,0:T(8,128)S(1)} %get-tuple-element.37.cut_ref), custom_call_target="tpu_custom_call" | custom-call | flops 1 | bytes 8388608 | tf_op jit(solution)/shard_map/shot_differences/pallas_call | solution.py:347
  53.6 2.9 %model_of_shots.1 = bf16[16,4,128,128]{3,2,1,0:T(8,128)(2,1)} custom-call(s32[209]{0:T(256)S(1)} %concatenate.19.number_ref, f32[48,16,8,128]{3,2,1,0:T(8,128)S(1)} %get-tuple-element.38.diff_ref, f32[48,16,8,128]{3,2,1,0:T(8,128)S(1)} %get-tuple-element.39.base_ref, f32[273,8,128]{2,1,0:T(8,128)S(1)} %get-tuple-element.37.cut_ref, f32[1,128]{1,0:T(1,128)S(1)} %bitcast.9, ...), custom_call_target="tpu_custom_call" | custom-call | tf_op jit(solution)/shard_map/model_of_shots/pallas_call | solution.py:397
  (40 shorter events, 0.3 us)
Async XLA Ops:
  0.6 12.9 %copy-start.4 = (s32[4]{0:T(128)S(1)}, s32[4]{0:T(128)}, u32[]{:S(2)}) copy-start(s32[4]{0:T(128)} %constant.138) | copy-start | bytes 52
  0.6 13.2 %copy-start.2 = (s32[256]{0:T(256)S(1)}, s32[256]{0:T(256)}, u32[]{:S(2)}) copy-start(s32[256]{0:T(256)} %param.6) | copy-start | bytes 3076
  4.0 9.8 %copy-start.3 = (bf16[16,128]{1,0:T(8,128)(2,1)S(1)}, bf16[16,128]{1,0:T(8,128)(2,1)}, u32[]{:S(2)}) copy-start(bf16[16,128]{1,0:T(8,128)(2,1)} %get-tuple-element.26) | copy-start | bytes 12292
  4.0 21.8 %copy-start = (bf16[128,256]{1,0:T(8,128)(2,1)S(1)}, bf16[128,256]{1,0:T(8,128)(2,1)}, u32[]{:S(2)}) copy-start(bf16[128,256]{1,0:T(8,128)(2,1)} %constant.143.both_hbm.both_ref) | copy-start | bytes 196612
  4.0 21.8 %copy-start.1 = (f32[128]{0:T(128)S(1)}, f32[128]{0:T(128)}, u32[]{:S(2)}) copy-start(f32[128]{0:T(128)} %param.7) | copy-start | bytes 1540
  4.1 9.7 %collective-permute-start.2 = (bf16[16,128]{1,0:T(8,128)(2,1)}, bf16[16,128]{1,0:T(8,128)(2,1)S(1)}, u32[]{:S(2)}, u32[]{:S(2)}) collective-permute-start(bf16[16,128]{1,0:T(8,128)(2,1)} %get-tuple-element.26), channel_id=1, source_target_pairs={{0,4},{1,5},{2,6},{3,7},{4,8},{5,9},{6,10},{7,11},{8,12},{9,13},{1... | collective-permute-start | bytes 12296 | tf_op jit(solution)/shard_map/ppermute | solution.py:423
  5.7 8.1 %collective-permute-start.1 = (bf16[16,128]{1,0:T(8,128)(2,1)}, bf16[16,128]{1,0:T(8,128)(2,1)S(1)}, u32[]{:S(2)}, u32[]{:S(2)}) collective-permute-start(bf16[16,128]{1,0:T(8,128)(2,1)} %get-tuple-element.26), channel_id=1, source_target_pairs={{0,12},{1,13},{2,14},{3,15},{4,0},{5,1},{6,2},{7,3},{8,4},{9,5},{1... | collective-permute-start | bytes 12296 | tf_op jit(solution)/shard_map/ppermute | solution.py:423
  6.1 7.7 %collective-permute-start = (bf16[16,128]{1,0:T(8,128)(2,1)}, bf16[16,128]{1,0:T(8,128)(2,1)S(1)}, u32[]{:S(2)}, u32[]{:S(2)}) collective-permute-start(bf16[16,128]{1,0:T(8,128)(2,1)} %get-tuple-element.26), channel_id=1, source_target_pairs={{0,8},{1,9},{2,10},{3,11},{4,12},{5,13},{6,14},{7,15},{8,0},{9,1},... | collective-permute-start | bytes 12296 | tf_op jit(solution)/shard_map/ppermute | solution.py:423
  8.1 42.3 %all-to-all-start = ((bf16[16,384,128]{2,1,0:T(8,128)(2,1)}), bf16[16,384,128]{2,1,0:T(8,128)(2,1)S(1)}, u32[]{:S(2)}, u32[]{:S(2)}) async-start(bf16[16,384,128]{2,1,0:T(8,128)(2,1)} %get-tuple-element.31), calls=%async_computation | async-start | bytes 3145728 | tf_op jit(solution)/shard_map/all_to_all | solution.py:449
  16.0 3.9 %collective-permute-start.3 = (bf16[64,128]{1,0:T(8,128)(2,1)S(1)}, bf16[64,128]{1,0:T(8,128)(2,1)S(1)}, u32[]{:S(2)}, u32[]{:S(2)}) collective-permute-start(bf16[64,128]{1,0:T(8,128)(2,1)S(1)} %pad_maximum_fusion), channel_id=1, source_target_pairs={{0,16},{16,0},{1,17},{17,1},{2,18},{18,2},{3,19},{19,3},{4,20},{20... | collective-permute-start | bytes 49160 | tf_op jit(solution)/shard_map/ppermute | solution.py:413
  20.0 2.7 %collective-permute-start.6 = (bf16[64,128]{1,0:T(8,128)(2,1)S(1)}, bf16[64,128]{1,0:T(8,128)(2,1)S(1)}, u32[]{:S(2)}, u32[]{:S(2)}) collective-permute-start(bf16[64,128]{1,0:T(8,128)(2,1)S(1)} %add_convert_fusion.refs_0_), channel_id=1, source_target_pairs={{0,3},{1,0},{2,1},{3,2},{4,7},{5,4},{6,5},{7,6},{8,11},{9,8},{10,9... | collective-permute-start | bytes 49160 | tf_op jit(solution)/shard_map/ppermute | solution.py:423
  21.0 4.9 %collective-permute-start.5 = (bf16[64,128]{1,0:T(8,128)(2,1)S(1)}, bf16[64,128]{1,0:T(8,128)(2,1)S(1)}, u32[]{:S(2)}, u32[]{:S(2)}) collective-permute-start(bf16[64,128]{1,0:T(8,128)(2,1)S(1)} %add_convert_fusion.refs_0_), channel_id=1, source_target_pairs={{0,2},{1,3},{2,0},{3,1},{4,6},{5,7},{6,4},{7,5},{8,10},{9,11},{10,... | collective-permute-start | bytes 49160 | tf_op jit(solution)/shard_map/ppermute | solution.py:423
  21.6 4.3 %collective-permute-start.4 = (bf16[64,128]{1,0:T(8,128)(2,1)S(1)}, bf16[64,128]{1,0:T(8,128)(2,1)S(1)}, u32[]{:S(2)}, u32[]{:S(2)}) collective-permute-start(bf16[64,128]{1,0:T(8,128)(2,1)S(1)} %add_convert_fusion.refs_0_), channel_id=1, source_target_pairs={{0,1},{1,2},{2,3},{3,0},{4,5},{5,6},{6,7},{7,4},{8,9},{9,10},{10,1... | collective-permute-start | bytes 49160 | tf_op jit(solution)/shard_map/ppermute | solution.py:423
  31.0 4.4 %collective-permute-start.7 = (f32[64,128]{1,0:T(8,128)S(1)}, f32[64,128]{1,0:T(8,128)S(1)}, u32[]{:S(2)}, u32[]{:S(2)}) collective-permute-start(f32[64,128]{1,0:T(8,128)S(1)} %get-tuple-element.41), channel_id=1, source_target_pairs={{0,1},{1,2},{2,3},{3,0},{4,5},{5,6},{6,7},{7,4},{8,9},{9,10},{10,1... | collective-permute-start | bytes 98312 | tf_op jit(solution)/shard_map/ppermute | solution.py:423
  31.0 4.3 %collective-permute-start.8 = (f32[64,128]{1,0:T(8,128)S(1)}, f32[64,128]{1,0:T(8,128)S(1)}, u32[]{:S(2)}, u32[]{:S(2)}) collective-permute-start(f32[64,128]{1,0:T(8,128)S(1)} %get-tuple-element.42), channel_id=1, source_target_pairs={{0,2},{1,3},{2,0},{3,1},{4,6},{5,7},{6,4},{7,5},{8,10},{9,11},{10,... | collective-permute-start | bytes 98312 | tf_op jit(solution)/shard_map/ppermute | solution.py:423
  31.5 4.5 %collective-permute-start.9 = (f32[64,128]{1,0:T(8,128)S(1)}, f32[64,128]{1,0:T(8,128)S(1)}, u32[]{:S(2)}, u32[]{:S(2)}) collective-permute-start(f32[64,128]{1,0:T(8,128)S(1)} %get-tuple-element.43), channel_id=1, source_target_pairs={{0,3},{1,0},{2,1},{3,2},{4,7},{5,4},{6,5},{7,6},{8,11},{9,8},{10,9... | collective-permute-start | bytes 98312 | tf_op jit(solution)/shard_map/ppermute | solution.py:423
  36.0 4.2 %collective-permute-start.10 = (f32[64,128]{1,0:T(8,128)S(1)}, f32[64,128]{1,0:T(8,128)S(1)}, u32[]{:S(2)}, u32[]{:S(2)}) collective-permute-start(f32[64,128]{1,0:T(8,128)S(1)} %add_add_fusion), channel_id=1, source_target_pairs={{0,16},{16,0},{1,17},{17,1},{2,18},{18,2},{3,19},{19,3},{4,20},{20... | collective-permute-start | bytes 98312 | tf_op jit(solution)/shard_map/ppermute | solution.py:413
  40.2 13.3 %collective-permute-start.13 = (f32[16,128]{1,0:T(8,128)S(1)}, f32[16,128]{1,0:T(8,128)S(1)}, u32[]{:S(2)}, u32[]{:S(2)}) collective-permute-start(f32[16,128]{1,0:T(8,128)S(1)} %get-tuple-element.65), channel_id=1, source_target_pairs={{0,12},{1,13},{2,14},{3,15},{4,0},{5,1},{6,2},{7,3},{8,4},{9,5},{1... | collective-permute-start | bytes 24584 | tf_op jit(solution)/shard_map/ppermute | solution.py:423
  41.1 12.5 %collective-permute-start.12 = (f32[16,128]{1,0:T(8,128)S(1)}, f32[16,128]{1,0:T(8,128)S(1)}, u32[]{:S(2)}, u32[]{:S(2)}) collective-permute-start(f32[16,128]{1,0:T(8,128)S(1)} %get-tuple-element.66), channel_id=1, source_target_pairs={{0,8},{1,9},{2,10},{3,11},{4,12},{5,13},{6,14},{7,15},{8,0},{9,1},... | collective-permute-start | bytes 24584 | tf_op jit(solution)/shard_map/ppermute | solution.py:423
  43.0 10.5 %collective-permute-start.11 = (f32[16,128]{1,0:T(8,128)S(1)}, f32[16,128]{1,0:T(8,128)S(1)}, u32[]{:S(2)}, u32[]{:S(2)}) collective-permute-start(f32[16,128]{1,0:T(8,128)S(1)} %get-tuple-element.67), channel_id=1, source_target_pairs={{0,4},{1,5},{2,6},{3,7},{4,8},{5,9},{6,10},{7,11},{8,12},{9,13},{1... | collective-permute-start | bytes 24584 | tf_op jit(solution)/shard_map/ppermute | solution.py:423

commit v11 on v10

--- a/solution.py
+++ b/solution.py
@@ -318,14 +318,15 @@
     )(records, sums, both)
 
 
-def differences(arrived, cuts, numbers, capacity):
+def second(arrived, cuts, numbers, capacity, shot_dev):
     owners, rows, block = arrived.shape
     rcv = rows // capacity
     tiles = rcv // 8
     count = owners * capacity
     none = cuts.shape[0] - 1
-
-    def body(number_ref, in_ref, cut_ref, diff_ref, base_ref):
+    shots = none - shot_dev
+
+    def body(number_ref, in_ref, cut_ref, out_ref, diff_ref, base_ref):
         def one_block(place):
             slot = number_ref[place]
             owner = slot // capacity
@@ -343,45 +344,49 @@
 
         lax.fori_loop(0, number_ref[number_ref.shape[0] - 1], some_blocks, 0)
 
-    shape = jax.ShapeDtypeStruct((count, tiles, 8, block), jnp.float32)
+        def one_shot(shot, _):
+            cut = step_size * cut_ref[shots + shot][None]
+            for q in range(SHOT_BLK):
+                entry = shot * SHOT_BLK + q
+                slot = number_ref[3 * count + entry]
+                value = diff_ref[slot] - jnp.minimum(jnp.maximum(base_ref[slot], -cut), cut)
+                out_ref[entry] = value.reshape(rcv, block)
+            return 0
+
+        lax.fori_loop(0, shot_dev, one_shot, 0, unroll=2)
+
+    terms = pltpu.VMEM((count, tiles, 8, block), jnp.float32)
     return pl.pallas_call(
         body,
         in_specs=[full_smem()] + [full_vmem()] * 2,
-        out_specs=[full_vmem()] * 2,
-        out_shape=[shape] * 2,
+        out_specs=full_vmem(),
+        out_shape=jax.ShapeDtypeStruct((shot_dev * SHOT_BLK, rcv, block), jnp.float32),
+        scratch_shapes=[terms, terms],
         compiler_params=params(),
         cost_estimate=pl.CostEstimate(flops=1, bytes_accessed=8 << 20, transcendentals=0),
-        name="shot_differences",
+        name="second_coefficients",
     )(numbers, arrived, cuts)
 
 
-def finish(diffs, bases, cuts, energies, thresholds, numbers, both, receivers):
-    count, tiles, _, block = diffs.shape
-    rcv = tiles * 8
-    shot_dev = (numbers.shape[0] - 1 - 3 * count) // SHOT_BLK
-    shots = cuts.shape[0] - 1 - shot_dev
+def finish(values, energies, thresholds, both, receivers):
+    entries, rcv, block = values.shape
+    shot_dev = entries // SHOT_BLK
     step = min(2, shot_dev)
 
-    def body(number_ref, diff_ref, base_ref, cut_ref, thr_ref, both_ref, *refs):
+    def body(in_ref, thr_ref, both_ref, *refs):
         out_hbm, out_ref, sem = refs[-3:]
         energy = refs[0][...]
         for ref in refs[1:-3]:
             energy = energy + ref[...]
-        seconds = thr_ref[...] * jnp.sqrt(energy / (SHOT_BLK * receivers) + epsilon)
+        cuts = thr_ref[...] * jnp.sqrt(energy / (SHOT_BLK * receivers) + epsilon)
         copies = []
         for at in range(0, shot_dev, step):
             for i in range(at, at + step):
-                first = step_size * cut_ref[shots + i][None]
-                cut = seconds[i : i + 1, :]
-                parts = []
-                for q in range(SHOT_BLK):
-                    slot = number_ref[3 * count + i * SHOT_BLK + q]
-                    value = diff_ref[slot] - jnp.minimum(jnp.maximum(base_ref[slot], -first), first)
-                    value = value.reshape(rcv, block)
-                    shrunk = value - jnp.minimum(jnp.maximum(value, -cut), cut)
-                    parts.append(shrunk.astype(jnp.bfloat16))
+                cut = cuts[i : i + 1, :]
+                value = in_ref[i * SHOT_BLK : (i + 1) * SHOT_BLK].reshape(SHOT_BLK * rcv, block)
+                shrunk = value - jnp.minimum(jnp.maximum(value, -cut), cut)
                 model = lax.dot_general(
-                    both_ref[:, :block], jnp.concatenate(parts, axis=0), (((1,), (1,)), ((), ())),
+                    both_ref[:, :block], shrunk.astype(jnp.bfloat16), (((1,), (1,)), ((), ())),
                     preferred_element_type=jnp.float32,
                 )
                 for q in range(SHOT_BLK):
@@ -396,7 +401,7 @@
 
     return pl.pallas_call(
         body,
-        in_specs=[full_smem()] + [full_vmem()] * (5 + len(energies)),
+        in_specs=[full_vmem()] * (3 + len(energies)),
         out_specs=pl.BlockSpec(memory_space=pl.ANY),
         out_shape=jax.ShapeDtypeStruct((shot_dev, SHOT_BLK, block, rcv), jnp.bfloat16),
         scratch_shapes=[
@@ -405,7 +410,7 @@
         ],
         compiler_params=params(),
         name="model_of_shots",
-    )(numbers, diffs, bases, cuts, thresholds, both, *energies)
+    )(values, thresholds, both, *energies)
 
 
 def over_receivers(values):
@@ -521,8 +526,8 @@
     energies = [plane[:shot_dev]] + [
         rotate(plane[j * shot_dev : (j + 1) * shot_dev], near, j, far) for j in range(1, far)
     ]
-    diffs, bases = differences(arrived, cuts, numbers, capacity)
-    model = finish(diffs, bases, cuts, energies, thr, numbers, both, receivers)
+    values = second(arrived, cuts, numbers, capacity, shot_dev)
+    model = finish(values, energies, thr, both, receivers)
     return (model, residual.reshape(windows, 1, block, rcv))
 
 

time: 56.8 us -> 56.1 us (0.988)
  starting transfers between devices: 19.8 us -> 23.4 us
  waiting for transfers between devices: 13 us -> 9.58 us
  Pallas kernels: 16.9 us -> 16 us
    ppermute x12, starting transfers between devices: 11.5 us -> 14.9 us  [rotate(): return lax.ppermute(values, 'shot', pairs)]
    ppermute x12, waiting for transfers between devices: 3.81 us -> 1.54 us  [rotate(): return lax.ppermute(values, 'shot', pairs)]
    all_to_all x1, waiting for transfers between devices: 6.42 us -> 5.55 us  [local(): lax.all_to_all(packed, 'shot', split_axis=0, concat_axis=0, tiled=True)]
    pallas_call x2, Pallas kernels: 6.06 us -> 5.21 us  [the longest x1 3.55 us: second(): pl.pallas_call(body, in_specs=[full_smem()] + [full_vmem()] * 2, out_spec...]
  transfers between devices with their start and end apart: 15 -> 15, of which waited for: 4 -> 6; matrix products, arithmetic and copies ran while one was open for 9% -> 9% of each run, Pallas kernels for 19% -> 20%
where the time goes in v11:
time: 56.1 us; the launch traced here: 55.7 us
  starting transfers between devices  23.4 us (42%)
  Pallas kernels  16 us (29%)
  waiting for transfers between devices  9.58 us (17%)
  other arithmetic  4.18 us (7%)
  between operations  1.62 us (3%)
  local copies, waits for them, and re-layouts  0.88 us (2%)
    ppermute x12, starting transfers between devices, rotate(): return lax.ppermute(values, 'shot', pairs)  14.9 us
    all_to_all x1, waiting for transfers between devices, local(): lax.all_to_all(packed, 'shot', split_axis=0, concat_axis=0, tiled=True)  5.55 us
    all_to_all x1, starting transfers between devices, local(): lax.all_to_all(packed, 'shot', split_axis=0, concat_axis=0, tiled=True)  5.47 us
    pallas_call x1, Pallas kernels, landed_energies(): pl.pallas_call(body, in_specs=[full_smem(), pl.BlockSpec(memory_space=plt...  5.06 us
    pallas_call x1, Pallas kernels, second(): pl.pallas_call(body, in_specs=[full_smem()] + [full_vmem()] * 2, out_spec...  3.55 us
    pallas_call x1, Pallas kernels, head(): pl.pallas_call(body, in_specs=[full_smem(), hbm, hbm, hbm], out_specs=[pl...  3.34 us
    ppermute x2, starting transfers between devices, over_receivers(): return [values, lax.ppermute(values, 'rcv', [(0, 1), (1, 0)])]  3.05 us
    ppermute x2, waiting for transfers between devices, over_receivers(): return [values, lax.ppermute(values, 'rcv', [(0, 1), (1, 0)])]  2.49 us
  transfers between devices with their start and end apart: 15, of which 6 were waited for; matrix products, arithmetic and copies ran while one was open for 9% of the time, Pallas kernels for 20%

profile of v11, /device:TPU:16, one launch (start us, length us, event | category | flops | bytes accessed | tf_op | source)
XLA Modules:
  0.0 55.7 jit_solution(11257469905225093816)
XLA Ops:
  0.6 3.3 %pack_coefficients.1 = (bf16[16,384,128]{2,1,0:T(8,128)(2,1)}, bf16[16,128]{1,0:T(8,128)(2,1)}) custom-call(s32[1]{0:T(128)} %bitcast.me_ref, s32[1,256]{1,0:T(1,128)} %bitcast.14, f32[16,128,128]{2,1,0:T(8,128)} %bitcast.10, bf16[128,256]{1,0:T(8,128)(2,1)} %constant.143.both_hbm.both_ref), custom_call_target="tpu_custom_call" | custom-call | tf_op jit(solution)/shard_map/pack_coefficients/pallas_call | solution.py:148
  4.0 1.6 %collective-permute-start.2 = (bf16[16,128]{1,0:T(8,128)(2,1)}, bf16[16,128]{1,0:T(8,128)(2,1)S(1)}, u32[]{:S(2)}, u32[]{:S(2)}) collective-permute-start(bf16[16,128]{1,0:T(8,128)(2,1)} %get-tuple-element.24), channel_id=1, source_target_pairs={{0,4},{1,5},{2,6},{3,7},{4,8},{5,9},{6,10},{7,11},{8,12},{9,13},{1... | collective-permute-start | bytes 12296 | tf_op jit(solution)/shard_map/ppermute | solution.py:428
  5.6 0.4 collective-permute-start.1
  6.1 2.0 %collective-permute-start = (bf16[16,128]{1,0:T(8,128)(2,1)}, bf16[16,128]{1,0:T(8,128)(2,1)S(1)}, u32[]{:S(2)}, u32[]{:S(2)}) collective-permute-start(bf16[16,128]{1,0:T(8,128)(2,1)} %get-tuple-element.24), channel_id=1, source_target_pairs={{0,8},{1,9},{2,10},{3,11},{4,12},{5,13},{6,14},{7,15},{8,0},{9,1},... | collective-permute-start | bytes 12296 | tf_op jit(solution)/shard_map/ppermute | solution.py:428
  8.1 5.5 %all-to-all-start = ((bf16[16,384,128]{2,1,0:T(8,128)(2,1)}), bf16[16,384,128]{2,1,0:T(8,128)(2,1)S(1)}, u32[]{:S(2)}, u32[]{:S(2)}) async-start(bf16[16,384,128]{2,1,0:T(8,128)(2,1)} %get-tuple-element.29), calls=%async_computation | async-start | bytes 3145728 | tf_op jit(solution)/shard_map/all_to_all | solution.py:454
  13.7 0.1 broadcast_add_fusion.1
  13.8 0.1 add.272
  14.0 0.1 dynamic_slice.3
  14.0 0.4 convert_reduce_fusion.1
  14.5 0.1 multiply_reduce_fusion
  14.6 0.7 %convert_reduce_fusion.4 = (s32[]{:T(128)}, s32[16,3]{0,1:T(4,128)S(1)}, s32[16,3]{0,1:T(4,128)S(1)}) fusion(s32[16,16]{1,0:T(8,128)S(1)} %multiply_reduce_fusion, pred[16,16]{1,0:T(8,128)(4,1)S(1)} %broadcast_compare_fusion, s32[16,16]{1,0:T(8,128)S(1)} %iota_add_fusion.1), kind=kLoop, calls=%fused_computation.19 | loop fusion | flops 5279 | bytes 2692 | tf_op jit(solution)/shard_map/reduce_sum | solution.py:506
  15.3 0.1 copy.9
  15.4 0.1 broadcast_in_dim.67
  15.5 0.3 convert_reduce_fusion.2
  15.8 0.1 copy.11
  15.9 0.1 reduce_sum.143
  15.9 0.1 copy.10
  16.0 0.1 reduce_sum.141
  16.1 1.6 %collective-permute-start.3 = (bf16[64,128]{1,0:T(8,128)(2,1)S(1)}, bf16[64,128]{1,0:T(8,128)(2,1)S(1)}, u32[]{:S(2)}, u32[]{:S(2)}) collective-permute-start(bf16[64,128]{1,0:T(8,128)(2,1)S(1)} %pad_maximum_fusion), channel_id=1, source_target_pairs={{0,16},{16,0},{1,17},{17,1},{2,18},{18,2},{3,19},{19,3},{4,20},{20... | collective-permute-start | bytes 49160 | tf_op jit(solution)/shard_map/ppermute | solution.py:418
  17.7 0.2 convert_reduce_fusion
  17.9 0.2 select_reduce_fusion.1
  18.1 0.1 select_reduce_fusion.5
  18.2 0.2 convert_reduce_fusion.7
  18.5 1.3 %select_reduce_fusion = s32[16,4]{1,0:T(8,128)S(1)} fusion(s32[16,16]{1,0:T(8,128)S(1)} %broadcast_add_fusion, s32[16,16]{1,0:T(8,128)S(1)} %iota_add_fusion.1, s32[16,4]{1,0:T(8,128)S(1)} %iota_add_fusion), kind=kLoop, calls=%fused_computation | loop fusion | flops 49088 | bytes 2560 | tf_op jit(solution)/shard_map/reduce_sum | solution.py:496
  19.8 0.1 fusion.1.hit_ref
  19.9 0.1 select_reduce_fusion.4
  20.2 1.5 %collective-permute-start.5 = (bf16[64,128]{1,0:T(8,128)(2,1)S(1)}, bf16[64,128]{1,0:T(8,128)(2,1)S(1)}, u32[]{:S(2)}, u32[]{:S(2)}) collective-permute-start(bf16[64,128]{1,0:T(8,128)(2,1)S(1)} %add_convert_fusion.refs_0_), channel_id=1, source_target_pairs={{0,2},{1,3},{2,0},{3,1},{4,6},{5,7},{6,4},{7,5},{8,10},{9,11},{10,... | collective-permute-start | bytes 49160 | tf_op jit(solution)/shard_map/ppermute | solution.py:428
  21.7 1.4 %collective-permute-start.6 = (bf16[64,128]{1,0:T(8,128)(2,1)S(1)}, bf16[64,128]{1,0:T(8,128)(2,1)S(1)}, u32[]{:S(2)}, u32[]{:S(2)}) collective-permute-start(bf16[64,128]{1,0:T(8,128)(2,1)S(1)} %add_convert_fusion.refs_0_), channel_id=1, source_target_pairs={{0,3},{1,0},{2,1},{3,2},{4,7},{5,4},{6,5},{7,6},{8,11},{9,8},{10,9... | collective-permute-start | bytes 49160 | tf_op jit(solution)/shard_map/ppermute | solution.py:428
  23.1 0.1 pad_add_fusion.1.number_ref
  23.8 0.1 reshape.324
  23.9 0.1 concatenate.19.number_ref
  24.0 0.1 collective-permute-done.5.refs_2_
  24.1 0.4 collective-permute-done.6.refs_3_
  24.5 5.1 %second_energies.1 = (f32[273,8,128]{2,1,0:T(8,128)S(1)}, f32[64,128]{1,0:T(8,128)S(1)}, f32[64,128]{1,0:T(8,128)S(1)}, f32[64,128]{1,0:T(8,128)S(1)}, f32[64,12...) custom-call(s32[288]{0:T(512)S(1)} %pad_add_fusion.1.number_ref, f32[16,128,128]{2,1,0:T(8,128)} %bitcast.11, ...), custom_call_target="tpu_custom_call" | custom-call | flops 1 | bytes 6291456 | tf_op jit(solution)/shard_map/second_energies/pallas_call | solution.py:263
  29.6 1.6 %collective-permute-start.7 = (f32[64,128]{1,0:T(8,128)S(1)}, f32[64,128]{1,0:T(8,128)S(1)}, u32[]{:S(2)}, u32[]{:S(2)}) collective-permute-start(f32[64,128]{1,0:T(8,128)S(1)} %get-tuple-element.37), channel_id=1, source_target_pairs={{0,1},{1,2},{2,3},{3,0},{4,5},{5,6},{6,7},{7,4},{8,9},{9,10},{10,1... | collective-permute-start | bytes 98312 | tf_op jit(solution)/shard_map/ppermute | solution.py:428
  31.2 1.1 %collective-permute-start.8 = (f32[64,128]{1,0:T(8,128)S(1)}, f32[64,128]{1,0:T(8,128)S(1)}, u32[]{:S(2)}, u32[]{:S(2)}) collective-permute-start(f32[64,128]{1,0:T(8,128)S(1)} %get-tuple-element.38), channel_id=1, source_target_pairs={{0,2},{1,3},{2,0},{3,1},{4,6},{5,7},{6,4},{7,5},{8,10},{9,11},{10,... | collective-permute-start | bytes 98312 | tf_op jit(solution)/shard_map/ppermute | solution.py:428
  32.3 0.3 collective-permute-start.9
  32.6 2.4 %residual_of_records.1 = f32[16,128,128]{2,1,0:T(8,128)} custom-call(f32[16,128,128]{2,1,0:T(8,128)} %bitcast.12, bf16[16,128,128]{2,1,0:T(8,128)(2,1)S(1)} %get-tuple-element.40.sum_ref, bf16[128,256]{1,0:T(8,128)(2,1)S(1)} %copy-done), custom_call_target="tpu_custom_call" | custom-call | flops 1 | bytes 4194304 | tf_op jit(solution)/shard_map/residual_of_records/pallas_call | solution.py:309
  35.1 0.6 %collective-permute-done.8 = f32[64,128]{1,0:T(8,128)S(1)} collective-permute-done((f32[64,128]{1,0:T(8,128)S(1)}, f32[64,128]{1,0:T(8,128)S(1)}, u32[]{:S(2)}, u32[]{:S(2)}) %collective-permute-start.8) | collective-permute-done | bytes 32800 | tf_op jit(solution)/shard_map/ppermute | solution.py:428
  35.6 0.5 collective-permute-done.9
  36.1 1.5 %collective-permute-start.10 = (f32[64,128]{1,0:T(8,128)S(1)}, f32[64,128]{1,0:T(8,128)S(1)}, u32[]{:S(2)}, u32[]{:S(2)}) collective-permute-start(f32[64,128]{1,0:T(8,128)S(1)} %add_add_fusion), channel_id=1, source_target_pairs={{0,16},{16,0},{1,17},{17,1},{2,18},{18,2},{3,19},{19,3},{4,20},{20... | collective-permute-start | bytes 98312 | tf_op jit(solution)/shard_map/ppermute | solution.py:418
  37.6 2.5 %collective-permute-done.10 = f32[64,128]{1,0:T(8,128)S(1)} collective-permute-done((f32[64,128]{1,0:T(8,128)S(1)}, f32[64,128]{1,0:T(8,128)S(1)}, u32[]{:S(2)}, u32[]{:S(2)}) %collective-permute-start.10) | collective-permute-done | bytes 32800 | tf_op jit(solution)/shard_map/ppermute | solution.py:418
  40.1 1.0 %collective-permute-start.11 = (f32[16,128]{1,0:T(8,128)S(1)}, f32[16,128]{1,0:T(8,128)S(1)}, u32[]{:S(2)}, u32[]{:S(2)}) collective-permute-start(f32[16,128]{1,0:T(8,128)S(1)} %get-tuple-element.63), channel_id=1, source_target_pairs={{0,4},{1,5},{2,6},{3,7},{4,8},{5,9},{6,10},{7,11},{8,12},{9,13},{1... | collective-permute-start | bytes 24584 | tf_op jit(solution)/shard_map/ppermute | solution.py:428
  41.1 1.0 %collective-permute-start.12 = (f32[16,128]{1,0:T(8,128)S(1)}, f32[16,128]{1,0:T(8,128)S(1)}, u32[]{:S(2)}, u32[]{:S(2)}) collective-permute-start(f32[16,128]{1,0:T(8,128)S(1)} %get-tuple-element.62), channel_id=1, source_target_pairs={{0,8},{1,9},{2,10},{3,11},{4,12},{5,13},{6,14},{7,15},{8,0},{9,1},... | collective-permute-start | bytes 24584 | tf_op jit(solution)/shard_map/ppermute | solution.py:428
  42.1 2.8 %collective-permute-start.13 = (f32[16,128]{1,0:T(8,128)S(1)}, f32[16,128]{1,0:T(8,128)S(1)}, u32[]{:S(2)}, u32[]{:S(2)}) collective-permute-start(f32[16,128]{1,0:T(8,128)S(1)} %get-tuple-element.61), channel_id=1, source_target_pairs={{0,12},{1,13},{2,14},{3,15},{4,0},{5,1},{6,2},{7,3},{8,4},{9,5},{1... | collective-permute-start | bytes 24584 | tf_op jit(solution)/shard_map/ppermute | solution.py:428
  44.9 5.5 %all-to-all-done.in_ref = bf16[16,384,128]{2,1,0:T(8,128)(2,1)S(1)} async-done(((bf16[16,384,128]{2,1,0:T(8,128)(2,1)}), bf16[16,384,128]{2,1,0:T(8,128)(2,1)S(1)}, u32[]{:S(2)}, u32[]{:S(2)}) %all-to-all-start) | async-done | bytes 1572896 | tf_op jit(solution)/shard_map/all_to_all | solution.py:454
  50.5 3.6 %second_coefficients.1.in_ref = f32[64,128,128]{2,1,0:T(8,128)S(1)} custom-call(s32[209]{0:T(256)S(1)} %concatenate.19.number_ref, bf16[16,384,128]{2,1,0:T(8,128)(2,1)S(1)} %all-to-all-done.in_ref, f32[273,8,128]{2,1,0:T(8,128)S(1)} %get-tuple-element.35.cut_ref), custom_call_target="tpu_custom_call" | custom-call | flops 1 | bytes 8388608 | tf_op jit(solution)/shard_map/second_coefficients/pallas_call | solution.py:359
  54.1 1.7 %model_of_shots.1 = bf16[16,4,128,128]{3,2,1,0:T(8,128)(2,1)} custom-call(f32[64,128,128]{2,1,0:T(8,128)S(1)} %second_coefficients.1.in_ref, f32[1,128]{1,0:T(1,128)S(1)} %bitcast.9, bf16[128,256]{1,0:T(8,128)(2,1)S(1)} %copy-done, f32[16,128]{1,0:T(8,128)S(1)} %get-tuple-element.64.refs_0_, f32[16,128]{1,0:T(8,128)S(1)} %collective-permute-done.11.refs_1_, ...), custom_call_target="tpu_custom_call" | custom-call | tf_op jit(solution)/shard_map/model_of_shots/pallas_call | solution.py:402
  (40 shorter events, 0.4 us)
Async XLA Ops:
  4.0 9.9 %collective-permute-start.2 = (bf16[16,128]{1,0:T(8,128)(2,1)}, bf16[16,128]{1,0:T(8,128)(2,1)S(1)}, u32[]{:S(2)}, u32[]{:S(2)}) collective-permute-start(bf16[16,128]{1,0:T(8,128)(2,1)} %get-tuple-element.24), channel_id=1, source_target_pairs={{0,4},{1,5},{2,6},{3,7},{4,8},{5,9},{6,10},{7,11},{8,12},{9,13},{1... | collective-permute-start | bytes 12296 | tf_op jit(solution)/shard_map/ppermute | solution.py:428
  5.6 8.3 %collective-permute-start.1 = (bf16[16,128]{1,0:T(8,128)(2,1)}, bf16[16,128]{1,0:T(8,128)(2,1)S(1)}, u32[]{:S(2)}, u32[]{:S(2)}) collective-permute-start(bf16[16,128]{1,0:T(8,128)(2,1)} %get-tuple-element.24), channel_id=1, source_target_pairs={{0,12},{1,13},{2,14},{3,15},{4,0},{5,1},{6,2},{7,3},{8,4},{9,5},{1... | collective-permute-start | bytes 12296 | tf_op jit(solution)/shard_map/ppermute | solution.py:428
  6.1 7.8 %collective-permute-start = (bf16[16,128]{1,0:T(8,128)(2,1)}, bf16[16,128]{1,0:T(8,128)(2,1)S(1)}, u32[]{:S(2)}, u32[]{:S(2)}) collective-permute-start(bf16[16,128]{1,0:T(8,128)(2,1)} %get-tuple-element.24), channel_id=1, source_target_pairs={{0,8},{1,9},{2,10},{3,11},{4,12},{5,13},{6,14},{7,15},{8,0},{9,1},... | collective-permute-start | bytes 12296 | tf_op jit(solution)/shard_map/ppermute | solution.py:428
  8.0 5.6 %copy-start.4 = (s32[4]{0:T(128)S(1)}, s32[4]{0:T(128)}, u32[]{:S(2)}) copy-start(s32[4]{0:T(128)} %constant.138) | copy-start | bytes 52
  8.0 5.9 %copy-start.3 = (bf16[16,128]{1,0:T(8,128)(2,1)S(1)}, bf16[16,128]{1,0:T(8,128)(2,1)}, u32[]{:S(2)}) copy-start(bf16[16,128]{1,0:T(8,128)(2,1)} %get-tuple-element.24) | copy-start | bytes 12292
  8.0 5.9 %copy-start.2 = (s32[256]{0:T(256)S(1)}, s32[256]{0:T(256)}, u32[]{:S(2)}) copy-start(s32[256]{0:T(256)} %param.6) | copy-start | bytes 3076
  8.0 16.5 %copy-start = (bf16[128,256]{1,0:T(8,128)(2,1)S(1)}, bf16[128,256]{1,0:T(8,128)(2,1)}, u32[]{:S(2)}) copy-start(bf16[128,256]{1,0:T(8,128)(2,1)} %constant.143.both_hbm.both_ref) | copy-start | bytes 196612
  8.1 16.5 %copy-start.1 = (f32[128]{0:T(128)S(1)}, f32[128]{0:T(128)}, u32[]{:S(2)}) copy-start(f32[128]{0:T(128)} %param.7) | copy-start | bytes 1540
  8.1 42.4 %all-to-all-start = ((bf16[16,384,128]{2,1,0:T(8,128)(2,1)}), bf16[16,384,128]{2,1,0:T(8,128)(2,1)S(1)}, u32[]{:S(2)}, u32[]{:S(2)}) async-start(bf16[16,384,128]{2,1,0:T(8,128)(2,1)} %get-tuple-element.29), calls=%async_computation | async-start | bytes 3145728 | tf_op jit(solution)/shard_map/all_to_all | solution.py:454
  16.1 3.9 %collective-permute-start.3 = (bf16[64,128]{1,0:T(8,128)(2,1)S(1)}, bf16[64,128]{1,0:T(8,128)(2,1)S(1)}, u32[]{:S(2)}, u32[]{:S(2)}) collective-permute-start(bf16[64,128]{1,0:T(8,128)(2,1)S(1)} %pad_maximum_fusion), channel_id=1, source_target_pairs={{0,16},{16,0},{1,17},{17,1},{2,18},{18,2},{3,19},{19,3},{4,20},{20... | collective-permute-start | bytes 49160 | tf_op jit(solution)/shard_map/ppermute | solution.py:418
  20.1 3.9 %collective-permute-start.4 = (bf16[64,128]{1,0:T(8,128)(2,1)S(1)}, bf16[64,128]{1,0:T(8,128)(2,1)S(1)}, u32[]{:S(2)}, u32[]{:S(2)}) collective-permute-start(bf16[64,128]{1,0:T(8,128)(2,1)S(1)} %add_convert_fusion.refs_0_), channel_id=1, source_target_pairs={{0,1},{1,2},{2,3},{3,0},{4,5},{5,6},{6,7},{7,4},{8,9},{9,10},{10,1... | collective-permute-start | bytes 49160 | tf_op jit(solution)/shard_map/ppermute | solution.py:428
  20.2 4.0 %collective-permute-start.5 = (bf16[64,128]{1,0:T(8,128)(2,1)S(1)}, bf16[64,128]{1,0:T(8,128)(2,1)S(1)}, u32[]{:S(2)}, u32[]{:S(2)}) collective-permute-start(bf16[64,128]{1,0:T(8,128)(2,1)S(1)} %add_convert_fusion.refs_0_), channel_id=1, source_target_pairs={{0,2},{1,3},{2,0},{3,1},{4,6},{5,7},{6,4},{7,5},{8,10},{9,11},{10,... | collective-permute-start | bytes 49160 | tf_op jit(solution)/shard_map/ppermute | solution.py:428
  21.7 2.8 %collective-permute-start.6 = (bf16[64,128]{1,0:T(8,128)(2,1)S(1)}, bf16[64,128]{1,0:T(8,128)(2,1)S(1)}, u32[]{:S(2)}, u32[]{:S(2)}) collective-permute-start(bf16[64,128]{1,0:T(8,128)(2,1)S(1)} %add_convert_fusion.refs_0_), channel_id=1, source_target_pairs={{0,3},{1,0},{2,1},{3,2},{4,7},{5,4},{6,5},{7,6},{8,11},{9,8},{10,9... | collective-permute-start | bytes 49160 | tf_op jit(solution)/shard_map/ppermute | solution.py:428
  29.6 5.5 %collective-permute-start.7 = (f32[64,128]{1,0:T(8,128)S(1)}, f32[64,128]{1,0:T(8,128)S(1)}, u32[]{:S(2)}, u32[]{:S(2)}) collective-permute-start(f32[64,128]{1,0:T(8,128)S(1)} %get-tuple-element.37), channel_id=1, source_target_pairs={{0,1},{1,2},{2,3},{3,0},{4,5},{5,6},{6,7},{7,4},{8,9},{9,10},{10,1... | collective-permute-start | bytes 98312 | tf_op jit(solution)/shard_map/ppermute | solution.py:428
  31.2 4.4 %collective-permute-start.8 = (f32[64,128]{1,0:T(8,128)S(1)}, f32[64,128]{1,0:T(8,128)S(1)}, u32[]{:S(2)}, u32[]{:S(2)}) collective-permute-start(f32[64,128]{1,0:T(8,128)S(1)} %get-tuple-element.38), channel_id=1, source_target_pairs={{0,2},{1,3},{2,0},{3,1},{4,6},{5,7},{6,4},{7,5},{8,10},{9,11},{10,... | collective-permute-start | bytes 98312 | tf_op jit(solution)/shard_map/ppermute | solution.py:428
  32.3 3.8 %collective-permute-start.9 = (f32[64,128]{1,0:T(8,128)S(1)}, f32[64,128]{1,0:T(8,128)S(1)}, u32[]{:S(2)}, u32[]{:S(2)}) collective-permute-start(f32[64,128]{1,0:T(8,128)S(1)} %get-tuple-element.39), channel_id=1, source_target_pairs={{0,3},{1,0},{2,1},{3,2},{4,7},{5,4},{6,5},{7,6},{8,11},{9,8},{10,9... | collective-permute-start | bytes 98312 | tf_op jit(solution)/shard_map/ppermute | solution.py:428
  36.1 4.0 %collective-permute-start.10 = (f32[64,128]{1,0:T(8,128)S(1)}, f32[64,128]{1,0:T(8,128)S(1)}, u32[]{:S(2)}, u32[]{:S(2)}) collective-permute-start(f32[64,128]{1,0:T(8,128)S(1)} %add_add_fusion), channel_id=1, source_target_pairs={{0,16},{16,0},{1,17},{17,1},{2,18},{18,2},{3,19},{19,3},{4,20},{20... | collective-permute-start | bytes 98312 | tf_op jit(solution)/shard_map/ppermute | solution.py:418
  40.1 14.0 %collective-permute-start.11 = (f32[16,128]{1,0:T(8,128)S(1)}, f32[16,128]{1,0:T(8,128)S(1)}, u32[]{:S(2)}, u32[]{:S(2)}) collective-permute-start(f32[16,128]{1,0:T(8,128)S(1)} %get-tuple-element.63), channel_id=1, source_target_pairs={{0,4},{1,5},{2,6},{3,7},{4,8},{5,9},{6,10},{7,11},{8,12},{9,13},{1... | collective-permute-start | bytes 24584 | tf_op jit(solution)/shard_map/ppermute | solution.py:428
  41.1 12.9 %collective-permute-start.12 = (f32[16,128]{1,0:T(8,128)S(1)}, f32[16,128]{1,0:T(8,128)S(1)}, u32[]{:S(2)}, u32[]{:S(2)}) collective-permute-start(f32[16,128]{1,0:T(8,128)S(1)} %get-tuple-element.62), channel_id=1, source_target_pairs={{0,8},{1,9},{2,10},{3,11},{4,12},{5,13},{6,14},{7,15},{8,0},{9,1},... | collective-permute-start | bytes 24584 | tf_op jit(solution)/shard_map/ppermute | solution.py:428
  42.1 12.0 %collective-permute-start.13 = (f32[16,128]{1,0:T(8,128)S(1)}, f32[16,128]{1,0:T(8,128)S(1)}, u32[]{:S(2)}, u32[]{:S(2)}) collective-permute-start(f32[16,128]{1,0:T(8,128)S(1)} %get-tuple-element.61), channel_id=1, source_target_pairs={{0,12},{1,13},{2,14},{3,15},{4,0},{5,1},{6,2},{7,3},{8,4},{9,5},{1... | collective-permute-start | bytes 24584 | tf_op jit(solution)/shard_map/ppermute | solution.py:428

commit v12 on v11

--- a/solution.py
+++ b/solution.py
@@ -257,7 +257,8 @@
 
         lax.fori_loop(0, windows, energies_of_window, 0)
         for g in range(groups):
-            energy_refs[g][...] = jnp.sum(sum_ref[g * size : (g + 1) * size], axis=1)
+            energies_out = jnp.sum(sum_ref[g * size : (g + 1) * size], axis=1)
+            energy_refs[g][...] = energies_out.astype(jnp.bfloat16)
 
     terms = pltpu.VMEM((windows, tiles, 8, block), jnp.float32)
     return pl.pallas_call(
@@ -266,7 +267,7 @@
         + [full_vmem()] * (3 + len(energies)),
         out_specs=[full_vmem()] * (groups + 2),
         out_shape=[jax.ShapeDtypeStruct((none + 1, 8, block), jnp.float32)]
-        + [jax.ShapeDtypeStruct((size, block), jnp.float32)] * groups
+        + [jax.ShapeDtypeStruct((size, block), jnp.bfloat16)] * groups
         + [jax.ShapeDtypeStruct((windows, rcv, block), jnp.bfloat16)],
         scratch_shapes=[
             pltpu.VMEM((none, block), jnp.float32),
@@ -353,7 +354,7 @@
                 out_ref[entry] = value.reshape(rcv, block)
             return 0
 
-        lax.fori_loop(0, shot_dev, one_shot, 0, unroll=2)
+        lax.fori_loop(0, shot_dev, one_shot, 0, unroll=4)
 
     terms = pltpu.VMEM((count, tiles, 8, block), jnp.float32)
     return pl.pallas_call(
@@ -375,9 +376,9 @@
 
     def body(in_ref, thr_ref, both_ref, *refs):
         out_hbm, out_ref, sem = refs[-3:]
-        energy = refs[0][...]
+        energy = refs[0][...].astype(jnp.float32)
         for ref in refs[1:-3]:
-            energy = energy + ref[...]
+            energy = energy + ref[...].astype(jnp.float32)
         cuts = thr_ref[...] * jnp.sqrt(energy / (SHOT_BLK * receivers) + epsilon)
         copies = []
         for at in range(0, shot_dev, step):
@@ -521,8 +522,8 @@
     residual = remainder(records, sums, both)
     plane = [landed_parts[0]] + [rotate(landed_parts[j], 1, j, near) for j in range(1, near)]
     *plane, residual = lax.optimization_barrier((*plane, residual))
-    plane = sum(plane)
-    plane = sum(over_receivers(plane))
+    plane = sum(part.astype(jnp.float32) for part in plane).astype(jnp.bfloat16)
+    plane = sum(part.astype(jnp.float32) for part in over_receivers(plane)).astype(jnp.bfloat16)
     energies = [plane[:shot_dev]] + [
         rotate(plane[j * shot_dev : (j + 1) * shot_dev], near, j, far) for j in range(1, far)
     ]

time: 56.1 us -> 56.1 us (level)
  waiting for transfers between devices: 9.58 us -> 9 us
    ppermute x12, waiting for transfers between devices: 1.54 us -> 0.54 us  [rotate(): return lax.ppermute(values, 'shot', pairs)]
    all_to_all x1, waiting for transfers between devices: 5.55 us -> 6.18 us  [local(): lax.all_to_all(packed, 'shot', split_axis=0, concat_axis=0, tiled=True)]
  transfers between devices with their start and end apart: 15 -> 15, of which waited for: 6 -> 4; matrix products, arithmetic and copies ran while one was open for 9% -> 9% of each run, Pallas kernels for 20% -> 20%
where the time goes in v12:
time: 56.1 us; the launch traced here: 55.6 us
  starting transfers between devices  23.5 us (42%)
  Pallas kernels  16.4 us (29%)
  waiting for transfers between devices  9 us (16%)
  other arithmetic  4.19 us (7%)
  between operations  1.65 us (3%)
  local copies, waits for them, and re-layouts  0.88 us (2%)
    ppermute x12, starting transfers between devices, rotate(): return lax.ppermute(values, 'shot', pairs)  15 us
    all_to_all x1, waiting for transfers between devices, local(): lax.all_to_all(packed, 'shot', split_axis=0, concat_axis=0, tiled=True)  6.18 us
    all_to_all x1, starting transfers between devices, local(): lax.all_to_all(packed, 'shot', split_axis=0, concat_axis=0, tiled=True)  5.47 us
    pallas_call x1, Pallas kernels, landed_energies(): pl.pallas_call(body, in_specs=[full_smem(), pl.BlockSpec(memory_space=plt...  5.22 us
    pallas_call x1, Pallas kernels, second(): pl.pallas_call(body, in_specs=[full_smem()] + [full_vmem()] * 2, out_spec...  3.73 us
    pallas_call x1, Pallas kernels, head(): pl.pallas_call(body, in_specs=[full_smem(), hbm, hbm, hbm], out_specs=[pl...  3.34 us
    ppermute x2, starting transfers between devices, over_receivers(): return [values, lax.ppermute(values, 'rcv', [(0, 1), (1, 0)])]  3.08 us
    pallas_call x1, Pallas kernels, remainder(): pl.pallas_call(body, in_specs=[pl.BlockSpec(memory_space=pltpu.HBM), full...  2.42 us
  transfers between devices with their start and end apart: 15, of which 4 were waited for; matrix products, arithmetic and copies ran while one was open for 9% of the time, Pallas kernels for 20%

profile of v12, /device:TPU:16, one launch (start us, length us, event | category | flops | bytes accessed | tf_op | source)
XLA Modules:
  0.0 55.6 jit_solution(8245428318760411740)
XLA Ops:
  0.6 3.3 %pack_coefficients.1 = (bf16[16,384,128]{2,1,0:T(8,128)(2,1)}, bf16[16,128]{1,0:T(8,128)(2,1)}) custom-call(s32[1]{0:T(128)} %bitcast.me_ref, s32[1,256]{1,0:T(1,128)} %bitcast.14, f32[16,128,128]{2,1,0:T(8,128)} %bitcast.10, bf16[128,256]{1,0:T(8,128)(2,1)} %constant.143.both_hbm.both_ref), custom_call_target="tpu_custom_call" | custom-call | tf_op jit(solution)/shard_map/pack_coefficients/pallas_call | solution.py:148
  4.0 1.6 %collective-permute-start.2 = (bf16[16,128]{1,0:T(8,128)(2,1)}, bf16[16,128]{1,0:T(8,128)(2,1)S(1)}, u32[]{:S(2)}, u32[]{:S(2)}) collective-permute-start(bf16[16,128]{1,0:T(8,128)(2,1)} %get-tuple-element.24), channel_id=1, source_target_pairs={{0,4},{1,5},{2,6},{3,7},{4,8},{5,9},{6,10},{7,11},{8,12},{9,13},{1... | collective-permute-start | bytes 12296 | tf_op jit(solution)/shard_map/ppermute | solution.py:429
  5.6 0.4 collective-permute-start.1
  6.1 2.0 %collective-permute-start = (bf16[16,128]{1,0:T(8,128)(2,1)}, bf16[16,128]{1,0:T(8,128)(2,1)S(1)}, u32[]{:S(2)}, u32[]{:S(2)}) collective-permute-start(bf16[16,128]{1,0:T(8,128)(2,1)} %get-tuple-element.24), channel_id=1, source_target_pairs={{0,8},{1,9},{2,10},{3,11},{4,12},{5,13},{6,14},{7,15},{8,0},{9,1},... | collective-permute-start | bytes 12296 | tf_op jit(solution)/shard_map/ppermute | solution.py:429
  8.1 5.5 %all-to-all-start = ((bf16[16,384,128]{2,1,0:T(8,128)(2,1)}), bf16[16,384,128]{2,1,0:T(8,128)(2,1)S(1)}, u32[]{:S(2)}, u32[]{:S(2)}) async-start(bf16[16,384,128]{2,1,0:T(8,128)(2,1)} %get-tuple-element.29), calls=%async_computation | async-start | bytes 3145728 | tf_op jit(solution)/shard_map/all_to_all | solution.py:455
  13.7 0.1 broadcast_add_fusion.3
  13.7 0.1 broadcast_add_fusion.1
  13.8 0.1 add.272
  14.0 0.1 dynamic_slice.3
  14.0 0.4 convert_reduce_fusion.1
  14.5 0.1 multiply_reduce_fusion
  14.6 0.7 %convert_reduce_fusion.4 = (s32[]{:T(128)}, s32[16,3]{0,1:T(4,128)S(1)}, s32[16,3]{0,1:T(4,128)S(1)}) fusion(s32[16,16]{1,0:T(8,128)S(1)} %multiply_reduce_fusion, pred[16,16]{1,0:T(8,128)(4,1)S(1)} %broadcast_compare_fusion, s32[16,16]{1,0:T(8,128)S(1)} %iota_add_fusion.1), kind=kLoop, calls=%fused_computation.19 | loop fusion | flops 5279 | bytes 2692 | tf_op jit(solution)/shard_map/reduce_sum | solution.py:507
  15.3 0.1 copy.9
  15.4 0.1 broadcast_in_dim.67
  15.5 0.3 convert_reduce_fusion.2
  15.8 0.1 copy.11
  15.9 0.1 reduce_sum.143
  16.0 0.1 copy.10
  16.0 0.1 reduce_sum.141
  16.1 1.6 %collective-permute-start.3 = (bf16[64,128]{1,0:T(8,128)(2,1)S(1)}, bf16[64,128]{1,0:T(8,128)(2,1)S(1)}, u32[]{:S(2)}, u32[]{:S(2)}) collective-permute-start(bf16[64,128]{1,0:T(8,128)(2,1)S(1)} %pad_maximum_fusion), channel_id=1, source_target_pairs={{0,16},{16,0},{1,17},{17,1},{2,18},{18,2},{3,19},{19,3},{4,20},{20... | collective-permute-start | bytes 49160 | tf_op jit(solution)/shard_map/ppermute | solution.py:419
  17.7 0.2 convert_reduce_fusion
  17.9 0.2 select_reduce_fusion.1
  18.1 0.1 select_reduce_fusion.5
  18.2 0.2 convert_reduce_fusion.7
  18.4 0.1 iota_add_fusion
  18.5 1.3 %select_reduce_fusion = s32[16,4]{1,0:T(8,128)S(1)} fusion(s32[16,16]{1,0:T(8,128)S(1)} %broadcast_add_fusion, s32[16,16]{1,0:T(8,128)S(1)} %iota_add_fusion.1, s32[16,4]{1,0:T(8,128)S(1)} %iota_add_fusion), kind=kLoop, calls=%fused_computation | loop fusion | flops 49088 | bytes 2560 | tf_op jit(solution)/shard_map/reduce_sum | solution.py:497
  19.8 0.1 fusion.1.hit_ref
  20.0 0.1 select_reduce_fusion.4
  20.2 1.5 %collective-permute-start.5 = (bf16[64,128]{1,0:T(8,128)(2,1)S(1)}, bf16[64,128]{1,0:T(8,128)(2,1)S(1)}, u32[]{:S(2)}, u32[]{:S(2)}) collective-permute-start(bf16[64,128]{1,0:T(8,128)(2,1)S(1)} %add_convert_fusion.2.refs_0_), channel_id=1, source_target_pairs={{0,2},{1,3},{2,0},{3,1},{4,6},{5,7},{6,4},{7,5},{8,10},{9,11},{10,... | collective-permute-start | bytes 49160 | tf_op jit(solution)/shard_map/ppermute | solution.py:429
  21.7 1.4 %collective-permute-start.6 = (bf16[64,128]{1,0:T(8,128)(2,1)S(1)}, bf16[64,128]{1,0:T(8,128)(2,1)S(1)}, u32[]{:S(2)}, u32[]{:S(2)}) collective-permute-start(bf16[64,128]{1,0:T(8,128)(2,1)S(1)} %add_convert_fusion.2.refs_0_), channel_id=1, source_target_pairs={{0,3},{1,0},{2,1},{3,2},{4,7},{5,4},{6,5},{7,6},{8,11},{9,8},{10,9... | collective-permute-start | bytes 49160 | tf_op jit(solution)/shard_map/ppermute | solution.py:429
  23.1 0.1 pad_add_fusion.1.number_ref
  23.8 0.1 reshape.324
  23.9 0.1 concatenate.19.number_ref
  24.0 0.1 collective-permute-done.5.refs_2_
  24.1 0.4 collective-permute-done.6.refs_3_
  24.5 5.2 %second_energies.1 = (f32[273,8,128]{2,1,0:T(8,128)S(1)}, bf16[64,128]{1,0:T(8,128)(2,1)S(1)}, bf16[64,128]{1,0:T(8,128)(2,1)S(1)}, bf16[64,128]{1,0:T(8,128)(2,...) custom-call(s32[288]{0:T(512)S(1)} %pad_add_fusion.1.number_ref, f32[16,128,128]{2,1,0:T(8,128)} %bitcast.11, ...), custom_call_target="tpu_custom_call" | custom-call | flops 1 | bytes 6291456 | tf_op jit(solution)/shard_map/second_energies/pallas_call | solution.py:264
  29.8 1.5 %collective-permute-start.7 = (bf16[64,128]{1,0:T(8,128)(2,1)S(1)}, bf16[64,128]{1,0:T(8,128)(2,1)S(1)}, u32[]{:S(2)}, u32[]{:S(2)}) collective-permute-start(bf16[64,128]{1,0:T(8,128)(2,1)S(1)} %get-tuple-element.37), channel_id=1, source_target_pairs={{0,1},{1,2},{2,3},{3,0},{4,5},{5,6},{6,7},{7,4},{8,9},{9,10},{10,1... | collective-permute-start | bytes 49160 | tf_op jit(solution)/shard_map/ppermute | solution.py:429
  31.3 0.9 %collective-permute-start.8 = (bf16[64,128]{1,0:T(8,128)(2,1)S(1)}, bf16[64,128]{1,0:T(8,128)(2,1)S(1)}, u32[]{:S(2)}, u32[]{:S(2)}) collective-permute-start(bf16[64,128]{1,0:T(8,128)(2,1)S(1)} %get-tuple-element.38), channel_id=1, source_target_pairs={{0,2},{1,3},{2,0},{3,1},{4,6},{5,7},{6,4},{7,5},{8,10},{9,11},{10,... | collective-permute-start | bytes 49160 | tf_op jit(solution)/shard_map/ppermute | solution.py:429
  32.2 0.5 collective-permute-start.9
  32.7 2.4 %residual_of_records.1 = f32[16,128,128]{2,1,0:T(8,128)} custom-call(f32[16,128,128]{2,1,0:T(8,128)} %bitcast.12, bf16[16,128,128]{2,1,0:T(8,128)(2,1)S(1)} %get-tuple-element.40.sum_ref, bf16[128,256]{1,0:T(8,128)(2,1)S(1)} %copy-done), custom_call_target="tpu_custom_call" | custom-call | flops 1 | bytes 4194304 | tf_op jit(solution)/shard_map/residual_of_records/pallas_call | solution.py:310
  35.2 1.5 %collective-permute-start.10 = (bf16[64,128]{1,0:T(8,128)(2,1)S(1)}, bf16[64,128]{1,0:T(8,128)(2,1)S(1)}, u32[]{:S(2)}, u32[]{:S(2)}) collective-permute-start(bf16[64,128]{1,0:T(8,128)(2,1)S(1)} %add_convert_fusion.1), channel_id=1, source_target_pairs={{0,16},{16,0},{1,17},{17,1},{2,18},{18,2},{3,19},{19,3},{4,20},{20... | collective-permute-start | bytes 49160 | tf_op jit(solution)/shard_map/ppermute | solution.py:419
  36.7 2.3 %collective-permute-done.10 = bf16[64,128]{1,0:T(8,128)(2,1)S(1)} collective-permute-done((bf16[64,128]{1,0:T(8,128)(2,1)S(1)}, bf16[64,128]{1,0:T(8,128)(2,1)S(1)}, u32[]{:S(2)}, u32[]{:S(2)}) %collective-permute-start.10) | collective-permute-done | bytes 16416 | tf_op jit(solution)/shard_map/ppermute | solution.py:419
  39.0 1.8 %collective-permute-start.11 = (bf16[16,128]{1,0:T(8,128)(2,1)S(1)}, bf16[16,128]{1,0:T(8,128)(2,1)S(1)}, u32[]{:S(2)}, u32[]{:S(2)}) collective-permute-start(bf16[16,128]{1,0:T(8,128)(2,1)S(1)} %get-tuple-element.63), channel_id=1, source_target_pairs={{0,4},{1,5},{2,6},{3,7},{4,8},{5,9},{6,10},{7,11},{8,12},{9,13},{1... | collective-permute-start | bytes 12296 | tf_op jit(solution)/shard_map/ppermute | solution.py:429
  40.8 0.6 %collective-permute-start.12 = (bf16[16,128]{1,0:T(8,128)(2,1)S(1)}, bf16[16,128]{1,0:T(8,128)(2,1)S(1)}, u32[]{:S(2)}, u32[]{:S(2)}) collective-permute-start(bf16[16,128]{1,0:T(8,128)(2,1)S(1)} %get-tuple-element.62), channel_id=1, source_target_pairs={{0,8},{1,9},{2,10},{3,11},{4,12},{5,13},{6,14},{7,15},{8,0},{9,1},... | collective-permute-start | bytes 12296 | tf_op jit(solution)/shard_map/ppermute | solution.py:429
  41.4 2.6 %collective-permute-start.13 = (bf16[16,128]{1,0:T(8,128)(2,1)S(1)}, bf16[16,128]{1,0:T(8,128)(2,1)S(1)}, u32[]{:S(2)}, u32[]{:S(2)}) collective-permute-start(bf16[16,128]{1,0:T(8,128)(2,1)S(1)} %get-tuple-element.61), channel_id=1, source_target_pairs={{0,12},{1,13},{2,14},{3,15},{4,0},{5,1},{6,2},{7,3},{8,4},{9,5},{1... | collective-permute-start | bytes 12296 | tf_op jit(solution)/shard_map/ppermute | solution.py:429
  44.0 6.2 %all-to-all-done.in_ref = bf16[16,384,128]{2,1,0:T(8,128)(2,1)S(1)} async-done(((bf16[16,384,128]{2,1,0:T(8,128)(2,1)}), bf16[16,384,128]{2,1,0:T(8,128)(2,1)S(1)}, u32[]{:S(2)}, u32[]{:S(2)}) %all-to-all-start) | async-done | bytes 1572896 | tf_op jit(solution)/shard_map/all_to_all | solution.py:455
  50.2 3.7 %second_coefficients.1.in_ref = f32[64,128,128]{2,1,0:T(8,128)S(1)} custom-call(s32[209]{0:T(256)S(1)} %concatenate.19.number_ref, bf16[16,384,128]{2,1,0:T(8,128)(2,1)S(1)} %all-to-all-done.in_ref, f32[273,8,128]{2,1,0:T(8,128)S(1)} %get-tuple-element.35.cut_ref), custom_call_target="tpu_custom_call" | custom-call | flops 1 | bytes 8388608 | tf_op jit(solution)/shard_map/second_coefficients/pallas_call | solution.py:360
  54.0 1.7 %model_of_shots.1 = bf16[16,4,128,128]{3,2,1,0:T(8,128)(2,1)} custom-call(f32[64,128,128]{2,1,0:T(8,128)S(1)} %second_coefficients.1.in_ref, f32[1,128]{1,0:T(1,128)S(1)} %bitcast.9, bf16[128,256]{1,0:T(8,128)(2,1)S(1)} %copy-done, bf16[16,128]{1,0:T(8,128)(2,1)S(1)} %get-tuple-element.64.refs_0_, bf16[16,128]{1,0:T(8,128)(2,1)S(1)} %collective-permute-done.11.refs_1_, ...), custom_call_target="tpu_custom_call" | custom-call | tf_op jit(solution)/shard_map/model_of_shots/pallas_call | solution.py:403
  (40 shorter events, 0.3 us)
Async XLA Ops:
  4.0 9.9 %collective-permute-start.2 = (bf16[16,128]{1,0:T(8,128)(2,1)}, bf16[16,128]{1,0:T(8,128)(2,1)S(1)}, u32[]{:S(2)}, u32[]{:S(2)}) collective-permute-start(bf16[16,128]{1,0:T(8,128)(2,1)} %get-tuple-element.24), channel_id=1, source_target_pairs={{0,4},{1,5},{2,6},{3,7},{4,8},{5,9},{6,10},{7,11},{8,12},{9,13},{1... | collective-permute-start | bytes 12296 | tf_op jit(solution)/shard_map/ppermute | solution.py:429
  5.6 8.3 %collective-permute-start.1 = (bf16[16,128]{1,0:T(8,128)(2,1)}, bf16[16,128]{1,0:T(8,128)(2,1)S(1)}, u32[]{:S(2)}, u32[]{:S(2)}) collective-permute-start(bf16[16,128]{1,0:T(8,128)(2,1)} %get-tuple-element.24), channel_id=1, source_target_pairs={{0,12},{1,13},{2,14},{3,15},{4,0},{5,1},{6,2},{7,3},{8,4},{9,5},{1... | collective-permute-start | bytes 12296 | tf_op jit(solution)/shard_map/ppermute | solution.py:429
  6.1 7.8 %collective-permute-start = (bf16[16,128]{1,0:T(8,128)(2,1)}, bf16[16,128]{1,0:T(8,128)(2,1)S(1)}, u32[]{:S(2)}, u32[]{:S(2)}) collective-permute-start(bf16[16,128]{1,0:T(8,128)(2,1)} %get-tuple-element.24), channel_id=1, source_target_pairs={{0,8},{1,9},{2,10},{3,11},{4,12},{5,13},{6,14},{7,15},{8,0},{9,1},... | collective-permute-start | bytes 12296 | tf_op jit(solution)/shard_map/ppermute | solution.py:429
  8.0 5.6 %copy-start.4 = (s32[4]{0:T(128)S(1)}, s32[4]{0:T(128)}, u32[]{:S(2)}) copy-start(s32[4]{0:T(128)} %constant.138) | copy-start | bytes 52
  8.0 5.9 %copy-start.3 = (bf16[16,128]{1,0:T(8,128)(2,1)S(1)}, bf16[16,128]{1,0:T(8,128)(2,1)}, u32[]{:S(2)}) copy-start(bf16[16,128]{1,0:T(8,128)(2,1)} %get-tuple-element.24) | copy-start | bytes 12292
  8.0 5.9 %copy-start.2 = (s32[256]{0:T(256)S(1)}, s32[256]{0:T(256)}, u32[]{:S(2)}) copy-start(s32[256]{0:T(256)} %param.6) | copy-start | bytes 3076
  8.0 16.5 %copy-start = (bf16[128,256]{1,0:T(8,128)(2,1)S(1)}, bf16[128,256]{1,0:T(8,128)(2,1)}, u32[]{:S(2)}) copy-start(bf16[128,256]{1,0:T(8,128)(2,1)} %constant.143.both_hbm.both_ref) | copy-start | bytes 196612
  8.1 16.5 %copy-start.1 = (f32[128]{0:T(128)S(1)}, f32[128]{0:T(128)}, u32[]{:S(2)}) copy-start(f32[128]{0:T(128)} %param.7) | copy-start | bytes 1540
  8.1 42.1 %all-to-all-start = ((bf16[16,384,128]{2,1,0:T(8,128)(2,1)}), bf16[16,384,128]{2,1,0:T(8,128)(2,1)S(1)}, u32[]{:S(2)}, u32[]{:S(2)}) async-start(bf16[16,384,128]{2,1,0:T(8,128)(2,1)} %get-tuple-element.29), calls=%async_computation | async-start | bytes 3145728 | tf_op jit(solution)/shard_map/all_to_all | solution.py:455
  16.1 3.9 %collective-permute-start.3 = (bf16[64,128]{1,0:T(8,128)(2,1)S(1)}, bf16[64,128]{1,0:T(8,128)(2,1)S(1)}, u32[]{:S(2)}, u32[]{:S(2)}) collective-permute-start(bf16[64,128]{1,0:T(8,128)(2,1)S(1)} %pad_maximum_fusion), channel_id=1, source_target_pairs={{0,16},{16,0},{1,17},{17,1},{2,18},{18,2},{3,19},{19,3},{4,20},{20... | collective-permute-start | bytes 49160 | tf_op jit(solution)/shard_map/ppermute | solution.py:419
  20.1 3.9 %collective-permute-start.4 = (bf16[64,128]{1,0:T(8,128)(2,1)S(1)}, bf16[64,128]{1,0:T(8,128)(2,1)S(1)}, u32[]{:S(2)}, u32[]{:S(2)}) collective-permute-start(bf16[64,128]{1,0:T(8,128)(2,1)S(1)} %add_convert_fusion.2.refs_0_), channel_id=1, source_target_pairs={{0,1},{1,2},{2,3},{3,0},{4,5},{5,6},{6,7},{7,4},{8,9},{9,10},{10,1... | collective-permute-start | bytes 49160 | tf_op jit(solution)/shard_map/ppermute | solution.py:429
  20.2 4.0 %collective-permute-start.5 = (bf16[64,128]{1,0:T(8,128)(2,1)S(1)}, bf16[64,128]{1,0:T(8,128)(2,1)S(1)}, u32[]{:S(2)}, u32[]{:S(2)}) collective-permute-start(bf16[64,128]{1,0:T(8,128)(2,1)S(1)} %add_convert_fusion.2.refs_0_), channel_id=1, source_target_pairs={{0,2},{1,3},{2,0},{3,1},{4,6},{5,7},{6,4},{7,5},{8,10},{9,11},{10,... | collective-permute-start | bytes 49160 | tf_op jit(solution)/shard_map/ppermute | solution.py:429
  21.7 2.8 %collective-permute-start.6 = (bf16[64,128]{1,0:T(8,128)(2,1)S(1)}, bf16[64,128]{1,0:T(8,128)(2,1)S(1)}, u32[]{:S(2)}, u32[]{:S(2)}) collective-permute-start(bf16[64,128]{1,0:T(8,128)(2,1)S(1)} %add_convert_fusion.2.refs_0_), channel_id=1, source_target_pairs={{0,3},{1,0},{2,1},{3,2},{4,7},{5,4},{6,5},{7,6},{8,11},{9,8},{10,9... | collective-permute-start | bytes 49160 | tf_op jit(solution)/shard_map/ppermute | solution.py:429
  29.8 5.4 %collective-permute-start.7 = (bf16[64,128]{1,0:T(8,128)(2,1)S(1)}, bf16[64,128]{1,0:T(8,128)(2,1)S(1)}, u32[]{:S(2)}, u32[]{:S(2)}) collective-permute-start(bf16[64,128]{1,0:T(8,128)(2,1)S(1)} %get-tuple-element.37), channel_id=1, source_target_pairs={{0,1},{1,2},{2,3},{3,0},{4,5},{5,6},{6,7},{7,4},{8,9},{9,10},{10,1... | collective-permute-start | bytes 49160 | tf_op jit(solution)/shard_map/ppermute | solution.py:429
  31.3 3.9 %collective-permute-start.8 = (bf16[64,128]{1,0:T(8,128)(2,1)S(1)}, bf16[64,128]{1,0:T(8,128)(2,1)S(1)}, u32[]{:S(2)}, u32[]{:S(2)}) collective-permute-start(bf16[64,128]{1,0:T(8,128)(2,1)S(1)} %get-tuple-element.38), channel_id=1, source_target_pairs={{0,2},{1,3},{2,0},{3,1},{4,6},{5,7},{6,4},{7,5},{8,10},{9,11},{10,... | collective-permute-start | bytes 49160 | tf_op jit(solution)/shard_map/ppermute | solution.py:429
  32.2 3.0 %collective-permute-start.9 = (bf16[64,128]{1,0:T(8,128)(2,1)S(1)}, bf16[64,128]{1,0:T(8,128)(2,1)S(1)}, u32[]{:S(2)}, u32[]{:S(2)}) collective-permute-start(bf16[64,128]{1,0:T(8,128)(2,1)S(1)} %get-tuple-element.39), channel_id=1, source_target_pairs={{0,3},{1,0},{2,1},{3,2},{4,7},{5,4},{6,5},{7,6},{8,11},{9,8},{10,9... | collective-permute-start | bytes 49160 | tf_op jit(solution)/shard_map/ppermute | solution.py:429
  35.2 3.8 %collective-permute-start.10 = (bf16[64,128]{1,0:T(8,128)(2,1)S(1)}, bf16[64,128]{1,0:T(8,128)(2,1)S(1)}, u32[]{:S(2)}, u32[]{:S(2)}) collective-permute-start(bf16[64,128]{1,0:T(8,128)(2,1)S(1)} %add_convert_fusion.1), channel_id=1, source_target_pairs={{0,16},{16,0},{1,17},{17,1},{2,18},{18,2},{3,19},{19,3},{4,20},{20... | collective-permute-start | bytes 49160 | tf_op jit(solution)/shard_map/ppermute | solution.py:419
  39.0 14.9 %collective-permute-start.11 = (bf16[16,128]{1,0:T(8,128)(2,1)S(1)}, bf16[16,128]{1,0:T(8,128)(2,1)S(1)}, u32[]{:S(2)}, u32[]{:S(2)}) collective-permute-start(bf16[16,128]{1,0:T(8,128)(2,1)S(1)} %get-tuple-element.63), channel_id=1, source_target_pairs={{0,4},{1,5},{2,6},{3,7},{4,8},{5,9},{6,10},{7,11},{8,12},{9,13},{1... | collective-permute-start | bytes 12296 | tf_op jit(solution)/shard_map/ppermute | solution.py:429
  40.8 13.1 %collective-permute-start.12 = (bf16[16,128]{1,0:T(8,128)(2,1)S(1)}, bf16[16,128]{1,0:T(8,128)(2,1)S(1)}, u32[]{:S(2)}, u32[]{:S(2)}) collective-permute-start(bf16[16,128]{1,0:T(8,128)(2,1)S(1)} %get-tuple-element.62), channel_id=1, source_target_pairs={{0,8},{1,9},{2,10},{3,11},{4,12},{5,13},{6,14},{7,15},{8,0},{9,1},... | collective-permute-start | bytes 12296 | tf_op jit(solution)/shard_map/ppermute | solution.py:429
  41.4 12.5 %collective-permute-start.13 = (bf16[16,128]{1,0:T(8,128)(2,1)S(1)}, bf16[16,128]{1,0:T(8,128)(2,1)S(1)}, u32[]{:S(2)}, u32[]{:S(2)}) collective-permute-start(bf16[16,128]{1,0:T(8,128)(2,1)S(1)} %get-tuple-element.61), channel_id=1, source_target_pairs={{0,12},{1,13},{2,14},{3,15},{4,0},{5,1},{6,2},{7,3},{8,4},{9,5},{1... | collective-permute-start | bytes 12296 | tf_op jit(solution)/shard_map/ppermute | solution.py:429

commit v13 on v12

--- a/solution.py
+++ b/solution.py
@@ -119,7 +119,10 @@
             get_rec[c].wait()
             for w in range(c * chunk, (c + 1) * chunk):
                 spread = (rec_ref[w] * scale[w : w + 1, 0:1]).astype(bf16)
-                coef = forward(both_ref[...], spread)
+                coef = lax.dot_general(
+                    spread, both_ref[:, :block], (((0,), (0,)), ((), ())),
+                    preferred_element_type=f32,
+                )
                 sent_ref[w] = coef.astype(bf16)
                 rows.append(jnp.sum(coef * coef, axis=0, keepdims=True))
 

time: 56.1 us -> 55.8 us (level)
  Pallas kernels: 16.4 us -> 15.7 us
  transfers between devices with their start and end apart: 15 -> 15, of which waited for: 4 -> 5; matrix products, arithmetic and copies ran while one was open for 9% -> 9% of each run, Pallas kernels for 20% -> 20%
where the time goes in v13:
time: 55.8 us; the launch traced here: 55.1 us
  starting transfers between devices  23.2 us (42%)
  Pallas kernels  15.7 us (28%)
  waiting for transfers between devices  9.43 us (17%)
  other arithmetic  4.19 us (8%)
  between operations  1.64 us (3%)
  local copies, waits for them, and re-layouts  0.88 us (2%)
    ppermute x12, starting transfers between devices, rotate(): return lax.ppermute(values, 'shot', pairs)  14.9 us
    all_to_all x1, waiting for transfers between devices, local(): lax.all_to_all(packed, 'shot', split_axis=0, concat_axis=0, tiled=True)  6.12 us
    all_to_all x1, starting transfers between devices, local(): lax.all_to_all(packed, 'shot', split_axis=0, concat_axis=0, tiled=True)  5.47 us
    pallas_call x1, Pallas kernels, landed_energies(): pl.pallas_call(body, in_specs=[full_smem(), pl.BlockSpec(memory_space=plt...  5.18 us
    pallas_call x1, Pallas kernels, second(): pl.pallas_call(body, in_specs=[full_smem()] + [full_vmem()] * 2, out_spec...  3.26 us
    pallas_call x1, Pallas kernels, head(): pl.pallas_call(body, in_specs=[full_smem(), hbm, hbm, hbm], out_specs=[pl...  3.22 us
    ppermute x2, starting transfers between devices, over_receivers(): return [values, lax.ppermute(values, 'rcv', [(0, 1), (1, 0)])]  2.84 us
    ppermute x2, waiting for transfers between devices, over_receivers(): return [values, lax.ppermute(values, 'rcv', [(0, 1), (1, 0)])]  2.53 us
  transfers between devices with their start and end apart: 15, of which 5 were waited for; matrix products, arithmetic and copies ran while one was open for 9% of the time, Pallas kernels for 20%

profile of v13, /device:TPU:16, one launch (start us, length us, event | category | flops | bytes accessed | tf_op | source)
XLA Modules:
  0.0 55.1 jit_solution(1725721079845663253)
XLA Ops:
  0.6 3.2 %pack_coefficients.1 = (bf16[16,384,128]{2,1,0:T(8,128)(2,1)}, bf16[16,128]{1,0:T(8,128)(2,1)}) custom-call(s32[1]{0:T(128)} %bitcast.me_ref, s32[1,256]{1,0:T(1,128)} %bitcast.14, f32[16,128,128]{2,1,0:T(8,128)} %bitcast.10, bf16[128,256]{1,0:T(8,128)(2,1)} %constant.143.both_hbm.both_ref), custom_call_target="tpu_custom_call" | custom-call | tf_op jit(solution)/shard_map/pack_coefficients/pallas_call | solution.py:151
  3.9 1.6 %collective-permute-start.2 = (bf16[16,128]{1,0:T(8,128)(2,1)}, bf16[16,128]{1,0:T(8,128)(2,1)S(1)}, u32[]{:S(2)}, u32[]{:S(2)}) collective-permute-start(bf16[16,128]{1,0:T(8,128)(2,1)} %get-tuple-element.24), channel_id=1, source_target_pairs={{0,4},{1,5},{2,6},{3,7},{4,8},{5,9},{6,10},{7,11},{8,12},{9,13},{1... | collective-permute-start | bytes 12296 | tf_op jit(solution)/shard_map/ppermute | solution.py:432
  5.5 0.4 collective-permute-start.1
  5.9 2.0 %collective-permute-start = (bf16[16,128]{1,0:T(8,128)(2,1)}, bf16[16,128]{1,0:T(8,128)(2,1)S(1)}, u32[]{:S(2)}, u32[]{:S(2)}) collective-permute-start(bf16[16,128]{1,0:T(8,128)(2,1)} %get-tuple-element.24), channel_id=1, source_target_pairs={{0,8},{1,9},{2,10},{3,11},{4,12},{5,13},{6,14},{7,15},{8,0},{9,1},... | collective-permute-start | bytes 12296 | tf_op jit(solution)/shard_map/ppermute | solution.py:432
  7.9 5.5 %all-to-all-start = ((bf16[16,384,128]{2,1,0:T(8,128)(2,1)}), bf16[16,384,128]{2,1,0:T(8,128)(2,1)S(1)}, u32[]{:S(2)}, u32[]{:S(2)}) async-start(bf16[16,384,128]{2,1,0:T(8,128)(2,1)} %get-tuple-element.29), calls=%async_computation | async-start | bytes 3145728 | tf_op jit(solution)/shard_map/all_to_all | solution.py:458
  13.5 0.1 broadcast_add_fusion.3
  13.6 0.1 broadcast_add_fusion.1
  13.7 0.1 add.272
  13.8 0.1 dynamic_slice.3
  13.9 0.4 convert_reduce_fusion.1
  14.4 0.1 multiply_reduce_fusion
  14.5 0.7 %convert_reduce_fusion.4 = (s32[]{:T(128)}, s32[16,3]{0,1:T(4,128)S(1)}, s32[16,3]{0,1:T(4,128)S(1)}) fusion(s32[16,16]{1,0:T(8,128)S(1)} %multiply_reduce_fusion, pred[16,16]{1,0:T(8,128)(4,1)S(1)} %broadcast_compare_fusion, s32[16,16]{1,0:T(8,128)S(1)} %iota_add_fusion.1), kind=kLoop, calls=%fused_computation.19 | loop fusion | flops 5279 | bytes 2692 | tf_op jit(solution)/shard_map/reduce_sum | solution.py:510
  15.2 0.1 copy.9
  15.3 0.1 broadcast_in_dim.67
  15.4 0.3 convert_reduce_fusion.2
  15.7 0.1 copy.11
  15.7 0.1 reduce_sum.143
  15.8 0.1 copy.10
  15.9 0.1 reduce_sum.141
  16.0 1.6 %collective-permute-start.3 = (bf16[64,128]{1,0:T(8,128)(2,1)S(1)}, bf16[64,128]{1,0:T(8,128)(2,1)S(1)}, u32[]{:S(2)}, u32[]{:S(2)}) collective-permute-start(bf16[64,128]{1,0:T(8,128)(2,1)S(1)} %pad_maximum_fusion), channel_id=1, source_target_pairs={{0,16},{16,0},{1,17},{17,1},{2,18},{18,2},{3,19},{19,3},{4,20},{20... | collective-permute-start | bytes 49160 | tf_op jit(solution)/shard_map/ppermute | solution.py:422
  17.6 0.2 convert_reduce_fusion
  17.8 0.2 select_reduce_fusion.1
  17.9 0.1 select_reduce_fusion.5
  18.0 0.2 convert_reduce_fusion.7
  18.4 1.3 %select_reduce_fusion = s32[16,4]{1,0:T(8,128)S(1)} fusion(s32[16,16]{1,0:T(8,128)S(1)} %broadcast_add_fusion, s32[16,16]{1,0:T(8,128)S(1)} %iota_add_fusion.1, s32[16,4]{1,0:T(8,128)S(1)} %iota_add_fusion), kind=kLoop, calls=%fused_computation | loop fusion | flops 49088 | bytes 2560 | tf_op jit(solution)/shard_map/reduce_sum | solution.py:500
  19.7 0.1 fusion.1.hit_ref
  19.8 0.1 select_reduce_fusion.4
  20.0 1.5 %collective-permute-start.5 = (bf16[64,128]{1,0:T(8,128)(2,1)S(1)}, bf16[64,128]{1,0:T(8,128)(2,1)S(1)}, u32[]{:S(2)}, u32[]{:S(2)}) collective-permute-start(bf16[64,128]{1,0:T(8,128)(2,1)S(1)} %add_convert_fusion.2.refs_0_), channel_id=1, source_target_pairs={{0,2},{1,3},{2,0},{3,1},{4,6},{5,7},{6,4},{7,5},{8,10},{9,11},{10,... | collective-permute-start | bytes 49160 | tf_op jit(solution)/shard_map/ppermute | solution.py:432
  21.6 1.4 %collective-permute-start.6 = (bf16[64,128]{1,0:T(8,128)(2,1)S(1)}, bf16[64,128]{1,0:T(8,128)(2,1)S(1)}, u32[]{:S(2)}, u32[]{:S(2)}) collective-permute-start(bf16[64,128]{1,0:T(8,128)(2,1)S(1)} %add_convert_fusion.2.refs_0_), channel_id=1, source_target_pairs={{0,3},{1,0},{2,1},{3,2},{4,7},{5,4},{6,5},{7,6},{8,11},{9,8},{10,9... | collective-permute-start | bytes 49160 | tf_op jit(solution)/shard_map/ppermute | solution.py:432
  23.0 0.1 pad_add_fusion.1.number_ref
  23.7 0.1 reshape.324
  23.8 0.1 concatenate.19.number_ref
  23.9 0.1 collective-permute-done.5.refs_2_
  24.0 0.4 collective-permute-done.6.refs_3_
  24.4 5.2 %second_energies.1 = (f32[273,8,128]{2,1,0:T(8,128)S(1)}, bf16[64,128]{1,0:T(8,128)(2,1)S(1)}, bf16[64,128]{1,0:T(8,128)(2,1)S(1)}, bf16[64,128]{1,0:T(8,128)(2,...) custom-call(s32[288]{0:T(512)S(1)} %pad_add_fusion.1.number_ref, f32[16,128,128]{2,1,0:T(8,128)} %bitcast.11, ...), custom_call_target="tpu_custom_call" | custom-call | flops 1 | bytes 6291456 | tf_op jit(solution)/shard_map/second_energies/pallas_call | solution.py:267
  29.6 1.8 %collective-permute-start.7 = (bf16[64,128]{1,0:T(8,128)(2,1)S(1)}, bf16[64,128]{1,0:T(8,128)(2,1)S(1)}, u32[]{:S(2)}, u32[]{:S(2)}) collective-permute-start(bf16[64,128]{1,0:T(8,128)(2,1)S(1)} %get-tuple-element.37), channel_id=1, source_target_pairs={{0,1},{1,2},{2,3},{3,0},{4,5},{5,6},{6,7},{7,4},{8,9},{9,10},{10,1... | collective-permute-start | bytes 49160 | tf_op jit(solution)/shard_map/ppermute | solution.py:432
  31.4 0.8 %collective-permute-start.8 = (bf16[64,128]{1,0:T(8,128)(2,1)S(1)}, bf16[64,128]{1,0:T(8,128)(2,1)S(1)}, u32[]{:S(2)}, u32[]{:S(2)}) collective-permute-start(bf16[64,128]{1,0:T(8,128)(2,1)S(1)} %get-tuple-element.38), channel_id=1, source_target_pairs={{0,2},{1,3},{2,0},{3,1},{4,6},{5,7},{6,4},{7,5},{8,10},{9,11},{10,... | collective-permute-start | bytes 49160 | tf_op jit(solution)/shard_map/ppermute | solution.py:432
  32.2 0.6 %collective-permute-start.9 = (bf16[64,128]{1,0:T(8,128)(2,1)S(1)}, bf16[64,128]{1,0:T(8,128)(2,1)S(1)}, u32[]{:S(2)}, u32[]{:S(2)}) collective-permute-start(bf16[64,128]{1,0:T(8,128)(2,1)S(1)} %get-tuple-element.39), channel_id=1, source_target_pairs={{0,3},{1,0},{2,1},{3,2},{4,7},{5,4},{6,5},{7,6},{8,11},{9,8},{10,9... | collective-permute-start | bytes 49160 | tf_op jit(solution)/shard_map/ppermute | solution.py:432
  32.8 2.4 %residual_of_records.1 = f32[16,128,128]{2,1,0:T(8,128)} custom-call(f32[16,128,128]{2,1,0:T(8,128)} %bitcast.12, bf16[16,128,128]{2,1,0:T(8,128)(2,1)S(1)} %get-tuple-element.40.sum_ref, bf16[128,256]{1,0:T(8,128)(2,1)S(1)} %copy-done), custom_call_target="tpu_custom_call" | custom-call | flops 1 | bytes 4194304 | tf_op jit(solution)/shard_map/residual_of_records/pallas_call | solution.py:313
  35.3 0.2 collective-permute-done.9
  35.5 1.3 %collective-permute-start.10 = (bf16[64,128]{1,0:T(8,128)(2,1)S(1)}, bf16[64,128]{1,0:T(8,128)(2,1)S(1)}, u32[]{:S(2)}, u32[]{:S(2)}) collective-permute-start(bf16[64,128]{1,0:T(8,128)(2,1)S(1)} %add_convert_fusion.1), channel_id=1, source_target_pairs={{0,16},{16,0},{1,17},{17,1},{2,18},{18,2},{3,19},{19,3},{4,20},{20... | collective-permute-start | bytes 49160 | tf_op jit(solution)/shard_map/ppermute | solution.py:422
  36.8 2.5 %collective-permute-done.10 = bf16[64,128]{1,0:T(8,128)(2,1)S(1)} collective-permute-done((bf16[64,128]{1,0:T(8,128)(2,1)S(1)}, bf16[64,128]{1,0:T(8,128)(2,1)S(1)}, u32[]{:S(2)}, u32[]{:S(2)}) %collective-permute-start.10) | collective-permute-done | bytes 16416 | tf_op jit(solution)/shard_map/ppermute | solution.py:422
  39.4 1.4 %collective-permute-start.11 = (bf16[16,128]{1,0:T(8,128)(2,1)S(1)}, bf16[16,128]{1,0:T(8,128)(2,1)S(1)}, u32[]{:S(2)}, u32[]{:S(2)}) collective-permute-start(bf16[16,128]{1,0:T(8,128)(2,1)S(1)} %get-tuple-element.63), channel_id=1, source_target_pairs={{0,4},{1,5},{2,6},{3,7},{4,8},{5,9},{6,10},{7,11},{8,12},{9,13},{1... | collective-permute-start | bytes 12296 | tf_op jit(solution)/shard_map/ppermute | solution.py:432
  40.8 0.5 collective-permute-start.12
  41.3 2.7 %collective-permute-start.13 = (bf16[16,128]{1,0:T(8,128)(2,1)S(1)}, bf16[16,128]{1,0:T(8,128)(2,1)S(1)}, u32[]{:S(2)}, u32[]{:S(2)}) collective-permute-start(bf16[16,128]{1,0:T(8,128)(2,1)S(1)} %get-tuple-element.61), channel_id=1, source_target_pairs={{0,12},{1,13},{2,14},{3,15},{4,0},{5,1},{6,2},{7,3},{8,4},{9,5},{1... | collective-permute-start | bytes 12296 | tf_op jit(solution)/shard_map/ppermute | solution.py:432
  44.0 6.1 %all-to-all-done.in_ref = bf16[16,384,128]{2,1,0:T(8,128)(2,1)S(1)} async-done(((bf16[16,384,128]{2,1,0:T(8,128)(2,1)}), bf16[16,384,128]{2,1,0:T(8,128)(2,1)S(1)}, u32[]{:S(2)}, u32[]{:S(2)}) %all-to-all-start) | async-done | bytes 1572896 | tf_op jit(solution)/shard_map/all_to_all | solution.py:458
  50.1 3.3 %second_coefficients.1.in_ref = f32[64,128,128]{2,1,0:T(8,128)S(1)} custom-call(s32[209]{0:T(256)S(1)} %concatenate.19.number_ref, bf16[16,384,128]{2,1,0:T(8,128)(2,1)S(1)} %all-to-all-done.in_ref, f32[273,8,128]{2,1,0:T(8,128)S(1)} %get-tuple-element.35.cut_ref), custom_call_target="tpu_custom_call" | custom-call | flops 1 | bytes 8388608 | tf_op jit(solution)/shard_map/second_coefficients/pallas_call | solution.py:363
  53.4 1.7 %model_of_shots.1 = bf16[16,4,128,128]{3,2,1,0:T(8,128)(2,1)} custom-call(f32[64,128,128]{2,1,0:T(8,128)S(1)} %second_coefficients.1.in_ref, f32[1,128]{1,0:T(1,128)S(1)} %bitcast.9, bf16[128,256]{1,0:T(8,128)(2,1)S(1)} %copy-done, bf16[16,128]{1,0:T(8,128)(2,1)S(1)} %get-tuple-element.64.refs_0_, bf16[16,128]{1,0:T(8,128)(2,1)S(1)} %collective-permute-done.11.refs_1_, ...), custom_call_target="tpu_custom_call" | custom-call | tf_op jit(solution)/shard_map/model_of_shots/pallas_call | solution.py:406
  (40 shorter events, 0.4 us)
Async XLA Ops:
  3.9 9.9 %collective-permute-start.2 = (bf16[16,128]{1,0:T(8,128)(2,1)}, bf16[16,128]{1,0:T(8,128)(2,1)S(1)}, u32[]{:S(2)}, u32[]{:S(2)}) collective-permute-start(bf16[16,128]{1,0:T(8,128)(2,1)} %get-tuple-element.24), channel_id=1, source_target_pairs={{0,4},{1,5},{2,6},{3,7},{4,8},{5,9},{6,10},{7,11},{8,12},{9,13},{1... | collective-permute-start | bytes 12296 | tf_op jit(solution)/shard_map/ppermute | solution.py:432
  5.5 8.3 %collective-permute-start.1 = (bf16[16,128]{1,0:T(8,128)(2,1)}, bf16[16,128]{1,0:T(8,128)(2,1)S(1)}, u32[]{:S(2)}, u32[]{:S(2)}) collective-permute-start(bf16[16,128]{1,0:T(8,128)(2,1)} %get-tuple-element.24), channel_id=1, source_target_pairs={{0,12},{1,13},{2,14},{3,15},{4,0},{5,1},{6,2},{7,3},{8,4},{9,5},{1... | collective-permute-start | bytes 12296 | tf_op jit(solution)/shard_map/ppermute | solution.py:432
  5.9 7.8 %collective-permute-start = (bf16[16,128]{1,0:T(8,128)(2,1)}, bf16[16,128]{1,0:T(8,128)(2,1)S(1)}, u32[]{:S(2)}, u32[]{:S(2)}) collective-permute-start(bf16[16,128]{1,0:T(8,128)(2,1)} %get-tuple-element.24), channel_id=1, source_target_pairs={{0,8},{1,9},{2,10},{3,11},{4,12},{5,13},{6,14},{7,15},{8,0},{9,1},... | collective-permute-start | bytes 12296 | tf_op jit(solution)/shard_map/ppermute | solution.py:432
  7.9 5.6 %copy-start.4 = (s32[4]{0:T(128)S(1)}, s32[4]{0:T(128)}, u32[]{:S(2)}) copy-start(s32[4]{0:T(128)} %constant.138) | copy-start | bytes 52
  7.9 5.9 %copy-start.3 = (bf16[16,128]{1,0:T(8,128)(2,1)S(1)}, bf16[16,128]{1,0:T(8,128)(2,1)}, u32[]{:S(2)}) copy-start(bf16[16,128]{1,0:T(8,128)(2,1)} %get-tuple-element.24) | copy-start | bytes 12292
  7.9 5.9 %copy-start.2 = (s32[256]{0:T(256)S(1)}, s32[256]{0:T(256)}, u32[]{:S(2)}) copy-start(s32[256]{0:T(256)} %param.6) | copy-start | bytes 3076
  7.9 16.5 %copy-start = (bf16[128,256]{1,0:T(8,128)(2,1)S(1)}, bf16[128,256]{1,0:T(8,128)(2,1)}, u32[]{:S(2)}) copy-start(bf16[128,256]{1,0:T(8,128)(2,1)} %constant.143.both_hbm.both_ref) | copy-start | bytes 196612
  7.9 16.5 %copy-start.1 = (f32[128]{0:T(128)S(1)}, f32[128]{0:T(128)}, u32[]{:S(2)}) copy-start(f32[128]{0:T(128)} %param.7) | copy-start | bytes 1540
  7.9 42.1 %all-to-all-start = ((bf16[16,384,128]{2,1,0:T(8,128)(2,1)}), bf16[16,384,128]{2,1,0:T(8,128)(2,1)S(1)}, u32[]{:S(2)}, u32[]{:S(2)}) async-start(bf16[16,384,128]{2,1,0:T(8,128)(2,1)} %get-tuple-element.29), calls=%async_computation | async-start | bytes 3145728 | tf_op jit(solution)/shard_map/all_to_all | solution.py:458
  16.0 3.9 %collective-permute-start.3 = (bf16[64,128]{1,0:T(8,128)(2,1)S(1)}, bf16[64,128]{1,0:T(8,128)(2,1)S(1)}, u32[]{:S(2)}, u32[]{:S(2)}) collective-permute-start(bf16[64,128]{1,0:T(8,128)(2,1)S(1)} %pad_maximum_fusion), channel_id=1, source_target_pairs={{0,16},{16,0},{1,17},{17,1},{2,18},{18,2},{3,19},{19,3},{4,20},{20... | collective-permute-start | bytes 49160 | tf_op jit(solution)/shard_map/ppermute | solution.py:422
  20.0 3.9 %collective-permute-start.4 = (bf16[64,128]{1,0:T(8,128)(2,1)S(1)}, bf16[64,128]{1,0:T(8,128)(2,1)S(1)}, u32[]{:S(2)}, u32[]{:S(2)}) collective-permute-start(bf16[64,128]{1,0:T(8,128)(2,1)S(1)} %add_convert_fusion.2.refs_0_), channel_id=1, source_target_pairs={{0,1},{1,2},{2,3},{3,0},{4,5},{5,6},{6,7},{7,4},{8,9},{9,10},{10,1... | collective-permute-start | bytes 49160 | tf_op jit(solution)/shard_map/ppermute | solution.py:432
  20.0 4.0 %collective-permute-start.5 = (bf16[64,128]{1,0:T(8,128)(2,1)S(1)}, bf16[64,128]{1,0:T(8,128)(2,1)S(1)}, u32[]{:S(2)}, u32[]{:S(2)}) collective-permute-start(bf16[64,128]{1,0:T(8,128)(2,1)S(1)} %add_convert_fusion.2.refs_0_), channel_id=1, source_target_pairs={{0,2},{1,3},{2,0},{3,1},{4,6},{5,7},{6,4},{7,5},{8,10},{9,11},{10,... | collective-permute-start | bytes 49160 | tf_op jit(solution)/shard_map/ppermute | solution.py:432
  21.6 2.8 %collective-permute-start.6 = (bf16[64,128]{1,0:T(8,128)(2,1)S(1)}, bf16[64,128]{1,0:T(8,128)(2,1)S(1)}, u32[]{:S(2)}, u32[]{:S(2)}) collective-permute-start(bf16[64,128]{1,0:T(8,128)(2,1)S(1)} %add_convert_fusion.2.refs_0_), channel_id=1, source_target_pairs={{0,3},{1,0},{2,1},{3,2},{4,7},{5,4},{6,5},{7,6},{8,11},{9,8},{10,9... | collective-permute-start | bytes 49160 | tf_op jit(solution)/shard_map/ppermute | solution.py:432
  29.6 5.7 %collective-permute-start.7 = (bf16[64,128]{1,0:T(8,128)(2,1)S(1)}, bf16[64,128]{1,0:T(8,128)(2,1)S(1)}, u32[]{:S(2)}, u32[]{:S(2)}) collective-permute-start(bf16[64,128]{1,0:T(8,128)(2,1)S(1)} %get-tuple-element.37), channel_id=1, source_target_pairs={{0,1},{1,2},{2,3},{3,0},{4,5},{5,6},{6,7},{7,4},{8,9},{9,10},{10,1... | collective-permute-start | bytes 49160 | tf_op jit(solution)/shard_map/ppermute | solution.py:432
  31.4 3.9 %collective-permute-start.8 = (bf16[64,128]{1,0:T(8,128)(2,1)S(1)}, bf16[64,128]{1,0:T(8,128)(2,1)S(1)}, u32[]{:S(2)}, u32[]{:S(2)}) collective-permute-start(bf16[64,128]{1,0:T(8,128)(2,1)S(1)} %get-tuple-element.38), channel_id=1, source_target_pairs={{0,2},{1,3},{2,0},{3,1},{4,6},{5,7},{6,4},{7,5},{8,10},{9,11},{10,... | collective-permute-start | bytes 49160 | tf_op jit(solution)/shard_map/ppermute | solution.py:432
  32.2 3.3 %collective-permute-start.9 = (bf16[64,128]{1,0:T(8,128)(2,1)S(1)}, bf16[64,128]{1,0:T(8,128)(2,1)S(1)}, u32[]{:S(2)}, u32[]{:S(2)}) collective-permute-start(bf16[64,128]{1,0:T(8,128)(2,1)S(1)} %get-tuple-element.39), channel_id=1, source_target_pairs={{0,3},{1,0},{2,1},{3,2},{4,7},{5,4},{6,5},{7,6},{8,11},{9,8},{10,9... | collective-permute-start | bytes 49160 | tf_op jit(solution)/shard_map/ppermute | solution.py:432
  35.5 3.8 %collective-permute-start.10 = (bf16[64,128]{1,0:T(8,128)(2,1)S(1)}, bf16[64,128]{1,0:T(8,128)(2,1)S(1)}, u32[]{:S(2)}, u32[]{:S(2)}) collective-permute-start(bf16[64,128]{1,0:T(8,128)(2,1)S(1)} %add_convert_fusion.1), channel_id=1, source_target_pairs={{0,16},{16,0},{1,17},{17,1},{2,18},{18,2},{3,19},{19,3},{4,20},{20... | collective-permute-start | bytes 49160 | tf_op jit(solution)/shard_map/ppermute | solution.py:422
  39.4 14.0 %collective-permute-start.11 = (bf16[16,128]{1,0:T(8,128)(2,1)S(1)}, bf16[16,128]{1,0:T(8,128)(2,1)S(1)}, u32[]{:S(2)}, u32[]{:S(2)}) collective-permute-start(bf16[16,128]{1,0:T(8,128)(2,1)S(1)} %get-tuple-element.63), channel_id=1, source_target_pairs={{0,4},{1,5},{2,6},{3,7},{4,8},{5,9},{6,10},{7,11},{8,12},{9,13},{1... | collective-permute-start | bytes 12296 | tf_op jit(solution)/shard_map/ppermute | solution.py:432
  40.8 12.6 %collective-permute-start.12 = (bf16[16,128]{1,0:T(8,128)(2,1)S(1)}, bf16[16,128]{1,0:T(8,128)(2,1)S(1)}, u32[]{:S(2)}, u32[]{:S(2)}) collective-permute-start(bf16[16,128]{1,0:T(8,128)(2,1)S(1)} %get-tuple-element.62), channel_id=1, source_target_pairs={{0,8},{1,9},{2,10},{3,11},{4,12},{5,13},{6,14},{7,15},{8,0},{9,1},... | collective-permute-start | bytes 12296 | tf_op jit(solution)/shard_map/ppermute | solution.py:432
  41.3 12.1 %collective-permute-start.13 = (bf16[16,128]{1,0:T(8,128)(2,1)S(1)}, bf16[16,128]{1,0:T(8,128)(2,1)S(1)}, u32[]{:S(2)}, u32[]{:S(2)}) collective-permute-start(bf16[16,128]{1,0:T(8,128)(2,1)S(1)} %get-tuple-element.61), channel_id=1, source_target_pairs={{0,12},{1,13},{2,14},{3,15},{4,0},{5,1},{6,2},{7,3},{8,4},{9,5},{1... | collective-permute-start | bytes 12296 | tf_op jit(solution)/shard_map/ppermute | solution.py:432
